TPU v7x, 32 devices: a whole 2x2x4 slice. The times are simulated.
32 devices in a mesh: wide: 16 (over z, x, core), grp: 2 (over y).
Axes of the slice: x: 2, y: 2, z: 4, core: 2. Of those that a mesh axis runs over, the one named last changes fastest.
Arguments:
- measured: float32 [512, 16, 2048], P(('wide', 'grp')), may hold values from -192 to 192
- drift: int32 [512], replicated, may hold values from -4 to 4
- start_volume: float32 [16, 8, 2048], P('wide', 'grp'), may hold values from -6 to 6
Outputs:
- estimate: float32 [16, 8, 2048], P('wide', 'grp')
All inputs are finite; a program needn't handle non-finite values.
Results may differ from a plain program's by a relative error of at most 0.0001.
Values sent between devices are 32-bit elements; how exact they have to be, the bound alone decides.
No kernel may reach another device: no remote copies, remote signals or barrier semaphores. Data moves between devices by JAX's collectives and lax.ppermute only.
A program may use at most 128 MiB of HBM per device.

v0:
```python
from functools import reduce
import math

import jax
import jax.numpy as jnp
from jax import lax
from jax.sharding import PartitionSpec as P

ITERS = 2
DMAX = 4


TILT_MAX = math.pi / 4
SMOOTH_EPS = 0.05
TV_STEP = 0.1


def with_halo(block, sides, width):
    for axis, dim in sides:
        count = lax.axis_size(axis)
        forward = [(i, i + 1) for i in range(count - 1)]
        backward = [(target, source) for source, target in forward]
        low = lax.ppermute(
            lax.slice_in_dim(block, block.shape[dim] - width, None, axis=dim), axis, forward
        )
        high = lax.ppermute(lax.slice_in_dim(block, 0, width, axis=dim), axis, backward)
        block = jnp.concatenate([low, block, high], axis=dim)
    return block


def geometry(angle_ids, drift_vals, total_angles, rows, band_extent):
    angle_rad = TILT_MAX * (2.0 * angle_ids.astype(jnp.float32) / (total_angles - 1) - 1.0)
    secant = 1.0 / jnp.cos(angle_rad)
    height = jnp.arange(rows, dtype=jnp.float32) - (rows - 1) / 2.0
    offsets = jnp.arange(2 * band_extent + 1, dtype=jnp.float32) - band_extent
    shifts = height[None, :] * jnp.tan(angle_rad)[:, None] - drift_vals.astype(jnp.float32)[:, None]
    weight_factors = secant[:, None, None] * jnp.maximum(
        0.0, 1.0 - jnp.abs(shifts[:, :, None] - offsets[None, None, :])
    )
    return (weight_factors, jnp.cos(angle_rad) / rows)


def secant_sum(total_angles):
    angle_rad = TILT_MAX * (
        2.0 * jnp.arange(total_angles, dtype=jnp.float32) / (total_angles - 1) - 1.0
    )
    return jnp.sum(1.0 / jnp.cos(angle_rad))


def local_geometry(angle_ids, drift, total_angles, rows_all, band_extent):
    matches = angle_ids[:, None] == jnp.arange(total_angles, dtype=jnp.int32)[None, :]
    local_drift = jnp.sum(jnp.where(matches, drift[None, :], 0), axis=1)
    return geometry(angle_ids, local_drift, total_angles, rows_all, band_extent)


def apply_correction(
    row_band_strip, measurement_part, weight_factors, residual_scale, global_scale, band_extent
):
    col_count = row_band_strip.shape[2]
    span = 2 * band_extent + 1
    padded = jnp.pad(row_band_strip, ((0, 0), (0, 0), (band_extent, band_extent)))
    shifted = jnp.stack(
        [padded[:, :, shift_id : shift_id + col_count] for shift_id in range(span)], axis=2
    )
    forward_projected = jnp.einsum(
        "ark,zrku->azu", weight_factors, shifted, precision=lax.Precision.HIGHEST
    )
    residual_error = residual_scale[:, None, None] * (measurement_part - forward_projected)
    spread = jnp.einsum(
        "ark,azu->kzru", weight_factors, residual_error, precision=lax.Precision.HIGHEST
    )
    spread = jnp.pad(spread, ((0, 0), (0, 0), (0, 0), (band_extent, band_extent)))
    pieces = [
        spread[shift_id, :, :, 2 * band_extent - shift_id : 2 * band_extent - shift_id + col_count]
        for shift_id in range(span)
    ]
    return global_scale * reduce(lambda left, right: left + right, pieces)


def divergence(extended, z_first, r_first, zcount, rcount):
    plane_count, height, col_count = extended.shape
    z_index = z_first + jnp.arange(plane_count, dtype=jnp.int32)[:, None, None]
    row_index = r_first + jnp.arange(height, dtype=jnp.int32)[None, :, None]
    col_index = jnp.arange(col_count, dtype=jnp.int32)[None, None, :]
    diff_z = jnp.concatenate([extended[1:] - extended[:-1], jnp.zeros_like(extended[:1])], axis=0)
    diff_z = jnp.where((z_index >= 0) & (z_index < zcount - 1), diff_z, 0.0)
    diff_r = jnp.concatenate(
        [extended[:, 1:] - extended[:, :-1], jnp.zeros_like(extended[:, :1])], axis=1
    )
    diff_r = jnp.where((row_index >= 0) & (row_index < rcount - 1), diff_r, 0.0)
    diff_c = jnp.concatenate(
        [extended[:, :, 1:] - extended[:, :, :-1], jnp.zeros_like(extended[:, :, :1])], axis=2
    )
    diff_c = jnp.where(col_index < col_count - 1, diff_c, 0.0)
    magnitude = jnp.sqrt(
        diff_z * diff_z + diff_r * diff_r + diff_c * diff_c + SMOOTH_EPS * SMOOTH_EPS
    )
    unit_z = diff_z / magnitude
    unit_r = diff_r / magnitude
    unit_c = diff_c / magnitude
    back_c = unit_c - jnp.concatenate([jnp.zeros_like(unit_c[:, :, :1]), unit_c[:, :, :-1]], axis=2)
    return (
        unit_z[1:-1, 1:-1]
        - unit_z[:-2, 1:-1]
        + (unit_r[1:-1, 1:-1] - unit_r[1:-1, :-2])
        + back_c[1:-1, 1:-1]
    )


def on_device(measured, drift, start_volume):
    wide_count = lax.axis_size("wide")
    groups = lax.axis_size("grp")
    slab_count, rows_tile, col_count = start_volume.shape
    rows_all = rows_tile * groups
    band_extent = rows_all // 2 + DMAX + 2
    per_device = measured.shape[0]
    total_angles = per_device * wide_count * groups
    global_scale = 1.0 / secant_sum(total_angles)
    z_first = lax.axis_index("wide") * slab_count - 1
    zcount = slab_count * wide_count
    local_measurement = lax.all_to_all(measured, "wide", split_axis=1, concat_axis=0, tiled=True)
    bin_position = jnp.arange(local_measurement.shape[0], dtype=jnp.int32)
    angle_ids = (
        bin_position // per_device * groups + lax.axis_index("grp")
    ) * per_device + bin_position % per_device
    weight_factors, residual_scale = local_geometry(
        angle_ids, drift, total_angles, rows_all, band_extent
    )
    own_tile = start_volume
    r_first = lax.axis_index("grp") * rows_tile - 1
    for sweep in range(ITERS):
        row_band_strip = lax.all_gather(own_tile, "grp", axis=1, tiled=True)
        volume_update = apply_correction(
            row_band_strip,
            local_measurement,
            weight_factors,
            residual_scale,
            global_scale,
            band_extent,
        )
        own_tile = own_tile + lax.psum_scatter(
            volume_update, "grp", scatter_dimension=1, tiled=True
        )
        extended = with_halo(own_tile, (("wide", 0), ("grp", 1)), 1)
        own_tile = own_tile + TV_STEP * divergence(extended, z_first, r_first, zcount, rows_all)
    return own_tile


def solution(mesh):
    in_specs = (P(("wide", "grp"), None, None), P(), P("wide", "grp", None))
    out_specs = P("wide", "grp", None)
    return jax.shard_map(
        on_device, mesh=mesh, in_specs=in_specs, out_specs=out_specs, check_vma=False
    )
```

profile of v0, /device:TPU:0, one launch (start us, length us, event | category | flops | bytes accessed | tf_op | source)
XLA Modules:
  0.0 172.8 jit_solution(17510084264592135695)
XLA Ops:
  6.5 4.2 %copy.35 = f32[16,16,2048]{2,0,1:T(8,128)} copy(f32[16,16,2048]{2,1,0:T(8,128)} %param.3) | data formatting | bytes 4194304 | tf_op args[0]
  10.7 7.5 %all-to-all-start = ((f32[16,16,2048]{2,0,1:T(8,128)}), f32[16,16,2048]{2,0,1:T(8,128)S(1)}, u32[]{:S(2)}, u32[]{:S(2)}) async-start(f32[16,16,2048]{2,0,1:T(8,128)} %copy.35), calls=%async_computation | async-start | bytes 4194304 | tf_op jit(solution)/shard_map/all_to_all | solution.py:121
  18.3 0.2 select_reduce_fusion
  18.5 0.7 fusion.88
  19.9 0.6 dynamic-slice
  21.1 4.6 %all_gather.6 = f32[1,8,2048]{2,0,1:T(1,128)S(1)} all-gather(f32[1,4,2048]{2,0,1:T(1,128)S(1)} %copy.56), channel_id=1, replica_groups=mesh['wide'=16,'grp'=2] {'grp'}, dimensions={1}, use_global_device_ids=true | all-gather | bytes 98304 | tf_op jit(solution)/shard_map/all_gather | solution.py:132
  25.7 0.3 slice_bitcast_fusion.2
  26.1 1.3 slice_bitcast_fusion
  27.4 1.3 slice_bitcast_fusion.1
  28.6 4.1 %stack.153 = f32[1,8,21,2048]{3,2,1,0:T(8,128)} concatenate(f32[1,8,1,2048]{3,2,1,0:T(1,128)S(1)} %get-tuple-element.36, f32[1,8,1,2048]{3,2,1,0:T(1,128)S(1)} %get-tuple-element.18, f32[1,8,1,2048]{3,2,1,0:T(1,128)S(1)} %get-tuple-element.19, f32[1,8,1,2048]{3,2,1,0:T(1,128)S(1)} %get-tuple-element.20, f32[1,8,1,2048]{3,2,1,0:T(1,128)S(1)} %get-tuple-element.21, ...), dimensions={2} | concatenate | bytes 2752512 | tf_op jit(solution)/shard_map/stack | solution.py:62
  33.0 26.3 %all-to-all-done = f32[16,16,2048]{2,0,1:T(8,128)S(1)} async-done(((f32[16,16,2048]{2,0,1:T(8,128)}), f32[16,16,2048]{2,0,1:T(8,128)S(1)}, u32[]{:S(2)}, u32[]{:S(2)}) %all-to-all-start) | async-done | bytes 2097184 | tf_op jit(solution)/shard_map/all_to_all | solution.py:121
  59.3 3.5 %fusion.2 = f32[256,2048,1]{1,0,2:T(8,128)S(1)} fusion(f32[256,2048]{1,0:T(8,128)S(1)} %bitcast.239, f32[1,8,21,2048]{3,2,1,0:T(8,128)} %stack.153, f32[256]{0:T(256)S(1)} %get-tuple-element.38, f32[21]{0:T(128)S(1)} %iota_add_fusion, f32[256,8]{0,1:T(8,128)S(1)} %multiply_subtract_fusion, f32[256]{0:T(256)S(1)} %get-tuple-element.37), kind=kOutput, calls=%fused_computation.4 | convolution fusion | flops 1058228224 | bytes 5580884 | tf_op jit(solution)/shard_map/ark,zrku->azu/dot_general | solution.py:65
  62.8 1.7 convolution_bitcast_fusion.3
  64.5 3.9 %fusion.83 = f32[1,8,2048]{2,0,1:T(1,128)} fusion(f32[21,1,8,2048]{3,0,2,1:T(8,128)S(1)} %convolution_bitcast_fusion.3, f32[]{:T(128)S(6)} %div.60), kind=kLoop, calls=%fused_computation.187 | loop fusion | flops 344064 | bytes 1703940 | tf_op jit(solution)/shard_map/mul | solution.py:77
  68.5 27.4 %all-reduce.17.cloned.1.call-done = f32[1,8,2048]{2,0,1:T(1,128)} async-done(((f32[1,8,2048]{2,0,1:T(1,128)}), f32[1,8,2048]{2,0,1:T(1,128)}) %all-reduce.17.cloned.1.call-update) | async-done | bytes 65552
  95.9 0.8 dynamic-slice_add_fusion.1
  96.7 1.3 collective-permute-start.1
  98.0 3.0 %collective-permute-start = (f32[1,4,2048]{2,0,1:T(1,128)S(1)}, f32[1,4,2048]{2,0,1:T(1,128)S(1)}, u32[]{:S(2)}, u32[]{:S(2)}) collective-permute-start(f32[1,4,2048]{2,0,1:T(1,128)S(1)} %dynamic-slice_add_fusion.1), channel_id=1, source_target_pairs={{0,2},{2,4},{4,6},{6,8},{8,10},{10,12},{12,14},{14,16},{16,18},{18... | collective-permute-start | bytes 98312 | tf_op jit(solution)/shard_map/ppermute | solution.py:23
  101.1 0.8 collective-permute-done
  102.0 1.3 collective-permute-start.3
  103.3 4.5 %collective-permute-start.2 = (f32[3,1,2048]{2,0,1:T(4,128)S(1)}, f32[3,1,2048]{2,0,1:T(4,128)S(1)}, u32[]{:S(2)}, u32[]{:S(2)}) collective-permute-start(f32[3,1,2048]{2,0,1:T(4,128)S(1)} %get-tuple-element.15), channel_id=1, source_target_pairs={{0,1},{2,3},{4,5},{6,7},{8,9},{10,11},{12,13},{14,15},{16,17},{18,... | collective-permute-start | bytes 73736 | tf_op jit(solution)/shard_map/ppermute | solution.py:23
  107.8 1.7 %collective-permute-done.2 = f32[3,1,2048]{2,0,1:T(4,128)S(1)} collective-permute-done((f32[3,1,2048]{2,0,1:T(4,128)S(1)}, f32[3,1,2048]{2,0,1:T(4,128)S(1)}, u32[]{:S(2)}, u32[]{:S(2)}) %collective-permute-start.2) | collective-permute-done | bytes 24608 | tf_op jit(solution)/shard_map/ppermute | solution.py:23
  109.6 0.1 pad_maximum_fusion
  109.8 0.2 slice_subtract_fusion.1
  109.9 0.1 maximum_subtract_fusion
  110.0 0.3 fusion.9
  110.4 0.1 fusion.10
  110.5 0.2 multiply_add_fusion.1
  110.6 5.2 %all_gather.7 = f32[1,8,2048]{2,0,1:T(1,128)S(1)} all-gather(f32[1,4,2048]{2,0,1:T(1,128)S(1)} %multiply_add_fusion.1), channel_id=1, replica_groups=mesh['wide'=16,'grp'=2] {'grp'}, dimensions={1}, use_global_device_ids=true | all-gather | bytes 98304 | tf_op jit(solution)/shard_map/all_gather | solution.py:132
  116.0 0.1 bitcast_dynamic-update-slice_fusion.18
  116.1 0.1 bitcast_dynamic-update-slice_fusion.17
  116.2 0.1 bitcast_dynamic-update-slice_fusion.16
  116.3 0.1 bitcast_dynamic-update-slice_fusion.15
  116.4 0.1 bitcast_dynamic-update-slice_fusion.14
  116.5 0.1 bitcast_dynamic-update-slice_fusion.13
  116.6 0.1 bitcast_dynamic-update-slice_fusion.12
  116.6 0.1 bitcast_dynamic-update-slice_fusion.11
  116.8 0.1 bitcast_dynamic-update-slice_fusion.9
  116.9 0.1 bitcast_dynamic-update-slice_fusion.8
  117.0 0.1 bitcast_dynamic-update-slice_fusion.7
  117.1 0.1 bitcast_dynamic-update-slice_fusion.6
  117.2 0.1 bitcast_dynamic-update-slice_fusion.5
  117.3 0.1 bitcast_dynamic-update-slice_fusion.4
  117.4 0.1 bitcast_dynamic-update-slice_fusion.3
  117.5 0.1 bitcast_dynamic-update-slice_fusion.2
  117.5 0.1 bitcast_dynamic-update-slice_fusion.1
  117.6 2.9 %fusion.5 = f32[256,2048,1]{1,0,2:T(8,128)S(1)} fusion(f32[256,2048]{1,0:T(8,128)S(1)} %bitcast.240, f32[8,21,2048]{2,0,1:T(8,128)S(1)} %bitcast.244, f32[256]{0:T(256)S(1)} %get-tuple-element.38, f32[21]{0:T(128)S(1)} %iota_add_fusion, f32[256,8]{0,1:T(8,128)S(1)} %multiply_subtract_fusion, f32[256]{0:T(256)S(1)} %get-tuple-element.37), kind=kOutput, calls=%fused_computation.7 | convolution fusion | flops 1058228224 | bytes 5580884 | tf_op jit(solution)/shard_map/ark,zrku->azu/dot_general | solution.py:65
  120.5 1.7 convolution_bitcast_fusion.2
  122.2 3.9 %fusion.82 = f32[1,8,2048]{2,0,1:T(1,128)} fusion(f32[21,1,8,2048]{3,0,2,1:T(8,128)S(1)} %convolution_bitcast_fusion.2, f32[]{:T(128)S(6)} %div.60), kind=kLoop, calls=%fused_computation.186 | loop fusion | flops 344064 | bytes 1703940 | tf_op jit(solution)/shard_map/mul | solution.py:77
  126.1 24.5 %all-reduce.19.cloned.1.call-done = f32[1,8,2048]{2,0,1:T(1,128)} async-done(((f32[1,8,2048]{2,0,1:T(1,128)}), f32[1,8,2048]{2,0,1:T(1,128)}) %all-reduce.19.cloned.1.call-update) | async-done | bytes 65552
  150.6 0.8 dynamic-slice_add_fusion
  151.4 1.3 collective-permute-start.5
  152.7 3.0 %collective-permute-start.4 = (f32[1,4,2048]{2,0,1:T(1,128)S(1)}, f32[1,4,2048]{2,0,1:T(1,128)S(1)}, u32[]{:S(2)}, u32[]{:S(2)}) collective-permute-start(f32[1,4,2048]{2,0,1:T(1,128)S(1)} %dynamic-slice_add_fusion), channel_id=1, source_target_pairs={{0,2},{2,4},{4,6},{6,8},{8,10},{10,12},{12,14},{14,16},{16,18},{18... | collective-permute-start | bytes 98312 | tf_op jit(solution)/shard_map/ppermute | solution.py:23
  155.7 0.8 collective-permute-done.4
  156.6 1.3 collective-permute-start.7
  157.9 4.5 %collective-permute-start.6 = (f32[3,1,2048]{2,0,1:T(4,128)S(1)}, f32[3,1,2048]{2,0,1:T(4,128)S(1)}, u32[]{:S(2)}, u32[]{:S(2)}) collective-permute-start(f32[3,1,2048]{2,0,1:T(4,128)S(1)} %get-tuple-element.13), channel_id=1, source_target_pairs={{0,1},{2,3},{4,5},{6,7},{8,9},{10,11},{12,13},{14,15},{16,17},{18,... | collective-permute-start | bytes 73736 | tf_op jit(solution)/shard_map/ppermute | solution.py:23
  162.5 1.7 %collective-permute-done.6 = f32[3,1,2048]{2,0,1:T(4,128)S(1)} collective-permute-done((f32[3,1,2048]{2,0,1:T(4,128)S(1)}, f32[3,1,2048]{2,0,1:T(4,128)S(1)}, u32[]{:S(2)}, u32[]{:S(2)}) %collective-permute-start.6) | collective-permute-done | bytes 24608 | tf_op jit(solution)/shard_map/ppermute | solution.py:23
  164.2 0.1 pad_maximum_fusion.1
  164.4 0.2 slice_subtract_fusion
  164.6 0.1 maximum_subtract_fusion.1
  164.7 0.3 fusion.8
  165.0 0.1 fusion.11
  165.1 0.2 multiply_add_fusion
  165.3 0.6 copy.59
  (34 shorter events, 0.9 us)
Async XLA Ops:
  10.7 7.6 %copy-start = (f32[1,4,2048]{2,1,0:T(4,128)S(1)}, f32[1,4,2048]{2,1,0:T(4,128)}, u32[]{:S(2)}) copy-start(f32[1,4,2048]{2,1,0:T(4,128)} %param.5) | copy-start | bytes 98308
  10.7 7.6 %copy-start.1 = (s32[512]{0:T(512)S(1)}, s32[512]{0:T(512)}, u32[]{:S(2)}) copy-start(s32[512]{0:T(512)} %param.4) | copy-start | bytes 6148
  10.7 9.2 %copy-start.2 = (u32[32]{0:T(128)S(1)}, u32[32]{0:T(128)}, u32[]{:S(2)}) copy-start(u32[32]{0:T(128)} %constant.133) | copy-start | bytes 388
  10.7 48.6 %all-to-all-start = ((f32[16,16,2048]{2,0,1:T(8,128)}), f32[16,16,2048]{2,0,1:T(8,128)S(1)}, u32[]{:S(2)}, u32[]{:S(2)}) async-start(f32[16,16,2048]{2,0,1:T(8,128)} %copy.35), calls=%async_computation | async-start | bytes 4194304 | tf_op jit(solution)/shard_map/all_to_all | solution.py:121
  18.2 77.7 %all-reduce.17.cloned.1.call-start = ((), (), s32[]{:S(2)}) async-start(), calls=%async_computation.1 | async-start | bytes 131072
  68.5 82.1 %all-reduce.19.cloned.1.call-start = ((), (), s32[]{:S(2)}) async-start(), calls=%async_computation.2 | async-start | bytes 131072
  96.7 4.4 %collective-permute-start.1 = (f32[1,4,2048]{2,0,1:T(1,128)S(1)}, f32[1,4,2048]{2,0,1:T(1,128)S(1)}, u32[]{:S(2)}, u32[]{:S(2)}) collective-permute-start(f32[1,4,2048]{2,0,1:T(1,128)S(1)} %dynamic-slice_add_fusion.1), channel_id=1, source_target_pairs={{2,0},{4,2},{6,4},{8,6},{10,8},{12,10},{14,12},{16,14},{18,16},{20... | collective-permute-start | bytes 98312 | tf_op jit(solution)/shard_map/ppermute | solution.py:26
  98.0 3.9 %collective-permute-start = (f32[1,4,2048]{2,0,1:T(1,128)S(1)}, f32[1,4,2048]{2,0,1:T(1,128)S(1)}, u32[]{:S(2)}, u32[]{:S(2)}) collective-permute-start(f32[1,4,2048]{2,0,1:T(1,128)S(1)} %dynamic-slice_add_fusion.1), channel_id=1, source_target_pairs={{0,2},{2,4},{4,6},{6,8},{8,10},{10,12},{12,14},{14,16},{16,18},{18... | collective-permute-start | bytes 98312 | tf_op jit(solution)/shard_map/ppermute | solution.py:23
  102.0 5.9 %collective-permute-start.3 = (f32[3,1,2048]{2,0,1:T(4,128)S(1)}, f32[3,1,2048]{2,0,1:T(4,128)S(1)}, u32[]{:S(2)}, u32[]{:S(2)}) collective-permute-start(f32[3,1,2048]{2,0,1:T(4,128)S(1)} %get-tuple-element.16), channel_id=1, source_target_pairs={{1,0},{3,2},{5,4},{7,6},{9,8},{11,10},{13,12},{15,14},{17,16},{19,... | collective-permute-start | bytes 73736 | tf_op jit(solution)/shard_map/ppermute | solution.py:26
  103.3 6.3 %collective-permute-start.2 = (f32[3,1,2048]{2,0,1:T(4,128)S(1)}, f32[3,1,2048]{2,0,1:T(4,128)S(1)}, u32[]{:S(2)}, u32[]{:S(2)}) collective-permute-start(f32[3,1,2048]{2,0,1:T(4,128)S(1)} %get-tuple-element.15), channel_id=1, source_target_pairs={{0,1},{2,3},{4,5},{6,7},{8,9},{10,11},{12,13},{14,15},{16,17},{18,... | collective-permute-start | bytes 73736 | tf_op jit(solution)/shard_map/ppermute | solution.py:23
  151.4 4.3 %collective-permute-start.5 = (f32[1,4,2048]{2,0,1:T(1,128)S(1)}, f32[1,4,2048]{2,0,1:T(1,128)S(1)}, u32[]{:S(2)}, u32[]{:S(2)}) collective-permute-start(f32[1,4,2048]{2,0,1:T(1,128)S(1)} %dynamic-slice_add_fusion), channel_id=1, source_target_pairs={{2,0},{4,2},{6,4},{8,6},{10,8},{12,10},{14,12},{16,14},{18,16},{20... | collective-permute-start | bytes 98312 | tf_op jit(solution)/shard_map/ppermute | solution.py:26
  152.7 3.9 %collective-permute-start.4 = (f32[1,4,2048]{2,0,1:T(1,128)S(1)}, f32[1,4,2048]{2,0,1:T(1,128)S(1)}, u32[]{:S(2)}, u32[]{:S(2)}) collective-permute-start(f32[1,4,2048]{2,0,1:T(1,128)S(1)} %dynamic-slice_add_fusion), channel_id=1, source_target_pairs={{0,2},{2,4},{4,6},{6,8},{8,10},{10,12},{12,14},{14,16},{16,18},{18... | collective-permute-start | bytes 98312 | tf_op jit(solution)/shard_map/ppermute | solution.py:23
  156.6 5.9 %collective-permute-start.7 = (f32[3,1,2048]{2,0,1:T(4,128)S(1)}, f32[3,1,2048]{2,0,1:T(4,128)S(1)}, u32[]{:S(2)}, u32[]{:S(2)}) collective-permute-start(f32[3,1,2048]{2,0,1:T(4,128)S(1)} %get-tuple-element.14), channel_id=1, source_target_pairs={{1,0},{3,2},{5,4},{7,6},{9,8},{11,10},{13,12},{15,14},{17,16},{19,... | collective-permute-start | bytes 73736 | tf_op jit(solution)/shard_map/ppermute | solution.py:26
  157.9 6.3 %collective-permute-start.6 = (f32[3,1,2048]{2,0,1:T(4,128)S(1)}, f32[3,1,2048]{2,0,1:T(4,128)S(1)}, u32[]{:S(2)}, u32[]{:S(2)}) collective-permute-start(f32[3,1,2048]{2,0,1:T(4,128)S(1)} %get-tuple-element.13), channel_id=1, source_target_pairs={{0,1},{2,3},{4,5},{6,7},{8,9},{10,11},{12,13},{14,15},{16,17},{18,... | collective-permute-start | bytes 73736 | tf_op jit(solution)/shard_map/ppermute | solution.py:23
Sparse Core Ops, SparseCore 0:
  68.6 27.3 all-reduce.16
  126.2 24.3 all-reduce.18
where the time goes:
time: 176 us; the launch traced here: 173 us
  waiting for transfers between devices  83.4 us (47%)
  starting transfers between devices  27.9 us (16%)
  between operations  15.1 us (9%)
  local copies, waits for them, and re-layouts  14.2 us (8%)
  other arithmetic  12.6 us (7%)
  matrix products  9.81 us (6%)
  blocking collectives  9.8 us (6%)
    unnamed x4, waiting for transfers between devices  51.9 us
    all_to_all x1, waiting for transfers between devices, on_device(): lax.all_to_all(measured, 'wide', split_axis=1, concat_axis=0, tiled=True)  26.3 us
    ppermute x4, starting transfers between devices, with_halo(): lax.ppermute(lax.slice_in_dim(block, block.shape[dim] - width, None, axis...  15.2 us
    all_gather x2, blocking collectives, on_device(): row_band_strip = lax.all_gather(own_tile, 'grp', axis=1, tiled=True)  9.8 us
    mul x2, other arithmetic, apply_correction(): return global_scale * reduce(lambda left, right: left + right, pieces)  7.75 us
    all_to_all x1, starting transfers between devices, on_device(): lax.all_to_all(measured, 'wide', split_axis=1, concat_axis=0, tiled=True)  7.49 us
    another operation x5, local copies, waits for them, and re-layouts, apply_correction(): jnp.stack([padded[:, :, shift_id:shift_id + col_count] for shift_id in ra...  7.13 us
    unnamed x29, local copies, waits for them, and re-layouts  6.43 us
  transfers between devices with their start and end apart: 11, of which 7 were waited for; matrix products, arithmetic and copies ran while one was open for 5% of the time, Pallas kernels for 0%

commit v1 on v0

--- a/solution.py
+++ b/solution.py
@@ -1,9 +1,13 @@
+import functools
 from functools import reduce
 import math
 
 import jax
 import jax.numpy as jnp
+import numpy as np
 from jax import lax
+from jax.experimental import pallas as pl
+from jax.experimental.pallas import tpu as pltpu
 from jax.sharding import PartitionSpec as P
 
 ITERS = 2
@@ -146,9 +150,454 @@
     return own_tile
 
 
+LANES = 128
+SUB = 8
+HALO = 64
+
+
+def tan_and_secant(total_angles):
+    angle = TILT_MAX * (2.0 * np.arange(total_angles) / (total_angles - 1) - 1.0)
+    return np.tan(angle), 1.0 / np.cos(angle)
+
+
+def coords():
+    wide, y = lax.axis_index("wide"), lax.axis_index("grp")
+    return wide // 4, wide // 2 % 2, wide % 2, y
+
+
+def move(value, target):
+    pairs = []
+    for z in range(4):
+        for x in range(2):
+            for c in range(2):
+                for y in range(2):
+                    to = target(z, x, c, y)
+                    if to is not None and 0 <= to[0] < 4:
+                        tz, tx, tc, ty = to
+                        pairs.append((((z * 2 + x) * 2 + c) * 2 + y, ((tz * 2 + tx) * 2 + tc) * 2 + ty))
+    return lax.ppermute(value, ("wide", "grp"), pairs)
+
+
+def split_rows(value):
+    high = value.astype(jnp.bfloat16).astype(jnp.float32)
+    return jnp.concatenate([high, value - high], axis=0)
+
+
+def split_terms(value):
+    high = value.astype(jnp.bfloat16)
+    low = (value - high.astype(jnp.float32)).astype(jnp.bfloat16)
+    return jnp.concatenate([high, low], axis=0)
+
+
+def lane_iota(shape):
+    return lax.broadcasted_iota(jnp.int32, shape, len(shape) - 1)
+
+
+def row_iota(shape):
+    return lax.broadcasted_iota(jnp.int32, shape, len(shape) - 2)
+
+
+def back_project_kernel(
+    sibling, views, slices, rows, half_cols, band, scale, tan_ref, drift_ref, meas_ref, out_ref, buf, sem
+):
+    in_cols = half_cols + LANES
+    z, x, c, y = coords()
+    half = 1 - c if sibling else c
+    first = pl.multiple_of(half * (half_cols - LANES), LANES)
+    tiles = in_cols // LANES
+    copies = [
+        pltpu.make_async_copy(meas_ref.at[:, pl.ds(first + t * LANES, LANES)], buf.at[t + 1], sem.at[t])
+        for t in range(tiles)
+    ]
+    for copy in copies:
+        copy.start()
+    buf[0] = jnp.zeros((views * slices, LANES), jnp.float32)
+    buf[tiles + 1] = jnp.zeros((views * slices, LANES), jnp.float32)
+    first_view = (((z * 2 + x) * 2 + c) * 2 + y) * views
+    step = 7
+    parts = 2 * band // step + 1
+    shape = (parts * rows, step * views)
+    lane, row = lane_iota(shape), row_iota(shape)
+    view_of = lane % views
+    tan_lane = jnp.zeros(shape, jnp.float32)
+    drift_lane = jnp.zeros(shape, jnp.float32)
+    for a in range(views):
+        tan_lane = jnp.where(view_of == a, tan_ref[first_view + a], tan_lane)
+        drift_lane = jnp.where(view_of == a, drift_ref[first_view + a].astype(jnp.float32), drift_lane)
+    shift = ((row % rows).astype(jnp.float32) - (rows - 1) / 2.0) * tan_lane - drift_lane
+    offset = ((row // rows) * step + lane // views - band).astype(jnp.float32)
+    weights = (scale / rows) * jnp.maximum(0.0, 1.0 - jnp.abs(shift - offset))
+    weights = split_rows(weights)
+    weights = jnp.concatenate([weights, weights], axis=1).astype(jnp.bfloat16)
+    width = in_cols + LANES
+    for copy in copies:
+        copy.wait()
+
+    def one_slice(s, carry):
+        strip = jnp.concatenate([buf[half + t, pl.ds(s, views, stride=slices), :] for t in range(tiles + 1)], axis=1)
+        moved = jnp.concatenate(
+            [pltpu.roll(strip, width - (HALO + band - j), 1) for j in range(step)], axis=0
+        )
+        spread = jnp.dot(weights, split_terms(moved), preferred_element_type=jnp.float32)
+        spread = spread[: parts * rows] + spread[parts * rows :]
+        total = spread[0:rows]
+        for i in range(1, parts):
+            total = total + pltpu.roll(spread[i * rows : (i + 1) * rows], step * i, 1)
+        out_ref[s] = total[:, :in_cols]
+        return carry
+
+    lax.fori_loop(0, slices, one_slice, 0, unroll=2)
+
+
+def plane_pack_kernel(block, own_ref, got_ref, vol_ref, halo_ref, mine, to_x, to_y, to_xy, acc, vbuf):
+    slices, rows, half_cols = own_ref.shape
+    width = block + 2 * HALO
+    z, x, c, y = coords()
+    acc[...] = own_ref[...] + got_ref[...]
+    part = vol_ref.shape[1]
+    cols = vol_ref.shape[2]
+    vbuf[:, 0:LANES] = jnp.zeros((2 * part, LANES), jnp.float32)
+    vbuf[:, cols + LANES :] = jnp.zeros((2 * part, LANES), jnp.float32)
+    both = jnp.concatenate([vol_ref[0], halo_ref[0]], axis=0)
+    vbuf[:, LANES : LANES + cols] = both
+    for out, (px, py) in ((mine, (x, y)), (to_x, (1 - x, y)), (to_y, (x, 1 - y)), (to_xy, (1 - x, 1 - y))):
+        q = 2 * px + py
+        out[0:slices] = acc[:, :, pl.ds(pl.multiple_of(q * block, LANES), width)]
+        for h in range(2):
+            begin = pl.multiple_of((4 * h + q) * block, LANES)
+            window = vbuf[:, pl.ds(begin, width + LANES)]
+            window = pltpu.roll(window, width + LANES - HALO, 1)
+            out[slices + h] = window[:, :width]
+
+
+def depth_pack_kernel(mine, got_x, got_y, got_xy, own_win, to_1, to_2, to_3, vol_own, vol_sib, acc):
+    slices = mine.shape[0] - 2
+    rows = mine.shape[1]
+    part = rows // 2
+    z, x, c, y = coords()
+    acc[0:2] = jnp.zeros((2,) + acc.shape[1:], jnp.float32)
+    acc[slices + 2 :] = jnp.zeros((2,) + acc.shape[1:], jnp.float32)
+    acc[2 : slices + 2] = (mine[0:slices] + got_x[0:slices]) + (got_y[0:slices] + got_xy[0:slices])
+    for out, zz in (
+        (own_win, z),
+        (to_1, jnp.where(z % 2 == 0, z + 1, z - 1)),
+        (to_2, jnp.where(z < 2, z + 2, z - 2)),
+        (to_3, 3 - z),
+    ):
+        out[...] = acc[pl.ds(4 * zz, 8)]
+    for out, h in ((vol_own, c), (vol_sib, 1 - c)):
+        here, there = mine[slices + h], got_y[slices + h]
+        x_here, x_there = got_x[slices + h], got_xy[slices + h]
+        for source_x in range(2):
+            same = x == source_x
+            a = jnp.where(same, here, x_here)
+            b = jnp.where(same, there, x_there)
+            upper = jnp.where(y == 0, a, b)
+            lower = jnp.where(y == 0, b, a)
+            own_slice = jnp.concatenate([upper[:part], lower[:part]], axis=0)
+            halo_slice = jnp.concatenate([upper[part:], lower[part:]], axis=0)
+            out[1 + source_x] = own_slice
+            out[3 * source_x] = halo_slice
+
+
+def gram_kernel(rows, band, scale, tan_ref, sec_ref, drift_ref, after_ref, conv_ref, low_ref, high_ref):
+    views = tan_ref.shape[1]
+    span = 2 * band + 1
+    shape = (span * rows, views)
+    row = row_iota(shape)
+    shift = ((row % rows).astype(jnp.float32) - (rows - 1) / 2.0) * tan_ref[...] - drift_ref[...].astype(jnp.float32)
+    hat = jnp.maximum(0.0, 1.0 - jnp.abs(shift - (row // rows - band).astype(jnp.float32)))
+    gram = lax.dot_general(
+        hat * ((scale / rows) * sec_ref[...]),
+        hat,
+        (((1,), (1,)), ((), ())),
+        precision=lax.Precision.HIGHEST,
+        preferred_element_type=jnp.float32,
+    )
+    edge = band * rows
+    low_ref[...] = gram[edge + rows :, edge + rows :]
+    high_ref[...] = gram[:edge, :edge]
+    width = conv_ref.shape[1] // 2 * 3
+    padded = jnp.concatenate([gram, jnp.zeros((span * rows, width - span * rows), jnp.float32)], axis=1)
+    total = jnp.zeros((rows, width), jnp.float32)
+    for k in range(span):
+        total = total + pltpu.roll(padded[k * rows : (k + 1) * rows], rows * (2 * band - k), 1)
+    lanes = width // 3
+    stacked = jnp.concatenate([total[:, i * lanes : (i + 1) * lanes] for i in range(3)], axis=0)
+    stacked = split_rows(stacked)
+    conv_ref[...] = jnp.concatenate([stacked, stacked], axis=1)
+
+
+def normal(volumes, conv, low_ref, high_ref, out, band, is_low, is_high):
+    rows, width = volumes[0].shape
+    count = len(volumes)
+    step = conv.shape[1] // 2 // rows
+    parts = conv.shape[0] // 2 // rows
+    for s in range(count):
+        moved = jnp.concatenate(
+            [pltpu.roll(volumes[s], (2 * band - j) % width, 1) for j in range(step)], axis=0
+        )
+        spread = jnp.dot(conv, split_terms(moved), preferred_element_type=jnp.float32)
+        spread = spread[: parts * rows] + spread[parts * rows :]
+        total = spread[0:rows]
+        for i in range(1, parts):
+            total = total + pltpu.roll(spread[i * rows : (i + 1) * rows], width - step * i, 1)
+        out[s] = total
+
+    lane = lane_iota((rows, LANES))
+
+    @pl.when(is_low)
+    def _():
+        tiles = [v[:, :LANES] for v in volumes]
+        moved = jnp.concatenate(
+            [jnp.concatenate([pltpu.roll(t, LANES - k, 1) for k in range(1, band + 1)], axis=0) for t in tiles], axis=1
+        )
+        spread = jnp.dot(low_ref[...], moved, precision=lax.Precision.HIGHEST, preferred_element_type=jnp.float32)
+        for s in range(count):
+            total = jnp.zeros((rows, LANES), jnp.float32)
+            for k in range(1, band + 1):
+                piece = spread[(k - 1) * rows : k * rows, s * LANES : (s + 1) * LANES]
+                piece = jnp.where((lane >= HALO - band) & (lane < HALO), piece, 0.0)
+                total = total + pltpu.roll(piece, k, 1)
+            out[s, :, 0:LANES] = out[s, :, 0:LANES] - total
+
+    @pl.when(is_high)
+    def _():
+        tiles = [v[:, width - LANES :] for v in volumes]
+        moved = jnp.concatenate(
+            [jnp.concatenate([pltpu.roll(t, k, 1) for k in range(band, 0, -1)], axis=0) for t in tiles], axis=1
+        )
+        spread = jnp.dot(high_ref[...], moved, precision=lax.Precision.HIGHEST, preferred_element_type=jnp.float32)
+        for s in range(count):
+            total = jnp.zeros((rows, LANES), jnp.float32)
+            for k in range(band, 0, -1):
+                piece = spread[(band - k) * rows : (band - k + 1) * rows, s * LANES : (s + 1) * LANES]
+                piece = jnp.where((lane >= LANES - HALO) & (lane < LANES - HALO + band), piece, 0.0)
+                total = total + pltpu.roll(piece, LANES - k, 1)
+            out[s, :, width - LANES :] = out[s, :, width - LANES :] - total
+
+
+def block_place(block, total_cols):
+    z, x, c, y = coords()
+    index = (c * 2 + x) * 2 + y
+    return z, index * block - HALO, index == 0, index == total_cols // block - 1
+
+
+def first_normal_kernel(band, block, total_cols, vol_own, vol_sib, conv_ref, low_ref, high_ref, out, vols, work):
+    _, _, is_low, is_high = block_place(block, total_cols)
+    _, _, c, _ = coords()
+    for m in range(4):
+        vols[2 * m + c] = vol_own[m]
+        vols[2 * m + 1 - c] = vol_sib[m]
+    volumes = [vols[s] for s in range(8)]
+    normal(volumes, conv_ref[...].astype(jnp.bfloat16), low_ref, high_ref, work, band, is_low, is_high)
+    for s in range(8):
+        out[s] = volumes[s] - work[s]
+
+
+def variation_step(half, z_of, first_col, depth, total_cols):
+    rows, width = half[0].shape
+    col = first_col + lane_iota((rows, width))
+    row = row_iota((rows, width))
+    inside = (col >= 0) & (col < total_cols - 1)
+    units = []
+    for w in range(len(half) - 1):
+        v = half[w]
+        keep = (z_of(w) >= 0) & (z_of(w) < depth - 1)
+        dz = jnp.where(keep, half[w + 1] - v, 0.0)
+        dr = jnp.where(row < rows - 1, pltpu.roll(v, rows - 1, 0) - v, 0.0)
+        dc = jnp.where(inside, pltpu.roll(v, width - 1, 1) - v, 0.0)
+        inverse = 1.0 / jnp.sqrt(dz * dz + dr * dr + dc * dc + SMOOTH_EPS * SMOOTH_EPS)
+        units.append((dz * inverse, dr * inverse, dc * inverse))
+    result = []
+    for w in range(1, len(half) - 1):
+        uz, ur, uc = units[w]
+        div = (uz - units[w - 1][0]) + (ur - pltpu.roll(ur, 1, 0)) + (uc - pltpu.roll(uc, 1, 1))
+        result.append(jnp.where((col >= 0) & (col < total_cols), half[w] + TV_STEP * div, 0.0))
+    return result
+
+
+def finish_kernel(
+    band, block, depth, total_cols,
+    first_ref, own_win, got_1, got_2, got_3, conv_ref, low_ref, high_ref, keep_ref, send_ref, corr, work, done,
+):
+    z, first_col, is_low, is_high = block_place(block, total_cols)
+    _, _, c, _ = coords()
+    corr[...] = (own_win[...] + got_1[...]) + (got_2[...] + got_3[...])
+    half = [first_ref[s] + corr[s] for s in range(8)]
+    volumes = variation_step(half, lambda w: 4 * z - 2 + w, first_col, depth, total_cols)
+    normal(volumes, conv_ref[...].astype(jnp.bfloat16), low_ref, high_ref, work, band, is_low, is_high)
+    half = [volumes[s] + corr[s + 1] - work[s] for s in range(6)]
+    volumes = variation_step(half, lambda w: 4 * z - 1 + w, first_col, depth, total_cols)
+    width = volumes[0].shape[1]
+    for s in range(4):
+        done[s] = pltpu.roll(volumes[s], width - HALO, 1)[:, :block]
+    for px in range(2):
+        keep_ref[px] = done[2 * px + c]
+        send_ref[px] = done[2 * px + 1 - c]
+
+
+def result_pack_kernel(own_ref, got_ref, mine, to_x, to_y, to_xy):
+    z, x, c, y = coords()
+    part = own_ref.shape[1] // 2
+    for out, (px, py) in ((mine, (x, y)), (to_x, (1 - x, y)), (to_y, (x, 1 - y)), (to_xy, (1 - x, 1 - y))):
+        own, got = own_ref[px], got_ref[px]
+        out[c] = jnp.where(py == 0, own[:part], own[part:])
+        out[1 - c] = jnp.where(py == 0, got[:part], got[part:])
+
+
+def result_kernel(mine, got_x, got_y, got_xy, out):
+    z, x, c, y = coords()
+    block = mine.shape[2]
+    for ref, (px, py) in ((mine, (x, y)), (got_x, (1 - x, y)), (got_y, (x, 1 - y)), (got_xy, (1 - x, 1 - y))):
+        for h in range(2):
+            begin = pl.multiple_of((4 * h + 2 * px + py) * block, LANES)
+            out[0, :, pl.ds(begin, block)] = ref[h]
+
+
+def f32(*shape):
+    return jax.ShapeDtypeStruct(shape, jnp.float32)
+
+
+VMEM_SPEC = pl.BlockSpec(memory_space=pltpu.VMEM)
+SMEM_SPEC = pl.BlockSpec(memory_space=pltpu.SMEM)
+ANY_SPEC = pl.BlockSpec(memory_space=pl.ANY)
+PARAMS = pltpu.CompilerParams(vmem_limit_bytes=40 * 1024 * 1024)
+
+
+def kernel_call(body, outs, in_specs, scratch, name, flops=0, size=0):
+    many = isinstance(outs, (list, tuple))
+    return pl.pallas_call(
+        body,
+        out_shape=outs,
+        in_specs=in_specs,
+        out_specs=[VMEM_SPEC] * len(outs) if many else VMEM_SPEC,
+        scratch_shapes=scratch,
+        compiler_params=PARAMS,
+        name=name,
+        cost_estimate=pl.CostEstimate(flops=flops, bytes_accessed=size, transcendentals=0),
+    )
+
+
+def summed_plan(measured, drift, start_volume):
+    views, slices, cols = measured.shape
+    part = start_volume.shape[1]
+    rows = 2 * part
+    band = rows // 2 + DMAX + 2
+    total_angles = drift.shape[0]
+    block = cols // 8
+    half_cols = cols // 2
+    half_width = half_cols + LANES
+    width = block + 2 * HALO
+    tangent, secant = tan_and_secant(total_angles)
+    scale = float(1.0 / np.sum(secant))
+    tangent, secant = tangent.astype(np.float32), secant.astype(np.float32)
+
+    flat = measured.reshape(views * slices, cols)
+    halo = move(start_volume, lambda z, x, c, y: (z + 1, 0, c, y) if x else (z - 1, 1, c, y))
+
+    def back_project(sibling):
+        return kernel_call(
+            functools.partial(back_project_kernel, sibling, views, slices, rows, half_cols, band, scale),
+            f32(slices, rows, half_width),
+            [SMEM_SPEC, SMEM_SPEC, ANY_SPEC],
+            [
+                pltpu.VMEM((half_width // LANES + 2, views * slices, LANES), jnp.float32),
+                pltpu.SemaphoreType.DMA((half_width // LANES,)),
+            ],
+            "back_project_sibling" if sibling else "back_project_own",
+            flops=2 * 10**9,
+            size=2**21,
+        )(tangent, drift, flat)
+
+    got = move(back_project(True), lambda z, x, c, y: (z, x, 1 - c, y))
+    own = back_project(False)
+
+    message = f32(slices + 2, rows, width)
+    mine, to_x, to_y, to_xy = kernel_call(
+        functools.partial(plane_pack_kernel, block),
+        [message] * 4,
+        [VMEM_SPEC] * 4,
+        [pltpu.VMEM((slices, rows, half_width), jnp.float32), pltpu.VMEM((2 * part, cols + 2 * LANES), jnp.float32)],
+        "plane_pack",
+    )(own, got, start_volume, halo)
+    got_xy = move(to_xy, lambda z, x, c, y: (z, 1 - x, c, 1 - y))
+    got_x = move(to_x, lambda z, x, c, y: (z, 1 - x, c, y))
+    got_y = move(to_y, lambda z, x, c, y: (z, x, c, 1 - y))
+
+    edge = band * rows
+    conv, low, high = kernel_call(
+        functools.partial(gram_kernel, rows, band, scale),
+        [f32(6 * rows, 2 * LANES), f32(edge, edge), f32(edge, edge)],
+        [VMEM_SPEC] * 3 + [ANY_SPEC],
+        [],
+        "gram",
+        flops=10**9,
+    )(tangent[None], secant[None], drift[None], mine)
+
+    window = f32(8, rows, width)
+    own_win, to_1, to_2, to_3, vol_own, vol_sib = kernel_call(
+        depth_pack_kernel,
+        [window] * 4 + [f32(4, rows, width)] * 2,
+        [VMEM_SPEC] * 4,
+        [pltpu.VMEM((slices + 4, rows, width), jnp.float32)],
+        "depth_pack",
+    )(mine, got_x, got_y, got_xy)
+    got_2 = move(to_2, lambda z, x, c, y: (z ^ 2, x, c, y))
+    got_1 = move(to_1, lambda z, x, c, y: (z ^ 1, x, c, y))
+    got_3 = move(to_3, lambda z, x, c, y: (z ^ 3, x, c, y))
+    vol_got = move(vol_sib, lambda z, x, c, y: (z, x, 1 - c, y))
+
+    work = pltpu.VMEM((8, rows, width), jnp.float32)
+    first = kernel_call(
+        functools.partial(first_normal_kernel, band, block, cols),
+        window,
+        [VMEM_SPEC] * 5,
+        [work, work],
+        "first_normal",
+        flops=10**9,
+    )(vol_own, vol_got, conv, low, high)
+
+    piece = f32(2, rows, block)
+    keep, send = kernel_call(
+        functools.partial(finish_kernel, band, block, slices, cols),
+        [piece, piece],
+        [VMEM_SPEC] * 8,
+        [work, work, pltpu.VMEM((4, rows, block), jnp.float32)],
+        "finish",
+    )(first, own_win, got_1, got_2, got_3, conv, low, high)
+    swapped = move(send, lambda z, x, c, y: (z, x, 1 - c, y))
+    small = f32(2, part, block)
+    mine, to_x, to_y, to_xy = kernel_call(result_pack_kernel, [small] * 4, [VMEM_SPEC] * 2, [], "result_pack")(
+        keep, swapped
+    )
+    got_xy = move(to_xy, lambda z, x, c, y: (z, 1 - x, c, 1 - y))
+    got_x = move(to_x, lambda z, x, c, y: (z, 1 - x, c, y))
+    got_y = move(to_y, lambda z, x, c, y: (z, x, c, 1 - y))
+    return kernel_call(result_kernel, f32(1, part, cols), [VMEM_SPEC] * 4, [], "result")(mine, got_x, got_y, got_xy)
+
+
+def summed_plan_fits(mesh, measured, start_volume):
+    rows = start_volume.shape[1]
+    cols = measured.shape[2]
+    return (
+        ITERS == 2
+        and dict(mesh.shape) == {"wide": 16, "grp": 2}
+        and measured.shape[1] == start_volume.shape[0] == 16
+        and rows == SUB
+        and cols % (16 * LANES) == 0
+        and measured.shape[0] % 256 == 0
+    )
+
+
 def solution(mesh):
     in_specs = (P(("wide", "grp"), None, None), P(), P("wide", "grp", None))
     out_specs = P("wide", "grp", None)
-    return jax.shard_map(
-        on_device, mesh=mesh, in_specs=in_specs, out_specs=out_specs, check_vma=False
-    )
+
+    def run(measured, drift, start_volume):
+        plan = summed_plan if summed_plan_fits(mesh, measured, start_volume) else on_device
+        return jax.shard_map(plan, mesh=mesh, in_specs=in_specs, out_specs=out_specs, check_vma=False)(
+            measured, drift, start_volume
+        )
+
+    return run

time: 176 us -> 56.2 us (0.32); the launches traced: 173 us -> 56 us
  waiting for transfers between devices: 83.4 us -> 19.9 us
  Pallas kernels: 0 us -> 16.7 us
  between operations: 15.1 us -> 0.15 us
  other arithmetic: 12.6 us -> 0 us
  starting transfers between devices: 27.9 us -> 16.2 us
  local copies, waits for them, and re-layouts: 14.2 us -> 2.98 us
  matrix products: 9.81 us -> 0 us
  blocking collectives: 9.8 us -> 0 us
    unnamed x4 -> x0, waiting for transfers between devices: 51.9 us -> none
    all_to_all x1 -> x0, waiting for transfers between devices: 26.3 us -> none  [on_device(): lax.all_to_all(measured, 'wide', split_axis=1, concat_axis=0, tiled=True)]
    pallas_call x0 -> x9, Pallas kernels: none -> 16.7 us  [the longest x2 12.2 us: back_project(): kernel_call(functools.partial(back_project_kernel, sibling, views, slices...]
    ppermute x8 -> x13, waiting for transfers between devices: 5.15 us -> 19.9 us  [move(): return lax.ppermute(value, ('wide', 'grp'), pairs)]
    dot_general x4 -> x0, matrix products: 9.81 us -> none  [the longest x2 6.38 us: apply_correction(): jnp.einsum('ark,zrku->azu', weight_factors, shifted, precision=lax.Precis...]
    all_gather x2 -> x0, blocking collectives: 9.8 us -> none  [on_device(): row_band_strip = lax.all_gather(own_tile, 'grp', axis=1, tiled=True)]
    mul x2 -> x0, other arithmetic: 7.75 us -> none  [apply_correction(): return global_scale * reduce(lambda left, right: left + right, pieces)]
    all_to_all x1 -> x0, starting transfers between devices: 7.49 us -> none  [on_device(): lax.all_to_all(measured, 'wide', split_axis=1, concat_axis=0, tiled=True)]
  transfers between devices with their start and end apart: 11 -> 13, of which waited for: 7 -> 7; matrix products, arithmetic and copies ran while one was open for 5% -> 0% of each run, Pallas kernels for 0% -> 15%
where the time goes in v1:
time: 56.2 us; the launch traced here: 56 us
  waiting for transfers between devices  19.9 us (35%)
  Pallas kernels  16.7 us (30%)
  starting transfers between devices  16.2 us (29%)
  local copies, waits for them, and re-layouts  2.98 us (5%)
    ppermute x13, waiting for transfers between devices, move(): return lax.ppermute(value, ('wide', 'grp'), pairs)  19.9 us
    ppermute x13, starting transfers between devices, move(): return lax.ppermute(value, ('wide', 'grp'), pairs)  16.2 us
    pallas_call x2, Pallas kernels, back_project(): kernel_call(functools.partial(back_project_kernel, sibling, views, slices...  12.2 us
    unnamed x14, local copies, waits for them, and re-layouts  2.98 us
    pallas_call x1, Pallas kernels, summed_plan(): kernel_call(functools.partial(finish_kernel, band, block, slices, cols),...  1.57 us
    pallas_call x1, Pallas kernels, summed_plan(): kernel_call(functools.partial(first_normal_kernel, band, block, cols), wi...  1.38 us
  transfers between devices with their start and end apart: 13, of which 7 were waited for; matrix products, arithmetic and copies ran while one was open for 0% of the time, Pallas kernels for 15%

profile of v1, /device:TPU:0, one launch (start us, length us, event | category | flops | bytes accessed | tf_op | source)
XLA Modules:
  0.0 56.0 jit_solution(10904576880259292142)
XLA Ops:
  0.0 0.0 copy-start.1
  0.0 1.6 %copy-done.1 = f32[16,16,2048]{2,1,0:T(8,128)S(1)} copy-done((f32[16,16,2048]{2,1,0:T(8,128)S(1)}, f32[16,16,2048]{2,1,0:T(8,128)}, u32[]{:S(2)}) %copy-start.1) | copy-done | bytes 2097176
  1.6 0.0 copy-start.2
  1.6 0.7 %copy-done.2 = s32[512]{0:T(512)S(1)} copy-done((s32[512]{0:T(512)S(1)}, s32[512]{0:T(512)}, u32[]{:S(2)}) %copy-start.2) | copy-done | bytes 2072
  2.3 0.0 copy-start.6
  2.3 0.7 %copy-done.6 = f32[512]{0:T(512)S(1)} copy-done((f32[512]{0:T(512)S(1)}, f32[512]{0:T(512)}, u32[]{:S(2)}) %copy-start.6) | copy-done | bytes 2072
  3.0 0.0 copy-start
  3.0 6.1 %back_project_sibling.1 = f32[16,8,1152]{2,1,0:T(8,128)S(1)} custom-call(f32[512]{0:T(512)S(1)} %copy-done.6, s32[512]{0:T(512)S(1)} %copy-done.2, f32[256,2048]{1,0:T(8,128)S(1)} %bitcast.2), custom_call_target="tpu_custom_call" | custom-call | flops 2000000000 | bytes 2097152 | tf_op jit(solution)/shard_map/back_project_sibling/pallas_call | solution.py:500
  9.1 0.5 collective-permute-start
  9.6 0.0 copy-done
  9.6 0.7 %collective-permute-start.1 = (f32[1,4,2048]{2,1,0:T(4,128)S(1)}, f32[1,4,2048]{2,1,0:T(4,128)S(1)}, u32[]{:S(2)}, u32[]{:S(2)}) collective-permute-start(f32[1,4,2048]{2,1,0:T(4,128)S(1)} %copy-done), channel_id=1, source_target_pairs={{4,8},{5,9},{6,10},{7,11},{8,4},{9,5},{10,6},{11,7},{12,16},{13,17... | collective-permute-start | bytes 98312 | tf_op jit(solution)/shard_map/ppermute | solution.py:178
  10.3 6.1 %back_project_own.1.own_ref = f32[16,8,1152]{2,1,0:T(8,128)S(1)} custom-call(f32[512]{0:T(512)S(1)} %copy-done.6, s32[512]{0:T(512)S(1)} %copy-done.2, f32[256,2048]{1,0:T(8,128)S(1)} %bitcast.3), custom_call_target="tpu_custom_call" | custom-call | flops 2000000000 | bytes 2097152 | tf_op jit(solution)/shard_map/back_project_own/pallas_call | solution.py:500
  16.4 0.0 copy-start.3
  16.4 0.0 copy-start.4
  16.4 0.0 copy-start.5
  16.4 0.0 collective-permute-done.1.halo_ref
  16.5 0.0 collective-permute-done.got_ref
  16.5 0.2 plane_pack.1
  16.6 5.4 %collective-permute-start.2 = (f32[18,8,384]{2,1,0:T(8,128)S(1)}, f32[18,8,384]{2,1,0:T(8,128)S(1)}, u32[]{:S(2)}, u32[]{:S(2)}) collective-permute-start(f32[18,8,384]{2,1,0:T(8,128)S(1)} %get-tuple-element.25), channel_id=1, source_target_pairs={{0,4},{1,5},{2,6},{3,7},{4,0},{5,1},{6,2},{7,3},{8,12},{9,13},{10,... | collective-permute-start | bytes 663560 | tf_op jit(solution)/shard_map/ppermute | solution.py:178
  22.0 1.5 %collective-permute-start.3 = (f32[18,8,384]{2,1,0:T(8,128)S(1)}, f32[18,8,384]{2,1,0:T(8,128)S(1)}, u32[]{:S(2)}, u32[]{:S(2)}) collective-permute-start(f32[18,8,384]{2,1,0:T(8,128)S(1)} %get-tuple-element.26), channel_id=1, source_target_pairs={{0,1},{1,0},{2,3},{3,2},{4,5},{5,4},{6,7},{7,6},{8,9},{9,8},{10,11... | collective-permute-start | bytes 663560 | tf_op jit(solution)/shard_map/ppermute | solution.py:178
  23.5 0.0 collective-permute-start.4
  23.5 4.7 %collective-permute-done.2.got_x = f32[18,8,384]{2,1,0:T(8,128)S(1)} collective-permute-done((f32[18,8,384]{2,1,0:T(8,128)S(1)}, f32[18,8,384]{2,1,0:T(8,128)S(1)}, u32[]{:S(2)}, u32[]{:S(2)}) %collective-permute-start.2) | collective-permute-done | bytes 221216 | tf_op jit(solution)/shard_map/ppermute | solution.py:178
  28.2 5.8 %collective-permute-done.3.got_y = f32[18,8,384]{2,1,0:T(8,128)S(1)} collective-permute-done((f32[18,8,384]{2,1,0:T(8,128)S(1)}, f32[18,8,384]{2,1,0:T(8,128)S(1)}, u32[]{:S(2)}, u32[]{:S(2)}) %collective-permute-start.3) | collective-permute-done | bytes 221216 | tf_op jit(solution)/shard_map/ppermute | solution.py:178
  34.0 0.0 collective-permute-done.4.got_xy
  34.0 0.1 depth_pack.1
  34.1 0.1 collective-permute-start.5
  34.2 1.6 %collective-permute-start.6 = (f32[8,8,384]{2,1,0:T(8,128)S(1)}, f32[8,8,384]{2,1,0:T(8,128)S(1)}, u32[]{:S(2)}, u32[]{:S(2)}) collective-permute-start(f32[8,8,384]{2,1,0:T(8,128)S(1)} %get-tuple-element.34), channel_id=1, source_target_pairs={{0,8},{1,9},{2,10},{3,11},{4,12},{5,13},{6,14},{7,15},{8,0},{9,1},... | collective-permute-start | bytes 294920 | tf_op jit(solution)/shard_map/ppermute | solution.py:178
  35.8 2.2 %collective-permute-start.7 = (f32[8,8,384]{2,1,0:T(8,128)S(1)}, f32[8,8,384]{2,1,0:T(8,128)S(1)}, u32[]{:S(2)}, u32[]{:S(2)}) collective-permute-start(f32[8,8,384]{2,1,0:T(8,128)S(1)} %get-tuple-element.35), channel_id=1, source_target_pairs={{0,16},{1,17},{2,18},{3,19},{4,20},{5,21},{6,22},{7,23},{8,24},{9,... | collective-permute-start | bytes 294920 | tf_op jit(solution)/shard_map/ppermute | solution.py:178
  38.0 0.7 %collective-permute-start.8 = (f32[8,8,384]{2,1,0:T(8,128)S(1)}, f32[8,8,384]{2,1,0:T(8,128)S(1)}, u32[]{:S(2)}, u32[]{:S(2)}) collective-permute-start(f32[8,8,384]{2,1,0:T(8,128)S(1)} %get-tuple-element.36), channel_id=1, source_target_pairs={{0,24},{1,25},{2,26},{3,27},{4,28},{5,29},{6,30},{7,31},{8,16},{9,... | collective-permute-start | bytes 294920 | tf_op jit(solution)/shard_map/ppermute | solution.py:178
  38.6 0.0 copy-done.3
  38.6 0.0 copy-done.4
  38.6 0.0 copy-done.5
  38.6 0.7 %gram.1 = (f32[48,256]{1,0:T(8,128)S(1)}, f32[80,80]{1,0:T(8,128)S(1)}, f32[80,80]{1,0:T(8,128)S(1)}) custom-call(f32[1,512]{1,0:T(1,128)S(1)} %copy-done.5, f32[1,512]{1,0:T(1,128)S(1)} %copy-done.4, s32[1,512]{1,0:T(1,128)S(1)} %bitcast.4, f32[18,8,384]{2,1,0:T(8,128)S(1)} %get-tuple-element.24.mine.after_ref), custom_call_target="tpu_custom_call" | custom-call | flops 1000000000 | tf_op jit(solution)/shard_map/gram/pallas_call | solution.py:529
  39.3 0.0 collective-permute-done.5.vol_sib
  39.3 1.4 %first_normal.1.first_ref = f32[8,8,384]{2,1,0:T(8,128)S(1)} custom-call(f32[4,8,384]{2,1,0:T(8,128)S(1)} %get-tuple-element.28.vol_own, f32[4,8,384]{2,1,0:T(8,128)S(1)} %collective-permute-done.5.vol_sib, f32[48,256]{1,0:T(8,128)S(1)} %get-tuple-element.30.conv_ref, f32[80,80]{1,0:T(8,128)S(1)} %get-tuple-element.31.low_ref, ...), custom_call_target="tpu_custom_call" | custom-call | flops 1000000000 | tf_op jit(solution)/shard_map/first_normal/pallas_call | solution.py:552
  40.7 0.0 collective-permute-done.6.got_1
  40.7 5.9 %collective-permute-done.7.got_2 = f32[8,8,384]{2,1,0:T(8,128)S(1)} collective-permute-done((f32[8,8,384]{2,1,0:T(8,128)S(1)}, f32[8,8,384]{2,1,0:T(8,128)S(1)}, u32[]{:S(2)}, u32[]{:S(2)}) %collective-permute-start.7) | collective-permute-done | bytes 98336 | tf_op jit(solution)/shard_map/ppermute | solution.py:178
  46.6 0.0 collective-permute-done.8.got_3
  46.6 1.6 %finish.1 = (f32[2,8,256]{2,1,0:T(8,128)S(1)}, f32[2,8,256]{2,1,0:T(8,128)S(1)}) custom-call(f32[8,8,384]{2,1,0:T(8,128)S(1)} %first_normal.1.first_ref, f32[8,8,384]{2,1,0:T(8,128)S(1)} %get-tuple-element.33.own_win, f32[8,8,384]{2,1,0:T(8,128)S(1)} %collective-permute-done.6.got_1, f32[8,8,384]{2,1,0:T(8,128)S(1)} %collective-permute-done.7.got_2, ...), custom_call_target="tpu_custom_call" | custom-call | tf_op jit(solution)/shard_map/finish/pallas_call | solution.py:562
  48.1 0.1 collective-permute-start.9
  48.2 1.2 %collective-permute-done.9.got_ref = f32[2,8,256]{2,1,0:T(8,128)S(1)} collective-permute-done((f32[2,8,256]{2,1,0:T(8,128)S(1)}, f32[2,8,256]{2,1,0:T(8,128)S(1)}, u32[]{:S(2)}, u32[]{:S(2)}) %collective-permute-start.9) | collective-permute-done | bytes 16416 | tf_op jit(solution)/shard_map/ppermute | solution.py:178
  49.4 0.8 %collective-permute-start.10 = (f32[2,4,256]{2,1,0:T(4,128)S(1)}, f32[2,4,256]{2,1,0:T(4,128)S(1)}, u32[]{:S(2)}, u32[]{:S(2)}) collective-permute-start(f32[2,4,256]{2,1,0:T(4,128)S(1)} %get-tuple-element.40), channel_id=1, source_target_pairs={{0,4},{1,5},{2,6},{3,7},{4,0},{5,1},{6,2},{7,3},{8,12},{9,13},{10,... | collective-permute-start | bytes 24584 | tf_op jit(solution)/shard_map/ppermute | solution.py:178
  50.2 0.7 %collective-permute-start.11 = (f32[2,4,256]{2,1,0:T(4,128)S(1)}, f32[2,4,256]{2,1,0:T(4,128)S(1)}, u32[]{:S(2)}, u32[]{:S(2)}) collective-permute-start(f32[2,4,256]{2,1,0:T(4,128)S(1)} %get-tuple-element.41), channel_id=1, source_target_pairs={{0,1},{1,0},{2,3},{3,2},{4,5},{5,4},{6,7},{7,6},{8,9},{9,8},{10,11... | collective-permute-start | bytes 24584 | tf_op jit(solution)/shard_map/ppermute | solution.py:178
  50.9 2.1 %collective-permute-start.12 = (f32[2,4,256]{2,1,0:T(4,128)S(1)}, f32[2,4,256]{2,1,0:T(4,128)S(1)}, u32[]{:S(2)}, u32[]{:S(2)}) collective-permute-start(f32[2,4,256]{2,1,0:T(4,128)S(1)} %get-tuple-element.42), channel_id=1, source_target_pairs={{0,5},{1,4},{2,7},{3,6},{4,1},{5,0},{6,3},{7,2},{8,13},{9,12},{10,... | collective-permute-start | bytes 24584 | tf_op jit(solution)/shard_map/ppermute | solution.py:178
  53.0 0.2 collective-permute-done.10.got_x
  53.1 0.7 %collective-permute-done.11.got_y = f32[2,4,256]{2,1,0:T(4,128)S(1)} collective-permute-done((f32[2,4,256]{2,1,0:T(4,128)S(1)}, f32[2,4,256]{2,1,0:T(4,128)S(1)}, u32[]{:S(2)}, u32[]{:S(2)}) %collective-permute-start.11) | collective-permute-done | bytes 8224 | tf_op jit(solution)/shard_map/ppermute | solution.py:178
  53.8 1.6 %collective-permute-done.12.got_xy = f32[2,4,256]{2,1,0:T(4,128)S(1)} collective-permute-done((f32[2,4,256]{2,1,0:T(4,128)S(1)}, f32[2,4,256]{2,1,0:T(4,128)S(1)}, u32[]{:S(2)}, u32[]{:S(2)}) %collective-permute-start.12) | collective-permute-done | bytes 8224 | tf_op jit(solution)/shard_map/ppermute | solution.py:178
  55.4 0.6 %result.1 = f32[1,4,2048]{2,1,0:T(4,128)} custom-call(f32[2,4,256]{2,1,0:T(4,128)S(1)} %get-tuple-element.39.mine, f32[2,4,256]{2,1,0:T(4,128)S(1)} %collective-permute-done.10.got_x, f32[2,4,256]{2,1,0:T(4,128)S(1)} %collective-permute-done.11.got_y, f32[2,4,256]{2,1,0:T(4,128)S(1)} %collective-permute-done.12.got_xy), custom_call_target="tpu_custom_call" | custom-call | tf_op jit(solution)/shard_map/result/pallas_call | solution.py:577
  (1 shorter events, 0.0 us)
Async XLA Ops:
  0.0 1.6 %copy-start.1 = (f32[16,16,2048]{2,1,0:T(8,128)S(1)}, f32[16,16,2048]{2,1,0:T(8,128)}, u32[]{:S(2)}) copy-start(f32[16,16,2048]{2,1,0:T(8,128)} %param.6) | copy-start | bytes 6291460
  1.6 0.7 %copy-start.2 = (s32[512]{0:T(512)S(1)}, s32[512]{0:T(512)}, u32[]{:S(2)}) copy-start(s32[512]{0:T(512)} %drift_ref.3) | copy-start | bytes 6148
  2.3 0.7 %copy-start.6 = (f32[512]{0:T(512)S(1)}, f32[512]{0:T(512)}, u32[]{:S(2)}) copy-start(f32[512]{0:T(512)} %constant.6.clone.tan_ref) | copy-start | bytes 6148
  3.0 6.7 %copy-start = (f32[1,4,2048]{2,1,0:T(4,128)S(1)}, f32[1,4,2048]{2,1,0:T(4,128)}, u32[]{:S(2)}) copy-start(f32[1,4,2048]{2,1,0:T(4,128)} %vol_ref.1) | copy-start | bytes 98308
  9.1 7.4 %collective-permute-start = (f32[16,8,1152]{2,1,0:T(8,128)S(1)}, f32[16,8,1152]{2,1,0:T(8,128)S(1)}, u32[]{:S(2)}, u32[]{:S(2)}) collective-permute-start(f32[16,8,1152]{2,1,0:T(8,128)S(1)} %back_project_sibling.1), channel_id=1, source_target_pairs={{0,2},{1,3},{2,0},{3,1},{4,6},{5,7},{6,4},{7,5},{8,10},{9,11},{10,... | collective-permute-start | bytes 1769480 | tf_op jit(solution)/shard_map/ppermute | solution.py:178
  9.6 6.8 %collective-permute-start.1 = (f32[1,4,2048]{2,1,0:T(4,128)S(1)}, f32[1,4,2048]{2,1,0:T(4,128)S(1)}, u32[]{:S(2)}, u32[]{:S(2)}) collective-permute-start(f32[1,4,2048]{2,1,0:T(4,128)S(1)} %copy-done), channel_id=1, source_target_pairs={{4,8},{5,9},{6,10},{7,11},{8,4},{9,5},{10,6},{11,7},{12,16},{13,17... | collective-permute-start | bytes 98312 | tf_op jit(solution)/shard_map/ppermute | solution.py:178
  16.4 22.2 %copy-start.3 = (s32[512]{0:T(512)S(1)}, s32[512]{0:T(512)}, u32[]{:S(2)}) copy-start(s32[512]{0:T(512)} %drift_ref.3) | copy-start | bytes 6148
  16.4 22.2 %copy-start.4 = (f32[1,512]{1,0:T(1,128)S(1)}, f32[1,512]{1,0:T(1,128)}, u32[]{:S(2)}) copy-start(f32[1,512]{1,0:T(1,128)} %constant.8.clone.sec_ref) | copy-start | bytes 6148
  16.4 22.2 %copy-start.5 = (f32[1,512]{1,0:T(1,128)S(1)}, f32[1,512]{1,0:T(1,128)}, u32[]{:S(2)}) copy-start(f32[1,512]{1,0:T(1,128)} %constant.7.clone.tan_ref) | copy-start | bytes 6148
  16.6 11.6 %collective-permute-start.2 = (f32[18,8,384]{2,1,0:T(8,128)S(1)}, f32[18,8,384]{2,1,0:T(8,128)S(1)}, u32[]{:S(2)}, u32[]{:S(2)}) collective-permute-start(f32[18,8,384]{2,1,0:T(8,128)S(1)} %get-tuple-element.25), channel_id=1, source_target_pairs={{0,4},{1,5},{2,6},{3,7},{4,0},{5,1},{6,2},{7,3},{8,12},{9,13},{10,... | collective-permute-start | bytes 663560 | tf_op jit(solution)/shard_map/ppermute | solution.py:178
  22.0 12.0 %collective-permute-start.3 = (f32[18,8,384]{2,1,0:T(8,128)S(1)}, f32[18,8,384]{2,1,0:T(8,128)S(1)}, u32[]{:S(2)}, u32[]{:S(2)}) collective-permute-start(f32[18,8,384]{2,1,0:T(8,128)S(1)} %get-tuple-element.26), channel_id=1, source_target_pairs={{0,1},{1,0},{2,3},{3,2},{4,5},{5,4},{6,7},{7,6},{8,9},{9,8},{10,11... | collective-permute-start | bytes 663560 | tf_op jit(solution)/shard_map/ppermute | solution.py:178
  23.5 10.5 %collective-permute-start.4 = (f32[18,8,384]{2,1,0:T(8,128)S(1)}, f32[18,8,384]{2,1,0:T(8,128)S(1)}, u32[]{:S(2)}, u32[]{:S(2)}) collective-permute-start(f32[18,8,384]{2,1,0:T(8,128)S(1)} %get-tuple-element.27), channel_id=1, source_target_pairs={{0,5},{1,4},{2,7},{3,6},{4,1},{5,0},{6,3},{7,2},{8,13},{9,12},{10,... | collective-permute-start | bytes 663560 | tf_op jit(solution)/shard_map/ppermute | solution.py:178
  34.1 5.2 %collective-permute-start.5 = (f32[4,8,384]{2,1,0:T(8,128)S(1)}, f32[4,8,384]{2,1,0:T(8,128)S(1)}, u32[]{:S(2)}, u32[]{:S(2)}) collective-permute-start(f32[4,8,384]{2,1,0:T(8,128)S(1)} %get-tuple-element.29), channel_id=1, source_target_pairs={{0,2},{1,3},{2,0},{3,1},{4,6},{5,7},{6,4},{7,5},{8,10},{9,11},{10,... | collective-permute-start | bytes 147464 | tf_op jit(solution)/shard_map/ppermute | solution.py:178
  34.2 6.5 %collective-permute-start.6 = (f32[8,8,384]{2,1,0:T(8,128)S(1)}, f32[8,8,384]{2,1,0:T(8,128)S(1)}, u32[]{:S(2)}, u32[]{:S(2)}) collective-permute-start(f32[8,8,384]{2,1,0:T(8,128)S(1)} %get-tuple-element.34), channel_id=1, source_target_pairs={{0,8},{1,9},{2,10},{3,11},{4,12},{5,13},{6,14},{7,15},{8,0},{9,1},... | collective-permute-start | bytes 294920 | tf_op jit(solution)/shard_map/ppermute | solution.py:178
  35.8 10.8 %collective-permute-start.7 = (f32[8,8,384]{2,1,0:T(8,128)S(1)}, f32[8,8,384]{2,1,0:T(8,128)S(1)}, u32[]{:S(2)}, u32[]{:S(2)}) collective-permute-start(f32[8,8,384]{2,1,0:T(8,128)S(1)} %get-tuple-element.35), channel_id=1, source_target_pairs={{0,16},{1,17},{2,18},{3,19},{4,20},{5,21},{6,22},{7,23},{8,24},{9,... | collective-permute-start | bytes 294920 | tf_op jit(solution)/shard_map/ppermute | solution.py:178
  38.0 8.6 %collective-permute-start.8 = (f32[8,8,384]{2,1,0:T(8,128)S(1)}, f32[8,8,384]{2,1,0:T(8,128)S(1)}, u32[]{:S(2)}, u32[]{:S(2)}) collective-permute-start(f32[8,8,384]{2,1,0:T(8,128)S(1)} %get-tuple-element.36), channel_id=1, source_target_pairs={{0,24},{1,25},{2,26},{3,27},{4,28},{5,29},{6,30},{7,31},{8,16},{9,... | collective-permute-start | bytes 294920 | tf_op jit(solution)/shard_map/ppermute | solution.py:178
  48.1 1.2 %collective-permute-start.9 = (f32[2,8,256]{2,1,0:T(8,128)S(1)}, f32[2,8,256]{2,1,0:T(8,128)S(1)}, u32[]{:S(2)}, u32[]{:S(2)}) collective-permute-start(f32[2,8,256]{2,1,0:T(8,128)S(1)} %get-tuple-element.38), channel_id=1, source_target_pairs={{0,2},{1,3},{2,0},{3,1},{4,6},{5,7},{6,4},{7,5},{8,10},{9,11},{10,... | collective-permute-start | bytes 49160 | tf_op jit(solution)/shard_map/ppermute | solution.py:178
  49.4 3.7 %collective-permute-start.10 = (f32[2,4,256]{2,1,0:T(4,128)S(1)}, f32[2,4,256]{2,1,0:T(4,128)S(1)}, u32[]{:S(2)}, u32[]{:S(2)}) collective-permute-start(f32[2,4,256]{2,1,0:T(4,128)S(1)} %get-tuple-element.40), channel_id=1, source_target_pairs={{0,4},{1,5},{2,6},{3,7},{4,0},{5,1},{6,2},{7,3},{8,12},{9,13},{10,... | collective-permute-start | bytes 24584 | tf_op jit(solution)/shard_map/ppermute | solution.py:178
  50.2 3.7 %collective-permute-start.11 = (f32[2,4,256]{2,1,0:T(4,128)S(1)}, f32[2,4,256]{2,1,0:T(4,128)S(1)}, u32[]{:S(2)}, u32[]{:S(2)}) collective-permute-start(f32[2,4,256]{2,1,0:T(4,128)S(1)} %get-tuple-element.41), channel_id=1, source_target_pairs={{0,1},{1,0},{2,3},{3,2},{4,5},{5,4},{6,7},{7,6},{8,9},{9,8},{10,11... | collective-permute-start | bytes 24584 | tf_op jit(solution)/shard_map/ppermute | solution.py:178
  50.9 4.5 %collective-permute-start.12 = (f32[2,4,256]{2,1,0:T(4,128)S(1)}, f32[2,4,256]{2,1,0:T(4,128)S(1)}, u32[]{:S(2)}, u32[]{:S(2)}) collective-permute-start(f32[2,4,256]{2,1,0:T(4,128)S(1)} %get-tuple-element.42), channel_id=1, source_target_pairs={{0,5},{1,4},{2,7},{3,6},{4,1},{5,0},{6,3},{7,2},{8,13},{9,12},{10,... | collective-permute-start | bytes 24584 | tf_op jit(solution)/shard_map/ppermute | solution.py:178

commit v2 on v1

--- a/solution.py
+++ b/solution.py
@@ -197,56 +197,113 @@
     return lax.broadcasted_iota(jnp.int32, shape, len(shape) - 2)
 
 
-def back_project_kernel(
-    sibling, views, slices, rows, half_cols, band, scale, tan_ref, drift_ref, meas_ref, out_ref, buf, sem
-):
-    in_cols = half_cols + LANES
+STEP = 3
+
+
+def view_weights(views, rows, band, scale, tan_ref, drift_ref):
     z, x, c, y = coords()
-    half = 1 - c if sibling else c
-    first = pl.multiple_of(half * (half_cols - LANES), LANES)
-    tiles = in_cols // LANES
-    copies = [
-        pltpu.make_async_copy(meas_ref.at[:, pl.ds(first + t * LANES, LANES)], buf.at[t + 1], sem.at[t])
-        for t in range(tiles)
-    ]
-    for copy in copies:
-        copy.start()
-    buf[0] = jnp.zeros((views * slices, LANES), jnp.float32)
-    buf[tiles + 1] = jnp.zeros((views * slices, LANES), jnp.float32)
     first_view = (((z * 2 + x) * 2 + c) * 2 + y) * views
-    step = 7
-    parts = 2 * band // step + 1
-    shape = (parts * rows, step * views)
+    parts = 2 * band // STEP + 1
+    shape = (parts * rows, STEP * views)
     lane, row = lane_iota(shape), row_iota(shape)
-    view_of = lane % views
-    tan_lane = jnp.zeros(shape, jnp.float32)
-    drift_lane = jnp.zeros(shape, jnp.float32)
+    view_of = lane_iota((1, STEP * views)) % views
+    tan_lane = jnp.zeros((1, STEP * views), jnp.float32)
+    drift_lane = tan_lane
     for a in range(views):
         tan_lane = jnp.where(view_of == a, tan_ref[first_view + a], tan_lane)
         drift_lane = jnp.where(view_of == a, drift_ref[first_view + a].astype(jnp.float32), drift_lane)
     shift = ((row % rows).astype(jnp.float32) - (rows - 1) / 2.0) * tan_lane - drift_lane
-    offset = ((row // rows) * step + lane // views - band).astype(jnp.float32)
+    offset = ((row // rows) * STEP + lane // views - band).astype(jnp.float32)
     weights = (scale / rows) * jnp.maximum(0.0, 1.0 - jnp.abs(shift - offset))
     weights = split_rows(weights)
-    weights = jnp.concatenate([weights, weights], axis=1).astype(jnp.bfloat16)
-    width = in_cols + LANES
-    for copy in copies:
+    return jnp.concatenate([weights, weights], axis=1).astype(jnp.bfloat16)
+
+
+def back_project(views, slices, rows, band, weights, load_strip, out_ref, terms):
+    out_cols = out_ref.shape[2]
+    width = terms.shape[2]
+    parts = 2 * band // STEP + 1
+
+    def prepare(s, buf):
+        strip = load_strip(s)
+        high = strip.astype(jnp.bfloat16)
+        low = (strip - high.astype(jnp.float32)).astype(jnp.bfloat16)
+        for j in range(STEP):
+            buf[j * views : (j + 1) * views] = pltpu.roll(high, j, 1) if j else high
+            buf[(STEP + j) * views : (STEP + j + 1) * views] = pltpu.roll(low, j, 1) if j else low
+
+    prepare(0, terms.at[0])
+    for s in range(slices):
+        if s + 1 < slices:
+            prepare(s + 1, terms.at[(s + 1) % 2])
+        spread = jnp.dot(weights, terms[s % 2], preferred_element_type=jnp.float32)
+        spread = spread[: parts * rows] + spread[parts * rows :]
+        total = None
+        for i in range(parts):
+            piece = pltpu.roll(spread[i * rows : (i + 1) * rows], width - HALO - band + STEP * i, 1)
+            total = piece if total is None else total + piece
+        out_ref[s] = total[:, :out_cols]
+
+
+def strip_loader(buf, half, views, tiles):
+    def load(s):
+        return jnp.concatenate(
+            [buf[s // SUB, half + t, pl.ds(s % SUB, views, stride=SUB), :] for t in range(tiles + 1)], axis=1
+        )
+
+    return load
+
+
+def sibling_kernel(views, slices, rows, band, scale, tan_hbm, drift_hbm, meas_ref, out_ref, own_buf, weights_ref,
+                   tan_ref, drift_ref, buf, terms, table_sem, sem, own_sem):
+    _, _, c, _ = coords()
+    tiles = out_ref.shape[2] // LANES
+    groups = slices // SUB
+
+    def fetch(half, g, t, target, semaphore):
+        first = pl.multiple_of((half * (tiles - 1) + t - half) * LANES, LANES)
+        return pltpu.make_async_copy(
+            meas_ref.at[:, pl.ds(g * SUB, SUB), pl.ds(first, LANES)], target.at[g, t + 1], semaphore
+        )
+
+    tables = [
+        pltpu.make_async_copy(tan_hbm, tan_ref, table_sem.at[0]),
+        pltpu.make_async_copy(drift_hbm, drift_ref, table_sem.at[1]),
+    ]
+    first = [[fetch(1 - c, g, t, buf, sem.at[g, t]) for t in range(tiles)] for g in range(groups)]
+    later = [[fetch(c, g, t, own_buf, own_sem.at[g, t]) for t in range(tiles)] for g in range(groups)]
+    for copy in tables + first[0] + first[1] + later[0] + later[1]:
+        copy.start()
+    zero = jnp.zeros((views, SUB, LANES), jnp.float32)
+    for g in range(groups):
+        for target in (buf, own_buf):
+            target[g, 0] = zero
+            target[g, tiles + 1] = zero
+    for copy in tables:
         copy.wait()
-
-    def one_slice(s, carry):
-        strip = jnp.concatenate([buf[half + t, pl.ds(s, views, stride=slices), :] for t in range(tiles + 1)], axis=1)
-        moved = jnp.concatenate(
-            [pltpu.roll(strip, width - (HALO + band - j), 1) for j in range(step)], axis=0
-        )
-        spread = jnp.dot(weights, split_terms(moved), preferred_element_type=jnp.float32)
-        spread = spread[: parts * rows] + spread[parts * rows :]
-        total = spread[0:rows]
-        for i in range(1, parts):
-            total = total + pltpu.roll(spread[i * rows : (i + 1) * rows], step * i, 1)
-        out_ref[s] = total[:, :in_cols]
-        return carry
-
-    lax.fori_loop(0, slices, one_slice, 0, unroll=2)
+    weights = view_weights(views, rows, band, scale, tan_ref, drift_ref)
+    weights_ref[...] = weights.astype(jnp.float32)
+    flat = buf.reshape(groups, tiles + 2, views * SUB, LANES)
+    load = strip_loader(flat, 1 - c, views, tiles)
+
+    def load_strip(s):
+        if s % SUB == 0:
+            for copy in first[s // SUB]:
+                copy.wait()
+        return load(s)
+
+    back_project(views, slices, rows, band, weights, load_strip, out_ref, terms)
+    for group in later:
+        for copy in group:
+            copy.wait()
+
+
+def own_kernel(views, slices, rows, band, buf, weights_ref, out_ref, terms):
+    _, _, c, _ = coords()
+    tiles = out_ref.shape[2] // LANES
+    flat = buf.reshape(slices // SUB, tiles + 2, views * SUB, LANES)
+    load = strip_loader(flat, c, views, tiles)
+    back_project(views, slices, rows, band, weights_ref[...].astype(jnp.bfloat16), load, out_ref, terms)
 
 
 def plane_pack_kernel(block, own_ref, got_ref, vol_ref, halo_ref, mine, to_x, to_y, to_xy, acc, vbuf):
@@ -462,6 +519,7 @@
 VMEM_SPEC = pl.BlockSpec(memory_space=pltpu.VMEM)
 SMEM_SPEC = pl.BlockSpec(memory_space=pltpu.SMEM)
 ANY_SPEC = pl.BlockSpec(memory_space=pl.ANY)
+HBM_SPEC = pl.BlockSpec(memory_space=pltpu.HBM)
 PARAMS = pltpu.CompilerParams(vmem_limit_bytes=40 * 1024 * 1024)
 
 
@@ -493,25 +551,40 @@
     scale = float(1.0 / np.sum(secant))
     tangent, secant = tangent.astype(np.float32), secant.astype(np.float32)
 
-    flat = measured.reshape(views * slices, cols)
     halo = move(start_volume, lambda z, x, c, y: (z + 1, 0, c, y) if x else (z - 1, 1, c, y))
 
-    def back_project(sibling):
-        return kernel_call(
-            functools.partial(back_project_kernel, sibling, views, slices, rows, half_cols, band, scale),
-            f32(slices, rows, half_width),
-            [SMEM_SPEC, SMEM_SPEC, ANY_SPEC],
-            [
-                pltpu.VMEM((half_width // LANES + 2, views * slices, LANES), jnp.float32),
-                pltpu.SemaphoreType.DMA((half_width // LANES,)),
-            ],
-            "back_project_sibling" if sibling else "back_project_own",
-            flops=2 * 10**9,
-            size=2**21,
-        )(tangent, drift, flat)
-
-    got = move(back_project(True), lambda z, x, c, y: (z, x, 1 - c, y))
-    own = back_project(False)
+    tiles = half_width // LANES
+    groups = slices // SUB
+    window = (groups, tiles + 2, views, SUB, LANES)
+    table = (2 * (2 * band // STEP + 1) * rows, 2 * STEP * views)
+    terms = pltpu.VMEM((2, 2 * STEP * views, half_width + LANES), jnp.bfloat16)
+    sibling, own_buf, weights = kernel_call(
+        functools.partial(sibling_kernel, views, slices, rows, band, scale),
+        [f32(slices, rows, half_width), f32(*window), f32(*table)],
+        [HBM_SPEC] * 3,
+        [
+            pltpu.SMEM((total_angles,), jnp.float32),
+            pltpu.SMEM((total_angles,), jnp.int32),
+            pltpu.VMEM(window, jnp.float32),
+            terms,
+            pltpu.SemaphoreType.DMA((2,)),
+            pltpu.SemaphoreType.DMA((groups, tiles)),
+            pltpu.SemaphoreType.DMA((groups, tiles)),
+        ],
+        "back_project_sibling",
+        flops=2 * 10**9,
+        size=2**21,
+    )(tangent, drift, measured)
+    got = move(sibling, lambda z, x, c, y: (z, x, 1 - c, y))
+    own = kernel_call(
+        functools.partial(own_kernel, views, slices, rows, band),
+        f32(slices, rows, half_width),
+        [VMEM_SPEC] * 2,
+        [terms],
+        "back_project_own",
+        flops=2 * 10**9,
+        size=2**21,
+    )(own_buf, weights)
 
     message = f32(slices + 2, rows, width)
     mine, to_x, to_y, to_xy = kernel_call(

time: 56.2 us -> 50.8 us (0.904)
  Pallas kernels: 16.7 us -> 11.3 us
    pallas_call x2, Pallas kernels: 12.2 us -> 6.83 us  [the longest x1 3.88 us: summed_plan(): kernel_call(functools.partial(sibling_kernel, views, slices, rows, band,...]
  transfers between devices with their start and end apart: 13 -> 13, of which waited for: 7 -> 7; matrix products, arithmetic and copies ran while one was open for 0% -> 0% of each run, Pallas kernels for 15% -> 10%
where the time goes in v2:
time: 50.8 us; the launch traced here: 50.6 us
  waiting for transfers between devices  19.7 us (39%)
  starting transfers between devices  16.5 us (32%)
  Pallas kernels  11.3 us (22%)
  local copies, waits for them, and re-layouts  2.98 us (6%)
    ppermute x13, waiting for transfers between devices, move(): return lax.ppermute(value, ('wide', 'grp'), pairs)  19.7 us
    ppermute x13, starting transfers between devices, move(): return lax.ppermute(value, ('wide', 'grp'), pairs)  16.5 us
    pallas_call x1, Pallas kernels, summed_plan(): kernel_call(functools.partial(sibling_kernel, views, slices, rows, band,...  3.88 us
    unnamed x14, local copies, waits for them, and re-layouts  2.98 us
    pallas_call x1, Pallas kernels, summed_plan(): kernel_call(functools.partial(own_kernel, views, slices, rows, band), f32...  2.95 us
    pallas_call x1, Pallas kernels, summed_plan(): kernel_call(functools.partial(finish_kernel, band, block, slices, cols),...  1.56 us
    pallas_call x1, Pallas kernels, summed_plan(): kernel_call(functools.partial(first_normal_kernel, band, block, cols), wi...  1.38 us
  transfers between devices with their start and end apart: 13, of which 7 were waited for; matrix products, arithmetic and copies ran while one was open for 0% of the time, Pallas kernels for 10%

profile of v2, /device:TPU:0, one launch (start us, length us, event | category | flops | bytes accessed | tf_op | source)
XLA Modules:
  0.0 50.6 jit_solution(9344246810900375656)
XLA Ops:
  0.0 0.0 copy-start.1
  0.0 1.6 %copy-done.1 = f32[16,16,2048]{2,1,0:T(8,128)S(1)} copy-done((f32[16,16,2048]{2,1,0:T(8,128)S(1)}, f32[16,16,2048]{2,1,0:T(8,128)}, u32[]{:S(2)}) %copy-start.1) | copy-done | bytes 2097176
  1.6 0.0 copy-start.2
  1.6 0.7 %copy-done.2 = s32[512]{0:T(512)S(1)} copy-done((s32[512]{0:T(512)S(1)}, s32[512]{0:T(512)}, u32[]{:S(2)}) %copy-start.2) | copy-done | bytes 2072
  2.3 0.0 copy-start.6
  2.3 0.7 %copy-done.6 = f32[512]{0:T(512)S(1)} copy-done((f32[512]{0:T(512)S(1)}, f32[512]{0:T(512)}, u32[]{:S(2)}) %copy-start.6) | copy-done | bytes 2072
  3.0 0.0 copy-start
  3.0 3.9 %back_project_sibling.1 = (f32[16,8,1152]{2,1,0:T(8,128)S(1)}, f32[2,11,16,8,128]{4,3,2,1,0:T(8,128)S(1)}, f32[112,96]{1,0:T(8,128)S(1)}) custom-call(f32[512]{0:T(512)S(1)} %copy-done.6, s32[512]{0:T(512)S(1)} %copy-done.2, f32[16,16,2048]{2,1,0:T(8,128)S(1)} %copy-done.1), custom_call_target="tpu_custom_call" | custom-call | flops 2000000000 | bytes 2097152 | tf_op jit(solution)/shard_map/back_project_sibling/pallas_call | solution.py:561
  6.8 0.5 %collective-permute-start = (f32[16,8,1152]{2,1,0:T(8,128)S(1)}, f32[16,8,1152]{2,1,0:T(8,128)S(1)}, u32[]{:S(2)}, u32[]{:S(2)}) collective-permute-start(f32[16,8,1152]{2,1,0:T(8,128)S(1)} %get-tuple-element.29), channel_id=1, source_target_pairs={{0,2},{1,3},{2,0},{3,1},{4,6},{5,7},{6,4},{7,5},{8,10},{9,11},{10,... | collective-permute-start | bytes 1769480 | tf_op jit(solution)/shard_map/ppermute | solution.py:178
  7.4 0.0 copy-done
  7.4 0.7 %collective-permute-start.1 = (f32[1,4,2048]{2,1,0:T(4,128)S(1)}, f32[1,4,2048]{2,1,0:T(4,128)S(1)}, u32[]{:S(2)}, u32[]{:S(2)}) collective-permute-start(f32[1,4,2048]{2,1,0:T(4,128)S(1)} %copy-done), channel_id=1, source_target_pairs={{4,8},{5,9},{6,10},{7,11},{8,4},{9,5},{10,6},{11,7},{12,16},{13,17... | collective-permute-start | bytes 98312 | tf_op jit(solution)/shard_map/ppermute | solution.py:178
  8.0 3.0 %back_project_own.1.own_ref = f32[16,8,1152]{2,1,0:T(8,128)S(1)} custom-call(f32[2,11,16,8,128]{4,3,2,1,0:T(8,128)S(1)} %get-tuple-element.27.buf, f32[112,96]{1,0:T(8,128)S(1)} %get-tuple-element.28.weights_ref), custom_call_target="tpu_custom_call" | custom-call | flops 2000000000 | bytes 2097152 | tf_op jit(solution)/shard_map/back_project_own/pallas_call | solution.py:579
  11.0 0.0 copy-start.3
  11.0 0.0 copy-start.4
  11.0 0.0 copy-start.5
  11.0 0.0 collective-permute-done.1.halo_ref
  11.0 0.0 collective-permute-done.got_ref
  11.0 0.2 plane_pack.1
  11.2 5.6 %collective-permute-start.2 = (f32[18,8,384]{2,1,0:T(8,128)S(1)}, f32[18,8,384]{2,1,0:T(8,128)S(1)}, u32[]{:S(2)}, u32[]{:S(2)}) collective-permute-start(f32[18,8,384]{2,1,0:T(8,128)S(1)} %get-tuple-element.31), channel_id=1, source_target_pairs={{0,4},{1,5},{2,6},{3,7},{4,0},{5,1},{6,2},{7,3},{8,12},{9,13},{10,... | collective-permute-start | bytes 663560 | tf_op jit(solution)/shard_map/ppermute | solution.py:178
  16.8 1.5 %collective-permute-start.3 = (f32[18,8,384]{2,1,0:T(8,128)S(1)}, f32[18,8,384]{2,1,0:T(8,128)S(1)}, u32[]{:S(2)}, u32[]{:S(2)}) collective-permute-start(f32[18,8,384]{2,1,0:T(8,128)S(1)} %get-tuple-element.32), channel_id=1, source_target_pairs={{0,1},{1,0},{2,3},{3,2},{4,5},{5,4},{6,7},{7,6},{8,9},{9,8},{10,11... | collective-permute-start | bytes 663560 | tf_op jit(solution)/shard_map/ppermute | solution.py:178
  18.3 0.0 collective-permute-start.4
  18.3 4.7 %collective-permute-done.2.got_x = f32[18,8,384]{2,1,0:T(8,128)S(1)} collective-permute-done((f32[18,8,384]{2,1,0:T(8,128)S(1)}, f32[18,8,384]{2,1,0:T(8,128)S(1)}, u32[]{:S(2)}, u32[]{:S(2)}) %collective-permute-start.2) | collective-permute-done | bytes 221216 | tf_op jit(solution)/shard_map/ppermute | solution.py:178
  23.0 5.5 %collective-permute-done.3.got_y = f32[18,8,384]{2,1,0:T(8,128)S(1)} collective-permute-done((f32[18,8,384]{2,1,0:T(8,128)S(1)}, f32[18,8,384]{2,1,0:T(8,128)S(1)}, u32[]{:S(2)}, u32[]{:S(2)}) %collective-permute-start.3) | collective-permute-done | bytes 221216 | tf_op jit(solution)/shard_map/ppermute | solution.py:178
  28.6 0.0 collective-permute-done.4.got_xy
  28.6 0.1 depth_pack.1
  28.7 0.1 collective-permute-start.5
  28.8 1.6 %collective-permute-start.6 = (f32[8,8,384]{2,1,0:T(8,128)S(1)}, f32[8,8,384]{2,1,0:T(8,128)S(1)}, u32[]{:S(2)}, u32[]{:S(2)}) collective-permute-start(f32[8,8,384]{2,1,0:T(8,128)S(1)} %get-tuple-element.40), channel_id=1, source_target_pairs={{0,8},{1,9},{2,10},{3,11},{4,12},{5,13},{6,14},{7,15},{8,0},{9,1},... | collective-permute-start | bytes 294920 | tf_op jit(solution)/shard_map/ppermute | solution.py:178
  30.4 2.2 %collective-permute-start.7 = (f32[8,8,384]{2,1,0:T(8,128)S(1)}, f32[8,8,384]{2,1,0:T(8,128)S(1)}, u32[]{:S(2)}, u32[]{:S(2)}) collective-permute-start(f32[8,8,384]{2,1,0:T(8,128)S(1)} %get-tuple-element.41), channel_id=1, source_target_pairs={{0,16},{1,17},{2,18},{3,19},{4,20},{5,21},{6,22},{7,23},{8,24},{9,... | collective-permute-start | bytes 294920 | tf_op jit(solution)/shard_map/ppermute | solution.py:178
  32.6 0.7 %collective-permute-start.8 = (f32[8,8,384]{2,1,0:T(8,128)S(1)}, f32[8,8,384]{2,1,0:T(8,128)S(1)}, u32[]{:S(2)}, u32[]{:S(2)}) collective-permute-start(f32[8,8,384]{2,1,0:T(8,128)S(1)} %get-tuple-element.42), channel_id=1, source_target_pairs={{0,24},{1,25},{2,26},{3,27},{4,28},{5,29},{6,30},{7,31},{8,16},{9,... | collective-permute-start | bytes 294920 | tf_op jit(solution)/shard_map/ppermute | solution.py:178
  33.2 0.0 copy-done.3
  33.2 0.0 copy-done.4
  33.2 0.0 copy-done.5
  33.2 0.7 %gram.1 = (f32[48,256]{1,0:T(8,128)S(1)}, f32[80,80]{1,0:T(8,128)S(1)}, f32[80,80]{1,0:T(8,128)S(1)}) custom-call(f32[1,512]{1,0:T(1,128)S(1)} %copy-done.4, f32[1,512]{1,0:T(1,128)S(1)} %copy-done.5, s32[1,512]{1,0:T(1,128)S(1)} %bitcast.1, f32[18,8,384]{2,1,0:T(8,128)S(1)} %get-tuple-element.30.mine.after_ref), custom_call_target="tpu_custom_call" | custom-call | flops 1000000000 | tf_op jit(solution)/shard_map/gram/pallas_call | solution.py:602
  33.9 0.0 collective-permute-done.5.vol_sib
  33.9 1.4 %first_normal.1.first_ref = f32[8,8,384]{2,1,0:T(8,128)S(1)} custom-call(f32[4,8,384]{2,1,0:T(8,128)S(1)} %get-tuple-element.34.vol_own, f32[4,8,384]{2,1,0:T(8,128)S(1)} %collective-permute-done.5.vol_sib, f32[48,256]{1,0:T(8,128)S(1)} %get-tuple-element.36.conv_ref, f32[80,80]{1,0:T(8,128)S(1)} %get-tuple-element.37.low_ref, ...), custom_call_target="tpu_custom_call" | custom-call | flops 1000000000 | tf_op jit(solution)/shard_map/first_normal/pallas_call | solution.py:625
  35.3 0.0 collective-permute-done.6.got_1
  35.3 5.9 %collective-permute-done.7.got_2 = f32[8,8,384]{2,1,0:T(8,128)S(1)} collective-permute-done((f32[8,8,384]{2,1,0:T(8,128)S(1)}, f32[8,8,384]{2,1,0:T(8,128)S(1)}, u32[]{:S(2)}, u32[]{:S(2)}) %collective-permute-start.7) | collective-permute-done | bytes 98336 | tf_op jit(solution)/shard_map/ppermute | solution.py:178
  41.1 0.0 collective-permute-done.8.got_3
  41.1 1.6 %finish.1 = (f32[2,8,256]{2,1,0:T(8,128)S(1)}, f32[2,8,256]{2,1,0:T(8,128)S(1)}) custom-call(f32[8,8,384]{2,1,0:T(8,128)S(1)} %first_normal.1.first_ref, f32[8,8,384]{2,1,0:T(8,128)S(1)} %get-tuple-element.39.own_win, f32[8,8,384]{2,1,0:T(8,128)S(1)} %collective-permute-done.6.got_1, f32[8,8,384]{2,1,0:T(8,128)S(1)} %collective-permute-done.7.got_2, ...), custom_call_target="tpu_custom_call" | custom-call | tf_op jit(solution)/shard_map/finish/pallas_call | solution.py:635
  42.7 0.1 collective-permute-start.9
  42.8 1.2 %collective-permute-done.9.got_ref = f32[2,8,256]{2,1,0:T(8,128)S(1)} collective-permute-done((f32[2,8,256]{2,1,0:T(8,128)S(1)}, f32[2,8,256]{2,1,0:T(8,128)S(1)}, u32[]{:S(2)}, u32[]{:S(2)}) %collective-permute-start.9) | collective-permute-done | bytes 16416 | tf_op jit(solution)/shard_map/ppermute | solution.py:178
  44.0 0.8 %collective-permute-start.10 = (f32[2,4,256]{2,1,0:T(4,128)S(1)}, f32[2,4,256]{2,1,0:T(4,128)S(1)}, u32[]{:S(2)}, u32[]{:S(2)}) collective-permute-start(f32[2,4,256]{2,1,0:T(4,128)S(1)} %get-tuple-element.46), channel_id=1, source_target_pairs={{0,4},{1,5},{2,6},{3,7},{4,0},{5,1},{6,2},{7,3},{8,12},{9,13},{10,... | collective-permute-start | bytes 24584 | tf_op jit(solution)/shard_map/ppermute | solution.py:178
  44.8 0.6 %collective-permute-start.11 = (f32[2,4,256]{2,1,0:T(4,128)S(1)}, f32[2,4,256]{2,1,0:T(4,128)S(1)}, u32[]{:S(2)}, u32[]{:S(2)}) collective-permute-start(f32[2,4,256]{2,1,0:T(4,128)S(1)} %get-tuple-element.47), channel_id=1, source_target_pairs={{0,1},{1,0},{2,3},{3,2},{4,5},{5,4},{6,7},{7,6},{8,9},{9,8},{10,11... | collective-permute-start | bytes 24584 | tf_op jit(solution)/shard_map/ppermute | solution.py:178
  45.4 2.1 %collective-permute-start.12 = (f32[2,4,256]{2,1,0:T(4,128)S(1)}, f32[2,4,256]{2,1,0:T(4,128)S(1)}, u32[]{:S(2)}, u32[]{:S(2)}) collective-permute-start(f32[2,4,256]{2,1,0:T(4,128)S(1)} %get-tuple-element.48), channel_id=1, source_target_pairs={{0,5},{1,4},{2,7},{3,6},{4,1},{5,0},{6,3},{7,2},{8,13},{9,12},{10,... | collective-permute-start | bytes 24584 | tf_op jit(solution)/shard_map/ppermute | solution.py:178
  47.5 0.2 collective-permute-done.10.got_x
  47.7 0.7 %collective-permute-done.11.got_y = f32[2,4,256]{2,1,0:T(4,128)S(1)} collective-permute-done((f32[2,4,256]{2,1,0:T(4,128)S(1)}, f32[2,4,256]{2,1,0:T(4,128)S(1)}, u32[]{:S(2)}, u32[]{:S(2)}) %collective-permute-start.11) | collective-permute-done | bytes 8224 | tf_op jit(solution)/shard_map/ppermute | solution.py:178
  48.4 1.5 %collective-permute-done.12.got_xy = f32[2,4,256]{2,1,0:T(4,128)S(1)} collective-permute-done((f32[2,4,256]{2,1,0:T(4,128)S(1)}, f32[2,4,256]{2,1,0:T(4,128)S(1)}, u32[]{:S(2)}, u32[]{:S(2)}) %collective-permute-start.12) | collective-permute-done | bytes 8224 | tf_op jit(solution)/shard_map/ppermute | solution.py:178
  50.0 0.6 %result.1 = f32[1,4,2048]{2,1,0:T(4,128)} custom-call(f32[2,4,256]{2,1,0:T(4,128)S(1)} %get-tuple-element.45.mine, f32[2,4,256]{2,1,0:T(4,128)S(1)} %collective-permute-done.10.got_x, f32[2,4,256]{2,1,0:T(4,128)S(1)} %collective-permute-done.11.got_y, f32[2,4,256]{2,1,0:T(4,128)S(1)} %collective-permute-done.12.got_xy), custom_call_target="tpu_custom_call" | custom-call | tf_op jit(solution)/shard_map/result/pallas_call | solution.py:650
  (1 shorter events, 0.0 us)
Async XLA Ops:
  0.0 1.6 %copy-start.1 = (f32[16,16,2048]{2,1,0:T(8,128)S(1)}, f32[16,16,2048]{2,1,0:T(8,128)}, u32[]{:S(2)}) copy-start(f32[16,16,2048]{2,1,0:T(8,128)} %meas_ref.1) | copy-start | bytes 6291460
  1.6 0.7 %copy-start.2 = (s32[512]{0:T(512)S(1)}, s32[512]{0:T(512)}, u32[]{:S(2)}) copy-start(s32[512]{0:T(512)} %drift_hbm.1) | copy-start | bytes 6148
  2.3 0.7 %copy-start.6 = (f32[512]{0:T(512)S(1)}, f32[512]{0:T(512)}, u32[]{:S(2)}) copy-start(f32[512]{0:T(512)} %constant.6.clone.tan_hbm) | copy-start | bytes 6148
  3.0 4.4 %copy-start = (f32[1,4,2048]{2,1,0:T(4,128)S(1)}, f32[1,4,2048]{2,1,0:T(4,128)}, u32[]{:S(2)}) copy-start(f32[1,4,2048]{2,1,0:T(4,128)} %vol_ref.1) | copy-start | bytes 98308
  6.8 4.2 %collective-permute-start = (f32[16,8,1152]{2,1,0:T(8,128)S(1)}, f32[16,8,1152]{2,1,0:T(8,128)S(1)}, u32[]{:S(2)}, u32[]{:S(2)}) collective-permute-start(f32[16,8,1152]{2,1,0:T(8,128)S(1)} %get-tuple-element.29), channel_id=1, source_target_pairs={{0,2},{1,3},{2,0},{3,1},{4,6},{5,7},{6,4},{7,5},{8,10},{9,11},{10,... | collective-permute-start | bytes 1769480 | tf_op jit(solution)/shard_map/ppermute | solution.py:178
  7.4 3.7 %collective-permute-start.1 = (f32[1,4,2048]{2,1,0:T(4,128)S(1)}, f32[1,4,2048]{2,1,0:T(4,128)S(1)}, u32[]{:S(2)}, u32[]{:S(2)}) collective-permute-start(f32[1,4,2048]{2,1,0:T(4,128)S(1)} %copy-done), channel_id=1, source_target_pairs={{4,8},{5,9},{6,10},{7,11},{8,4},{9,5},{10,6},{11,7},{12,16},{13,17... | collective-permute-start | bytes 98312 | tf_op jit(solution)/shard_map/ppermute | solution.py:178
  11.0 22.2 %copy-start.3 = (s32[512]{0:T(512)S(1)}, s32[512]{0:T(512)}, u32[]{:S(2)}) copy-start(s32[512]{0:T(512)} %drift_hbm.1) | copy-start | bytes 6148
  11.0 22.2 %copy-start.4 = (f32[1,512]{1,0:T(1,128)S(1)}, f32[1,512]{1,0:T(1,128)}, u32[]{:S(2)}) copy-start(f32[1,512]{1,0:T(1,128)} %constant.7.clone.tan_ref) | copy-start | bytes 6148
  11.0 22.2 %copy-start.5 = (f32[1,512]{1,0:T(1,128)S(1)}, f32[1,512]{1,0:T(1,128)}, u32[]{:S(2)}) copy-start(f32[1,512]{1,0:T(1,128)} %constant.8.clone.sec_ref) | copy-start | bytes 6148
  11.2 11.8 %collective-permute-start.2 = (f32[18,8,384]{2,1,0:T(8,128)S(1)}, f32[18,8,384]{2,1,0:T(8,128)S(1)}, u32[]{:S(2)}, u32[]{:S(2)}) collective-permute-start(f32[18,8,384]{2,1,0:T(8,128)S(1)} %get-tuple-element.31), channel_id=1, source_target_pairs={{0,4},{1,5},{2,6},{3,7},{4,0},{5,1},{6,2},{7,3},{8,12},{9,13},{10,... | collective-permute-start | bytes 663560 | tf_op jit(solution)/shard_map/ppermute | solution.py:178
  16.8 11.8 %collective-permute-start.3 = (f32[18,8,384]{2,1,0:T(8,128)S(1)}, f32[18,8,384]{2,1,0:T(8,128)S(1)}, u32[]{:S(2)}, u32[]{:S(2)}) collective-permute-start(f32[18,8,384]{2,1,0:T(8,128)S(1)} %get-tuple-element.32), channel_id=1, source_target_pairs={{0,1},{1,0},{2,3},{3,2},{4,5},{5,4},{6,7},{7,6},{8,9},{9,8},{10,11... | collective-permute-start | bytes 663560 | tf_op jit(solution)/shard_map/ppermute | solution.py:178
  18.3 10.3 %collective-permute-start.4 = (f32[18,8,384]{2,1,0:T(8,128)S(1)}, f32[18,8,384]{2,1,0:T(8,128)S(1)}, u32[]{:S(2)}, u32[]{:S(2)}) collective-permute-start(f32[18,8,384]{2,1,0:T(8,128)S(1)} %get-tuple-element.33), channel_id=1, source_target_pairs={{0,5},{1,4},{2,7},{3,6},{4,1},{5,0},{6,3},{7,2},{8,13},{9,12},{10,... | collective-permute-start | bytes 663560 | tf_op jit(solution)/shard_map/ppermute | solution.py:178
  28.7 5.2 %collective-permute-start.5 = (f32[4,8,384]{2,1,0:T(8,128)S(1)}, f32[4,8,384]{2,1,0:T(8,128)S(1)}, u32[]{:S(2)}, u32[]{:S(2)}) collective-permute-start(f32[4,8,384]{2,1,0:T(8,128)S(1)} %get-tuple-element.35), channel_id=1, source_target_pairs={{0,2},{1,3},{2,0},{3,1},{4,6},{5,7},{6,4},{7,5},{8,10},{9,11},{10,... | collective-permute-start | bytes 147464 | tf_op jit(solution)/shard_map/ppermute | solution.py:178
  28.8 6.5 %collective-permute-start.6 = (f32[8,8,384]{2,1,0:T(8,128)S(1)}, f32[8,8,384]{2,1,0:T(8,128)S(1)}, u32[]{:S(2)}, u32[]{:S(2)}) collective-permute-start(f32[8,8,384]{2,1,0:T(8,128)S(1)} %get-tuple-element.40), channel_id=1, source_target_pairs={{0,8},{1,9},{2,10},{3,11},{4,12},{5,13},{6,14},{7,15},{8,0},{9,1},... | collective-permute-start | bytes 294920 | tf_op jit(solution)/shard_map/ppermute | solution.py:178
  30.4 10.8 %collective-permute-start.7 = (f32[8,8,384]{2,1,0:T(8,128)S(1)}, f32[8,8,384]{2,1,0:T(8,128)S(1)}, u32[]{:S(2)}, u32[]{:S(2)}) collective-permute-start(f32[8,8,384]{2,1,0:T(8,128)S(1)} %get-tuple-element.41), channel_id=1, source_target_pairs={{0,16},{1,17},{2,18},{3,19},{4,20},{5,21},{6,22},{7,23},{8,24},{9,... | collective-permute-start | bytes 294920 | tf_op jit(solution)/shard_map/ppermute | solution.py:178
  32.6 8.6 %collective-permute-start.8 = (f32[8,8,384]{2,1,0:T(8,128)S(1)}, f32[8,8,384]{2,1,0:T(8,128)S(1)}, u32[]{:S(2)}, u32[]{:S(2)}) collective-permute-start(f32[8,8,384]{2,1,0:T(8,128)S(1)} %get-tuple-element.42), channel_id=1, source_target_pairs={{0,24},{1,25},{2,26},{3,27},{4,28},{5,29},{6,30},{7,31},{8,16},{9,... | collective-permute-start | bytes 294920 | tf_op jit(solution)/shard_map/ppermute | solution.py:178
  42.7 1.2 %collective-permute-start.9 = (f32[2,8,256]{2,1,0:T(8,128)S(1)}, f32[2,8,256]{2,1,0:T(8,128)S(1)}, u32[]{:S(2)}, u32[]{:S(2)}) collective-permute-start(f32[2,8,256]{2,1,0:T(8,128)S(1)} %get-tuple-element.44), channel_id=1, source_target_pairs={{0,2},{1,3},{2,0},{3,1},{4,6},{5,7},{6,4},{7,5},{8,10},{9,11},{10,... | collective-permute-start | bytes 49160 | tf_op jit(solution)/shard_map/ppermute | solution.py:178
  44.0 3.7 %collective-permute-start.10 = (f32[2,4,256]{2,1,0:T(4,128)S(1)}, f32[2,4,256]{2,1,0:T(4,128)S(1)}, u32[]{:S(2)}, u32[]{:S(2)}) collective-permute-start(f32[2,4,256]{2,1,0:T(4,128)S(1)} %get-tuple-element.46), channel_id=1, source_target_pairs={{0,4},{1,5},{2,6},{3,7},{4,0},{5,1},{6,2},{7,3},{8,12},{9,13},{10,... | collective-permute-start | bytes 24584 | tf_op jit(solution)/shard_map/ppermute | solution.py:178
  44.8 3.7 %collective-permute-start.11 = (f32[2,4,256]{2,1,0:T(4,128)S(1)}, f32[2,4,256]{2,1,0:T(4,128)S(1)}, u32[]{:S(2)}, u32[]{:S(2)}) collective-permute-start(f32[2,4,256]{2,1,0:T(4,128)S(1)} %get-tuple-element.47), channel_id=1, source_target_pairs={{0,1},{1,0},{2,3},{3,2},{4,5},{5,4},{6,7},{7,6},{8,9},{9,8},{10,11... | collective-permute-start | bytes 24584 | tf_op jit(solution)/shard_map/ppermute | solution.py:178
  45.4 4.5 %collective-permute-start.12 = (f32[2,4,256]{2,1,0:T(4,128)S(1)}, f32[2,4,256]{2,1,0:T(4,128)S(1)}, u32[]{:S(2)}, u32[]{:S(2)}) collective-permute-start(f32[2,4,256]{2,1,0:T(4,128)S(1)} %get-tuple-element.48), channel_id=1, source_target_pairs={{0,5},{1,4},{2,7},{3,6},{4,1},{5,0},{6,3},{7,2},{8,13},{9,12},{10,... | collective-permute-start | bytes 24584 | tf_op jit(solution)/shard_map/ppermute | solution.py:178

commit v3 on v2

--- a/solution.py
+++ b/solution.py
@@ -254,8 +254,18 @@
     return load
 
 
-def sibling_kernel(views, slices, rows, band, scale, tan_hbm, drift_hbm, meas_ref, out_ref, own_buf, weights_ref,
-                   tan_ref, drift_ref, buf, terms, table_sem, sem, own_sem):
+def volume_window(vol_ref, half, half_cols, vbuf):
+    part, cols = vol_ref.shape[1:]
+    vbuf[:, 0:LANES] = jnp.zeros((part, LANES), jnp.float32)
+    vbuf[:, LANES : LANES + cols] = vol_ref[0]
+    vbuf[:, LANES + cols :] = jnp.zeros((part, LANES), jnp.float32)
+    width = half_cols + 2 * LANES
+    window = vbuf[:, pl.ds(pl.multiple_of(half * half_cols, LANES), width)]
+    return pltpu.roll(window, width - HALO, 1)[:, : half_cols + LANES]
+
+
+def sibling_kernel(views, slices, rows, band, scale, tan_hbm, drift_hbm, meas_ref, vol_ref, out_ref, own_buf,
+                   weights_ref, tan_ref, drift_ref, buf, terms, vbuf, table_sem, sem, own_sem):
     _, _, c, _ = coords()
     tiles = out_ref.shape[2] // LANES
     groups = slices // SUB
@@ -279,6 +289,10 @@
         for target in (buf, own_buf):
             target[g, 0] = zero
             target[g, tiles + 1] = zero
+    half_cols = out_ref.shape[2] - LANES
+    part = vol_ref.shape[1]
+    out_ref[slices, 0:part] = volume_window(vol_ref, 1 - c, half_cols, vbuf)
+    out_ref[slices, part:] = jnp.zeros((rows - part, half_cols + LANES), jnp.float32)
     for copy in tables:
         copy.wait()
     weights = view_weights(views, rows, band, scale, tan_ref, drift_ref)
@@ -306,55 +320,41 @@
     back_project(views, slices, rows, band, weights_ref[...].astype(jnp.bfloat16), load, out_ref, terms)
 
 
-def plane_pack_kernel(block, own_ref, got_ref, vol_ref, halo_ref, mine, to_x, to_y, to_xy, acc, vbuf):
-    slices, rows, half_cols = own_ref.shape
-    width = block + 2 * HALO
+def plane_pack_kernel(own_ref, got_ref, vol_ref, mine, to_x, to_y, to_xy, acc, both, vbuf):
+    slices, rows, half_width = own_ref.shape
+    width = mine.shape[2]
+    part = vol_ref.shape[1]
     z, x, c, y = coords()
-    acc[...] = own_ref[...] + got_ref[...]
-    part = vol_ref.shape[1]
-    cols = vol_ref.shape[2]
-    vbuf[:, 0:LANES] = jnp.zeros((2 * part, LANES), jnp.float32)
-    vbuf[:, cols + LANES :] = jnp.zeros((2 * part, LANES), jnp.float32)
-    both = jnp.concatenate([vol_ref[0], halo_ref[0]], axis=0)
-    vbuf[:, LANES : LANES + cols] = both
-    for out, (px, py) in ((mine, (x, y)), (to_x, (1 - x, y)), (to_y, (x, 1 - y)), (to_xy, (1 - x, 1 - y))):
-        q = 2 * px + py
-        out[0:slices] = acc[:, :, pl.ds(pl.multiple_of(q * block, LANES), width)]
-        for h in range(2):
-            begin = pl.multiple_of((4 * h + q) * block, LANES)
-            window = vbuf[:, pl.ds(begin, width + LANES)]
-            window = pltpu.roll(window, width + LANES - HALO, 1)
-            out[slices + h] = window[:, :width]
-
-
-def depth_pack_kernel(mine, got_x, got_y, got_xy, own_win, to_1, to_2, to_3, vol_own, vol_sib, acc):
-    slices = mine.shape[0] - 2
-    rows = mine.shape[1]
+    acc[...] = own_ref[...] + got_ref[0:slices]
+    here = volume_window(vol_ref, c, half_width - LANES, vbuf)
+    there = got_ref[slices, 0:part]
+    both[0:part] = jnp.where(c == 0, here, there)
+    both[part:] = jnp.where(c == 0, there, here)
+    for out, px, py in ((mine, x, y), (to_x, 1 - x, y), (to_y, x, 1 - y), (to_xy, 1 - x, 1 - y)):
+        begin = pl.multiple_of(py * (width - LANES), LANES)
+        for pz in range(slices // 4):
+            out[2 * pz : 2 * pz + 2] = acc[pl.ds(4 * pz + 2 * px, 2), :, pl.ds(begin, width)]
+        if out.shape[0] > slices // 2:
+            out[slices // 2] = both[:, pl.ds(begin, width)]
+
+
+def depth_pack_kernel(mine, got_x, got_y, got_xy, own_pair, to_1, to_2, to_3, vol_pair, acc):
+    count, rows, _ = acc.shape
     part = rows // 2
     z, x, c, y = coords()
-    acc[0:2] = jnp.zeros((2,) + acc.shape[1:], jnp.float32)
-    acc[slices + 2 :] = jnp.zeros((2,) + acc.shape[1:], jnp.float32)
-    acc[2 : slices + 2] = (mine[0:slices] + got_x[0:slices]) + (got_y[0:slices] + got_xy[0:slices])
-    for out, zz in (
-        (own_win, z),
+    acc[...] = (mine[0:count] + got_x[...]) + (got_y[0:count] + got_xy[...])
+    for out, pz in (
+        (own_pair, z),
         (to_1, jnp.where(z % 2 == 0, z + 1, z - 1)),
         (to_2, jnp.where(z < 2, z + 2, z - 2)),
         (to_3, 3 - z),
     ):
-        out[...] = acc[pl.ds(4 * zz, 8)]
-    for out, h in ((vol_own, c), (vol_sib, 1 - c)):
-        here, there = mine[slices + h], got_y[slices + h]
-        x_here, x_there = got_x[slices + h], got_xy[slices + h]
-        for source_x in range(2):
-            same = x == source_x
-            a = jnp.where(same, here, x_here)
-            b = jnp.where(same, there, x_there)
-            upper = jnp.where(y == 0, a, b)
-            lower = jnp.where(y == 0, b, a)
-            own_slice = jnp.concatenate([upper[:part], lower[:part]], axis=0)
-            halo_slice = jnp.concatenate([upper[part:], lower[part:]], axis=0)
-            out[1 + source_x] = own_slice
-            out[3 * source_x] = halo_slice
+        out[...] = acc[pl.ds(2 * pz, 2)]
+    here, there = mine[count], got_y[count]
+    upper = jnp.where(y == 0, here, there)
+    lower = jnp.where(y == 0, there, here)
+    for i in range(2):
+        vol_pair[i] = jnp.concatenate([upper[i * part : (i + 1) * part], lower[i * part : (i + 1) * part]], axis=0)
 
 
 def gram_kernel(rows, band, scale, tan_ref, sec_ref, drift_ref, after_ref, conv_ref, low_ref, high_ref):
@@ -434,22 +434,31 @@
             out[s, :, width - LANES :] = out[s, :, width - LANES :] - total
 
 
-def block_place(block, total_cols):
+def block_place(width, total_cols):
     z, x, c, y = coords()
-    index = (c * 2 + x) * 2 + y
-    return z, index * block - HALO, index == 0, index == total_cols // block - 1
-
-
-def first_normal_kernel(band, block, total_cols, vol_own, vol_sib, conv_ref, low_ref, high_ref, out, vols, work):
-    _, _, is_low, is_high = block_place(block, total_cols)
-    _, _, c, _ = coords()
-    for m in range(4):
-        vols[2 * m + c] = vol_own[m]
-        vols[2 * m + 1 - c] = vol_sib[m]
-    volumes = [vols[s] for s in range(8)]
+    block = width - 2 * HALO
+    index = c * 2 + y
+    return index * block - HALO, index == 0, index == total_cols // block - 1
+
+
+def first_normal_kernel(band, total_cols, vol_pair, conv_ref, low_ref, high_ref, out, work):
+    _, is_low, is_high = block_place(vol_pair.shape[2], total_cols)
+    volumes = [vol_pair[i] for i in range(2)]
     normal(volumes, conv_ref[...].astype(jnp.bfloat16), low_ref, high_ref, work, band, is_low, is_high)
-    for s in range(8):
-        out[s] = volumes[s] - work[s]
+    for i in range(2):
+        out[i] = volumes[i] - work[i]
+
+
+def half_pair_kernel(first_ref, own_pair, got_1, got_2, got_3, mine, to_x, to_diag, corr):
+    _, x, _, _ = coords()
+    corr[...] = (own_pair[...] + got_1[...]) + (got_2[...] + got_3[...])
+    half = first_ref[...] + corr[...]
+    mine[0:2] = half
+    mine[2:4] = corr[...]
+    to_x[0:2] = half
+    to_x[2] = corr[1 - x]
+    to_diag[0:2] = half
+    to_diag[2] = corr[x]
 
 
 def variation_step(half, z_of, first_col, depth, total_cols):
@@ -475,41 +484,42 @@
 
 
 def finish_kernel(
-    band, block, depth, total_cols,
-    first_ref, own_win, got_1, got_2, got_3, conv_ref, low_ref, high_ref, keep_ref, send_ref, corr, work, done,
+    band, depth, total_cols, mine, got_x, got_diag, conv_ref, low_ref, high_ref, keep_ref, send_ref, work, done
 ):
-    z, first_col, is_low, is_high = block_place(block, total_cols)
-    _, _, c, _ = coords()
-    corr[...] = (own_win[...] + got_1[...]) + (got_2[...] + got_3[...])
-    half = [first_ref[s] + corr[s] for s in range(8)]
-    volumes = variation_step(half, lambda w: 4 * z - 2 + w, first_col, depth, total_cols)
+    width = mine.shape[2]
+    first_col, is_low, is_high = block_place(width, total_cols)
+    z, x, c, _ = coords()
+    before = [jnp.where(x == 0, got_diag[i], got_x[i]) for i in range(3)]
+    after = [jnp.where(x == 0, got_x[i], got_diag[i]) for i in range(3)]
+    half = [before[0], before[1], mine[0], mine[1], after[0], after[1]]
+    corr = [before[2], mine[2], mine[3], after[2]]
+    slice_0 = 4 * z + 2 * x
+    volumes = variation_step(half, lambda w: slice_0 - 2 + w, first_col, depth, total_cols)
     normal(volumes, conv_ref[...].astype(jnp.bfloat16), low_ref, high_ref, work, band, is_low, is_high)
-    half = [volumes[s] + corr[s + 1] - work[s] for s in range(6)]
-    volumes = variation_step(half, lambda w: 4 * z - 1 + w, first_col, depth, total_cols)
-    width = volumes[0].shape[1]
-    for s in range(4):
-        done[s] = pltpu.roll(volumes[s], width - HALO, 1)[:, :block]
-    for px in range(2):
-        keep_ref[px] = done[2 * px + c]
-        send_ref[px] = done[2 * px + 1 - c]
-
-
-def result_pack_kernel(own_ref, got_ref, mine, to_x, to_y, to_xy):
-    z, x, c, y = coords()
-    part = own_ref.shape[1] // 2
-    for out, (px, py) in ((mine, (x, y)), (to_x, (1 - x, y)), (to_y, (x, 1 - y)), (to_xy, (1 - x, 1 - y))):
-        own, got = own_ref[px], got_ref[px]
-        out[c] = jnp.where(py == 0, own[:part], own[part:])
-        out[1 - c] = jnp.where(py == 0, got[:part], got[part:])
-
-
-def result_kernel(mine, got_x, got_y, got_xy, out):
-    z, x, c, y = coords()
-    block = mine.shape[2]
-    for ref, (px, py) in ((mine, (x, y)), (got_x, (1 - x, y)), (got_y, (x, 1 - y)), (got_xy, (1 - x, 1 - y))):
-        for h in range(2):
-            begin = pl.multiple_of((4 * h + 2 * px + py) * block, LANES)
-            out[0, :, pl.ds(begin, block)] = ref[h]
+    half = [volumes[s] + corr[s] - work[s] for s in range(4)]
+    volumes = variation_step(half, lambda w: slice_0 - 1 + w, first_col, depth, total_cols)
+    for s in range(2):
+        done[s] = pltpu.roll(volumes[s], width - HALO, 1)[:, : width - LANES]
+    keep_ref[...] = done[c]
+    send_ref[...] = done[1 - c]
+
+
+def result_pack_kernel(own_ref, got_ref, to_y):
+    _, _, c, y = coords()
+    part = to_y.shape[1]
+    own, got = own_ref[...], got_ref[...]
+    to_y[c] = jnp.where(y == 0, own[part:], own[:part])
+    to_y[1 - c] = jnp.where(y == 0, got[part:], got[:part])
+
+
+def result_kernel(own_ref, got_ref, got_y, out):
+    _, _, c, y = coords()
+    _, part, block = got_y.shape
+    own, got = own_ref[...], got_ref[...]
+    here = jnp.where(y == 0, own[:part], own[part:])
+    there = jnp.where(y == 0, got[:part], got[part:])
+    for value, h, q in ((here, c, y), (there, 1 - c, y), (got_y[0], 0, 1 - y), (got_y[1], 1, 1 - y)):
+        out[0, :, pl.ds(pl.multiple_of((2 * h + q) * block, LANES), block)] = value
 
 
 def f32(*shape):
@@ -521,6 +531,10 @@
 ANY_SPEC = pl.BlockSpec(memory_space=pl.ANY)
 HBM_SPEC = pl.BlockSpec(memory_space=pltpu.HBM)
 PARAMS = pltpu.CompilerParams(vmem_limit_bytes=40 * 1024 * 1024)
+
+
+def in_hbm(value):
+    return pltpu.with_memory_space_constraint(value, pltpu.HBM)
 
 
 def kernel_call(body, outs, in_specs, scratch, name, flops=0, size=0):
@@ -543,30 +557,29 @@
     rows = 2 * part
     band = rows // 2 + DMAX + 2
     total_angles = drift.shape[0]
-    block = cols // 8
     half_cols = cols // 2
     half_width = half_cols + LANES
-    width = block + 2 * HALO
+    width = cols // 4 + 2 * HALO
     tangent, secant = tan_and_secant(total_angles)
     scale = float(1.0 / np.sum(secant))
     tangent, secant = tangent.astype(np.float32), secant.astype(np.float32)
-
-    halo = move(start_volume, lambda z, x, c, y: (z + 1, 0, c, y) if x else (z - 1, 1, c, y))
 
     tiles = half_width // LANES
     groups = slices // SUB
     window = (groups, tiles + 2, views, SUB, LANES)
     table = (2 * (2 * band // STEP + 1) * rows, 2 * STEP * views)
     terms = pltpu.VMEM((2, 2 * STEP * views, half_width + LANES), jnp.bfloat16)
+    vbuf = pltpu.VMEM((part, cols + 2 * LANES), jnp.float32)
     sibling, own_buf, weights = kernel_call(
         functools.partial(sibling_kernel, views, slices, rows, band, scale),
-        [f32(slices, rows, half_width), f32(*window), f32(*table)],
-        [HBM_SPEC] * 3,
+        [f32(slices + 1, rows, half_width), f32(*window), f32(*table)],
+        [HBM_SPEC] * 3 + [VMEM_SPEC],
         [
             pltpu.SMEM((total_angles,), jnp.float32),
             pltpu.SMEM((total_angles,), jnp.int32),
             pltpu.VMEM(window, jnp.float32),
             terms,
+            vbuf,
             pltpu.SemaphoreType.DMA((2,)),
             pltpu.SemaphoreType.DMA((groups, tiles)),
             pltpu.SemaphoreType.DMA((groups, tiles)),
@@ -574,7 +587,7 @@
         "back_project_sibling",
         flops=2 * 10**9,
         size=2**21,
-    )(tangent, drift, measured)
+    )(in_hbm(jnp.asarray(tangent)), in_hbm(drift), in_hbm(measured), start_volume)
     got = move(sibling, lambda z, x, c, y: (z, x, 1 - c, y))
     own = kernel_call(
         functools.partial(own_kernel, views, slices, rows, band),
@@ -586,14 +599,14 @@
         size=2**21,
     )(own_buf, weights)
 
-    message = f32(slices + 2, rows, width)
+    count = slices // 2
     mine, to_x, to_y, to_xy = kernel_call(
-        functools.partial(plane_pack_kernel, block),
-        [message] * 4,
-        [VMEM_SPEC] * 4,
-        [pltpu.VMEM((slices, rows, half_width), jnp.float32), pltpu.VMEM((2 * part, cols + 2 * LANES), jnp.float32)],
+        plane_pack_kernel,
+        [f32(count + 1, rows, width), f32(count, rows, width), f32(count + 1, rows, width), f32(count, rows, width)],
+        [VMEM_SPEC] * 3,
+        [pltpu.VMEM((slices, rows, half_width), jnp.float32), pltpu.VMEM((rows, half_width), jnp.float32), vbuf],
         "plane_pack",
-    )(own, got, start_volume, halo)
+    )(own, got, start_volume)
     got_xy = move(to_xy, lambda z, x, c, y: (z, 1 - x, c, 1 - y))
     got_x = move(to_x, lambda z, x, c, y: (z, 1 - x, c, y))
     got_y = move(to_y, lambda z, x, c, y: (z, x, c, 1 - y))
@@ -608,46 +621,51 @@
         flops=10**9,
     )(tangent[None], secant[None], drift[None], mine)
 
-    window = f32(8, rows, width)
-    own_win, to_1, to_2, to_3, vol_own, vol_sib = kernel_call(
+    pair = f32(2, rows, width)
+    own_pair, to_1, to_2, to_3, vol_pair = kernel_call(
         depth_pack_kernel,
-        [window] * 4 + [f32(4, rows, width)] * 2,
+        [pair] * 5,
         [VMEM_SPEC] * 4,
-        [pltpu.VMEM((slices + 4, rows, width), jnp.float32)],
+        [pltpu.VMEM((count, rows, width), jnp.float32)],
         "depth_pack",
     )(mine, got_x, got_y, got_xy)
     got_2 = move(to_2, lambda z, x, c, y: (z ^ 2, x, c, y))
     got_1 = move(to_1, lambda z, x, c, y: (z ^ 1, x, c, y))
     got_3 = move(to_3, lambda z, x, c, y: (z ^ 3, x, c, y))
-    vol_got = move(vol_sib, lambda z, x, c, y: (z, x, 1 - c, y))
-
-    work = pltpu.VMEM((8, rows, width), jnp.float32)
+
     first = kernel_call(
-        functools.partial(first_normal_kernel, band, block, cols),
-        window,
-        [VMEM_SPEC] * 5,
-        [work, work],
+        functools.partial(first_normal_kernel, band, cols),
+        pair,
+        [VMEM_SPEC] * 4,
+        [pltpu.VMEM((2, rows, width), jnp.float32)],
         "first_normal",
         flops=10**9,
-    )(vol_own, vol_got, conv, low, high)
-
-    piece = f32(2, rows, block)
+    )(vol_pair, conv, low, high)
+
+    three = f32(3, rows, width)
+    mine, to_x, to_diag = kernel_call(
+        half_pair_kernel,
+        [f32(4, rows, width), three, three],
+        [VMEM_SPEC] * 5,
+        [pltpu.VMEM((2, rows, width), jnp.float32)],
+        "half_pair",
+    )(first, own_pair, got_1, got_2, got_3)
+    got_diag = move(to_diag, lambda z, x, c, y: (z + 1, 0, c, y) if x else (z - 1, 1, c, y))
+    got_x = move(to_x, lambda z, x, c, y: (z, 1 - x, c, y))
+
+    block = width - 2 * HALO
+    quarter = f32(rows, block)
     keep, send = kernel_call(
-        functools.partial(finish_kernel, band, block, slices, cols),
-        [piece, piece],
-        [VMEM_SPEC] * 8,
-        [work, work, pltpu.VMEM((4, rows, block), jnp.float32)],
+        functools.partial(finish_kernel, band, slices, cols),
+        [quarter, quarter],
+        [VMEM_SPEC] * 6,
+        [pltpu.VMEM((4, rows, width), jnp.float32), pltpu.VMEM((2, rows, block), jnp.float32)],
         "finish",
-    )(first, own_win, got_1, got_2, got_3, conv, low, high)
+    )(mine, got_x, got_diag, conv, low, high)
     swapped = move(send, lambda z, x, c, y: (z, x, 1 - c, y))
-    small = f32(2, part, block)
-    mine, to_x, to_y, to_xy = kernel_call(result_pack_kernel, [small] * 4, [VMEM_SPEC] * 2, [], "result_pack")(
-        keep, swapped
-    )
-    got_xy = move(to_xy, lambda z, x, c, y: (z, 1 - x, c, 1 - y))
-    got_x = move(to_x, lambda z, x, c, y: (z, 1 - x, c, y))
+    to_y = kernel_call(result_pack_kernel, f32(2, part, block), [VMEM_SPEC] * 2, [], "result_pack")(keep, swapped)
     got_y = move(to_y, lambda z, x, c, y: (z, x, c, 1 - y))
-    return kernel_call(result_kernel, f32(1, part, cols), [VMEM_SPEC] * 4, [], "result")(mine, got_x, got_y, got_xy)
+    return kernel_call(result_kernel, f32(1, part, cols), [VMEM_SPEC] * 3, [], "result")(keep, swapped, got_y)
 
 
 def summed_plan_fits(mesh, measured, start_volume):

time: 50.8 us -> 45 us (0.89)
  the two profiles are of different devices: /device:TPU:0 before, /device:TPU:2 now
where the time goes in v3:
time: 45 us; the launch traced here: 44.7 us
  waiting for transfers between devices  20.8 us (46%)
  starting transfers between devices  11.7 us (26%)
  Pallas kernels  11.3 us (25%)
  local copies, waits for them, and re-layouts  0.78 us (2%)
    ppermute x11, waiting for transfers between devices, move(): return lax.ppermute(value, ('wide', 'grp'), pairs)  20.8 us
    ppermute x11, starting transfers between devices, move(): return lax.ppermute(value, ('wide', 'grp'), pairs)  11.7 us
    pallas_call x1, Pallas kernels, summed_plan(): kernel_call(functools.partial(sibling_kernel, views, slices, rows, band,...  4.43 us
    pallas_call x1, Pallas kernels, summed_plan(): kernel_call(functools.partial(own_kernel, views, slices, rows, band), f32...  2.95 us
    pallas_call x1, Pallas kernels, summed_plan(): kernel_call(functools.partial(finish_kernel, band, slices, cols), [quarte...  1.55 us
  transfers between devices with their start and end apart: 11, of which 8 were waited for; matrix products, arithmetic and copies ran while one was open for 0% of the time, Pallas kernels for 10%

profile of v3, /device:TPU:2, one launch (start us, length us, event | category | flops | bytes accessed | tf_op | source)
XLA Modules:
  0.0 44.7 jit_solution(14080403837986103288)
XLA Ops:
  0.0 0.0 copy-start
  0.0 0.8 %copy-done = f32[1,4,2048]{2,1,0:T(4,128)S(1)} copy-done((f32[1,4,2048]{2,1,0:T(4,128)S(1)}, f32[1,4,2048]{2,1,0:T(4,128)}, u32[]{:S(2)}) %copy-start) | copy-done | bytes 32792
  0.8 4.4 %back_project_sibling.1 = (f32[17,8,1152]{2,1,0:T(8,128)S(1)}, f32[2,11,16,8,128]{4,3,2,1,0:T(8,128)S(1)}, f32[112,96]{1,0:T(8,128)S(1)}) custom-call(f32[512]{0:T(512)} %constant.6.clone.tan_hbm, s32[512]{0:T(512)} %drift_hbm.1, f32[16,16,2048]{2,1,0:T(8,128)} %meas_ref.1, f32[1,4,2048]{2,1,0:T(4,128)S(1)} %copy-done), custom_call_target="tpu_custom_call" | custom-call | flops 2000000000 | bytes 2097152 | tf_op jit(solution)/shard_map/back_project_sibling/pallas_call | solution.py:573
  5.2 0.1 collective-permute-start
  5.3 0.0 copy-start.1
  5.3 0.0 copy-start.2
  5.3 0.0 copy-start.3
  5.3 0.0 copy-start.4
  5.3 3.0 %back_project_own.1.own_ref = f32[16,8,1152]{2,1,0:T(8,128)S(1)} custom-call(f32[2,11,16,8,128]{4,3,2,1,0:T(8,128)S(1)} %get-tuple-element.25.buf, f32[112,96]{1,0:T(8,128)S(1)} %get-tuple-element.26.weights_ref), custom_call_target="tpu_custom_call" | custom-call | flops 2000000000 | bytes 2097152 | tf_op jit(solution)/shard_map/back_project_own/pallas_call | solution.py:592
  8.3 0.0 collective-permute-done.got_ref
  8.3 0.0 copy-done.1
  8.3 0.2 plane_pack.1
  8.5 1.6 %collective-permute-start.2 = (f32[9,8,640]{2,1,0:T(8,128)S(1)}, f32[9,8,640]{2,1,0:T(8,128)S(1)}, u32[]{:S(2)}, u32[]{:S(2)}) collective-permute-start(f32[9,8,640]{2,1,0:T(8,128)S(1)} %get-tuple-element.30), channel_id=1, source_target_pairs={{0,1},{1,0},{2,3},{3,2},{4,5},{5,4},{6,7},{7,6},{8,9},{9,8},{10,11... | collective-permute-start | bytes 552968 | tf_op jit(solution)/shard_map/ppermute | solution.py:178
  10.1 0.5 %collective-permute-start.1 = (f32[8,8,640]{2,1,0:T(8,128)S(1)}, f32[8,8,640]{2,1,0:T(8,128)S(1)}, u32[]{:S(2)}, u32[]{:S(2)}) collective-permute-start(f32[8,8,640]{2,1,0:T(8,128)S(1)} %get-tuple-element.29), channel_id=1, source_target_pairs={{0,4},{1,5},{2,6},{3,7},{4,0},{5,1},{6,2},{7,3},{8,12},{9,13},{10,... | collective-permute-start | bytes 491528 | tf_op jit(solution)/shard_map/ppermute | solution.py:178
  10.6 1.4 %collective-permute-start.3 = (f32[8,8,640]{2,1,0:T(8,128)S(1)}, f32[8,8,640]{2,1,0:T(8,128)S(1)}, u32[]{:S(2)}, u32[]{:S(2)}) collective-permute-start(f32[8,8,640]{2,1,0:T(8,128)S(1)} %get-tuple-element.31), channel_id=1, source_target_pairs={{0,5},{1,4},{2,7},{3,6},{4,1},{5,0},{6,3},{7,2},{8,13},{9,12},{10,... | collective-permute-start | bytes 491528 | tf_op jit(solution)/shard_map/ppermute | solution.py:178
  12.0 0.0 copy-done.2
  12.0 0.0 copy-done.3
  12.0 0.0 copy-done.4
  12.0 0.7 %gram.1 = (f32[48,256]{1,0:T(8,128)S(1)}, f32[80,80]{1,0:T(8,128)S(1)}, f32[80,80]{1,0:T(8,128)S(1)}) custom-call(f32[1,512]{1,0:T(1,128)S(1)} %copy-done.4, f32[1,512]{1,0:T(1,128)S(1)} %copy-done.3, s32[1,512]{1,0:T(1,128)S(1)} %bitcast.1, f32[9,8,640]{2,1,0:T(8,128)S(1)} %get-tuple-element.28.mine.after_ref), custom_call_target="tpu_custom_call" | custom-call | flops 1000000000 | tf_op jit(solution)/shard_map/gram/pallas_call | solution.py:615
  12.7 4.4 %collective-permute-done.1.got_x = f32[8,8,640]{2,1,0:T(8,128)S(1)} collective-permute-done((f32[8,8,640]{2,1,0:T(8,128)S(1)}, f32[8,8,640]{2,1,0:T(8,128)S(1)}, u32[]{:S(2)}, u32[]{:S(2)}) %collective-permute-start.1) | collective-permute-done | bytes 163872 | tf_op jit(solution)/shard_map/ppermute | solution.py:178
  17.1 2.7 %collective-permute-done.3.got_xy = f32[8,8,640]{2,1,0:T(8,128)S(1)} collective-permute-done((f32[8,8,640]{2,1,0:T(8,128)S(1)}, f32[8,8,640]{2,1,0:T(8,128)S(1)}, u32[]{:S(2)}, u32[]{:S(2)}) %collective-permute-start.3) | collective-permute-done | bytes 163872 | tf_op jit(solution)/shard_map/ppermute | solution.py:178
  19.8 0.0 collective-permute-done.2.got_y
  19.8 0.1 depth_pack.1
  19.9 1.6 %collective-permute-start.4 = (f32[2,8,640]{2,1,0:T(8,128)S(1)}, f32[2,8,640]{2,1,0:T(8,128)S(1)}, u32[]{:S(2)}, u32[]{:S(2)}) collective-permute-start(f32[2,8,640]{2,1,0:T(8,128)S(1)} %get-tuple-element.37), channel_id=1, source_target_pairs={{0,8},{1,9},{2,10},{3,11},{4,12},{5,13},{6,14},{7,15},{8,0},{9,1},... | collective-permute-start | bytes 122888 | tf_op jit(solution)/shard_map/ppermute | solution.py:178
  21.5 2.6 %collective-permute-start.5 = (f32[2,8,640]{2,1,0:T(8,128)S(1)}, f32[2,8,640]{2,1,0:T(8,128)S(1)}, u32[]{:S(2)}, u32[]{:S(2)}) collective-permute-start(f32[2,8,640]{2,1,0:T(8,128)S(1)} %get-tuple-element.38), channel_id=1, source_target_pairs={{0,16},{1,17},{2,18},{3,19},{4,20},{5,21},{6,22},{7,23},{8,24},{9,... | collective-permute-start | bytes 122888 | tf_op jit(solution)/shard_map/ppermute | solution.py:178
  24.1 0.2 collective-permute-start.6
  24.3 0.8 %first_normal.1.first_ref = f32[2,8,640]{2,1,0:T(8,128)S(1)} custom-call(f32[2,8,640]{2,1,0:T(8,128)S(1)} %get-tuple-element.32.vol_pair, f32[48,256]{1,0:T(8,128)S(1)} %get-tuple-element.33.conv_ref, f32[80,80]{1,0:T(8,128)S(1)} %get-tuple-element.34.low_ref, f32[80,80]{1,0:T(8,128)S(1)} %get-tuple-element.35.high_ref), custom_call_target="tpu_custom_call" | custom-call | flops 1000000000 | tf_op jit(solution)/shard_map/first_normal/pallas_call | solution.py:636
  25.1 0.0 collective-permute-done.4.got_1
  25.1 1.7 %collective-permute-done.5.got_2 = f32[2,8,640]{2,1,0:T(8,128)S(1)} collective-permute-done((f32[2,8,640]{2,1,0:T(8,128)S(1)}, f32[2,8,640]{2,1,0:T(8,128)S(1)}, u32[]{:S(2)}, u32[]{:S(2)}) %collective-permute-start.5) | collective-permute-done | bytes 40992 | tf_op jit(solution)/shard_map/ppermute | solution.py:178
  26.8 3.1 %collective-permute-done.6.got_3 = f32[2,8,640]{2,1,0:T(8,128)S(1)} collective-permute-done((f32[2,8,640]{2,1,0:T(8,128)S(1)}, f32[2,8,640]{2,1,0:T(8,128)S(1)}, u32[]{:S(2)}, u32[]{:S(2)}) %collective-permute-start.6) | collective-permute-done | bytes 40992 | tf_op jit(solution)/shard_map/ppermute | solution.py:178
  29.9 0.6 %collective-permute-start.7 = (f32[3,8,640]{2,1,0:T(8,128)S(1)}, f32[3,8,640]{2,1,0:T(8,128)S(1)}, u32[]{:S(2)}, u32[]{:S(2)}) collective-permute-start(f32[3,8,640]{2,1,0:T(8,128)S(1)} %get-tuple-element.41), channel_id=1, source_target_pairs={{0,4},{1,5},{2,6},{3,7},{4,0},{5,1},{6,2},{7,3},{8,12},{9,13},{10,... | collective-permute-start | bytes 184328 | tf_op jit(solution)/shard_map/ppermute | solution.py:178
  30.5 1.9 %collective-permute-start.8 = (f32[3,8,640]{2,1,0:T(8,128)S(1)}, f32[3,8,640]{2,1,0:T(8,128)S(1)}, u32[]{:S(2)}, u32[]{:S(2)}) collective-permute-start(f32[3,8,640]{2,1,0:T(8,128)S(1)} %get-tuple-element.42), channel_id=1, source_target_pairs={{4,8},{5,9},{6,10},{7,11},{8,4},{9,5},{10,6},{11,7},{12,16},{13,17... | collective-permute-start | bytes 184328 | tf_op jit(solution)/shard_map/ppermute | solution.py:178
  32.4 2.1 %collective-permute-done.7.got_x = f32[3,8,640]{2,1,0:T(8,128)S(1)} collective-permute-done((f32[3,8,640]{2,1,0:T(8,128)S(1)}, f32[3,8,640]{2,1,0:T(8,128)S(1)}, u32[]{:S(2)}, u32[]{:S(2)}) %collective-permute-start.7) | collective-permute-done | bytes 61472 | tf_op jit(solution)/shard_map/ppermute | solution.py:178
  34.6 2.9 %collective-permute-done.8.got_diag = f32[3,8,640]{2,1,0:T(8,128)S(1)} collective-permute-done((f32[3,8,640]{2,1,0:T(8,128)S(1)}, f32[3,8,640]{2,1,0:T(8,128)S(1)}, u32[]{:S(2)}, u32[]{:S(2)}) %collective-permute-start.8) | collective-permute-done | bytes 61472 | tf_op jit(solution)/shard_map/ppermute | solution.py:178
  37.5 1.6 %finish.1 = (f32[8,512]{1,0:T(8,128)S(1)}, f32[8,512]{1,0:T(8,128)S(1)}) custom-call(f32[4,8,640]{2,1,0:T(8,128)S(1)} %get-tuple-element.40.mine, f32[3,8,640]{2,1,0:T(8,128)S(1)} %collective-permute-done.7.got_x, f32[3,8,640]{2,1,0:T(8,128)S(1)} %collective-permute-done.8.got_diag, f32[48,256]{1,0:T(8,128)S(1)} %get-tuple-element.33.conv_ref, ...), custom_call_target="tpu_custom_call" | custom-call | tf_op jit(solution)/shard_map/finish/pallas_call | solution.py:658
  39.1 0.1 collective-permute-start.9
  39.2 1.2 %collective-permute-done.9.got_ref = f32[8,512]{1,0:T(8,128)S(1)} collective-permute-done((f32[8,512]{1,0:T(8,128)S(1)}, f32[8,512]{1,0:T(8,128)S(1)}, u32[]{:S(2)}, u32[]{:S(2)}) %collective-permute-start.9) | collective-permute-done | bytes 16416 | tf_op jit(solution)/shard_map/ppermute | solution.py:178
  40.3 1.1 %collective-permute-start.10 = (f32[2,4,512]{2,1,0:T(4,128)S(1)}, f32[2,4,512]{2,1,0:T(4,128)S(1)}, u32[]{:S(2)}, u32[]{:S(2)}) collective-permute-start(f32[2,4,512]{2,1,0:T(4,128)S(1)} %result_pack.1), channel_id=1, source_target_pairs={{0,1},{1,0},{2,3},{3,2},{4,5},{5,4},{6,7},{7,6},{8,9},{9,8},{10,11... | collective-permute-start | bytes 49160 | tf_op jit(solution)/shard_map/ppermute | solution.py:178
  41.4 2.7 %collective-permute-done.10.got_y = f32[2,4,512]{2,1,0:T(4,128)S(1)} collective-permute-done((f32[2,4,512]{2,1,0:T(4,128)S(1)}, f32[2,4,512]{2,1,0:T(4,128)S(1)}, u32[]{:S(2)}, u32[]{:S(2)}) %collective-permute-start.10) | collective-permute-done | bytes 16416 | tf_op jit(solution)/shard_map/ppermute | solution.py:178
  44.1 0.6 %result.1 = f32[1,4,2048]{2,1,0:T(4,128)} custom-call(f32[8,512]{1,0:T(8,128)S(1)} %get-tuple-element.43.own_ref, f32[8,512]{1,0:T(8,128)S(1)} %collective-permute-done.9.got_ref, f32[2,4,512]{2,1,0:T(4,128)S(1)} %collective-permute-done.10.got_y), custom_call_target="tpu_custom_call" | custom-call | tf_op jit(solution)/shard_map/result/pallas_call | solution.py:668
  (2 shorter events, 0.0 us)
Async XLA Ops:
  0.0 0.8 %copy-start = (f32[1,4,2048]{2,1,0:T(4,128)S(1)}, f32[1,4,2048]{2,1,0:T(4,128)}, u32[]{:S(2)}) copy-start(f32[1,4,2048]{2,1,0:T(4,128)} %vol_ref.3) | copy-start | bytes 98308
  5.2 3.1 %collective-permute-start = (f32[17,8,1152]{2,1,0:T(8,128)S(1)}, f32[17,8,1152]{2,1,0:T(8,128)S(1)}, u32[]{:S(2)}, u32[]{:S(2)}) collective-permute-start(f32[17,8,1152]{2,1,0:T(8,128)S(1)} %get-tuple-element.27), channel_id=1, source_target_pairs={{0,2},{1,3},{2,0},{3,1},{4,6},{5,7},{6,4},{7,5},{8,10},{9,11},{10,... | collective-permute-start | bytes 1880072 | tf_op jit(solution)/shard_map/ppermute | solution.py:178
  5.3 3.0 %copy-start.1 = (f32[1,4,2048]{2,1,0:T(4,128)S(1)}, f32[1,4,2048]{2,1,0:T(4,128)}, u32[]{:S(2)}) copy-start(f32[1,4,2048]{2,1,0:T(4,128)} %vol_ref.3) | copy-start | bytes 98308
  5.3 6.7 %copy-start.2 = (s32[512]{0:T(512)S(1)}, s32[512]{0:T(512)}, u32[]{:S(2)}) copy-start(s32[512]{0:T(512)} %drift_hbm.1) | copy-start | bytes 6148
  5.3 6.7 %copy-start.3 = (f32[1,512]{1,0:T(1,128)S(1)}, f32[1,512]{1,0:T(1,128)}, u32[]{:S(2)}) copy-start(f32[1,512]{1,0:T(1,128)} %constant.8.clone.sec_ref) | copy-start | bytes 6148
  5.3 6.7 %copy-start.4 = (f32[1,512]{1,0:T(1,128)S(1)}, f32[1,512]{1,0:T(1,128)}, u32[]{:S(2)}) copy-start(f32[1,512]{1,0:T(1,128)} %constant.7.clone.tan_ref) | copy-start | bytes 6148
  8.5 11.3 %collective-permute-start.2 = (f32[9,8,640]{2,1,0:T(8,128)S(1)}, f32[9,8,640]{2,1,0:T(8,128)S(1)}, u32[]{:S(2)}, u32[]{:S(2)}) collective-permute-start(f32[9,8,640]{2,1,0:T(8,128)S(1)} %get-tuple-element.30), channel_id=1, source_target_pairs={{0,1},{1,0},{2,3},{3,2},{4,5},{5,4},{6,7},{7,6},{8,9},{9,8},{10,11... | collective-permute-start | bytes 552968 | tf_op jit(solution)/shard_map/ppermute | solution.py:178
  10.1 7.0 %collective-permute-start.1 = (f32[8,8,640]{2,1,0:T(8,128)S(1)}, f32[8,8,640]{2,1,0:T(8,128)S(1)}, u32[]{:S(2)}, u32[]{:S(2)}) collective-permute-start(f32[8,8,640]{2,1,0:T(8,128)S(1)} %get-tuple-element.29), channel_id=1, source_target_pairs={{0,4},{1,5},{2,6},{3,7},{4,0},{5,1},{6,2},{7,3},{8,12},{9,13},{10,... | collective-permute-start | bytes 491528 | tf_op jit(solution)/shard_map/ppermute | solution.py:178
  10.6 9.2 %collective-permute-start.3 = (f32[8,8,640]{2,1,0:T(8,128)S(1)}, f32[8,8,640]{2,1,0:T(8,128)S(1)}, u32[]{:S(2)}, u32[]{:S(2)}) collective-permute-start(f32[8,8,640]{2,1,0:T(8,128)S(1)} %get-tuple-element.31), channel_id=1, source_target_pairs={{0,5},{1,4},{2,7},{3,6},{4,1},{5,0},{6,3},{7,2},{8,13},{9,12},{10,... | collective-permute-start | bytes 491528 | tf_op jit(solution)/shard_map/ppermute | solution.py:178
  19.9 5.3 %collective-permute-start.4 = (f32[2,8,640]{2,1,0:T(8,128)S(1)}, f32[2,8,640]{2,1,0:T(8,128)S(1)}, u32[]{:S(2)}, u32[]{:S(2)}) collective-permute-start(f32[2,8,640]{2,1,0:T(8,128)S(1)} %get-tuple-element.37), channel_id=1, source_target_pairs={{0,8},{1,9},{2,10},{3,11},{4,12},{5,13},{6,14},{7,15},{8,0},{9,1},... | collective-permute-start | bytes 122888 | tf_op jit(solution)/shard_map/ppermute | solution.py:178
  21.5 5.3 %collective-permute-start.5 = (f32[2,8,640]{2,1,0:T(8,128)S(1)}, f32[2,8,640]{2,1,0:T(8,128)S(1)}, u32[]{:S(2)}, u32[]{:S(2)}) collective-permute-start(f32[2,8,640]{2,1,0:T(8,128)S(1)} %get-tuple-element.38), channel_id=1, source_target_pairs={{0,16},{1,17},{2,18},{3,19},{4,20},{5,21},{6,22},{7,23},{8,24},{9,... | collective-permute-start | bytes 122888 | tf_op jit(solution)/shard_map/ppermute | solution.py:178
  24.1 5.8 %collective-permute-start.6 = (f32[2,8,640]{2,1,0:T(8,128)S(1)}, f32[2,8,640]{2,1,0:T(8,128)S(1)}, u32[]{:S(2)}, u32[]{:S(2)}) collective-permute-start(f32[2,8,640]{2,1,0:T(8,128)S(1)} %get-tuple-element.39), channel_id=1, source_target_pairs={{0,24},{1,25},{2,26},{3,27},{4,28},{5,29},{6,30},{7,31},{8,16},{9,... | collective-permute-start | bytes 122888 | tf_op jit(solution)/shard_map/ppermute | solution.py:178
  29.9 4.7 %collective-permute-start.7 = (f32[3,8,640]{2,1,0:T(8,128)S(1)}, f32[3,8,640]{2,1,0:T(8,128)S(1)}, u32[]{:S(2)}, u32[]{:S(2)}) collective-permute-start(f32[3,8,640]{2,1,0:T(8,128)S(1)} %get-tuple-element.41), channel_id=1, source_target_pairs={{0,4},{1,5},{2,6},{3,7},{4,0},{5,1},{6,2},{7,3},{8,12},{9,13},{10,... | collective-permute-start | bytes 184328 | tf_op jit(solution)/shard_map/ppermute | solution.py:178
  30.5 7.0 %collective-permute-start.8 = (f32[3,8,640]{2,1,0:T(8,128)S(1)}, f32[3,8,640]{2,1,0:T(8,128)S(1)}, u32[]{:S(2)}, u32[]{:S(2)}) collective-permute-start(f32[3,8,640]{2,1,0:T(8,128)S(1)} %get-tuple-element.42), channel_id=1, source_target_pairs={{4,8},{5,9},{6,10},{7,11},{8,4},{9,5},{10,6},{11,7},{12,16},{13,17... | collective-permute-start | bytes 184328 | tf_op jit(solution)/shard_map/ppermute | solution.py:178
  39.1 1.2 %collective-permute-start.9 = (f32[8,512]{1,0:T(8,128)S(1)}, f32[8,512]{1,0:T(8,128)S(1)}, u32[]{:S(2)}, u32[]{:S(2)}) collective-permute-start(f32[8,512]{1,0:T(8,128)S(1)} %get-tuple-element.44), channel_id=1, source_target_pairs={{0,2},{1,3},{2,0},{3,1},{4,6},{5,7},{6,4},{7,5},{8,10},{9,11},{10,... | collective-permute-start | bytes 49160 | tf_op jit(solution)/shard_map/ppermute | solution.py:178
  40.3 3.7 %collective-permute-start.10 = (f32[2,4,512]{2,1,0:T(4,128)S(1)}, f32[2,4,512]{2,1,0:T(4,128)S(1)}, u32[]{:S(2)}, u32[]{:S(2)}) collective-permute-start(f32[2,4,512]{2,1,0:T(4,128)S(1)} %result_pack.1), channel_id=1, source_target_pairs={{0,1},{1,0},{2,3},{3,2},{4,5},{5,4},{6,7},{7,6},{8,9},{9,8},{10,11... | collective-permute-start | bytes 49160 | tf_op jit(solution)/shard_map/ppermute | solution.py:178

commit v4 on v3

--- a/solution.py
+++ b/solution.py
@@ -264,8 +264,8 @@
     return pltpu.roll(window, width - HALO, 1)[:, : half_cols + LANES]
 
 
-def sibling_kernel(views, slices, rows, band, scale, tan_hbm, drift_hbm, meas_ref, vol_ref, out_ref, own_buf,
-                   weights_ref, tan_ref, drift_ref, buf, terms, vbuf, table_sem, sem, own_sem):
+def sibling_kernel(views, slices, rows, band, scale, tan_hbm, drift_hbm, meas_ref, vol_hbm, out_ref, own_buf,
+                   weights_ref, tan_ref, drift_ref, vol_ref, buf, terms, vbuf, table_sem, sem, own_sem):
     _, _, c, _ = coords()
     tiles = out_ref.shape[2] // LANES
     groups = slices // SUB
@@ -280,19 +280,16 @@
         pltpu.make_async_copy(tan_hbm, tan_ref, table_sem.at[0]),
         pltpu.make_async_copy(drift_hbm, drift_ref, table_sem.at[1]),
     ]
+    vol_copy = pltpu.make_async_copy(vol_hbm, vol_ref, table_sem.at[2])
     first = [[fetch(1 - c, g, t, buf, sem.at[g, t]) for t in range(tiles)] for g in range(groups)]
     later = [[fetch(c, g, t, own_buf, own_sem.at[g, t]) for t in range(tiles)] for g in range(groups)]
-    for copy in tables + first[0] + first[1] + later[0] + later[1]:
+    for copy in tables + first[0] + first[1] + [vol_copy] + later[0] + later[1]:
         copy.start()
     zero = jnp.zeros((views, SUB, LANES), jnp.float32)
     for g in range(groups):
         for target in (buf, own_buf):
             target[g, 0] = zero
             target[g, tiles + 1] = zero
-    half_cols = out_ref.shape[2] - LANES
-    part = vol_ref.shape[1]
-    out_ref[slices, 0:part] = volume_window(vol_ref, 1 - c, half_cols, vbuf)
-    out_ref[slices, part:] = jnp.zeros((rows - part, half_cols + LANES), jnp.float32)
     for copy in tables:
         copy.wait()
     weights = view_weights(views, rows, band, scale, tan_ref, drift_ref)
@@ -307,6 +304,11 @@
         return load(s)
 
     back_project(views, slices, rows, band, weights, load_strip, out_ref, terms)
+    half_cols = out_ref.shape[2] - LANES
+    part = vol_ref.shape[1]
+    vol_copy.wait()
+    out_ref[slices, 0:part] = volume_window(vol_ref, 1 - c, half_cols, vbuf)
+    out_ref[slices, part:] = jnp.zeros((rows - part, half_cols + LANES), jnp.float32)
     for group in later:
         for copy in group:
             copy.wait()
@@ -338,7 +340,7 @@
             out[slices // 2] = both[:, pl.ds(begin, width)]
 
 
-def depth_pack_kernel(mine, got_x, got_y, got_xy, own_pair, to_1, to_2, to_3, vol_pair, acc):
+def depth_pack_kernel(mine, got_xy, got_x, got_y, own_pair, to_1, to_2, to_3, vol_pair, acc):
     count, rows, _ = acc.shape
     part = rows // 2
     z, x, c, y = coords()
@@ -449,7 +451,7 @@
         out[i] = volumes[i] - work[i]
 
 
-def half_pair_kernel(first_ref, own_pair, got_1, got_2, got_3, mine, to_x, to_diag, corr):
+def half_pair_kernel(first_ref, own_pair, got_3, got_2, got_1, mine, to_x, to_diag, corr):
     _, x, _, _ = coords()
     corr[...] = (own_pair[...] + got_1[...]) + (got_2[...] + got_3[...])
     half = first_ref[...] + corr[...]
@@ -484,7 +486,7 @@
 
 
 def finish_kernel(
-    band, depth, total_cols, mine, got_x, got_diag, conv_ref, low_ref, high_ref, keep_ref, send_ref, work, done
+    band, depth, total_cols, mine, got_diag, got_x, conv_ref, low_ref, high_ref, keep_ref, send_ref, work, done
 ):
     width = mine.shape[2]
     first_col, is_low, is_high = block_place(width, total_cols)
@@ -573,21 +575,22 @@
     sibling, own_buf, weights = kernel_call(
         functools.partial(sibling_kernel, views, slices, rows, band, scale),
         [f32(slices + 1, rows, half_width), f32(*window), f32(*table)],
-        [HBM_SPEC] * 3 + [VMEM_SPEC],
+        [HBM_SPEC] * 4,
         [
             pltpu.SMEM((total_angles,), jnp.float32),
             pltpu.SMEM((total_angles,), jnp.int32),
+            pltpu.VMEM((1, part, cols), jnp.float32),
             pltpu.VMEM(window, jnp.float32),
             terms,
             vbuf,
-            pltpu.SemaphoreType.DMA((2,)),
+            pltpu.SemaphoreType.DMA((3,)),
             pltpu.SemaphoreType.DMA((groups, tiles)),
             pltpu.SemaphoreType.DMA((groups, tiles)),
         ],
         "back_project_sibling",
         flops=2 * 10**9,
         size=2**21,
-    )(in_hbm(jnp.asarray(tangent)), in_hbm(drift), in_hbm(measured), start_volume)
+    )(in_hbm(jnp.asarray(tangent)), in_hbm(drift), in_hbm(measured), in_hbm(start_volume))
     got = move(sibling, lambda z, x, c, y: (z, x, 1 - c, y))
     own = kernel_call(
         functools.partial(own_kernel, views, slices, rows, band),
@@ -628,7 +631,7 @@
         [VMEM_SPEC] * 4,
         [pltpu.VMEM((count, rows, width), jnp.float32)],
         "depth_pack",
-    )(mine, got_x, got_y, got_xy)
+    )(mine, got_xy, got_x, got_y)
     got_2 = move(to_2, lambda z, x, c, y: (z ^ 2, x, c, y))
     got_1 = move(to_1, lambda z, x, c, y: (z ^ 1, x, c, y))
     got_3 = move(to_3, lambda z, x, c, y: (z ^ 3, x, c, y))
@@ -649,7 +652,7 @@
         [VMEM_SPEC] * 5,
         [pltpu.VMEM((2, rows, width), jnp.float32)],
         "half_pair",
-    )(first, own_pair, got_1, got_2, got_3)
+    )(first, own_pair, got_3, got_2, got_1)
     got_diag = move(to_diag, lambda z, x, c, y: (z + 1, 0, c, y) if x else (z - 1, 1, c, y))
     got_x = move(to_x, lambda z, x, c, y: (z, 1 - x, c, y))
 
@@ -661,7 +664,7 @@
         [VMEM_SPEC] * 6,
         [pltpu.VMEM((4, rows, width), jnp.float32), pltpu.VMEM((2, rows, block), jnp.float32)],
         "finish",
-    )(mine, got_x, got_diag, conv, low, high)
+    )(mine, got_diag, got_x, conv, low, high)
     swapped = move(send, lambda z, x, c, y: (z, x, 1 - c, y))
     to_y = kernel_call(result_pack_kernel, f32(2, part, block), [VMEM_SPEC] * 2, [], "result_pack")(keep, swapped)
     got_y = move(to_y, lambda z, x, c, y: (z, x, c, 1 - y))

time: 45 us -> 42.8 us (0.951)
  the two profiles are of different devices: /device:TPU:2 before, /device:TPU:0 now
where the time goes in v4:
time: 42.8 us; the launch traced here: 42.2 us
  waiting for transfers between devices  16.9 us (39%)
  starting transfers between devices  13.8 us (32%)
  Pallas kernels  11.4 us (27%)
    ppermute x11, waiting for transfers between devices, move(): return lax.ppermute(value, ('wide', 'grp'), pairs)  16.9 us
    ppermute x11, starting transfers between devices, move(): return lax.ppermute(value, ('wide', 'grp'), pairs)  13.8 us
    pallas_call x1, Pallas kernels, summed_plan(): kernel_call(functools.partial(sibling_kernel, views, slices, rows, band,...  4.51 us
    pallas_call x1, Pallas kernels, summed_plan(): kernel_call(functools.partial(own_kernel, views, slices, rows, band), f32...  2.95 us
    pallas_call x1, Pallas kernels, summed_plan(): kernel_call(functools.partial(finish_kernel, band, slices, cols), [quarte...  1.56 us
  transfers between devices with their start and end apart: 11, of which 7 were waited for; matrix products, arithmetic and copies ran while one was open for 0% of the time, Pallas kernels for 10%

profile of v4, /device:TPU:0, one launch (start us, length us, event | category | flops | bytes accessed | tf_op | source)
XLA Modules:
  0.0 42.2 jit_solution(10990788936817752842)
XLA Ops:
  0.0 4.5 %back_project_sibling.1 = (f32[17,8,1152]{2,1,0:T(8,128)S(1)}, f32[2,11,16,8,128]{4,3,2,1,0:T(8,128)S(1)}, f32[112,96]{1,0:T(8,128)S(1)}) custom-call(f32[512]{0:T(512)} %constant.6.clone.tan_hbm, s32[512]{0:T(512)} %drift_hbm.1, f32[16,16,2048]{2,1,0:T(8,128)} %meas_ref.1, f32[1,4,2048]{2,1,0:T(4,128)} %vol_ref.1), custom_call_target="tpu_custom_call" | custom-call | flops 2000000000 | bytes 2097152 | tf_op jit(solution)/shard_map/back_project_sibling/pallas_call | solution.py:575
  4.5 0.5 %collective-permute-start = (f32[17,8,1152]{2,1,0:T(8,128)S(1)}, f32[17,8,1152]{2,1,0:T(8,128)S(1)}, u32[]{:S(2)}, u32[]{:S(2)}) collective-permute-start(f32[17,8,1152]{2,1,0:T(8,128)S(1)} %get-tuple-element.27), channel_id=1, source_target_pairs={{0,2},{1,3},{2,0},{3,1},{4,6},{5,7},{6,4},{7,5},{8,10},{9,11},{10,... | collective-permute-start | bytes 1880072 | tf_op jit(solution)/shard_map/ppermute | solution.py:178
  5.0 0.0 copy-start
  5.0 0.0 copy-start.1
  5.0 0.0 copy-start.2
  5.0 0.0 copy-start.3
  5.1 3.0 %back_project_own.1.own_ref = f32[16,8,1152]{2,1,0:T(8,128)S(1)} custom-call(f32[2,11,16,8,128]{4,3,2,1,0:T(8,128)S(1)} %get-tuple-element.25.buf, f32[112,96]{1,0:T(8,128)S(1)} %get-tuple-element.26.weights_ref), custom_call_target="tpu_custom_call" | custom-call | flops 2000000000 | bytes 2097152 | tf_op jit(solution)/shard_map/back_project_own/pallas_call | solution.py:595
  8.0 0.0 collective-permute-done.got_ref
  8.0 0.0 copy-done
  8.0 0.2 plane_pack.1
  8.2 2.6 %collective-permute-start.3 = (f32[9,8,640]{2,1,0:T(8,128)S(1)}, f32[9,8,640]{2,1,0:T(8,128)S(1)}, u32[]{:S(2)}, u32[]{:S(2)}) collective-permute-start(f32[9,8,640]{2,1,0:T(8,128)S(1)} %get-tuple-element.31), channel_id=1, source_target_pairs={{0,1},{1,0},{2,3},{3,2},{4,5},{5,4},{6,7},{7,6},{8,9},{9,8},{10,11... | collective-permute-start | bytes 552968 | tf_op jit(solution)/shard_map/ppermute | solution.py:178
  10.8 1.4 %collective-permute-start.1 = (f32[8,8,640]{2,1,0:T(8,128)S(1)}, f32[8,8,640]{2,1,0:T(8,128)S(1)}, u32[]{:S(2)}, u32[]{:S(2)}) collective-permute-start(f32[8,8,640]{2,1,0:T(8,128)S(1)} %get-tuple-element.29), channel_id=1, source_target_pairs={{0,5},{1,4},{2,7},{3,6},{4,1},{5,0},{6,3},{7,2},{8,13},{9,12},{10,... | collective-permute-start | bytes 491528 | tf_op jit(solution)/shard_map/ppermute | solution.py:178
  12.3 0.1 collective-permute-start.2
  12.4 0.0 copy-done.1
  12.4 0.0 copy-done.2
  12.4 0.0 copy-done.3
  12.4 0.7 %gram.1 = (f32[48,256]{1,0:T(8,128)S(1)}, f32[80,80]{1,0:T(8,128)S(1)}, f32[80,80]{1,0:T(8,128)S(1)}) custom-call(f32[1,512]{1,0:T(1,128)S(1)} %copy-done.3, f32[1,512]{1,0:T(1,128)S(1)} %copy-done.2, s32[1,512]{1,0:T(1,128)S(1)} %bitcast.1, f32[9,8,640]{2,1,0:T(8,128)S(1)} %get-tuple-element.28.mine.after_ref), custom_call_target="tpu_custom_call" | custom-call | flops 1000000000 | tf_op jit(solution)/shard_map/gram/pallas_call | solution.py:618
  13.1 5.8 %collective-permute-done.1.got_xy = f32[8,8,640]{2,1,0:T(8,128)S(1)} collective-permute-done((f32[8,8,640]{2,1,0:T(8,128)S(1)}, f32[8,8,640]{2,1,0:T(8,128)S(1)}, u32[]{:S(2)}, u32[]{:S(2)}) %collective-permute-start.1) | collective-permute-done | bytes 163872 | tf_op jit(solution)/shard_map/ppermute | solution.py:178
  18.8 1.6 %collective-permute-done.2.got_x = f32[8,8,640]{2,1,0:T(8,128)S(1)} collective-permute-done((f32[8,8,640]{2,1,0:T(8,128)S(1)}, f32[8,8,640]{2,1,0:T(8,128)S(1)}, u32[]{:S(2)}, u32[]{:S(2)}) %collective-permute-start.2) | collective-permute-done | bytes 163872 | tf_op jit(solution)/shard_map/ppermute | solution.py:178
  20.5 0.0 collective-permute-done.3.got_y
  20.5 0.1 depth_pack.1
  20.5 3.8 %collective-permute-start.4 = (f32[2,8,640]{2,1,0:T(8,128)S(1)}, f32[2,8,640]{2,1,0:T(8,128)S(1)}, u32[]{:S(2)}, u32[]{:S(2)}) collective-permute-start(f32[2,8,640]{2,1,0:T(8,128)S(1)} %get-tuple-element.37), channel_id=1, source_target_pairs={{0,24},{1,25},{2,26},{3,27},{4,28},{5,29},{6,30},{7,31},{8,16},{9,... | collective-permute-start | bytes 122888 | tf_op jit(solution)/shard_map/ppermute | solution.py:178
  24.4 0.0 collective-permute-start.5
  24.4 0.6 %collective-permute-start.6 = (f32[2,8,640]{2,1,0:T(8,128)S(1)}, f32[2,8,640]{2,1,0:T(8,128)S(1)}, u32[]{:S(2)}, u32[]{:S(2)}) collective-permute-start(f32[2,8,640]{2,1,0:T(8,128)S(1)} %get-tuple-element.39), channel_id=1, source_target_pairs={{0,8},{1,9},{2,10},{3,11},{4,12},{5,13},{6,14},{7,15},{8,0},{9,1},... | collective-permute-start | bytes 122888 | tf_op jit(solution)/shard_map/ppermute | solution.py:178
  25.0 0.8 %first_normal.1.first_ref = f32[2,8,640]{2,1,0:T(8,128)S(1)} custom-call(f32[2,8,640]{2,1,0:T(8,128)S(1)} %get-tuple-element.32.vol_pair, f32[48,256]{1,0:T(8,128)S(1)} %get-tuple-element.33.conv_ref, f32[80,80]{1,0:T(8,128)S(1)} %get-tuple-element.34.low_ref, f32[80,80]{1,0:T(8,128)S(1)} %get-tuple-element.35.high_ref), custom_call_target="tpu_custom_call" | custom-call | flops 1000000000 | tf_op jit(solution)/shard_map/first_normal/pallas_call | solution.py:639
  25.8 1.0 %collective-permute-done.4.got_3 = f32[2,8,640]{2,1,0:T(8,128)S(1)} collective-permute-done((f32[2,8,640]{2,1,0:T(8,128)S(1)}, f32[2,8,640]{2,1,0:T(8,128)S(1)}, u32[]{:S(2)}, u32[]{:S(2)}) %collective-permute-start.4) | collective-permute-done | bytes 40992 | tf_op jit(solution)/shard_map/ppermute | solution.py:178
  26.9 2.4 %collective-permute-done.5.got_2 = f32[2,8,640]{2,1,0:T(8,128)S(1)} collective-permute-done((f32[2,8,640]{2,1,0:T(8,128)S(1)}, f32[2,8,640]{2,1,0:T(8,128)S(1)}, u32[]{:S(2)}, u32[]{:S(2)}) %collective-permute-start.5) | collective-permute-done | bytes 40992 | tf_op jit(solution)/shard_map/ppermute | solution.py:178
  29.3 0.0 collective-permute-done.6.got_1
  29.3 0.7 %collective-permute-start.7 = (f32[3,8,640]{2,1,0:T(8,128)S(1)}, f32[3,8,640]{2,1,0:T(8,128)S(1)}, u32[]{:S(2)}, u32[]{:S(2)}) collective-permute-start(f32[3,8,640]{2,1,0:T(8,128)S(1)} %get-tuple-element.41), channel_id=1, source_target_pairs={{4,8},{5,9},{6,10},{7,11},{8,4},{9,5},{10,6},{11,7},{12,16},{13,17... | collective-permute-start | bytes 184328 | tf_op jit(solution)/shard_map/ppermute | solution.py:178
  30.0 2.8 %collective-permute-start.8 = (f32[3,8,640]{2,1,0:T(8,128)S(1)}, f32[3,8,640]{2,1,0:T(8,128)S(1)}, u32[]{:S(2)}, u32[]{:S(2)}) collective-permute-start(f32[3,8,640]{2,1,0:T(8,128)S(1)} %get-tuple-element.42), channel_id=1, source_target_pairs={{0,4},{1,5},{2,6},{3,7},{4,0},{5,1},{6,2},{7,3},{8,12},{9,13},{10,... | collective-permute-start | bytes 184328 | tf_op jit(solution)/shard_map/ppermute | solution.py:178
  32.8 0.0 collective-permute-done.7.got_diag
  32.8 2.2 %collective-permute-done.8.got_x = f32[3,8,640]{2,1,0:T(8,128)S(1)} collective-permute-done((f32[3,8,640]{2,1,0:T(8,128)S(1)}, f32[3,8,640]{2,1,0:T(8,128)S(1)}, u32[]{:S(2)}, u32[]{:S(2)}) %collective-permute-start.8) | collective-permute-done | bytes 61472 | tf_op jit(solution)/shard_map/ppermute | solution.py:178
  35.0 1.6 %finish.1 = (f32[8,512]{1,0:T(8,128)S(1)}, f32[8,512]{1,0:T(8,128)S(1)}) custom-call(f32[4,8,640]{2,1,0:T(8,128)S(1)} %get-tuple-element.40.mine, f32[3,8,640]{2,1,0:T(8,128)S(1)} %collective-permute-done.7.got_diag, f32[3,8,640]{2,1,0:T(8,128)S(1)} %collective-permute-done.8.got_x, f32[48,256]{1,0:T(8,128)S(1)} %get-tuple-element.33.conv_ref, ...), custom_call_target="tpu_custom_call" | custom-call | tf_op jit(solution)/shard_map/finish/pallas_call | solution.py:661
  36.5 0.1 collective-permute-start.9
  36.6 1.2 %collective-permute-done.9.got_ref = f32[8,512]{1,0:T(8,128)S(1)} collective-permute-done((f32[8,512]{1,0:T(8,128)S(1)}, f32[8,512]{1,0:T(8,128)S(1)}, u32[]{:S(2)}, u32[]{:S(2)}) %collective-permute-start.9) | collective-permute-done | bytes 16416 | tf_op jit(solution)/shard_map/ppermute | solution.py:178
  37.8 1.1 %collective-permute-start.10 = (f32[2,4,512]{2,1,0:T(4,128)S(1)}, f32[2,4,512]{2,1,0:T(4,128)S(1)}, u32[]{:S(2)}, u32[]{:S(2)}) collective-permute-start(f32[2,4,512]{2,1,0:T(4,128)S(1)} %result_pack.1), channel_id=1, source_target_pairs={{0,1},{1,0},{2,3},{3,2},{4,5},{5,4},{6,7},{7,6},{8,9},{9,8},{10,11... | collective-permute-start | bytes 49160 | tf_op jit(solution)/shard_map/ppermute | solution.py:178
  38.8 2.7 %collective-permute-done.10.got_y = f32[2,4,512]{2,1,0:T(4,128)S(1)} collective-permute-done((f32[2,4,512]{2,1,0:T(4,128)S(1)}, f32[2,4,512]{2,1,0:T(4,128)S(1)}, u32[]{:S(2)}, u32[]{:S(2)}) %collective-permute-start.10) | collective-permute-done | bytes 16416 | tf_op jit(solution)/shard_map/ppermute | solution.py:178
  41.5 0.6 %result.1 = f32[1,4,2048]{2,1,0:T(4,128)} custom-call(f32[8,512]{1,0:T(8,128)S(1)} %get-tuple-element.43.own_ref, f32[8,512]{1,0:T(8,128)S(1)} %collective-permute-done.9.got_ref, f32[2,4,512]{2,1,0:T(4,128)S(1)} %collective-permute-done.10.got_y), custom_call_target="tpu_custom_call" | custom-call | tf_op jit(solution)/shard_map/result/pallas_call | solution.py:671
  (2 shorter events, 0.0 us)
Async XLA Ops:
  4.5 3.5 %collective-permute-start = (f32[17,8,1152]{2,1,0:T(8,128)S(1)}, f32[17,8,1152]{2,1,0:T(8,128)S(1)}, u32[]{:S(2)}, u32[]{:S(2)}) collective-permute-start(f32[17,8,1152]{2,1,0:T(8,128)S(1)} %get-tuple-element.27), channel_id=1, source_target_pairs={{0,2},{1,3},{2,0},{3,1},{4,6},{5,7},{6,4},{7,5},{8,10},{9,11},{10,... | collective-permute-start | bytes 1880072 | tf_op jit(solution)/shard_map/ppermute | solution.py:178
  5.0 3.0 %copy-start = (f32[1,4,2048]{2,1,0:T(4,128)S(1)}, f32[1,4,2048]{2,1,0:T(4,128)}, u32[]{:S(2)}) copy-start(f32[1,4,2048]{2,1,0:T(4,128)} %vol_ref.1) | copy-start | bytes 98308
  5.0 7.3 %copy-start.1 = (s32[512]{0:T(512)S(1)}, s32[512]{0:T(512)}, u32[]{:S(2)}) copy-start(s32[512]{0:T(512)} %drift_hbm.1) | copy-start | bytes 6148
  5.0 7.3 %copy-start.2 = (f32[1,512]{1,0:T(1,128)S(1)}, f32[1,512]{1,0:T(1,128)}, u32[]{:S(2)}) copy-start(f32[1,512]{1,0:T(1,128)} %constant.8.clone.sec_ref) | copy-start | bytes 6148
  5.0 7.3 %copy-start.3 = (f32[1,512]{1,0:T(1,128)S(1)}, f32[1,512]{1,0:T(1,128)}, u32[]{:S(2)}) copy-start(f32[1,512]{1,0:T(1,128)} %constant.7.clone.tan_ref) | copy-start | bytes 6148
  8.2 12.3 %collective-permute-start.3 = (f32[9,8,640]{2,1,0:T(8,128)S(1)}, f32[9,8,640]{2,1,0:T(8,128)S(1)}, u32[]{:S(2)}, u32[]{:S(2)}) collective-permute-start(f32[9,8,640]{2,1,0:T(8,128)S(1)} %get-tuple-element.31), channel_id=1, source_target_pairs={{0,1},{1,0},{2,3},{3,2},{4,5},{5,4},{6,7},{7,6},{8,9},{9,8},{10,11... | collective-permute-start | bytes 552968 | tf_op jit(solution)/shard_map/ppermute | solution.py:178
  10.8 8.0 %collective-permute-start.1 = (f32[8,8,640]{2,1,0:T(8,128)S(1)}, f32[8,8,640]{2,1,0:T(8,128)S(1)}, u32[]{:S(2)}, u32[]{:S(2)}) collective-permute-start(f32[8,8,640]{2,1,0:T(8,128)S(1)} %get-tuple-element.29), channel_id=1, source_target_pairs={{0,5},{1,4},{2,7},{3,6},{4,1},{5,0},{6,3},{7,2},{8,13},{9,12},{10,... | collective-permute-start | bytes 491528 | tf_op jit(solution)/shard_map/ppermute | solution.py:178
  12.3 8.2 %collective-permute-start.2 = (f32[8,8,640]{2,1,0:T(8,128)S(1)}, f32[8,8,640]{2,1,0:T(8,128)S(1)}, u32[]{:S(2)}, u32[]{:S(2)}) collective-permute-start(f32[8,8,640]{2,1,0:T(8,128)S(1)} %get-tuple-element.30), channel_id=1, source_target_pairs={{0,4},{1,5},{2,6},{3,7},{4,0},{5,1},{6,2},{7,3},{8,12},{9,13},{10,... | collective-permute-start | bytes 491528 | tf_op jit(solution)/shard_map/ppermute | solution.py:178
  20.5 6.3 %collective-permute-start.4 = (f32[2,8,640]{2,1,0:T(8,128)S(1)}, f32[2,8,640]{2,1,0:T(8,128)S(1)}, u32[]{:S(2)}, u32[]{:S(2)}) collective-permute-start(f32[2,8,640]{2,1,0:T(8,128)S(1)} %get-tuple-element.37), channel_id=1, source_target_pairs={{0,24},{1,25},{2,26},{3,27},{4,28},{5,29},{6,30},{7,31},{8,16},{9,... | collective-permute-start | bytes 122888 | tf_op jit(solution)/shard_map/ppermute | solution.py:178
  24.4 4.9 %collective-permute-start.5 = (f32[2,8,640]{2,1,0:T(8,128)S(1)}, f32[2,8,640]{2,1,0:T(8,128)S(1)}, u32[]{:S(2)}, u32[]{:S(2)}) collective-permute-start(f32[2,8,640]{2,1,0:T(8,128)S(1)} %get-tuple-element.38), channel_id=1, source_target_pairs={{0,16},{1,17},{2,18},{3,19},{4,20},{5,21},{6,22},{7,23},{8,24},{9,... | collective-permute-start | bytes 122888 | tf_op jit(solution)/shard_map/ppermute | solution.py:178
  24.4 4.9 %collective-permute-start.6 = (f32[2,8,640]{2,1,0:T(8,128)S(1)}, f32[2,8,640]{2,1,0:T(8,128)S(1)}, u32[]{:S(2)}, u32[]{:S(2)}) collective-permute-start(f32[2,8,640]{2,1,0:T(8,128)S(1)} %get-tuple-element.39), channel_id=1, source_target_pairs={{0,8},{1,9},{2,10},{3,11},{4,12},{5,13},{6,14},{7,15},{8,0},{9,1},... | collective-permute-start | bytes 122888 | tf_op jit(solution)/shard_map/ppermute | solution.py:178
  29.3 3.5 %collective-permute-start.7 = (f32[3,8,640]{2,1,0:T(8,128)S(1)}, f32[3,8,640]{2,1,0:T(8,128)S(1)}, u32[]{:S(2)}, u32[]{:S(2)}) collective-permute-start(f32[3,8,640]{2,1,0:T(8,128)S(1)} %get-tuple-element.41), channel_id=1, source_target_pairs={{4,8},{5,9},{6,10},{7,11},{8,4},{9,5},{10,6},{11,7},{12,16},{13,17... | collective-permute-start | bytes 184328 | tf_op jit(solution)/shard_map/ppermute | solution.py:178
  30.0 5.0 %collective-permute-start.8 = (f32[3,8,640]{2,1,0:T(8,128)S(1)}, f32[3,8,640]{2,1,0:T(8,128)S(1)}, u32[]{:S(2)}, u32[]{:S(2)}) collective-permute-start(f32[3,8,640]{2,1,0:T(8,128)S(1)} %get-tuple-element.42), channel_id=1, source_target_pairs={{0,4},{1,5},{2,6},{3,7},{4,0},{5,1},{6,2},{7,3},{8,12},{9,13},{10,... | collective-permute-start | bytes 184328 | tf_op jit(solution)/shard_map/ppermute | solution.py:178
  36.5 1.2 %collective-permute-start.9 = (f32[8,512]{1,0:T(8,128)S(1)}, f32[8,512]{1,0:T(8,128)S(1)}, u32[]{:S(2)}, u32[]{:S(2)}) collective-permute-start(f32[8,512]{1,0:T(8,128)S(1)} %get-tuple-element.44), channel_id=1, source_target_pairs={{0,2},{1,3},{2,0},{3,1},{4,6},{5,7},{6,4},{7,5},{8,10},{9,11},{10,... | collective-permute-start | bytes 49160 | tf_op jit(solution)/shard_map/ppermute | solution.py:178
  37.8 3.7 %collective-permute-start.10 = (f32[2,4,512]{2,1,0:T(4,128)S(1)}, f32[2,4,512]{2,1,0:T(4,128)S(1)}, u32[]{:S(2)}, u32[]{:S(2)}) collective-permute-start(f32[2,4,512]{2,1,0:T(4,128)S(1)} %result_pack.1), channel_id=1, source_target_pairs={{0,1},{1,0},{2,3},{3,2},{4,5},{5,4},{6,7},{7,6},{8,9},{9,8},{10,11... | collective-permute-start | bytes 49160 | tf_op jit(solution)/shard_map/ppermute | solution.py:178

commit v5 on v4

--- a/solution.py
+++ b/solution.py
@@ -171,22 +171,37 @@
         for x in range(2):
             for c in range(2):
                 for y in range(2):
-                    to = target(z, x, c, y)
-                    if to is not None and 0 <= to[0] < 4:
-                        tz, tx, tc, ty = to
-                        pairs.append((((z * 2 + x) * 2 + c) * 2 + y, ((tz * 2 + tx) * 2 + tc) * 2 + ty))
+                    tz, tx, tc, ty = target(z, x, c, y)
+                    pairs.append((((z * 2 + x) * 2 + c) * 2 + y, ((tz * 2 + tx) * 2 + tc) * 2 + ty))
     return lax.ppermute(value, ("wide", "grp"), pairs)
+
+
+def beside(z, x, c, y):
+    if (z, x) in ((0, 0), (3, 1)):
+        return z, x, 1 - c, y
+    return (z + 1, 0, c, y) if x else (z - 1, 1, c, y)
 
 
 def split_rows(value):
     high = value.astype(jnp.bfloat16).astype(jnp.float32)
     return jnp.concatenate([high, value - high], axis=0)
+
+
+def left_terms(value):
+    high = value.astype(jnp.bfloat16).astype(jnp.float32)
+    return jnp.concatenate([high, high, value - high], axis=1)
 
 
 def split_terms(value):
     high = value.astype(jnp.bfloat16)
     low = (value - high.astype(jnp.float32)).astype(jnp.bfloat16)
     return jnp.concatenate([high, low], axis=0)
+
+
+def right_terms(value):
+    high = value.astype(jnp.bfloat16)
+    low = (value - high.astype(jnp.float32)).astype(jnp.bfloat16)
+    return jnp.concatenate([high, low, high], axis=0)
 
 
 def lane_iota(shape):
@@ -215,8 +230,7 @@
     shift = ((row % rows).astype(jnp.float32) - (rows - 1) / 2.0) * tan_lane - drift_lane
     offset = ((row // rows) * STEP + lane // views - band).astype(jnp.float32)
     weights = (scale / rows) * jnp.maximum(0.0, 1.0 - jnp.abs(shift - offset))
-    weights = split_rows(weights)
-    return jnp.concatenate([weights, weights], axis=1).astype(jnp.bfloat16)
+    return left_terms(weights).astype(jnp.bfloat16)
 
 
 def back_project(views, slices, rows, band, weights, load_strip, out_ref, terms):
@@ -229,15 +243,16 @@
         high = strip.astype(jnp.bfloat16)
         low = (strip - high.astype(jnp.float32)).astype(jnp.bfloat16)
         for j in range(STEP):
-            buf[j * views : (j + 1) * views] = pltpu.roll(high, j, 1) if j else high
+            moved = pltpu.roll(high, j, 1) if j else high
+            buf[j * views : (j + 1) * views] = moved
             buf[(STEP + j) * views : (STEP + j + 1) * views] = pltpu.roll(low, j, 1) if j else low
+            buf[(2 * STEP + j) * views : (2 * STEP + j + 1) * views] = moved
 
     prepare(0, terms.at[0])
     for s in range(slices):
         if s + 1 < slices:
             prepare(s + 1, terms.at[(s + 1) % 2])
         spread = jnp.dot(weights, terms[s % 2], preferred_element_type=jnp.float32)
-        spread = spread[: parts * rows] + spread[parts * rows :]
         total = None
         for i in range(parts):
             piece = pltpu.roll(spread[i * rows : (i + 1) * rows], width - HALO - band + STEP * i, 1)
@@ -246,9 +261,12 @@
 
 
 def strip_loader(buf, half, views, tiles):
+    pitch = (tiles + 2) * SUB
+
     def load(s):
+        first = half * SUB + s % SUB
         return jnp.concatenate(
-            [buf[s // SUB, half + t, pl.ds(s % SUB, views, stride=SUB), :] for t in range(tiles + 1)], axis=1
+            [buf[s // SUB, pl.ds(first + t * SUB, views, stride=pitch), :] for t in range(tiles + 1)], axis=1
         )
 
     return load
@@ -264,16 +282,15 @@
     return pltpu.roll(window, width - HALO, 1)[:, : half_cols + LANES]
 
 
-def sibling_kernel(views, slices, rows, band, scale, tan_hbm, drift_hbm, meas_ref, vol_hbm, out_ref, own_buf,
-                   weights_ref, tan_ref, drift_ref, vol_ref, buf, terms, vbuf, table_sem, sem, own_sem):
+def sibling_kernel(views, slices, rows, band, scale, tan_hbm, drift_hbm, meas_hbm, vol_hbm, out_ref, own_buf,
+                   weights_ref, tan_ref, drift_ref, vol_ref, buf, terms, vbuf, table_sem, sem):
     _, _, c, _ = coords()
     tiles = out_ref.shape[2] // LANES
     groups = slices // SUB
 
-    def fetch(half, g, t, target, semaphore):
-        first = pl.multiple_of((half * (tiles - 1) + t - half) * LANES, LANES)
+    def fetch(half, target, g, semaphore):
         return pltpu.make_async_copy(
-            meas_ref.at[:, pl.ds(g * SUB, SUB), pl.ds(first, LANES)], target.at[g, t + 1], semaphore
+            meas_hbm.at[:, g, pl.ds(half * (tiles - 2), tiles)], target.at[g, :, 1 : tiles + 1], semaphore
         )
 
     tables = [
@@ -281,26 +298,24 @@
         pltpu.make_async_copy(drift_hbm, drift_ref, table_sem.at[1]),
     ]
     vol_copy = pltpu.make_async_copy(vol_hbm, vol_ref, table_sem.at[2])
-    first = [[fetch(1 - c, g, t, buf, sem.at[g, t]) for t in range(tiles)] for g in range(groups)]
-    later = [[fetch(c, g, t, own_buf, own_sem.at[g, t]) for t in range(tiles)] for g in range(groups)]
-    for copy in tables + first[0] + first[1] + [vol_copy] + later[0] + later[1]:
+    first = [fetch(1 - c, buf, g, sem.at[0, g]) for g in range(groups)]
+    later = [fetch(c, own_buf, g, sem.at[1, g]) for g in range(groups)]
+    for copy in tables + first + [vol_copy] + later:
         copy.start()
     zero = jnp.zeros((views, SUB, LANES), jnp.float32)
     for g in range(groups):
         for target in (buf, own_buf):
-            target[g, 0] = zero
-            target[g, tiles + 1] = zero
+            target[g, :, 0] = zero
+            target[g, :, tiles + 1] = zero
     for copy in tables:
         copy.wait()
     weights = view_weights(views, rows, band, scale, tan_ref, drift_ref)
     weights_ref[...] = weights.astype(jnp.float32)
-    flat = buf.reshape(groups, tiles + 2, views * SUB, LANES)
-    load = strip_loader(flat, 1 - c, views, tiles)
+    load = strip_loader(buf.reshape(groups, views * (tiles + 2) * SUB, LANES), 1 - c, views, tiles)
 
     def load_strip(s):
         if s % SUB == 0:
-            for copy in first[s // SUB]:
-                copy.wait()
+            first[s // SUB].wait()
         return load(s)
 
     back_project(views, slices, rows, band, weights, load_strip, out_ref, terms)
@@ -309,16 +324,14 @@
     vol_copy.wait()
     out_ref[slices, 0:part] = volume_window(vol_ref, 1 - c, half_cols, vbuf)
     out_ref[slices, part:] = jnp.zeros((rows - part, half_cols + LANES), jnp.float32)
-    for group in later:
-        for copy in group:
-            copy.wait()
+    for copy in later:
+        copy.wait()
 
 
 def own_kernel(views, slices, rows, band, buf, weights_ref, out_ref, terms):
     _, _, c, _ = coords()
     tiles = out_ref.shape[2] // LANES
-    flat = buf.reshape(slices // SUB, tiles + 2, views * SUB, LANES)
-    load = strip_loader(flat, c, views, tiles)
+    load = strip_loader(buf.reshape(slices // SUB, views * (tiles + 2) * SUB, LANES), c, views, tiles)
     back_project(views, slices, rows, band, weights_ref[...].astype(jnp.bfloat16), load, out_ref, terms)
 
 
@@ -374,8 +387,8 @@
         preferred_element_type=jnp.float32,
     )
     edge = band * rows
-    low_ref[...] = gram[edge + rows :, edge + rows :]
-    high_ref[...] = gram[:edge, :edge]
+    low_ref[...] = left_terms(gram[edge + rows :, edge + rows :])
+    high_ref[...] = left_terms(gram[:edge, :edge])
     width = conv_ref.shape[1] // 2 * 3
     padded = jnp.concatenate([gram, jnp.zeros((span * rows, width - span * rows), jnp.float32)], axis=1)
     total = jnp.zeros((rows, width), jnp.float32)
@@ -411,7 +424,7 @@
         moved = jnp.concatenate(
             [jnp.concatenate([pltpu.roll(t, LANES - k, 1) for k in range(1, band + 1)], axis=0) for t in tiles], axis=1
         )
-        spread = jnp.dot(low_ref[...], moved, precision=lax.Precision.HIGHEST, preferred_element_type=jnp.float32)
+        spread = jnp.dot(low_ref[...].astype(jnp.bfloat16), right_terms(moved), preferred_element_type=jnp.float32)
         for s in range(count):
             total = jnp.zeros((rows, LANES), jnp.float32)
             for k in range(1, band + 1):
@@ -426,7 +439,7 @@
         moved = jnp.concatenate(
             [jnp.concatenate([pltpu.roll(t, k, 1) for k in range(band, 0, -1)], axis=0) for t in tiles], axis=1
         )
-        spread = jnp.dot(high_ref[...], moved, precision=lax.Precision.HIGHEST, preferred_element_type=jnp.float32)
+        spread = jnp.dot(high_ref[...].astype(jnp.bfloat16), right_terms(moved), preferred_element_type=jnp.float32)
         for s in range(count):
             total = jnp.zeros((rows, LANES), jnp.float32)
             for k in range(band, 0, -1):
@@ -451,7 +464,7 @@
         out[i] = volumes[i] - work[i]
 
 
-def half_pair_kernel(first_ref, own_pair, got_3, got_2, got_1, mine, to_x, to_diag, corr):
+def half_pair_kernel(first_ref, own_pair, got_1, got_3, got_2, mine, to_x, to_diag, corr):
     _, x, _, _ = coords()
     corr[...] = (own_pair[...] + got_1[...]) + (got_2[...] + got_3[...])
     half = first_ref[...] + corr[...]
@@ -568,9 +581,10 @@
 
     tiles = half_width // LANES
     groups = slices // SUB
-    window = (groups, tiles + 2, views, SUB, LANES)
-    table = (2 * (2 * band // STEP + 1) * rows, 2 * STEP * views)
-    terms = pltpu.VMEM((2, 2 * STEP * views, half_width + LANES), jnp.bfloat16)
+    window = (groups, views, tiles + 2, SUB, LANES)
+    tiled = measured.reshape(views, groups, SUB, cols // LANES, LANES).transpose(0, 1, 3, 2, 4)
+    table = ((2 * band // STEP + 1) * rows, 3 * STEP * views)
+    terms = pltpu.VMEM((2, 3 * STEP * views, half_width + LANES), jnp.bfloat16)
     vbuf = pltpu.VMEM((part, cols + 2 * LANES), jnp.float32)
     sibling, own_buf, weights = kernel_call(
         functools.partial(sibling_kernel, views, slices, rows, band, scale),
@@ -584,13 +598,12 @@
             terms,
             vbuf,
             pltpu.SemaphoreType.DMA((3,)),
-            pltpu.SemaphoreType.DMA((groups, tiles)),
-            pltpu.SemaphoreType.DMA((groups, tiles)),
+            pltpu.SemaphoreType.DMA((2, groups)),
         ],
         "back_project_sibling",
         flops=2 * 10**9,
         size=2**21,
-    )(in_hbm(jnp.asarray(tangent)), in_hbm(drift), in_hbm(measured), in_hbm(start_volume))
+    )(in_hbm(jnp.asarray(tangent)), in_hbm(drift), in_hbm(tiled), in_hbm(start_volume))
     got = move(sibling, lambda z, x, c, y: (z, x, 1 - c, y))
     own = kernel_call(
         functools.partial(own_kernel, views, slices, rows, band),
@@ -617,7 +630,7 @@
     edge = band * rows
     conv, low, high = kernel_call(
         functools.partial(gram_kernel, rows, band, scale),
-        [f32(6 * rows, 2 * LANES), f32(edge, edge), f32(edge, edge)],
+        [f32(6 * rows, 2 * LANES), f32(edge, 3 * edge), f32(edge, 3 * edge)],
         [VMEM_SPEC] * 3 + [ANY_SPEC],
         [],
         "gram",
@@ -652,8 +665,8 @@
         [VMEM_SPEC] * 5,
         [pltpu.VMEM((2, rows, width), jnp.float32)],
         "half_pair",
-    )(first, own_pair, got_3, got_2, got_1)
-    got_diag = move(to_diag, lambda z, x, c, y: (z + 1, 0, c, y) if x else (z - 1, 1, c, y))
+    )(first, own_pair, got_1, got_3, got_2)
+    got_diag = move(to_diag, beside)
     got_x = move(to_x, lambda z, x, c, y: (z, 1 - x, c, y))
 
     block = width - 2 * HALO

time: 42.8 us -> 41.6 us (0.972); the launches traced: 42.2 us -> 41.4 us
  starting transfers between devices: 13.8 us -> 12.2 us
  waiting for transfers between devices: 16.9 us -> 18.2 us
  Pallas kernels: 11.4 us -> 10.9 us
    ppermute x11, starting transfers between devices: 13.8 us -> 12.2 us  [move(): return lax.ppermute(value, ('wide', 'grp'), pairs)]
    ppermute x11, waiting for transfers between devices: 16.9 us -> 18.2 us  [move(): return lax.ppermute(value, ('wide', 'grp'), pairs)]
  transfers between devices with their start and end apart: 11 -> 11, of which waited for: 7 -> 7; matrix products, arithmetic and copies ran while one was open for 0% -> 0% of each run, Pallas kernels for 10% -> 11%
where the time goes in v5:
time: 41.6 us; the launch traced here: 41.4 us
  waiting for transfers between devices  18.2 us (44%)
  starting transfers between devices  12.2 us (29%)
  Pallas kernels  10.9 us (26%)
    ppermute x11, waiting for transfers between devices, move(): return lax.ppermute(value, ('wide', 'grp'), pairs)  18.2 us
    ppermute x11, starting transfers between devices, move(): return lax.ppermute(value, ('wide', 'grp'), pairs)  12.2 us
    pallas_call x1, Pallas kernels, summed_plan(): kernel_call(functools.partial(sibling_kernel, views, slices, rows, band,...  4.15 us
    pallas_call x1, Pallas kernels, summed_plan(): kernel_call(functools.partial(own_kernel, views, slices, rows, band), f32...  2.96 us
    pallas_call x1, Pallas kernels, summed_plan(): kernel_call(functools.partial(finish_kernel, band, slices, cols), [quarte...  1.46 us
  transfers between devices with their start and end apart: 11, of which 7 were waited for; matrix products, arithmetic and copies ran while one was open for 0% of the time, Pallas kernels for 11%

profile of v5, /device:TPU:0, one launch (start us, length us, event | category | flops | bytes accessed | tf_op | source)
XLA Modules:
  0.0 41.4 jit_solution(954095970890989455)
XLA Ops:
  0.0 4.1 %back_project_sibling.1 = (f32[17,8,1152]{2,1,0:T(8,128)S(1)}, f32[2,16,11,8,128]{4,3,2,1,0:T(8,128)S(1)}, f32[56,144]{1,0:T(8,128)S(1)}) custom-call(f32[512]{0:T(512)} %constant.6.clone.tan_hbm, s32[512]{0:T(512)} %drift_hbm.1, f32[16,2,16,8,128]{4,3,2,1,0:T(8,128)} %bitcast.5, f32[1,4,2048]{2,1,0:T(4,128)} %vol_ref.1), custom_call_target="tpu_custom_call" | custom-call | flops 2000000000 | bytes 2097152 | tf_op jit(solution)/shard_map/back_project_sibling/pallas_call | solution.py:589
  4.2 0.5 %collective-permute-start = (f32[17,8,1152]{2,1,0:T(8,128)S(1)}, f32[17,8,1152]{2,1,0:T(8,128)S(1)}, u32[]{:S(2)}, u32[]{:S(2)}) collective-permute-start(f32[17,8,1152]{2,1,0:T(8,128)S(1)} %get-tuple-element.27), channel_id=1, source_target_pairs={{0,2},{1,3},{2,0},{3,1},{4,6},{5,7},{6,4},{7,5},{8,10},{9,11},{10,... | collective-permute-start | bytes 1880072 | tf_op jit(solution)/shard_map/ppermute | solution.py:176
  4.7 0.0 copy-start
  4.7 0.0 copy-start.1
  4.7 0.0 copy-start.2
  4.7 0.0 copy-start.3
  4.7 3.0 %back_project_own.1.own_ref = f32[16,8,1152]{2,1,0:T(8,128)S(1)} custom-call(f32[2,16,11,8,128]{4,3,2,1,0:T(8,128)S(1)} %get-tuple-element.25.buf, f32[56,144]{1,0:T(8,128)S(1)} %get-tuple-element.26.weights_ref), custom_call_target="tpu_custom_call" | custom-call | flops 2000000000 | bytes 2097152 | tf_op jit(solution)/shard_map/back_project_own/pallas_call | solution.py:608
  7.7 0.0 collective-permute-done.got_ref
  7.7 0.0 copy-done
  7.7 0.2 plane_pack.1
  7.8 2.6 %collective-permute-start.3 = (f32[9,8,640]{2,1,0:T(8,128)S(1)}, f32[9,8,640]{2,1,0:T(8,128)S(1)}, u32[]{:S(2)}, u32[]{:S(2)}) collective-permute-start(f32[9,8,640]{2,1,0:T(8,128)S(1)} %get-tuple-element.31), channel_id=1, source_target_pairs={{0,1},{1,0},{2,3},{3,2},{4,5},{5,4},{6,7},{7,6},{8,9},{9,8},{10,11... | collective-permute-start | bytes 552968 | tf_op jit(solution)/shard_map/ppermute | solution.py:176
  10.5 1.4 %collective-permute-start.1 = (f32[8,8,640]{2,1,0:T(8,128)S(1)}, f32[8,8,640]{2,1,0:T(8,128)S(1)}, u32[]{:S(2)}, u32[]{:S(2)}) collective-permute-start(f32[8,8,640]{2,1,0:T(8,128)S(1)} %get-tuple-element.29), channel_id=1, source_target_pairs={{0,5},{1,4},{2,7},{3,6},{4,1},{5,0},{6,3},{7,2},{8,13},{9,12},{10,... | collective-permute-start | bytes 491528 | tf_op jit(solution)/shard_map/ppermute | solution.py:176
  11.9 0.1 collective-permute-start.2
  12.0 0.0 copy-done.1
  12.0 0.0 copy-done.2
  12.0 0.0 copy-done.3
  12.0 0.7 %gram.1 = (f32[48,256]{1,0:T(8,128)S(1)}, f32[80,240]{1,0:T(8,128)S(1)}, f32[80,240]{1,0:T(8,128)S(1)}) custom-call(f32[1,512]{1,0:T(1,128)S(1)} %copy-done.3, f32[1,512]{1,0:T(1,128)S(1)} %copy-done.2, s32[1,512]{1,0:T(1,128)S(1)} %bitcast.4, f32[9,8,640]{2,1,0:T(8,128)S(1)} %get-tuple-element.28.mine.after_ref), custom_call_target="tpu_custom_call" | custom-call | flops 1000000000 | tf_op jit(solution)/shard_map/gram/pallas_call | solution.py:631
  12.7 5.7 %collective-permute-done.1.got_xy = f32[8,8,640]{2,1,0:T(8,128)S(1)} collective-permute-done((f32[8,8,640]{2,1,0:T(8,128)S(1)}, f32[8,8,640]{2,1,0:T(8,128)S(1)}, u32[]{:S(2)}, u32[]{:S(2)}) %collective-permute-start.1) | collective-permute-done | bytes 163872 | tf_op jit(solution)/shard_map/ppermute | solution.py:176
  18.5 1.6 %collective-permute-done.2.got_x = f32[8,8,640]{2,1,0:T(8,128)S(1)} collective-permute-done((f32[8,8,640]{2,1,0:T(8,128)S(1)}, f32[8,8,640]{2,1,0:T(8,128)S(1)}, u32[]{:S(2)}, u32[]{:S(2)}) %collective-permute-start.2) | collective-permute-done | bytes 163872 | tf_op jit(solution)/shard_map/ppermute | solution.py:176
  20.1 0.0 collective-permute-done.3.got_y
  20.1 0.1 depth_pack.1
  20.2 1.8 %collective-permute-start.4 = (f32[2,8,640]{2,1,0:T(8,128)S(1)}, f32[2,8,640]{2,1,0:T(8,128)S(1)}, u32[]{:S(2)}, u32[]{:S(2)}) collective-permute-start(f32[2,8,640]{2,1,0:T(8,128)S(1)} %get-tuple-element.37), channel_id=1, source_target_pairs={{0,8},{1,9},{2,10},{3,11},{4,12},{5,13},{6,14},{7,15},{8,0},{9,1},... | collective-permute-start | bytes 122888 | tf_op jit(solution)/shard_map/ppermute | solution.py:176
  22.0 2.5 %collective-permute-start.5 = (f32[2,8,640]{2,1,0:T(8,128)S(1)}, f32[2,8,640]{2,1,0:T(8,128)S(1)}, u32[]{:S(2)}, u32[]{:S(2)}) collective-permute-start(f32[2,8,640]{2,1,0:T(8,128)S(1)} %get-tuple-element.38), channel_id=1, source_target_pairs={{0,24},{1,25},{2,26},{3,27},{4,28},{5,29},{6,30},{7,31},{8,16},{9,... | collective-permute-start | bytes 122888 | tf_op jit(solution)/shard_map/ppermute | solution.py:176
  24.4 0.1 collective-permute-start.6
  24.6 0.7 %first_normal.1.first_ref = f32[2,8,640]{2,1,0:T(8,128)S(1)} custom-call(f32[2,8,640]{2,1,0:T(8,128)S(1)} %get-tuple-element.32.vol_pair, f32[48,256]{1,0:T(8,128)S(1)} %get-tuple-element.33.conv_ref, f32[80,240]{1,0:T(8,128)S(1)} %get-tuple-element.34.low_ref, f32[80,240]{1,0:T(8,128)S(1)} %get-tuple-element.35.high_ref), custom_call_target="tpu_custom_call" | custom-call | flops 1000000000 | tf_op jit(solution)/shard_map/first_normal/pallas_call | solution.py:652
  25.3 0.0 collective-permute-done.4.got_1
  25.3 2.5 %collective-permute-done.5.got_3 = f32[2,8,640]{2,1,0:T(8,128)S(1)} collective-permute-done((f32[2,8,640]{2,1,0:T(8,128)S(1)}, f32[2,8,640]{2,1,0:T(8,128)S(1)}, u32[]{:S(2)}, u32[]{:S(2)}) %collective-permute-start.5) | collective-permute-done | bytes 40992 | tf_op jit(solution)/shard_map/ppermute | solution.py:176
  27.8 2.0 %collective-permute-done.6.got_2 = f32[2,8,640]{2,1,0:T(8,128)S(1)} collective-permute-done((f32[2,8,640]{2,1,0:T(8,128)S(1)}, f32[2,8,640]{2,1,0:T(8,128)S(1)}, u32[]{:S(2)}, u32[]{:S(2)}) %collective-permute-start.6) | collective-permute-done | bytes 40992 | tf_op jit(solution)/shard_map/ppermute | solution.py:176
  29.8 0.1 collective-permute-start.7
  29.9 1.8 %collective-permute-start.8 = (f32[3,8,640]{2,1,0:T(8,128)S(1)}, f32[3,8,640]{2,1,0:T(8,128)S(1)}, u32[]{:S(2)}, u32[]{:S(2)}) collective-permute-start(f32[3,8,640]{2,1,0:T(8,128)S(1)} %get-tuple-element.42), channel_id=1, source_target_pairs={{0,4},{1,5},{2,6},{3,7},{4,0},{5,1},{6,2},{7,3},{8,12},{9,13},{10,... | collective-permute-start | bytes 184328 | tf_op jit(solution)/shard_map/ppermute | solution.py:176
  31.7 0.0 collective-permute-done.7.got_diag
  31.7 2.6 %collective-permute-done.8.got_x = f32[3,8,640]{2,1,0:T(8,128)S(1)} collective-permute-done((f32[3,8,640]{2,1,0:T(8,128)S(1)}, f32[3,8,640]{2,1,0:T(8,128)S(1)}, u32[]{:S(2)}, u32[]{:S(2)}) %collective-permute-start.8) | collective-permute-done | bytes 61472 | tf_op jit(solution)/shard_map/ppermute | solution.py:176
  34.3 1.5 %finish.1 = (f32[8,512]{1,0:T(8,128)S(1)}, f32[8,512]{1,0:T(8,128)S(1)}) custom-call(f32[4,8,640]{2,1,0:T(8,128)S(1)} %get-tuple-element.40.mine, f32[3,8,640]{2,1,0:T(8,128)S(1)} %collective-permute-done.7.got_diag, f32[3,8,640]{2,1,0:T(8,128)S(1)} %collective-permute-done.8.got_x, f32[48,256]{1,0:T(8,128)S(1)} %get-tuple-element.33.conv_ref, ...), custom_call_target="tpu_custom_call" | custom-call | tf_op jit(solution)/shard_map/finish/pallas_call | solution.py:674
  35.8 0.1 collective-permute-start.9
  35.9 1.2 %collective-permute-done.9.got_ref = f32[8,512]{1,0:T(8,128)S(1)} collective-permute-done((f32[8,512]{1,0:T(8,128)S(1)}, f32[8,512]{1,0:T(8,128)S(1)}, u32[]{:S(2)}, u32[]{:S(2)}) %collective-permute-start.9) | collective-permute-done | bytes 16416 | tf_op jit(solution)/shard_map/ppermute | solution.py:176
  37.0 1.2 %collective-permute-start.10 = (f32[2,4,512]{2,1,0:T(4,128)S(1)}, f32[2,4,512]{2,1,0:T(4,128)S(1)}, u32[]{:S(2)}, u32[]{:S(2)}) collective-permute-start(f32[2,4,512]{2,1,0:T(4,128)S(1)} %result_pack.1), channel_id=1, source_target_pairs={{0,1},{1,0},{2,3},{3,2},{4,5},{5,4},{6,7},{7,6},{8,9},{9,8},{10,11... | collective-permute-start | bytes 49160 | tf_op jit(solution)/shard_map/ppermute | solution.py:176
  38.2 2.6 %collective-permute-done.10.got_y = f32[2,4,512]{2,1,0:T(4,128)S(1)} collective-permute-done((f32[2,4,512]{2,1,0:T(4,128)S(1)}, f32[2,4,512]{2,1,0:T(4,128)S(1)}, u32[]{:S(2)}, u32[]{:S(2)}) %collective-permute-start.10) | collective-permute-done | bytes 16416 | tf_op jit(solution)/shard_map/ppermute | solution.py:176
  40.8 0.6 %result.1 = f32[1,4,2048]{2,1,0:T(4,128)} custom-call(f32[8,512]{1,0:T(8,128)S(1)} %get-tuple-element.43.own_ref, f32[8,512]{1,0:T(8,128)S(1)} %collective-permute-done.9.got_ref, f32[2,4,512]{2,1,0:T(4,128)S(1)} %collective-permute-done.10.got_y), custom_call_target="tpu_custom_call" | custom-call | tf_op jit(solution)/shard_map/result/pallas_call | solution.py:684
  (2 shorter events, 0.0 us)
Async XLA Ops:
  4.2 3.5 %collective-permute-start = (f32[17,8,1152]{2,1,0:T(8,128)S(1)}, f32[17,8,1152]{2,1,0:T(8,128)S(1)}, u32[]{:S(2)}, u32[]{:S(2)}) collective-permute-start(f32[17,8,1152]{2,1,0:T(8,128)S(1)} %get-tuple-element.27), channel_id=1, source_target_pairs={{0,2},{1,3},{2,0},{3,1},{4,6},{5,7},{6,4},{7,5},{8,10},{9,11},{10,... | collective-permute-start | bytes 1880072 | tf_op jit(solution)/shard_map/ppermute | solution.py:176
  4.7 3.0 %copy-start = (f32[1,4,2048]{2,1,0:T(4,128)S(1)}, f32[1,4,2048]{2,1,0:T(4,128)}, u32[]{:S(2)}) copy-start(f32[1,4,2048]{2,1,0:T(4,128)} %vol_ref.1) | copy-start | bytes 98308
  4.7 7.3 %copy-start.1 = (s32[512]{0:T(512)S(1)}, s32[512]{0:T(512)}, u32[]{:S(2)}) copy-start(s32[512]{0:T(512)} %drift_hbm.1) | copy-start | bytes 6148
  4.7 7.3 %copy-start.2 = (f32[1,512]{1,0:T(1,128)S(1)}, f32[1,512]{1,0:T(1,128)}, u32[]{:S(2)}) copy-start(f32[1,512]{1,0:T(1,128)} %constant.8.clone.sec_ref) | copy-start | bytes 6148
  4.7 7.3 %copy-start.3 = (f32[1,512]{1,0:T(1,128)S(1)}, f32[1,512]{1,0:T(1,128)}, u32[]{:S(2)}) copy-start(f32[1,512]{1,0:T(1,128)} %constant.7.clone.tan_ref) | copy-start | bytes 6148
  7.8 12.3 %collective-permute-start.3 = (f32[9,8,640]{2,1,0:T(8,128)S(1)}, f32[9,8,640]{2,1,0:T(8,128)S(1)}, u32[]{:S(2)}, u32[]{:S(2)}) collective-permute-start(f32[9,8,640]{2,1,0:T(8,128)S(1)} %get-tuple-element.31), channel_id=1, source_target_pairs={{0,1},{1,0},{2,3},{3,2},{4,5},{5,4},{6,7},{7,6},{8,9},{9,8},{10,11... | collective-permute-start | bytes 552968 | tf_op jit(solution)/shard_map/ppermute | solution.py:176
  10.5 8.0 %collective-permute-start.1 = (f32[8,8,640]{2,1,0:T(8,128)S(1)}, f32[8,8,640]{2,1,0:T(8,128)S(1)}, u32[]{:S(2)}, u32[]{:S(2)}) collective-permute-start(f32[8,8,640]{2,1,0:T(8,128)S(1)} %get-tuple-element.29), channel_id=1, source_target_pairs={{0,5},{1,4},{2,7},{3,6},{4,1},{5,0},{6,3},{7,2},{8,13},{9,12},{10,... | collective-permute-start | bytes 491528 | tf_op jit(solution)/shard_map/ppermute | solution.py:176
  11.9 8.2 %collective-permute-start.2 = (f32[8,8,640]{2,1,0:T(8,128)S(1)}, f32[8,8,640]{2,1,0:T(8,128)S(1)}, u32[]{:S(2)}, u32[]{:S(2)}) collective-permute-start(f32[8,8,640]{2,1,0:T(8,128)S(1)} %get-tuple-element.30), channel_id=1, source_target_pairs={{0,4},{1,5},{2,6},{3,7},{4,0},{5,1},{6,2},{7,3},{8,12},{9,13},{10,... | collective-permute-start | bytes 491528 | tf_op jit(solution)/shard_map/ppermute | solution.py:176
  20.2 5.1 %collective-permute-start.4 = (f32[2,8,640]{2,1,0:T(8,128)S(1)}, f32[2,8,640]{2,1,0:T(8,128)S(1)}, u32[]{:S(2)}, u32[]{:S(2)}) collective-permute-start(f32[2,8,640]{2,1,0:T(8,128)S(1)} %get-tuple-element.37), channel_id=1, source_target_pairs={{0,8},{1,9},{2,10},{3,11},{4,12},{5,13},{6,14},{7,15},{8,0},{9,1},... | collective-permute-start | bytes 122888 | tf_op jit(solution)/shard_map/ppermute | solution.py:176
  22.0 5.8 %collective-permute-start.5 = (f32[2,8,640]{2,1,0:T(8,128)S(1)}, f32[2,8,640]{2,1,0:T(8,128)S(1)}, u32[]{:S(2)}, u32[]{:S(2)}) collective-permute-start(f32[2,8,640]{2,1,0:T(8,128)S(1)} %get-tuple-element.38), channel_id=1, source_target_pairs={{0,24},{1,25},{2,26},{3,27},{4,28},{5,29},{6,30},{7,31},{8,16},{9,... | collective-permute-start | bytes 122888 | tf_op jit(solution)/shard_map/ppermute | solution.py:176
  24.4 5.3 %collective-permute-start.6 = (f32[2,8,640]{2,1,0:T(8,128)S(1)}, f32[2,8,640]{2,1,0:T(8,128)S(1)}, u32[]{:S(2)}, u32[]{:S(2)}) collective-permute-start(f32[2,8,640]{2,1,0:T(8,128)S(1)} %get-tuple-element.39), channel_id=1, source_target_pairs={{0,16},{1,17},{2,18},{3,19},{4,20},{5,21},{6,22},{7,23},{8,24},{9,... | collective-permute-start | bytes 122888 | tf_op jit(solution)/shard_map/ppermute | solution.py:176
  29.8 1.9 %collective-permute-start.7 = (f32[3,8,640]{2,1,0:T(8,128)S(1)}, f32[3,8,640]{2,1,0:T(8,128)S(1)}, u32[]{:S(2)}, u32[]{:S(2)}) collective-permute-start(f32[3,8,640]{2,1,0:T(8,128)S(1)} %get-tuple-element.41), channel_id=1, source_target_pairs={{0,2},{1,3},{2,0},{3,1},{4,8},{5,9},{6,10},{7,11},{8,4},{9,5},{10,... | collective-permute-start | bytes 184328 | tf_op jit(solution)/shard_map/ppermute | solution.py:176
  29.9 4.4 %collective-permute-start.8 = (f32[3,8,640]{2,1,0:T(8,128)S(1)}, f32[3,8,640]{2,1,0:T(8,128)S(1)}, u32[]{:S(2)}, u32[]{:S(2)}) collective-permute-start(f32[3,8,640]{2,1,0:T(8,128)S(1)} %get-tuple-element.42), channel_id=1, source_target_pairs={{0,4},{1,5},{2,6},{3,7},{4,0},{5,1},{6,2},{7,3},{8,12},{9,13},{10,... | collective-permute-start | bytes 184328 | tf_op jit(solution)/shard_map/ppermute | solution.py:176
  35.8 1.2 %collective-permute-start.9 = (f32[8,512]{1,0:T(8,128)S(1)}, f32[8,512]{1,0:T(8,128)S(1)}, u32[]{:S(2)}, u32[]{:S(2)}) collective-permute-start(f32[8,512]{1,0:T(8,128)S(1)} %get-tuple-element.44), channel_id=1, source_target_pairs={{0,2},{1,3},{2,0},{3,1},{4,6},{5,7},{6,4},{7,5},{8,10},{9,11},{10,... | collective-permute-start | bytes 49160 | tf_op jit(solution)/shard_map/ppermute | solution.py:176
  37.0 3.7 %collective-permute-start.10 = (f32[2,4,512]{2,1,0:T(4,128)S(1)}, f32[2,4,512]{2,1,0:T(4,128)S(1)}, u32[]{:S(2)}, u32[]{:S(2)}) collective-permute-start(f32[2,4,512]{2,1,0:T(4,128)S(1)} %result_pack.1), channel_id=1, source_target_pairs={{0,1},{1,0},{2,3},{3,2},{4,5},{5,4},{6,7},{7,6},{8,9},{9,8},{10,11... | collective-permute-start | bytes 49160 | tf_op jit(solution)/shard_map/ppermute | solution.py:176

commit v6 on v5

--- a/solution.py
+++ b/solution.py
@@ -233,40 +233,35 @@
     return left_terms(weights).astype(jnp.bfloat16)
 
 
-def back_project(views, slices, rows, band, weights, load_strip, out_ref, terms):
+def back_project(views, rows, band, weights, load_strip, out_ref, terms):
+    count, _, width = terms.shape
     out_cols = out_ref.shape[2]
-    width = terms.shape[2]
     parts = 2 * band // STEP + 1
-
-    def prepare(s, buf):
-        strip = load_strip(s)
+    for n in range(count):
+        strip = load_strip(n)
         high = strip.astype(jnp.bfloat16)
         low = (strip - high.astype(jnp.float32)).astype(jnp.bfloat16)
         for j in range(STEP):
             moved = pltpu.roll(high, j, 1) if j else high
-            buf[j * views : (j + 1) * views] = moved
-            buf[(STEP + j) * views : (STEP + j + 1) * views] = pltpu.roll(low, j, 1) if j else low
-            buf[(2 * STEP + j) * views : (2 * STEP + j + 1) * views] = moved
-
-    prepare(0, terms.at[0])
-    for s in range(slices):
-        if s + 1 < slices:
-            prepare(s + 1, terms.at[(s + 1) % 2])
-        spread = jnp.dot(weights, terms[s % 2], preferred_element_type=jnp.float32)
+            terms[n, j * views : (j + 1) * views] = moved
+            terms[n, (STEP + j) * views : (STEP + j + 1) * views] = pltpu.roll(low, j, 1) if j else low
+            terms[n, (2 * STEP + j) * views : (2 * STEP + j + 1) * views] = moved
+    for n in range(count):
+        spread = jnp.dot(weights, terms[n], preferred_element_type=jnp.float32)
         total = None
         for i in range(parts):
             piece = pltpu.roll(spread[i * rows : (i + 1) * rows], width - HALO - band + STEP * i, 1)
             total = piece if total is None else total + piece
-        out_ref[s] = total[:, :out_cols]
-
-
-def strip_loader(buf, half, views, tiles):
+        out_ref[n] = total[:, :out_cols]
+
+
+def strip_loader(buf, half, parity, views, tiles):
     pitch = (tiles + 2) * SUB
 
-    def load(s):
-        first = half * SUB + s % SUB
+    def load(n):
+        first = half * SUB + 4 * (n // 2 % 2) + 2 * parity + n % 2
         return jnp.concatenate(
-            [buf[s // SUB, pl.ds(first + t * SUB, views, stride=pitch), :] for t in range(tiles + 1)], axis=1
+            [buf[n // 4, pl.ds(first + t * SUB, views, stride=pitch), :] for t in range(tiles + 1)], axis=1
         )
 
     return load
@@ -282,11 +277,11 @@
     return pltpu.roll(window, width - HALO, 1)[:, : half_cols + LANES]
 
 
-def sibling_kernel(views, slices, rows, band, scale, tan_hbm, drift_hbm, meas_hbm, vol_hbm, out_ref, own_buf,
-                   weights_ref, tan_ref, drift_ref, vol_ref, buf, terms, vbuf, table_sem, sem):
-    _, _, c, _ = coords()
+def fetch_kernel(views, rows, band, scale, tan_hbm, drift_hbm, meas_hbm, vol_hbm, out_ref, sibling_buf, own_buf,
+                 weights_ref, vol_ref, tan_ref, drift_ref, terms, table_sem, sem):
+    _, x, c, _ = coords()
     tiles = out_ref.shape[2] // LANES
-    groups = slices // SUB
+    groups = sibling_buf.shape[0]
 
     def fetch(half, target, g, semaphore):
         return pltpu.make_async_copy(
@@ -298,59 +293,76 @@
         pltpu.make_async_copy(drift_hbm, drift_ref, table_sem.at[1]),
     ]
     vol_copy = pltpu.make_async_copy(vol_hbm, vol_ref, table_sem.at[2])
-    first = [fetch(1 - c, buf, g, sem.at[0, g]) for g in range(groups)]
+    first = [fetch(1 - c, sibling_buf, g, sem.at[0, g]) for g in range(groups)]
     later = [fetch(c, own_buf, g, sem.at[1, g]) for g in range(groups)]
     for copy in tables + first + [vol_copy] + later:
         copy.start()
     zero = jnp.zeros((views, SUB, LANES), jnp.float32)
     for g in range(groups):
-        for target in (buf, own_buf):
+        for target in (sibling_buf, own_buf):
             target[g, :, 0] = zero
             target[g, :, tiles + 1] = zero
     for copy in tables:
         copy.wait()
     weights = view_weights(views, rows, band, scale, tan_ref, drift_ref)
     weights_ref[...] = weights.astype(jnp.float32)
-    load = strip_loader(buf.reshape(groups, views * (tiles + 2) * SUB, LANES), 1 - c, views, tiles)
-
-    def load_strip(s):
-        if s % SUB == 0:
-            first[s // SUB].wait()
-        return load(s)
-
-    back_project(views, slices, rows, band, weights, load_strip, out_ref, terms)
+    load = strip_loader(flat_rows(sibling_buf), 1 - c, 1 - x, views, tiles)
+
+    def load_strip(n):
+        if n % 4 == 0:
+            first[n // 4].wait()
+        return load(n)
+
+    back_project(views, rows, band, weights, load_strip, out_ref, terms)
+    vol_copy.wait()
+    for copy in later:
+        copy.wait()
+
+
+def flat_rows(buf):
+    groups, views, tiles, sub, lanes = buf.shape
+    return buf.reshape(groups, views * tiles * sub, lanes)
+
+
+def sibling_kernel(views, rows, band, buf, weights_ref, vol_ref, out_ref, terms, vbuf):
+    _, x, c, _ = coords()
+    tiles = out_ref.shape[2] // LANES
+    load = strip_loader(flat_rows(buf), 1 - c, x, views, tiles)
+    back_project(views, rows, band, weights_ref[...].astype(jnp.bfloat16), load, out_ref, terms)
+    count = terms.shape[0]
     half_cols = out_ref.shape[2] - LANES
     part = vol_ref.shape[1]
-    vol_copy.wait()
-    out_ref[slices, 0:part] = volume_window(vol_ref, 1 - c, half_cols, vbuf)
-    out_ref[slices, part:] = jnp.zeros((rows - part, half_cols + LANES), jnp.float32)
-    for copy in later:
-        copy.wait()
-
-
-def own_kernel(views, slices, rows, band, buf, weights_ref, out_ref, terms):
-    _, _, c, _ = coords()
+    out_ref[count, 0:part] = volume_window(vol_ref, 1 - c, half_cols, vbuf)
+    out_ref[count, part:] = jnp.zeros((rows - part, half_cols + LANES), jnp.float32)
+
+
+def own_kernel(kept, views, rows, band, buf, weights_ref, after_ref, out_ref, terms):
+    _, x, c, _ = coords()
     tiles = out_ref.shape[2] // LANES
-    load = strip_loader(buf.reshape(slices // SUB, views * (tiles + 2) * SUB, LANES), c, views, tiles)
-    back_project(views, slices, rows, band, weights_ref[...].astype(jnp.bfloat16), load, out_ref, terms)
-
-
-def plane_pack_kernel(own_ref, got_ref, vol_ref, mine, to_x, to_y, to_xy, acc, both, vbuf):
-    slices, rows, half_width = own_ref.shape
+    load = strip_loader(flat_rows(buf), c, x if kept else 1 - x, views, tiles)
+    back_project(views, rows, band, weights_ref[...].astype(jnp.bfloat16), load, out_ref, terms)
+
+
+def pass_pack_kernel(own_ref, got_ref, to_x, to_xy, acc):
+    width = to_x.shape[2]
+    _, _, _, y = coords()
+    acc[...] = own_ref[...] + got_ref[...]
+    for out, py in ((to_x, y), (to_xy, 1 - y)):
+        out[...] = acc[:, :, pl.ds(pl.multiple_of(py * (width - LANES), LANES), width)]
+
+
+def keep_pack_kernel(own_ref, got_ref, vol_ref, mine, to_y, acc, vbuf):
+    count, rows, half_width = own_ref.shape
     width = mine.shape[2]
     part = vol_ref.shape[1]
-    z, x, c, y = coords()
-    acc[...] = own_ref[...] + got_ref[0:slices]
+    _, _, c, y = coords()
+    acc[0:count] = own_ref[...] + got_ref[0:count]
     here = volume_window(vol_ref, c, half_width - LANES, vbuf)
-    there = got_ref[slices, 0:part]
-    both[0:part] = jnp.where(c == 0, here, there)
-    both[part:] = jnp.where(c == 0, there, here)
-    for out, px, py in ((mine, x, y), (to_x, 1 - x, y), (to_y, x, 1 - y), (to_xy, 1 - x, 1 - y)):
-        begin = pl.multiple_of(py * (width - LANES), LANES)
-        for pz in range(slices // 4):
-            out[2 * pz : 2 * pz + 2] = acc[pl.ds(4 * pz + 2 * px, 2), :, pl.ds(begin, width)]
-        if out.shape[0] > slices // 2:
-            out[slices // 2] = both[:, pl.ds(begin, width)]
+    there = got_ref[count, 0:part]
+    acc[count, 0:part] = jnp.where(c == 0, here, there)
+    acc[count, part:] = jnp.where(c == 0, there, here)
+    for out, py in ((mine, y), (to_y, 1 - y)):
+        out[...] = acc[:, :, pl.ds(pl.multiple_of(py * (width - LANES), LANES), width)]
 
 
 def depth_pack_kernel(mine, got_xy, got_x, got_y, own_pair, to_1, to_2, to_3, vol_pair, acc):
@@ -584,47 +596,61 @@
     window = (groups, views, tiles + 2, SUB, LANES)
     tiled = measured.reshape(views, groups, SUB, cols // LANES, LANES).transpose(0, 1, 3, 2, 4)
     table = ((2 * band // STEP + 1) * rows, 3 * STEP * views)
-    terms = pltpu.VMEM((2, 3 * STEP * views, half_width + LANES), jnp.bfloat16)
+    count = slices // 2
+    terms = pltpu.VMEM((count, 3 * STEP * views, half_width + LANES), jnp.bfloat16)
     vbuf = pltpu.VMEM((part, cols + 2 * LANES), jnp.float32)
-    sibling, own_buf, weights = kernel_call(
-        functools.partial(sibling_kernel, views, slices, rows, band, scale),
-        [f32(slices + 1, rows, half_width), f32(*window), f32(*table)],
+    half_of = f32(count, rows, half_width)
+    half_and = f32(count + 1, rows, half_width)
+    across = lambda z, x, c, y: (z, x, 1 - c, y)
+
+    pass_sibling, sibling_buf, own_buf, weights, volume = kernel_call(
+        functools.partial(fetch_kernel, views, rows, band, scale),
+        [half_of, f32(*window), f32(*window), f32(*table), f32(1, part, cols)],
         [HBM_SPEC] * 4,
         [
             pltpu.SMEM((total_angles,), jnp.float32),
             pltpu.SMEM((total_angles,), jnp.int32),
-            pltpu.VMEM((1, part, cols), jnp.float32),
-            pltpu.VMEM(window, jnp.float32),
             terms,
-            vbuf,
             pltpu.SemaphoreType.DMA((3,)),
             pltpu.SemaphoreType.DMA((2, groups)),
         ],
-        "back_project_sibling",
-        flops=2 * 10**9,
-        size=2**21,
+        "pass_sibling",
+        flops=10**9,
     )(in_hbm(jnp.asarray(tangent)), in_hbm(drift), in_hbm(tiled), in_hbm(start_volume))
-    got = move(sibling, lambda z, x, c, y: (z, x, 1 - c, y))
-    own = kernel_call(
-        functools.partial(own_kernel, views, slices, rows, band),
-        f32(slices, rows, half_width),
-        [VMEM_SPEC] * 2,
-        [terms],
-        "back_project_own",
-        flops=2 * 10**9,
-        size=2**21,
-    )(own_buf, weights)
-
-    count = slices // 2
-    mine, to_x, to_y, to_xy = kernel_call(
-        plane_pack_kernel,
-        [f32(count + 1, rows, width), f32(count, rows, width), f32(count + 1, rows, width), f32(count, rows, width)],
+    pass_got = move(pass_sibling, across)
+    keep_sibling = kernel_call(
+        functools.partial(sibling_kernel, views, rows, band),
+        half_and,
         [VMEM_SPEC] * 3,
-        [pltpu.VMEM((slices, rows, half_width), jnp.float32), pltpu.VMEM((rows, half_width), jnp.float32), vbuf],
-        "plane_pack",
-    )(own, got, start_volume)
+        [terms, vbuf],
+        "keep_sibling",
+        flops=10**9,
+    )(sibling_buf, weights, volume)
+    keep_got = move(keep_sibling, across)
+
+    def own(kept, after):
+        return kernel_call(
+            functools.partial(own_kernel, kept, views, rows, band),
+            half_of,
+            [VMEM_SPEC] * 2 + [ANY_SPEC],
+            [terms],
+            "keep_own" if kept else "pass_own",
+            flops=10**9,
+        )(own_buf, weights, after)
+
+    message, longer = f32(count, rows, width), f32(count + 1, rows, width)
+    to_x, to_xy = kernel_call(
+        pass_pack_kernel, [message] * 2, [VMEM_SPEC] * 2, [pltpu.VMEM(half_of.shape, jnp.float32)], "pass_pack"
+    )(own(False, keep_sibling), pass_got)
     got_xy = move(to_xy, lambda z, x, c, y: (z, 1 - x, c, 1 - y))
     got_x = move(to_x, lambda z, x, c, y: (z, 1 - x, c, y))
+    mine, to_y = kernel_call(
+        keep_pack_kernel,
+        [longer] * 2,
+        [VMEM_SPEC] * 3,
+        [pltpu.VMEM(half_and.shape, jnp.float32), vbuf],
+        "keep_pack",
+    )(own(True, to_xy), keep_got, volume)
     got_y = move(to_y, lambda z, x, c, y: (z, x, c, 1 - y))
 
     edge = band * rows
@@ -634,7 +660,6 @@
         [VMEM_SPEC] * 3 + [ANY_SPEC],
         [],
         "gram",
-        flops=10**9,
     )(tangent[None], secant[None], drift[None], mine)
 
     pair = f32(2, rows, width)

time: 41.6 us -> 40.1 us (0.964)
  Pallas kernels: 10.9 us -> 9.26 us
  starting transfers between devices: 12.2 us -> 12.7 us
    pallas_call x3 -> x6, Pallas kernels: 7.27 us -> 5.68 us  [the longest x1 2.27 us: summed_plan(): kernel_call(functools.partial(fetch_kernel, views, rows, band, scale), [h...]
    ppermute x11 -> x12, starting transfers between devices: 12.2 us -> 12.7 us  [move(): return lax.ppermute(value, ('wide', 'grp'), pairs)]
    ppermute x11 -> x12, waiting for transfers between devices: 18.2 us -> 17.8 us  [move(): return lax.ppermute(value, ('wide', 'grp'), pairs)]
  transfers between devices with their start and end apart: 11 -> 12, of which waited for: 7 -> 7; matrix products, arithmetic and copies ran while one was open for 0% -> 0% of each run, Pallas kernels for 11% -> 12%
where the time goes in v6:
time: 40.1 us; the launch traced here: 39.9 us
  waiting for transfers between devices  17.8 us (44%)
  starting transfers between devices  12.7 us (32%)
  Pallas kernels  9.26 us (23%)
    ppermute x12, waiting for transfers between devices, move(): return lax.ppermute(value, ('wide', 'grp'), pairs)  17.8 us
    ppermute x12, starting transfers between devices, move(): return lax.ppermute(value, ('wide', 'grp'), pairs)  12.7 us
    pallas_call x1, Pallas kernels, summed_plan(): kernel_call(functools.partial(fetch_kernel, views, rows, band, scale), [h...  2.27 us
    pallas_call x2, Pallas kernels, own(): kernel_call(functools.partial(own_kernel, kept, views, rows, band), half_...  2.16 us
    pallas_call x1, Pallas kernels, summed_plan(): kernel_call(functools.partial(finish_kernel, band, slices, cols), [quarte...  1.46 us
    pallas_call x1, Pallas kernels, summed_plan(): kernel_call(functools.partial(sibling_kernel, views, rows, band), half_an...  1.08 us
  transfers between devices with their start and end apart: 12, of which 7 were waited for; matrix products, arithmetic and copies ran while one was open for 0% of the time, Pallas kernels for 12%

profile of v6, /device:TPU:0, one launch (start us, length us, event | category | flops | bytes accessed | tf_op | source)
XLA Modules:
  0.0 39.9 jit_solution(10758321941137205724)
XLA Ops:
  0.0 2.3 %pass_sibling.1 = (f32[8,8,1152]{2,1,0:T(8,128)S(1)}, f32[2,16,11,8,128]{4,3,2,1,0:T(8,128)S(1)}, f32[2,16,11,8,128]{4,3,2,1,0:T(8,128)S(1)}, f32[56,144]{1,0:T(8,128)S(1)}, f32[1,4,2048]{2,1,0:T(4,128)S(1)}) custom-call(f32[512]{0:T(512)} %constant.6.clone.tan_hbm, s32[512]{0:T(512)} %drift_hbm.1, f32[16,2,16,8,128]{4,3,2,1,0:T(8,128)} %bitcast.5, ...), custom_call_target="tpu_custom_call" | custom-call | flops 1000000000 | tf_op jit(solution)/shard_map/pass_sibling/pallas_call | solution.py:606
  2.3 0.5 %collective-permute-start = (f32[8,8,1152]{2,1,0:T(8,128)S(1)}, f32[8,8,1152]{2,1,0:T(8,128)S(1)}, u32[]{:S(2)}, u32[]{:S(2)}) collective-permute-start(f32[8,8,1152]{2,1,0:T(8,128)S(1)} %get-tuple-element.31), channel_id=1, source_target_pairs={{0,2},{1,3},{2,0},{3,1},{4,6},{5,7},{6,4},{7,5},{8,10},{9,11},{10,... | collective-permute-start | bytes 884744 | tf_op jit(solution)/shard_map/ppermute | solution.py:176
  2.8 1.1 %keep_sibling.1.after_ref = f32[9,8,1152]{2,1,0:T(8,128)S(1)} custom-call(f32[2,16,11,8,128]{4,3,2,1,0:T(8,128)S(1)} %get-tuple-element.29.buf, f32[56,144]{1,0:T(8,128)S(1)} %get-tuple-element.28.weights_ref, f32[1,4,2048]{2,1,0:T(4,128)S(1)} %get-tuple-element.30.vol_ref), custom_call_target="tpu_custom_call" | custom-call | flops 1000000000 | tf_op jit(solution)/shard_map/keep_sibling/pallas_call | solution.py:621
  3.9 0.1 collective-permute-start.1
  4.0 1.1 %pass_own.1.own_ref = f32[8,8,1152]{2,1,0:T(8,128)S(1)} custom-call(f32[2,16,11,8,128]{4,3,2,1,0:T(8,128)S(1)} %get-tuple-element.27.buf, f32[56,144]{1,0:T(8,128)S(1)} %get-tuple-element.28.weights_ref, f32[9,8,1152]{2,1,0:T(8,128)S(1)} %keep_sibling.1.after_ref), custom_call_target="tpu_custom_call" | custom-call | flops 1000000000 | tf_op jit(solution)/shard_map/pass_own/pallas_call | solution.py:632
  5.1 0.0 collective-permute-done.got_ref
  5.1 0.1 pass_pack.1
  5.2 0.0 copy-start
  5.2 0.0 copy-start.1
  5.2 0.0 copy-start.2
  5.2 1.1 %keep_own.1.own_ref = f32[8,8,1152]{2,1,0:T(8,128)S(1)} custom-call(f32[2,16,11,8,128]{4,3,2,1,0:T(8,128)S(1)} %get-tuple-element.27.buf, f32[56,144]{1,0:T(8,128)S(1)} %get-tuple-element.28.weights_ref, f32[8,8,640]{2,1,0:T(8,128)S(1)} %get-tuple-element.32.after_ref), custom_call_target="tpu_custom_call" | custom-call | flops 1000000000 | tf_op jit(solution)/shard_map/keep_own/pallas_call | solution.py:632
  6.3 0.0 collective-permute-done.1.got_ref
  6.3 0.1 keep_pack.1
  6.4 3.0 %collective-permute-start.4 = (f32[9,8,640]{2,1,0:T(8,128)S(1)}, f32[9,8,640]{2,1,0:T(8,128)S(1)}, u32[]{:S(2)}, u32[]{:S(2)}) collective-permute-start(f32[9,8,640]{2,1,0:T(8,128)S(1)} %get-tuple-element.35), channel_id=1, source_target_pairs={{0,1},{1,0},{2,3},{3,2},{4,5},{5,4},{6,7},{7,6},{8,9},{9,8},{10,11... | collective-permute-start | bytes 552968 | tf_op jit(solution)/shard_map/ppermute | solution.py:176
  9.5 1.5 %collective-permute-start.3 = (f32[8,8,640]{2,1,0:T(8,128)S(1)}, f32[8,8,640]{2,1,0:T(8,128)S(1)}, u32[]{:S(2)}, u32[]{:S(2)}) collective-permute-start(f32[8,8,640]{2,1,0:T(8,128)S(1)} %get-tuple-element.34), channel_id=1, source_target_pairs={{0,4},{1,5},{2,6},{3,7},{4,0},{5,1},{6,2},{7,3},{8,12},{9,13},{10,... | collective-permute-start | bytes 491528 | tf_op jit(solution)/shard_map/ppermute | solution.py:176
  10.9 0.1 collective-permute-start.2
  11.0 0.0 copy-done
  11.0 0.0 copy-done.1
  11.0 0.0 copy-done.2
  11.0 0.7 %gram.1 = (f32[48,256]{1,0:T(8,128)S(1)}, f32[80,240]{1,0:T(8,128)S(1)}, f32[80,240]{1,0:T(8,128)S(1)}) custom-call(f32[1,512]{1,0:T(1,128)S(1)} %copy-done.2, f32[1,512]{1,0:T(1,128)S(1)} %copy-done.1, s32[1,512]{1,0:T(1,128)S(1)} %bitcast.4, f32[9,8,640]{2,1,0:T(8,128)S(1)} %get-tuple-element.33.mine.after_ref), custom_call_target="tpu_custom_call" | custom-call | tf_op jit(solution)/shard_map/gram/pallas_call | solution.py:657
  11.7 4.9 %collective-permute-done.3.got_x = f32[8,8,640]{2,1,0:T(8,128)S(1)} collective-permute-done((f32[8,8,640]{2,1,0:T(8,128)S(1)}, f32[8,8,640]{2,1,0:T(8,128)S(1)}, u32[]{:S(2)}, u32[]{:S(2)}) %collective-permute-start.3) | collective-permute-done | bytes 163872 | tf_op jit(solution)/shard_map/ppermute | solution.py:176
  16.6 2.1 %collective-permute-done.2.got_xy = f32[8,8,640]{2,1,0:T(8,128)S(1)} collective-permute-done((f32[8,8,640]{2,1,0:T(8,128)S(1)}, f32[8,8,640]{2,1,0:T(8,128)S(1)}, u32[]{:S(2)}, u32[]{:S(2)}) %collective-permute-start.2) | collective-permute-done | bytes 163872 | tf_op jit(solution)/shard_map/ppermute | solution.py:176
  18.6 0.0 collective-permute-done.4.got_y
  18.6 0.1 depth_pack.1
  18.7 1.8 %collective-permute-start.5 = (f32[2,8,640]{2,1,0:T(8,128)S(1)}, f32[2,8,640]{2,1,0:T(8,128)S(1)}, u32[]{:S(2)}, u32[]{:S(2)}) collective-permute-start(f32[2,8,640]{2,1,0:T(8,128)S(1)} %get-tuple-element.41), channel_id=1, source_target_pairs={{0,8},{1,9},{2,10},{3,11},{4,12},{5,13},{6,14},{7,15},{8,0},{9,1},... | collective-permute-start | bytes 122888 | tf_op jit(solution)/shard_map/ppermute | solution.py:176
  20.5 2.5 %collective-permute-start.6 = (f32[2,8,640]{2,1,0:T(8,128)S(1)}, f32[2,8,640]{2,1,0:T(8,128)S(1)}, u32[]{:S(2)}, u32[]{:S(2)}) collective-permute-start(f32[2,8,640]{2,1,0:T(8,128)S(1)} %get-tuple-element.42), channel_id=1, source_target_pairs={{0,24},{1,25},{2,26},{3,27},{4,28},{5,29},{6,30},{7,31},{8,16},{9,... | collective-permute-start | bytes 122888 | tf_op jit(solution)/shard_map/ppermute | solution.py:176
  22.9 0.1 collective-permute-start.7
  23.1 0.7 %first_normal.1.first_ref = f32[2,8,640]{2,1,0:T(8,128)S(1)} custom-call(f32[2,8,640]{2,1,0:T(8,128)S(1)} %get-tuple-element.36.vol_pair, f32[48,256]{1,0:T(8,128)S(1)} %get-tuple-element.37.conv_ref, f32[80,240]{1,0:T(8,128)S(1)} %get-tuple-element.38.low_ref, f32[80,240]{1,0:T(8,128)S(1)} %get-tuple-element.39.high_ref), custom_call_target="tpu_custom_call" | custom-call | flops 1000000000 | tf_op jit(solution)/shard_map/first_normal/pallas_call | solution.py:677
  23.8 0.0 collective-permute-done.5.got_1
  23.8 2.5 %collective-permute-done.6.got_3 = f32[2,8,640]{2,1,0:T(8,128)S(1)} collective-permute-done((f32[2,8,640]{2,1,0:T(8,128)S(1)}, f32[2,8,640]{2,1,0:T(8,128)S(1)}, u32[]{:S(2)}, u32[]{:S(2)}) %collective-permute-start.6) | collective-permute-done | bytes 40992 | tf_op jit(solution)/shard_map/ppermute | solution.py:176
  26.3 2.0 %collective-permute-done.7.got_2 = f32[2,8,640]{2,1,0:T(8,128)S(1)} collective-permute-done((f32[2,8,640]{2,1,0:T(8,128)S(1)}, f32[2,8,640]{2,1,0:T(8,128)S(1)}, u32[]{:S(2)}, u32[]{:S(2)}) %collective-permute-start.7) | collective-permute-done | bytes 40992 | tf_op jit(solution)/shard_map/ppermute | solution.py:176
  28.3 0.1 collective-permute-start.8
  28.4 1.8 %collective-permute-start.9 = (f32[3,8,640]{2,1,0:T(8,128)S(1)}, f32[3,8,640]{2,1,0:T(8,128)S(1)}, u32[]{:S(2)}, u32[]{:S(2)}) collective-permute-start(f32[3,8,640]{2,1,0:T(8,128)S(1)} %get-tuple-element.46), channel_id=1, source_target_pairs={{0,4},{1,5},{2,6},{3,7},{4,0},{5,1},{6,2},{7,3},{8,12},{9,13},{10,... | collective-permute-start | bytes 184328 | tf_op jit(solution)/shard_map/ppermute | solution.py:176
  30.2 0.0 collective-permute-done.8.got_diag
  30.2 2.6 %collective-permute-done.9.got_x = f32[3,8,640]{2,1,0:T(8,128)S(1)} collective-permute-done((f32[3,8,640]{2,1,0:T(8,128)S(1)}, f32[3,8,640]{2,1,0:T(8,128)S(1)}, u32[]{:S(2)}, u32[]{:S(2)}) %collective-permute-start.9) | collective-permute-done | bytes 61472 | tf_op jit(solution)/shard_map/ppermute | solution.py:176
  32.8 1.5 %finish.1 = (f32[8,512]{1,0:T(8,128)S(1)}, f32[8,512]{1,0:T(8,128)S(1)}) custom-call(f32[4,8,640]{2,1,0:T(8,128)S(1)} %get-tuple-element.44.mine, f32[3,8,640]{2,1,0:T(8,128)S(1)} %collective-permute-done.8.got_diag, f32[3,8,640]{2,1,0:T(8,128)S(1)} %collective-permute-done.9.got_x, f32[48,256]{1,0:T(8,128)S(1)} %get-tuple-element.37.conv_ref, ...), custom_call_target="tpu_custom_call" | custom-call | tf_op jit(solution)/shard_map/finish/pallas_call | solution.py:699
  34.3 0.1 collective-permute-start.10
  34.4 1.2 %collective-permute-done.10.got_ref = f32[8,512]{1,0:T(8,128)S(1)} collective-permute-done((f32[8,512]{1,0:T(8,128)S(1)}, f32[8,512]{1,0:T(8,128)S(1)}, u32[]{:S(2)}, u32[]{:S(2)}) %collective-permute-start.10) | collective-permute-done | bytes 16416 | tf_op jit(solution)/shard_map/ppermute | solution.py:176
  35.5 1.2 %collective-permute-start.11 = (f32[2,4,512]{2,1,0:T(4,128)S(1)}, f32[2,4,512]{2,1,0:T(4,128)S(1)}, u32[]{:S(2)}, u32[]{:S(2)}) collective-permute-start(f32[2,4,512]{2,1,0:T(4,128)S(1)} %result_pack.1), channel_id=1, source_target_pairs={{0,1},{1,0},{2,3},{3,2},{4,5},{5,4},{6,7},{7,6},{8,9},{9,8},{10,11... | collective-permute-start | bytes 49160 | tf_op jit(solution)/shard_map/ppermute | solution.py:176
  36.7 2.6 %collective-permute-done.11.got_y = f32[2,4,512]{2,1,0:T(4,128)S(1)} collective-permute-done((f32[2,4,512]{2,1,0:T(4,128)S(1)}, f32[2,4,512]{2,1,0:T(4,128)S(1)}, u32[]{:S(2)}, u32[]{:S(2)}) %collective-permute-start.11) | collective-permute-done | bytes 16416 | tf_op jit(solution)/shard_map/ppermute | solution.py:176
  39.3 0.6 %result.1 = f32[1,4,2048]{2,1,0:T(4,128)} custom-call(f32[8,512]{1,0:T(8,128)S(1)} %get-tuple-element.47.own_ref, f32[8,512]{1,0:T(8,128)S(1)} %collective-permute-done.10.got_ref, f32[2,4,512]{2,1,0:T(4,128)S(1)} %collective-permute-done.11.got_y), custom_call_target="tpu_custom_call" | custom-call | tf_op jit(solution)/shard_map/result/pallas_call | solution.py:709
  (2 shorter events, 0.0 us)
Async XLA Ops:
  2.3 2.8 %collective-permute-start = (f32[8,8,1152]{2,1,0:T(8,128)S(1)}, f32[8,8,1152]{2,1,0:T(8,128)S(1)}, u32[]{:S(2)}, u32[]{:S(2)}) collective-permute-start(f32[8,8,1152]{2,1,0:T(8,128)S(1)} %get-tuple-element.31), channel_id=1, source_target_pairs={{0,2},{1,3},{2,0},{3,1},{4,6},{5,7},{6,4},{7,5},{8,10},{9,11},{10,... | collective-permute-start | bytes 884744 | tf_op jit(solution)/shard_map/ppermute | solution.py:176
  3.9 2.4 %collective-permute-start.1 = (f32[9,8,1152]{2,1,0:T(8,128)S(1)}, f32[9,8,1152]{2,1,0:T(8,128)S(1)}, u32[]{:S(2)}, u32[]{:S(2)}) collective-permute-start(f32[9,8,1152]{2,1,0:T(8,128)S(1)} %keep_sibling.1.after_ref), channel_id=1, source_target_pairs={{0,2},{1,3},{2,0},{3,1},{4,6},{5,7},{6,4},{7,5},{8,10},{9,11},{10,... | collective-permute-start | bytes 995336 | tf_op jit(solution)/shard_map/ppermute | solution.py:176
  5.2 5.8 %copy-start = (s32[512]{0:T(512)S(1)}, s32[512]{0:T(512)}, u32[]{:S(2)}) copy-start(s32[512]{0:T(512)} %drift_hbm.1) | copy-start | bytes 6148
  5.2 5.8 %copy-start.1 = (f32[1,512]{1,0:T(1,128)S(1)}, f32[1,512]{1,0:T(1,128)}, u32[]{:S(2)}) copy-start(f32[1,512]{1,0:T(1,128)} %constant.8.clone.sec_ref) | copy-start | bytes 6148
  5.2 5.8 %copy-start.2 = (f32[1,512]{1,0:T(1,128)S(1)}, f32[1,512]{1,0:T(1,128)}, u32[]{:S(2)}) copy-start(f32[1,512]{1,0:T(1,128)} %constant.7.clone.tan_ref) | copy-start | bytes 6148
  6.4 12.2 %collective-permute-start.4 = (f32[9,8,640]{2,1,0:T(8,128)S(1)}, f32[9,8,640]{2,1,0:T(8,128)S(1)}, u32[]{:S(2)}, u32[]{:S(2)}) collective-permute-start(f32[9,8,640]{2,1,0:T(8,128)S(1)} %get-tuple-element.35), channel_id=1, source_target_pairs={{0,1},{1,0},{2,3},{3,2},{4,5},{5,4},{6,7},{7,6},{8,9},{9,8},{10,11... | collective-permute-start | bytes 552968 | tf_op jit(solution)/shard_map/ppermute | solution.py:176
  9.5 7.1 %collective-permute-start.3 = (f32[8,8,640]{2,1,0:T(8,128)S(1)}, f32[8,8,640]{2,1,0:T(8,128)S(1)}, u32[]{:S(2)}, u32[]{:S(2)}) collective-permute-start(f32[8,8,640]{2,1,0:T(8,128)S(1)} %get-tuple-element.34), channel_id=1, source_target_pairs={{0,4},{1,5},{2,6},{3,7},{4,0},{5,1},{6,2},{7,3},{8,12},{9,13},{10,... | collective-permute-start | bytes 491528 | tf_op jit(solution)/shard_map/ppermute | solution.py:176
  10.9 7.7 %collective-permute-start.2 = (f32[8,8,640]{2,1,0:T(8,128)S(1)}, f32[8,8,640]{2,1,0:T(8,128)S(1)}, u32[]{:S(2)}, u32[]{:S(2)}) collective-permute-start(f32[8,8,640]{2,1,0:T(8,128)S(1)} %get-tuple-element.32.after_ref), channel_id=1, source_target_pairs={{0,5},{1,4},{2,7},{3,6},{4,1},{5,0},{6,3},{7,2},{8,13},{9,12},{10,... | collective-permute-start | bytes 491528 | tf_op jit(solution)/shard_map/ppermute | solution.py:176
  18.7 5.1 %collective-permute-start.5 = (f32[2,8,640]{2,1,0:T(8,128)S(1)}, f32[2,8,640]{2,1,0:T(8,128)S(1)}, u32[]{:S(2)}, u32[]{:S(2)}) collective-permute-start(f32[2,8,640]{2,1,0:T(8,128)S(1)} %get-tuple-element.41), channel_id=1, source_target_pairs={{0,8},{1,9},{2,10},{3,11},{4,12},{5,13},{6,14},{7,15},{8,0},{9,1},... | collective-permute-start | bytes 122888 | tf_op jit(solution)/shard_map/ppermute | solution.py:176
  20.5 5.8 %collective-permute-start.6 = (f32[2,8,640]{2,1,0:T(8,128)S(1)}, f32[2,8,640]{2,1,0:T(8,128)S(1)}, u32[]{:S(2)}, u32[]{:S(2)}) collective-permute-start(f32[2,8,640]{2,1,0:T(8,128)S(1)} %get-tuple-element.42), channel_id=1, source_target_pairs={{0,24},{1,25},{2,26},{3,27},{4,28},{5,29},{6,30},{7,31},{8,16},{9,... | collective-permute-start | bytes 122888 | tf_op jit(solution)/shard_map/ppermute | solution.py:176
  22.9 5.3 %collective-permute-start.7 = (f32[2,8,640]{2,1,0:T(8,128)S(1)}, f32[2,8,640]{2,1,0:T(8,128)S(1)}, u32[]{:S(2)}, u32[]{:S(2)}) collective-permute-start(f32[2,8,640]{2,1,0:T(8,128)S(1)} %get-tuple-element.43), channel_id=1, source_target_pairs={{0,16},{1,17},{2,18},{3,19},{4,20},{5,21},{6,22},{7,23},{8,24},{9,... | collective-permute-start | bytes 122888 | tf_op jit(solution)/shard_map/ppermute | solution.py:176
  28.3 1.9 %collective-permute-start.8 = (f32[3,8,640]{2,1,0:T(8,128)S(1)}, f32[3,8,640]{2,1,0:T(8,128)S(1)}, u32[]{:S(2)}, u32[]{:S(2)}) collective-permute-start(f32[3,8,640]{2,1,0:T(8,128)S(1)} %get-tuple-element.45), channel_id=1, source_target_pairs={{0,2},{1,3},{2,0},{3,1},{4,8},{5,9},{6,10},{7,11},{8,4},{9,5},{10,... | collective-permute-start | bytes 184328 | tf_op jit(solution)/shard_map/ppermute | solution.py:176
  28.4 4.4 %collective-permute-start.9 = (f32[3,8,640]{2,1,0:T(8,128)S(1)}, f32[3,8,640]{2,1,0:T(8,128)S(1)}, u32[]{:S(2)}, u32[]{:S(2)}) collective-permute-start(f32[3,8,640]{2,1,0:T(8,128)S(1)} %get-tuple-element.46), channel_id=1, source_target_pairs={{0,4},{1,5},{2,6},{3,7},{4,0},{5,1},{6,2},{7,3},{8,12},{9,13},{10,... | collective-permute-start | bytes 184328 | tf_op jit(solution)/shard_map/ppermute | solution.py:176
  34.3 1.2 %collective-permute-start.10 = (f32[8,512]{1,0:T(8,128)S(1)}, f32[8,512]{1,0:T(8,128)S(1)}, u32[]{:S(2)}, u32[]{:S(2)}) collective-permute-start(f32[8,512]{1,0:T(8,128)S(1)} %get-tuple-element.48), channel_id=1, source_target_pairs={{0,2},{1,3},{2,0},{3,1},{4,6},{5,7},{6,4},{7,5},{8,10},{9,11},{10,... | collective-permute-start | bytes 49160 | tf_op jit(solution)/shard_map/ppermute | solution.py:176
  35.5 3.7 %collective-permute-start.11 = (f32[2,4,512]{2,1,0:T(4,128)S(1)}, f32[2,4,512]{2,1,0:T(4,128)S(1)}, u32[]{:S(2)}, u32[]{:S(2)}) collective-permute-start(f32[2,4,512]{2,1,0:T(4,128)S(1)} %result_pack.1), channel_id=1, source_target_pairs={{0,1},{1,0},{2,3},{3,2},{4,5},{5,4},{6,7},{7,6},{8,9},{9,8},{10,11... | collective-permute-start | bytes 49160 | tf_op jit(solution)/shard_map/ppermute | solution.py:176

commit v7 on v6

--- a/solution.py
+++ b/solution.py
@@ -343,33 +343,34 @@
     back_project(views, rows, band, weights_ref[...].astype(jnp.bfloat16), load, out_ref, terms)
 
 
-def pass_pack_kernel(own_ref, got_ref, to_x, to_xy, acc):
-    width = to_x.shape[2]
+def pass_pack_kernel(own_ref, got_ref, to_xy, acc):
+    width = to_xy.shape[2]
     _, _, _, y = coords()
     acc[...] = own_ref[...] + got_ref[...]
-    for out, py in ((to_x, y), (to_xy, 1 - y)):
-        out[...] = acc[:, :, pl.ds(pl.multiple_of(py * (width - LANES), LANES), width)]
-
-
-def keep_pack_kernel(own_ref, got_ref, vol_ref, mine, to_y, acc, vbuf):
+    to_xy[...] = acc[:, :, pl.ds(pl.multiple_of((1 - y) * (width - LANES), LANES), width)]
+
+
+def keep_pack_kernel(pass_ref, pass_got, own_ref, got_ref, vol_ref, mine, to_x, to_y, vol_mine, vol_to_y, acc, both, vbuf):
     count, rows, half_width = own_ref.shape
     width = mine.shape[2]
     part = vol_ref.shape[1]
     _, _, c, y = coords()
-    acc[0:count] = own_ref[...] + got_ref[0:count]
+    acc[...] = own_ref[...] + got_ref[0:count]
     here = volume_window(vol_ref, c, half_width - LANES, vbuf)
     there = got_ref[count, 0:part]
-    acc[count, 0:part] = jnp.where(c == 0, here, there)
-    acc[count, part:] = jnp.where(c == 0, there, here)
-    for out, py in ((mine, y), (to_y, 1 - y)):
-        out[...] = acc[:, :, pl.ds(pl.multiple_of(py * (width - LANES), LANES), width)]
-
-
-def depth_pack_kernel(mine, got_xy, got_x, got_y, own_pair, to_1, to_2, to_3, vol_pair, acc):
-    count, rows, _ = acc.shape
-    part = rows // 2
-    z, x, c, y = coords()
-    acc[...] = (mine[0:count] + got_x[...]) + (got_y[0:count] + got_xy[...])
+    both[0:part] = jnp.where(c == 0, here, there)
+    both[part:] = jnp.where(c == 0, there, here)
+    window = pl.ds(pl.multiple_of(y * (width - LANES), LANES), width)
+    to_x[...] = pass_ref[:, :, window] + pass_got[:, :, window]
+    for out, vol, py in ((mine, vol_mine, y), (to_y, vol_to_y, 1 - y)):
+        begin = pl.multiple_of(py * (width - LANES), LANES)
+        out[...] = acc[:, :, pl.ds(begin, width)]
+        vol[...] = both[:, pl.ds(begin, width)]
+
+
+def depth_pack_kernel(mine, got_xy, got_x, got_y, own_pair, to_1, to_2, to_3, acc):
+    z, _, _, _ = coords()
+    acc[...] = (mine[...] + got_x[...]) + (got_y[...] + got_xy[...])
     for out, pz in (
         (own_pair, z),
         (to_1, jnp.where(z % 2 == 0, z + 1, z - 1)),
@@ -377,11 +378,6 @@
         (to_3, 3 - z),
     ):
         out[...] = acc[pl.ds(2 * pz, 2)]
-    here, there = mine[count], got_y[count]
-    upper = jnp.where(y == 0, here, there)
-    lower = jnp.where(y == 0, there, here)
-    for i in range(2):
-        vol_pair[i] = jnp.concatenate([upper[i * part : (i + 1) * part], lower[i * part : (i + 1) * part]], axis=0)
 
 
 def gram_kernel(rows, band, scale, tan_ref, sec_ref, drift_ref, after_ref, conv_ref, low_ref, high_ref):
@@ -468,9 +464,16 @@
     return index * block - HALO, index == 0, index == total_cols // block - 1
 
 
-def first_normal_kernel(band, total_cols, vol_pair, conv_ref, low_ref, high_ref, out, work):
-    _, is_low, is_high = block_place(vol_pair.shape[2], total_cols)
-    volumes = [vol_pair[i] for i in range(2)]
+def first_normal_kernel(band, total_cols, vol_mine, vol_got, conv_ref, low_ref, high_ref, out, work):
+    _, is_low, is_high = block_place(vol_mine.shape[1], total_cols)
+    _, _, _, y = coords()
+    part = vol_mine.shape[0] // 2
+    here, there = vol_mine[...], vol_got[...]
+    upper = jnp.where(y == 0, here, there)
+    lower = jnp.where(y == 0, there, here)
+    volumes = [
+        jnp.concatenate([upper[i * part : (i + 1) * part], lower[i * part : (i + 1) * part]], axis=0) for i in range(2)
+    ]
     normal(volumes, conv_ref[...].astype(jnp.bfloat16), low_ref, high_ref, work, band, is_low, is_high)
     for i in range(2):
         out[i] = volumes[i] - work[i]
@@ -638,20 +641,22 @@
             flops=10**9,
         )(own_buf, weights, after)
 
-    message, longer = f32(count, rows, width), f32(count + 1, rows, width)
-    to_x, to_xy = kernel_call(
-        pass_pack_kernel, [message] * 2, [VMEM_SPEC] * 2, [pltpu.VMEM(half_of.shape, jnp.float32)], "pass_pack"
-    )(own(False, keep_sibling), pass_got)
+    message = f32(count, rows, width)
+    pass_own = own(False, keep_sibling)
+    to_xy = kernel_call(pass_pack_kernel, message, [VMEM_SPEC] * 2, [pltpu.VMEM(half_of.shape, jnp.float32)], "pass_pack")(
+        pass_own, pass_got
+    )
     got_xy = move(to_xy, lambda z, x, c, y: (z, 1 - x, c, 1 - y))
+    mine, to_x, to_y, vol_mine, vol_to_y = kernel_call(
+        keep_pack_kernel,
+        [message] * 3 + [f32(rows, width)] * 2,
+        [VMEM_SPEC] * 5,
+        [pltpu.VMEM(half_of.shape, jnp.float32), pltpu.VMEM((rows, half_width), jnp.float32), vbuf],
+        "keep_pack",
+    )(pass_own, pass_got, own(True, to_xy), keep_got, volume)
     got_x = move(to_x, lambda z, x, c, y: (z, 1 - x, c, y))
-    mine, to_y = kernel_call(
-        keep_pack_kernel,
-        [longer] * 2,
-        [VMEM_SPEC] * 3,
-        [pltpu.VMEM(half_and.shape, jnp.float32), vbuf],
-        "keep_pack",
-    )(own(True, to_xy), keep_got, volume)
     got_y = move(to_y, lambda z, x, c, y: (z, x, c, 1 - y))
+    vol_got = move(vol_to_y, lambda z, x, c, y: (z, x, c, 1 - y))
 
     edge = band * rows
     conv, low, high = kernel_call(
@@ -663,9 +668,9 @@
     )(tangent[None], secant[None], drift[None], mine)
 
     pair = f32(2, rows, width)
-    own_pair, to_1, to_2, to_3, vol_pair = kernel_call(
+    own_pair, to_1, to_2, to_3 = kernel_call(
         depth_pack_kernel,
-        [pair] * 5,
+        [pair] * 4,
         [VMEM_SPEC] * 4,
         [pltpu.VMEM((count, rows, width), jnp.float32)],
         "depth_pack",
@@ -677,11 +682,11 @@
     first = kernel_call(
         functools.partial(first_normal_kernel, band, cols),
         pair,
-        [VMEM_SPEC] * 4,
+        [VMEM_SPEC] * 5,
         [pltpu.VMEM((2, rows, width), jnp.float32)],
         "first_normal",
         flops=10**9,
-    )(vol_pair, conv, low, high)
+    )(vol_mine, vol_got, conv, low, high)
 
     three = f32(3, rows, width)
     mine, to_x, to_diag = kernel_call(

time: 40.1 us -> 38.9 us (0.970)
  waiting for transfers between devices: 17.8 us -> 14.6 us
  starting transfers between devices: 12.7 us -> 14.7 us
    ppermute x12 -> x13, waiting for transfers between devices: 17.8 us -> 14.6 us  [move(): return lax.ppermute(value, ('wide', 'grp'), pairs)]
    ppermute x12 -> x13, starting transfers between devices: 12.7 us -> 14.7 us  [move(): return lax.ppermute(value, ('wide', 'grp'), pairs)]
  transfers between devices with their start and end apart: 12 -> 13, of which waited for: 7 -> 7; matrix products, arithmetic and copies ran while one was open for 0% -> 0% of each run, Pallas kernels for 12% -> 13%
where the time goes in v7:
time: 38.9 us; the launch traced here: 38.7 us
  starting transfers between devices  14.7 us (38%)
  waiting for transfers between devices  14.6 us (38%)
  Pallas kernels  9.27 us (24%)
    ppermute x13, starting transfers between devices, move(): return lax.ppermute(value, ('wide', 'grp'), pairs)  14.7 us
    ppermute x13, waiting for transfers between devices, move(): return lax.ppermute(value, ('wide', 'grp'), pairs)  14.6 us
    pallas_call x1, Pallas kernels, summed_plan(): kernel_call(functools.partial(fetch_kernel, views, rows, band, scale), [h...  2.27 us
    pallas_call x2, Pallas kernels, own(): kernel_call(functools.partial(own_kernel, kept, views, rows, band), half_...  2.14 us
    pallas_call x1, Pallas kernels, summed_plan(): kernel_call(functools.partial(finish_kernel, band, slices, cols), [quarte...  1.46 us
    pallas_call x1, Pallas kernels, summed_plan(): kernel_call(functools.partial(sibling_kernel, views, rows, band), half_an...  1.08 us
  transfers between devices with their start and end apart: 13, of which 7 were waited for; matrix products, arithmetic and copies ran while one was open for 0% of the time, Pallas kernels for 13%

profile of v7, /device:TPU:0, one launch (start us, length us, event | category | flops | bytes accessed | tf_op | source)
XLA Modules:
  0.0 38.7 jit_solution(887465205837998842)
XLA Ops:
  0.0 2.3 %pass_sibling.1 = (f32[8,8,1152]{2,1,0:T(8,128)S(1)}, f32[2,16,11,8,128]{4,3,2,1,0:T(8,128)S(1)}, f32[2,16,11,8,128]{4,3,2,1,0:T(8,128)S(1)}, f32[56,144]{1,0:T(8,128)S(1)}, f32[1,4,2048]{2,1,0:T(4,128)S(1)}) custom-call(f32[512]{0:T(512)} %constant.6.clone.tan_hbm, s32[512]{0:T(512)} %drift_hbm.1, f32[16,2,16,8,128]{4,3,2,1,0:T(8,128)} %bitcast.5, ...), custom_call_target="tpu_custom_call" | custom-call | flops 1000000000 | tf_op jit(solution)/shard_map/pass_sibling/pallas_call | solution.py:609
  2.3 0.5 %collective-permute-start = (f32[8,8,1152]{2,1,0:T(8,128)S(1)}, f32[8,8,1152]{2,1,0:T(8,128)S(1)}, u32[]{:S(2)}, u32[]{:S(2)}) collective-permute-start(f32[8,8,1152]{2,1,0:T(8,128)S(1)} %get-tuple-element.31), channel_id=1, source_target_pairs={{0,2},{1,3},{2,0},{3,1},{4,6},{5,7},{6,4},{7,5},{8,10},{9,11},{10,... | collective-permute-start | bytes 884744 | tf_op jit(solution)/shard_map/ppermute | solution.py:176
  2.8 1.1 %keep_sibling.1.after_ref = f32[9,8,1152]{2,1,0:T(8,128)S(1)} custom-call(f32[2,16,11,8,128]{4,3,2,1,0:T(8,128)S(1)} %get-tuple-element.29.buf, f32[56,144]{1,0:T(8,128)S(1)} %get-tuple-element.28.weights_ref, f32[1,4,2048]{2,1,0:T(4,128)S(1)} %get-tuple-element.30.vol_ref), custom_call_target="tpu_custom_call" | custom-call | flops 1000000000 | tf_op jit(solution)/shard_map/keep_sibling/pallas_call | solution.py:624
  3.9 0.1 collective-permute-start.1
  4.0 1.1 %pass_own.1.own_ref.pass_ref = f32[8,8,1152]{2,1,0:T(8,128)S(1)} custom-call(f32[2,16,11,8,128]{4,3,2,1,0:T(8,128)S(1)} %get-tuple-element.27.buf, f32[56,144]{1,0:T(8,128)S(1)} %get-tuple-element.28.weights_ref, f32[9,8,1152]{2,1,0:T(8,128)S(1)} %keep_sibling.1.after_ref), custom_call_target="tpu_custom_call" | custom-call | flops 1000000000 | tf_op jit(solution)/shard_map/pass_own/pallas_call | solution.py:635
  5.1 0.0 collective-permute-done.got_ref.pass_got
  5.1 0.0 copy-start
  5.2 0.0 copy-start.1
  5.2 0.0 copy-start.2
  5.2 4.0 %collective-permute-start.3 = (f32[8,8,640]{2,1,0:T(8,128)S(1)}, f32[8,8,640]{2,1,0:T(8,128)S(1)}, u32[]{:S(2)}, u32[]{:S(2)}) collective-permute-start(f32[8,8,640]{2,1,0:T(8,128)S(1)} %pass_pack.1.after_ref), channel_id=1, source_target_pairs={{0,5},{1,4},{2,7},{3,6},{4,1},{5,0},{6,3},{7,2},{8,13},{9,12},{10,... | collective-permute-start | bytes 491528 | tf_op jit(solution)/shard_map/ppermute | solution.py:176
  9.1 1.1 %keep_own.1.own_ref = f32[8,8,1152]{2,1,0:T(8,128)S(1)} custom-call(f32[2,16,11,8,128]{4,3,2,1,0:T(8,128)S(1)} %get-tuple-element.27.buf, f32[56,144]{1,0:T(8,128)S(1)} %get-tuple-element.28.weights_ref, f32[8,8,640]{2,1,0:T(8,128)S(1)} %pass_pack.1.after_ref), custom_call_target="tpu_custom_call" | custom-call | flops 1000000000 | tf_op jit(solution)/shard_map/keep_own/pallas_call | solution.py:635
  10.2 0.0 collective-permute-done.1.got_ref
  10.2 0.2 keep_pack.1
  10.4 0.6 %collective-permute-start.4 = (f32[8,8,640]{2,1,0:T(8,128)S(1)}, f32[8,8,640]{2,1,0:T(8,128)S(1)}, u32[]{:S(2)}, u32[]{:S(2)}) collective-permute-start(f32[8,8,640]{2,1,0:T(8,128)S(1)} %get-tuple-element.38), channel_id=1, source_target_pairs={{0,4},{1,5},{2,6},{3,7},{4,0},{5,1},{6,2},{7,3},{8,12},{9,13},{10,... | collective-permute-start | bytes 491528 | tf_op jit(solution)/shard_map/ppermute | solution.py:176
  11.0 0.1 collective-permute-start.5
  11.1 2.0 %collective-permute-start.2 = (f32[8,640]{1,0:T(8,128)S(1)}, f32[8,640]{1,0:T(8,128)S(1)}, u32[]{:S(2)}, u32[]{:S(2)}) collective-permute-start(f32[8,640]{1,0:T(8,128)S(1)} %get-tuple-element.33), channel_id=1, source_target_pairs={{0,1},{1,0},{2,3},{3,2},{4,5},{5,4},{6,7},{7,6},{8,9},{9,8},{10,11... | collective-permute-start | bytes 61448 | tf_op jit(solution)/shard_map/ppermute | solution.py:176
  13.0 0.0 copy-done
  13.0 0.0 copy-done.1
  13.0 0.0 copy-done.2
  13.0 0.7 %gram.1 = (f32[48,256]{1,0:T(8,128)S(1)}, f32[80,240]{1,0:T(8,128)S(1)}, f32[80,240]{1,0:T(8,128)S(1)}) custom-call(f32[1,512]{1,0:T(1,128)S(1)} %copy-done.2, f32[1,512]{1,0:T(1,128)S(1)} %copy-done.1, s32[1,512]{1,0:T(1,128)S(1)} %bitcast.4, f32[8,8,640]{2,1,0:T(8,128)S(1)} %get-tuple-element.34.after_ref.mine), custom_call_target="tpu_custom_call" | custom-call | tf_op jit(solution)/shard_map/gram/pallas_call | solution.py:662
  13.7 0.4 %collective-permute-done.3.got_xy = f32[8,8,640]{2,1,0:T(8,128)S(1)} collective-permute-done((f32[8,8,640]{2,1,0:T(8,128)S(1)}, f32[8,8,640]{2,1,0:T(8,128)S(1)}, u32[]{:S(2)}, u32[]{:S(2)}) %collective-permute-start.3) | collective-permute-done | bytes 163872 | tf_op jit(solution)/shard_map/ppermute | solution.py:176
  14.1 3.2 %collective-permute-done.4.got_x = f32[8,8,640]{2,1,0:T(8,128)S(1)} collective-permute-done((f32[8,8,640]{2,1,0:T(8,128)S(1)}, f32[8,8,640]{2,1,0:T(8,128)S(1)}, u32[]{:S(2)}, u32[]{:S(2)}) %collective-permute-start.4) | collective-permute-done | bytes 163872 | tf_op jit(solution)/shard_map/ppermute | solution.py:176
  17.3 0.0 collective-permute-done.5.got_y
  17.3 0.1 depth_pack.1
  17.4 1.9 %collective-permute-start.6 = (f32[2,8,640]{2,1,0:T(8,128)S(1)}, f32[2,8,640]{2,1,0:T(8,128)S(1)}, u32[]{:S(2)}, u32[]{:S(2)}) collective-permute-start(f32[2,8,640]{2,1,0:T(8,128)S(1)} %get-tuple-element.41), channel_id=1, source_target_pairs={{0,8},{1,9},{2,10},{3,11},{4,12},{5,13},{6,14},{7,15},{8,0},{9,1},... | collective-permute-start | bytes 122888 | tf_op jit(solution)/shard_map/ppermute | solution.py:176
  19.3 2.5 %collective-permute-start.7 = (f32[2,8,640]{2,1,0:T(8,128)S(1)}, f32[2,8,640]{2,1,0:T(8,128)S(1)}, u32[]{:S(2)}, u32[]{:S(2)}) collective-permute-start(f32[2,8,640]{2,1,0:T(8,128)S(1)} %get-tuple-element.42), channel_id=1, source_target_pairs={{0,24},{1,25},{2,26},{3,27},{4,28},{5,29},{6,30},{7,31},{8,16},{9,... | collective-permute-start | bytes 122888 | tf_op jit(solution)/shard_map/ppermute | solution.py:176
  21.8 0.1 collective-permute-start.8
  21.9 0.0 collective-permute-done.2.vol_got
  21.9 0.7 %first_normal.1.first_ref = f32[2,8,640]{2,1,0:T(8,128)S(1)} custom-call(f32[8,640]{1,0:T(8,128)S(1)} %get-tuple-element.32.vol_mine, f32[8,640]{1,0:T(8,128)S(1)} %collective-permute-done.2.vol_got, f32[48,256]{1,0:T(8,128)S(1)} %get-tuple-element.35.conv_ref, f32[80,240]{1,0:T(8,128)S(1)} %get-tuple-element.36.low_ref, ...), custom_call_target="tpu_custom_call" | custom-call | flops 1000000000 | tf_op jit(solution)/shard_map/first_normal/pallas_call | solution.py:682
  22.6 0.0 collective-permute-done.6.got_1
  22.6 2.5 %collective-permute-done.7.got_3 = f32[2,8,640]{2,1,0:T(8,128)S(1)} collective-permute-done((f32[2,8,640]{2,1,0:T(8,128)S(1)}, f32[2,8,640]{2,1,0:T(8,128)S(1)}, u32[]{:S(2)}, u32[]{:S(2)}) %collective-permute-start.7) | collective-permute-done | bytes 40992 | tf_op jit(solution)/shard_map/ppermute | solution.py:176
  25.1 2.0 %collective-permute-done.8.got_2 = f32[2,8,640]{2,1,0:T(8,128)S(1)} collective-permute-done((f32[2,8,640]{2,1,0:T(8,128)S(1)}, f32[2,8,640]{2,1,0:T(8,128)S(1)}, u32[]{:S(2)}, u32[]{:S(2)}) %collective-permute-start.8) | collective-permute-done | bytes 40992 | tf_op jit(solution)/shard_map/ppermute | solution.py:176
  27.1 0.1 collective-permute-start.9
  27.2 1.8 %collective-permute-start.10 = (f32[3,8,640]{2,1,0:T(8,128)S(1)}, f32[3,8,640]{2,1,0:T(8,128)S(1)}, u32[]{:S(2)}, u32[]{:S(2)}) collective-permute-start(f32[3,8,640]{2,1,0:T(8,128)S(1)} %get-tuple-element.46), channel_id=1, source_target_pairs={{0,4},{1,5},{2,6},{3,7},{4,0},{5,1},{6,2},{7,3},{8,12},{9,13},{10,... | collective-permute-start | bytes 184328 | tf_op jit(solution)/shard_map/ppermute | solution.py:176
  29.0 0.0 collective-permute-done.9.got_diag
  29.0 2.6 %collective-permute-done.10.got_x = f32[3,8,640]{2,1,0:T(8,128)S(1)} collective-permute-done((f32[3,8,640]{2,1,0:T(8,128)S(1)}, f32[3,8,640]{2,1,0:T(8,128)S(1)}, u32[]{:S(2)}, u32[]{:S(2)}) %collective-permute-start.10) | collective-permute-done | bytes 61472 | tf_op jit(solution)/shard_map/ppermute | solution.py:176
  31.6 1.5 %finish.1 = (f32[8,512]{1,0:T(8,128)S(1)}, f32[8,512]{1,0:T(8,128)S(1)}) custom-call(f32[4,8,640]{2,1,0:T(8,128)S(1)} %get-tuple-element.44.mine, f32[3,8,640]{2,1,0:T(8,128)S(1)} %collective-permute-done.9.got_diag, f32[3,8,640]{2,1,0:T(8,128)S(1)} %collective-permute-done.10.got_x, f32[48,256]{1,0:T(8,128)S(1)} %get-tuple-element.35.conv_ref, ...), custom_call_target="tpu_custom_call" | custom-call | tf_op jit(solution)/shard_map/finish/pallas_call | solution.py:704
  33.1 0.1 collective-permute-start.11
  33.2 1.2 %collective-permute-done.11.got_ref = f32[8,512]{1,0:T(8,128)S(1)} collective-permute-done((f32[8,512]{1,0:T(8,128)S(1)}, f32[8,512]{1,0:T(8,128)S(1)}, u32[]{:S(2)}, u32[]{:S(2)}) %collective-permute-start.11) | collective-permute-done | bytes 16416 | tf_op jit(solution)/shard_map/ppermute | solution.py:176
  34.3 1.0 %collective-permute-start.12 = (f32[2,4,512]{2,1,0:T(4,128)S(1)}, f32[2,4,512]{2,1,0:T(4,128)S(1)}, u32[]{:S(2)}, u32[]{:S(2)}) collective-permute-start(f32[2,4,512]{2,1,0:T(4,128)S(1)} %result_pack.1), channel_id=1, source_target_pairs={{0,1},{1,0},{2,3},{3,2},{4,5},{5,4},{6,7},{7,6},{8,9},{9,8},{10,11... | collective-permute-start | bytes 49160 | tf_op jit(solution)/shard_map/ppermute | solution.py:176
  35.4 2.7 %collective-permute-done.12.got_y = f32[2,4,512]{2,1,0:T(4,128)S(1)} collective-permute-done((f32[2,4,512]{2,1,0:T(4,128)S(1)}, f32[2,4,512]{2,1,0:T(4,128)S(1)}, u32[]{:S(2)}, u32[]{:S(2)}) %collective-permute-start.12) | collective-permute-done | bytes 16416 | tf_op jit(solution)/shard_map/ppermute | solution.py:176
  38.1 0.6 %result.1 = f32[1,4,2048]{2,1,0:T(4,128)} custom-call(f32[8,512]{1,0:T(8,128)S(1)} %get-tuple-element.47.own_ref, f32[8,512]{1,0:T(8,128)S(1)} %collective-permute-done.11.got_ref, f32[2,4,512]{2,1,0:T(4,128)S(1)} %collective-permute-done.12.got_y), custom_call_target="tpu_custom_call" | custom-call | tf_op jit(solution)/shard_map/result/pallas_call | solution.py:714
  (3 shorter events, 0.1 us)
Async XLA Ops:
  2.3 2.8 %collective-permute-start = (f32[8,8,1152]{2,1,0:T(8,128)S(1)}, f32[8,8,1152]{2,1,0:T(8,128)S(1)}, u32[]{:S(2)}, u32[]{:S(2)}) collective-permute-start(f32[8,8,1152]{2,1,0:T(8,128)S(1)} %get-tuple-element.31), channel_id=1, source_target_pairs={{0,2},{1,3},{2,0},{3,1},{4,6},{5,7},{6,4},{7,5},{8,10},{9,11},{10,... | collective-permute-start | bytes 884744 | tf_op jit(solution)/shard_map/ppermute | solution.py:176
  3.9 6.3 %collective-permute-start.1 = (f32[9,8,1152]{2,1,0:T(8,128)S(1)}, f32[9,8,1152]{2,1,0:T(8,128)S(1)}, u32[]{:S(2)}, u32[]{:S(2)}) collective-permute-start(f32[9,8,1152]{2,1,0:T(8,128)S(1)} %keep_sibling.1.after_ref), channel_id=1, source_target_pairs={{0,2},{1,3},{2,0},{3,1},{4,6},{5,7},{6,4},{7,5},{8,10},{9,11},{10,... | collective-permute-start | bytes 995336 | tf_op jit(solution)/shard_map/ppermute | solution.py:176
  5.1 7.9 %copy-start = (s32[512]{0:T(512)S(1)}, s32[512]{0:T(512)}, u32[]{:S(2)}) copy-start(s32[512]{0:T(512)} %drift_hbm.1) | copy-start | bytes 6148
  5.2 7.9 %copy-start.1 = (f32[1,512]{1,0:T(1,128)S(1)}, f32[1,512]{1,0:T(1,128)}, u32[]{:S(2)}) copy-start(f32[1,512]{1,0:T(1,128)} %constant.8.clone.sec_ref) | copy-start | bytes 6148
  5.2 7.9 %copy-start.2 = (f32[1,512]{1,0:T(1,128)S(1)}, f32[1,512]{1,0:T(1,128)}, u32[]{:S(2)}) copy-start(f32[1,512]{1,0:T(1,128)} %constant.7.clone.tan_ref) | copy-start | bytes 6148
  5.2 9.0 %collective-permute-start.3 = (f32[8,8,640]{2,1,0:T(8,128)S(1)}, f32[8,8,640]{2,1,0:T(8,128)S(1)}, u32[]{:S(2)}, u32[]{:S(2)}) collective-permute-start(f32[8,8,640]{2,1,0:T(8,128)S(1)} %pass_pack.1.after_ref), channel_id=1, source_target_pairs={{0,5},{1,4},{2,7},{3,6},{4,1},{5,0},{6,3},{7,2},{8,13},{9,12},{10,... | collective-permute-start | bytes 491528 | tf_op jit(solution)/shard_map/ppermute | solution.py:176
  10.4 6.9 %collective-permute-start.4 = (f32[8,8,640]{2,1,0:T(8,128)S(1)}, f32[8,8,640]{2,1,0:T(8,128)S(1)}, u32[]{:S(2)}, u32[]{:S(2)}) collective-permute-start(f32[8,8,640]{2,1,0:T(8,128)S(1)} %get-tuple-element.38), channel_id=1, source_target_pairs={{0,4},{1,5},{2,6},{3,7},{4,0},{5,1},{6,2},{7,3},{8,12},{9,13},{10,... | collective-permute-start | bytes 491528 | tf_op jit(solution)/shard_map/ppermute | solution.py:176
  11.0 6.3 %collective-permute-start.5 = (f32[8,8,640]{2,1,0:T(8,128)S(1)}, f32[8,8,640]{2,1,0:T(8,128)S(1)}, u32[]{:S(2)}, u32[]{:S(2)}) collective-permute-start(f32[8,8,640]{2,1,0:T(8,128)S(1)} %get-tuple-element.39), channel_id=1, source_target_pairs={{0,1},{1,0},{2,3},{3,2},{4,5},{5,4},{6,7},{7,6},{8,9},{9,8},{10,11... | collective-permute-start | bytes 491528 | tf_op jit(solution)/shard_map/ppermute | solution.py:176
  11.1 10.8 %collective-permute-start.2 = (f32[8,640]{1,0:T(8,128)S(1)}, f32[8,640]{1,0:T(8,128)S(1)}, u32[]{:S(2)}, u32[]{:S(2)}) collective-permute-start(f32[8,640]{1,0:T(8,128)S(1)} %get-tuple-element.33), channel_id=1, source_target_pairs={{0,1},{1,0},{2,3},{3,2},{4,5},{5,4},{6,7},{7,6},{8,9},{9,8},{10,11... | collective-permute-start | bytes 61448 | tf_op jit(solution)/shard_map/ppermute | solution.py:176
  17.4 5.2 %collective-permute-start.6 = (f32[2,8,640]{2,1,0:T(8,128)S(1)}, f32[2,8,640]{2,1,0:T(8,128)S(1)}, u32[]{:S(2)}, u32[]{:S(2)}) collective-permute-start(f32[2,8,640]{2,1,0:T(8,128)S(1)} %get-tuple-element.41), channel_id=1, source_target_pairs={{0,8},{1,9},{2,10},{3,11},{4,12},{5,13},{6,14},{7,15},{8,0},{9,1},... | collective-permute-start | bytes 122888 | tf_op jit(solution)/shard_map/ppermute | solution.py:176
  19.3 5.8 %collective-permute-start.7 = (f32[2,8,640]{2,1,0:T(8,128)S(1)}, f32[2,8,640]{2,1,0:T(8,128)S(1)}, u32[]{:S(2)}, u32[]{:S(2)}) collective-permute-start(f32[2,8,640]{2,1,0:T(8,128)S(1)} %get-tuple-element.42), channel_id=1, source_target_pairs={{0,24},{1,25},{2,26},{3,27},{4,28},{5,29},{6,30},{7,31},{8,16},{9,... | collective-permute-start | bytes 122888 | tf_op jit(solution)/shard_map/ppermute | solution.py:176
  21.8 5.3 %collective-permute-start.8 = (f32[2,8,640]{2,1,0:T(8,128)S(1)}, f32[2,8,640]{2,1,0:T(8,128)S(1)}, u32[]{:S(2)}, u32[]{:S(2)}) collective-permute-start(f32[2,8,640]{2,1,0:T(8,128)S(1)} %get-tuple-element.43), channel_id=1, source_target_pairs={{0,16},{1,17},{2,18},{3,19},{4,20},{5,21},{6,22},{7,23},{8,24},{9,... | collective-permute-start | bytes 122888 | tf_op jit(solution)/shard_map/ppermute | solution.py:176
  27.1 1.9 %collective-permute-start.9 = (f32[3,8,640]{2,1,0:T(8,128)S(1)}, f32[3,8,640]{2,1,0:T(8,128)S(1)}, u32[]{:S(2)}, u32[]{:S(2)}) collective-permute-start(f32[3,8,640]{2,1,0:T(8,128)S(1)} %get-tuple-element.45), channel_id=1, source_target_pairs={{0,2},{1,3},{2,0},{3,1},{4,8},{5,9},{6,10},{7,11},{8,4},{9,5},{10,... | collective-permute-start | bytes 184328 | tf_op jit(solution)/shard_map/ppermute | solution.py:176
  27.2 4.4 %collective-permute-start.10 = (f32[3,8,640]{2,1,0:T(8,128)S(1)}, f32[3,8,640]{2,1,0:T(8,128)S(1)}, u32[]{:S(2)}, u32[]{:S(2)}) collective-permute-start(f32[3,8,640]{2,1,0:T(8,128)S(1)} %get-tuple-element.46), channel_id=1, source_target_pairs={{0,4},{1,5},{2,6},{3,7},{4,0},{5,1},{6,2},{7,3},{8,12},{9,13},{10,... | collective-permute-start | bytes 184328 | tf_op jit(solution)/shard_map/ppermute | solution.py:176
  33.1 1.2 %collective-permute-start.11 = (f32[8,512]{1,0:T(8,128)S(1)}, f32[8,512]{1,0:T(8,128)S(1)}, u32[]{:S(2)}, u32[]{:S(2)}) collective-permute-start(f32[8,512]{1,0:T(8,128)S(1)} %get-tuple-element.48), channel_id=1, source_target_pairs={{0,2},{1,3},{2,0},{3,1},{4,6},{5,7},{6,4},{7,5},{8,10},{9,11},{10,... | collective-permute-start | bytes 49160 | tf_op jit(solution)/shard_map/ppermute | solution.py:176
  34.3 3.7 %collective-permute-start.12 = (f32[2,4,512]{2,1,0:T(4,128)S(1)}, f32[2,4,512]{2,1,0:T(4,128)S(1)}, u32[]{:S(2)}, u32[]{:S(2)}) collective-permute-start(f32[2,4,512]{2,1,0:T(4,128)S(1)} %result_pack.1), channel_id=1, source_target_pairs={{0,1},{1,0},{2,3},{3,2},{4,5},{5,4},{6,7},{7,6},{8,9},{9,8},{10,11... | collective-permute-start | bytes 49160 | tf_op jit(solution)/shard_map/ppermute | solution.py:176

commit v8 on v7

--- a/solution.py
+++ b/solution.py
@@ -255,13 +255,27 @@
         out_ref[n] = total[:, :out_cols]
 
 
-def strip_loader(buf, half, parity, views, tiles):
+def depth_partner(z, bits):
+    return {0: z, 1: z + 1 - 2 * (z % 2), 2: (z + 2) % 4, 3: 3 - z}[bits]
+
+
+def slice_place(half, kept, n):
+    z, x, _, _ = coords()
+    parity = x if kept else 1 - x
+    four = depth_partner(z, (1, 0)[n // 4] if kept else (2, 3)[n // 4])
+    group = jnp.where(half == 0, n // 4, four // 2)
+    place = jnp.where(half == 0, 4 * (n // 2 % 2) + 2 * parity + n % 2, 4 * (four % 2) + n % 4)
+    return group, place
+
+
+def strip_loader(buf, half, kept, views, tiles):
     pitch = (tiles + 2) * SUB
 
     def load(n):
-        first = half * SUB + 4 * (n // 2 % 2) + 2 * parity + n % 2
+        group, place = slice_place(half, kept, n)
+        first = half * SUB + place
         return jnp.concatenate(
-            [buf[n // 4, pl.ds(first + t * SUB, views, stride=pitch), :] for t in range(tiles + 1)], axis=1
+            [buf[group, pl.ds(first + t * SUB, views, stride=pitch), :] for t in range(tiles + 1)], axis=1
         )
 
     return load
@@ -279,7 +293,7 @@
 
 def fetch_kernel(views, rows, band, scale, tan_hbm, drift_hbm, meas_hbm, vol_hbm, out_ref, sibling_buf, own_buf,
                  weights_ref, vol_ref, tan_ref, drift_ref, terms, table_sem, sem):
-    _, x, c, _ = coords()
+    _, _, c, _ = coords()
     tiles = out_ref.shape[2] // LANES
     groups = sibling_buf.shape[0]
 
@@ -306,14 +320,11 @@
         copy.wait()
     weights = view_weights(views, rows, band, scale, tan_ref, drift_ref)
     weights_ref[...] = weights.astype(jnp.float32)
-    load = strip_loader(flat_rows(sibling_buf), 1 - c, 1 - x, views, tiles)
-
-    def load_strip(n):
-        if n % 4 == 0:
-            first[n // 4].wait()
-        return load(n)
-
-    back_project(views, rows, band, weights, load_strip, out_ref, terms)
+    load = strip_loader(flat_rows(sibling_buf), 1 - c, False, views, tiles)
+
+    for copy in first:
+        copy.wait()
+    back_project(views, rows, band, weights, load, out_ref, terms)
     vol_copy.wait()
     for copy in later:
         copy.wait()
@@ -325,9 +336,9 @@
 
 
 def sibling_kernel(views, rows, band, buf, weights_ref, vol_ref, out_ref, terms, vbuf):
-    _, x, c, _ = coords()
+    _, _, c, _ = coords()
     tiles = out_ref.shape[2] // LANES
-    load = strip_loader(flat_rows(buf), 1 - c, x, views, tiles)
+    load = strip_loader(flat_rows(buf), 1 - c, True, views, tiles)
     back_project(views, rows, band, weights_ref[...].astype(jnp.bfloat16), load, out_ref, terms)
     count = terms.shape[0]
     half_cols = out_ref.shape[2] - LANES
@@ -337,47 +348,85 @@
 
 
 def own_kernel(kept, views, rows, band, buf, weights_ref, after_ref, out_ref, terms):
-    _, x, c, _ = coords()
+    _, _, c, _ = coords()
     tiles = out_ref.shape[2] // LANES
-    load = strip_loader(flat_rows(buf), c, x if kept else 1 - x, views, tiles)
+    load = strip_loader(flat_rows(buf), c, kept, views, tiles)
     back_project(views, rows, band, weights_ref[...].astype(jnp.bfloat16), load, out_ref, terms)
 
 
-def pass_pack_kernel(own_ref, got_ref, to_xy, acc):
-    width = to_xy.shape[2]
-    _, _, _, y = coords()
+def put_quarter(out, acc, py, tiles):
+    for n in range(acc.shape[0]):
+        for t in range(tiles):
+            out[n * tiles + t] = acc[n, :, pl.ds(pl.multiple_of(((tiles - 1) * py + t) * LANES, LANES), LANES)]
+
+
+def put_four(out, acc, first):
+    tiles = acc.shape[2] // LANES
+    for n in range(4):
+        for t in range(tiles):
+            out[n * tiles + t] = acc[first + n, :, t * LANES : (t + 1) * LANES]
+    for t in range(4 * tiles, out.shape[0]):
+        out[t] = jnp.zeros(out.shape[1:], jnp.float32)
+
+
+def pass_pack_kernel(own_ref, got_ref, send, acc):
+    _, _, c, y = coords()
     acc[...] = own_ref[...] + got_ref[...]
-    to_xy[...] = acc[:, :, pl.ds(pl.multiple_of((1 - y) * (width - LANES), LANES), width)]
-
-
-def keep_pack_kernel(pass_ref, pass_got, own_ref, got_ref, vol_ref, mine, to_x, to_y, vol_mine, vol_to_y, acc, both, vbuf):
+
+    @pl.when(c == 0)
+    def _():
+        put_quarter(send, acc, 1 - y, send.shape[0] // acc.shape[0])
+
+    @pl.when(c == 1)
+    def _():
+        put_four(send, acc, 0)
+
+
+def keep_pack_kernel(pass_ref, pass_got, own_ref, got_ref, vol_ref, mine, send_2, send_3, vol_mine, vol_to_y,
+                     passed, acc, both, vbuf):
     count, rows, half_width = own_ref.shape
-    width = mine.shape[2]
+    tiles = mine.shape[0] // count
     part = vol_ref.shape[1]
     _, _, c, y = coords()
+    passed[...] = pass_ref[...] + pass_got[...]
     acc[...] = own_ref[...] + got_ref[0:count]
+
+    @pl.when(c == 0)
+    def _():
+        put_quarter(send_2, passed, y, tiles)
+        put_quarter(send_3, acc, 1 - y, tiles)
+        put_quarter(mine, acc, y, tiles)
+
+    @pl.when(c == 1)
+    def _():
+        put_four(send_2, passed, 4)
+        put_four(send_3, acc, 0)
+        put_four(mine, acc, 4)
+
     here = volume_window(vol_ref, c, half_width - LANES, vbuf)
     there = got_ref[count, 0:part]
     both[0:part] = jnp.where(c == 0, here, there)
     both[part:] = jnp.where(c == 0, there, here)
-    window = pl.ds(pl.multiple_of(y * (width - LANES), LANES), width)
-    to_x[...] = pass_ref[:, :, window] + pass_got[:, :, window]
-    for out, vol, py in ((mine, vol_mine, y), (to_y, vol_to_y, 1 - y)):
-        begin = pl.multiple_of(py * (width - LANES), LANES)
-        out[...] = acc[:, :, pl.ds(begin, width)]
-        vol[...] = both[:, pl.ds(begin, width)]
-
-
-def depth_pack_kernel(mine, got_xy, got_x, got_y, own_pair, to_1, to_2, to_3, acc):
-    z, _, _, _ = coords()
-    acc[...] = (mine[...] + got_x[...]) + (got_y[...] + got_xy[...])
-    for out, pz in (
-        (own_pair, z),
-        (to_1, jnp.where(z % 2 == 0, z + 1, z - 1)),
-        (to_2, jnp.where(z < 2, z + 2, z - 2)),
-        (to_3, 3 - z),
-    ):
-        out[...] = acc[pl.ds(2 * pz, 2)]
+    width = tiles * LANES
+    for vol, py in ((vol_mine, y), (vol_to_y, 1 - y)):
+        vol[...] = both[:, pl.ds(pl.multiple_of(py * (width - LANES), LANES), width)]
+
+
+def middle_pack_kernel(mine, got_1, got_2, got_3, own_pair, send_1, send_2, send_3, acc):
+    z, x, c, y = coords()
+    tiles = own_pair.shape[2] // LANES
+    half_tiles = 2 * tiles - 1
+    acc[...] = (mine[...] + got_1[...]) + (got_2[...] + got_3[...])
+
+    def put(out, first, pitch):
+        for i in range(2):
+            for t in range(tiles):
+                out[i, :, t * LANES : (t + 1) * LANES] = acc[first + i * pitch + t]
+
+    for out, bits, px, py in ((own_pair, 0, x, y), (send_1, 1, 1 - x, 1 - y), (send_2, 3, 1 - x, y), (send_3, 2, x, 1 - y)):
+        depth_first = 2 * tiles * depth_partner(z, bits)
+        plane_first = 2 * half_tiles * px + (tiles - 1) * py
+        put(out, jnp.where(c == 0, depth_first, plane_first), jnp.where(c == 0, tiles, half_tiles))
 
 
 def gram_kernel(rows, band, scale, tan_ref, sec_ref, drift_ref, after_ref, conv_ref, low_ref, high_ref):
@@ -479,7 +528,7 @@
         out[i] = volumes[i] - work[i]
 
 
-def half_pair_kernel(first_ref, own_pair, got_1, got_3, got_2, mine, to_x, to_diag, corr):
+def half_pair_kernel(first_ref, own_pair, got_1, got_2, got_3, mine, to_x, to_diag, corr):
     _, x, _, _ = coords()
     corr[...] = (own_pair[...] + got_1[...]) + (got_2[...] + got_3[...])
     half = first_ref[...] + corr[...]
@@ -641,21 +690,21 @@
             flops=10**9,
         )(own_buf, weights, after)
 
-    message = f32(count, rows, width)
+    message = f32(count * width // LANES, rows, LANES)
     pass_own = own(False, keep_sibling)
-    to_xy = kernel_call(pass_pack_kernel, message, [VMEM_SPEC] * 2, [pltpu.VMEM(half_of.shape, jnp.float32)], "pass_pack")(
+    send_1 = kernel_call(pass_pack_kernel, message, [VMEM_SPEC] * 2, [pltpu.VMEM(half_of.shape, jnp.float32)], "pass_pack")(
         pass_own, pass_got
     )
-    got_xy = move(to_xy, lambda z, x, c, y: (z, 1 - x, c, 1 - y))
-    mine, to_x, to_y, vol_mine, vol_to_y = kernel_call(
+    got_1 = move(send_1, lambda z, x, c, y: (z ^ 2, x, c, y) if c else (z, 1 - x, c, 1 - y))
+    mine, send_2, send_3, vol_mine, vol_to_y = kernel_call(
         keep_pack_kernel,
         [message] * 3 + [f32(rows, width)] * 2,
         [VMEM_SPEC] * 5,
-        [pltpu.VMEM(half_of.shape, jnp.float32), pltpu.VMEM((rows, half_width), jnp.float32), vbuf],
+        [pltpu.VMEM(half_of.shape, jnp.float32)] * 2 + [pltpu.VMEM((rows, half_width), jnp.float32), vbuf],
         "keep_pack",
-    )(pass_own, pass_got, own(True, to_xy), keep_got, volume)
-    got_x = move(to_x, lambda z, x, c, y: (z, 1 - x, c, y))
-    got_y = move(to_y, lambda z, x, c, y: (z, x, c, 1 - y))
+    )(pass_own, pass_got, own(True, send_1), keep_got, volume)
+    got_2 = move(send_2, lambda z, x, c, y: (z ^ 3, x, c, y) if c else (z, 1 - x, c, y))
+    got_3 = move(send_3, lambda z, x, c, y: (z ^ 1, x, c, y) if c else (z, x, c, 1 - y))
     vol_got = move(vol_to_y, lambda z, x, c, y: (z, x, c, 1 - y))
 
     edge = band * rows
@@ -668,16 +717,16 @@
     )(tangent[None], secant[None], drift[None], mine)
 
     pair = f32(2, rows, width)
-    own_pair, to_1, to_2, to_3 = kernel_call(
-        depth_pack_kernel,
+    own_pair, send_1, send_2, send_3 = kernel_call(
+        middle_pack_kernel,
         [pair] * 4,
         [VMEM_SPEC] * 4,
-        [pltpu.VMEM((count, rows, width), jnp.float32)],
-        "depth_pack",
-    )(mine, got_xy, got_x, got_y)
-    got_2 = move(to_2, lambda z, x, c, y: (z ^ 2, x, c, y))
-    got_1 = move(to_1, lambda z, x, c, y: (z ^ 1, x, c, y))
-    got_3 = move(to_3, lambda z, x, c, y: (z ^ 3, x, c, y))
+        [pltpu.VMEM(message.shape, jnp.float32)],
+        "middle_pack",
+    )(mine, got_1, got_2, got_3)
+    got_1 = move(send_1, lambda z, x, c, y: (z, 1 - x, c, 1 - y) if c else (z ^ 1, x, c, y))
+    got_2 = move(send_2, lambda z, x, c, y: (z, 1 - x, c, y) if c else (z ^ 3, x, c, y))
+    got_3 = move(send_3, lambda z, x, c, y: (z, x, c, 1 - y) if c else (z ^ 2, x, c, y))
 
     first = kernel_call(
         functools.partial(first_normal_kernel, band, cols),
@@ -695,7 +744,7 @@
         [VMEM_SPEC] * 5,
         [pltpu.VMEM((2, rows, width), jnp.float32)],
         "half_pair",
-    )(first, own_pair, got_1, got_3, got_2)
+    )(first, own_pair, got_1, got_2, got_3)
     got_diag = move(to_diag, beside)
     got_x = move(to_x, lambda z, x, c, y: (z, 1 - x, c, y))
 

time: 38.9 us -> 37.8 us (0.972)
  starting transfers between devices: 14.7 us -> 13.7 us
    ppermute x13, starting transfers between devices: 14.7 us -> 13.7 us  [move(): return lax.ppermute(value, ('wide', 'grp'), pairs)]
where the time goes in v8:
time: 37.8 us; the launch traced here: 37.6 us
  waiting for transfers between devices  14.3 us (38%)
  starting transfers between devices  13.7 us (36%)
  Pallas kernels  9.44 us (25%)
    ppermute x13, waiting for transfers between devices, move(): return lax.ppermute(value, ('wide', 'grp'), pairs)  14.3 us
    ppermute x13, starting transfers between devices, move(): return lax.ppermute(value, ('wide', 'grp'), pairs)  13.7 us
    pallas_call x1, Pallas kernels, summed_plan(): kernel_call(functools.partial(fetch_kernel, views, rows, band, scale), [h...  2.4 us
    pallas_call x2, Pallas kernels, own(): kernel_call(functools.partial(own_kernel, kept, views, rows, band), half_...  2.13 us
    pallas_call x1, Pallas kernels, summed_plan(): kernel_call(functools.partial(finish_kernel, band, slices, cols), [quarte...  1.46 us
    pallas_call x1, Pallas kernels, summed_plan(): kernel_call(functools.partial(sibling_kernel, views, rows, band), half_an...  1.08 us
  transfers between devices with their start and end apart: 13, of which 7 were waited for; matrix products, arithmetic and copies ran while one was open for 0% of the time, Pallas kernels for 13%

profile of v8, /device:TPU:0, one launch (start us, length us, event | category | flops | bytes accessed | tf_op | source)
XLA Modules:
  0.0 37.6 jit_solution(5528107709278778206)
XLA Ops:
  0.0 2.4 %pass_sibling.1 = (f32[8,8,1152]{2,1,0:T(8,128)S(1)}, f32[2,16,11,8,128]{4,3,2,1,0:T(8,128)S(1)}, f32[2,16,11,8,128]{4,3,2,1,0:T(8,128)S(1)}, f32[56,144]{1,0:T(8,128)S(1)}, f32[1,4,2048]{2,1,0:T(4,128)S(1)}) custom-call(f32[512]{0:T(512)} %constant.6.clone.tan_hbm, s32[512]{0:T(512)} %drift_hbm.1, f32[16,2,16,8,128]{4,3,2,1,0:T(8,128)} %bitcast.5, ...), custom_call_target="tpu_custom_call" | custom-call | flops 1000000000 | tf_op jit(solution)/shard_map/pass_sibling/pallas_call | solution.py:658
  2.4 0.5 %collective-permute-start = (f32[8,8,1152]{2,1,0:T(8,128)S(1)}, f32[8,8,1152]{2,1,0:T(8,128)S(1)}, u32[]{:S(2)}, u32[]{:S(2)}) collective-permute-start(f32[8,8,1152]{2,1,0:T(8,128)S(1)} %get-tuple-element.31), channel_id=1, source_target_pairs={{0,2},{1,3},{2,0},{3,1},{4,6},{5,7},{6,4},{7,5},{8,10},{9,11},{10,... | collective-permute-start | bytes 884744 | tf_op jit(solution)/shard_map/ppermute | solution.py:176
  2.9 1.1 %keep_sibling.1.after_ref = f32[9,8,1152]{2,1,0:T(8,128)S(1)} custom-call(f32[2,16,11,8,128]{4,3,2,1,0:T(8,128)S(1)} %get-tuple-element.29.buf, f32[56,144]{1,0:T(8,128)S(1)} %get-tuple-element.28.weights_ref, f32[1,4,2048]{2,1,0:T(4,128)S(1)} %get-tuple-element.30.vol_ref), custom_call_target="tpu_custom_call" | custom-call | flops 1000000000 | tf_op jit(solution)/shard_map/keep_sibling/pallas_call | solution.py:673
  4.0 0.1 collective-permute-start.1
  4.1 1.1 %pass_own.1.own_ref.pass_ref = f32[8,8,1152]{2,1,0:T(8,128)S(1)} custom-call(f32[2,16,11,8,128]{4,3,2,1,0:T(8,128)S(1)} %get-tuple-element.27.buf, f32[56,144]{1,0:T(8,128)S(1)} %get-tuple-element.28.weights_ref, f32[9,8,1152]{2,1,0:T(8,128)S(1)} %keep_sibling.1.after_ref), custom_call_target="tpu_custom_call" | custom-call | flops 1000000000 | tf_op jit(solution)/shard_map/pass_own/pallas_call | solution.py:684
  5.2 0.0 collective-permute-done.got_ref.pass_got
  5.2 0.1 pass_pack.1.after_ref
  5.3 0.0 copy-start
  5.3 0.0 copy-start.1
  5.3 0.0 copy-start.2
  5.3 4.0 %collective-permute-start.3 = (f32[40,8,128]{2,1,0:T(8,128)S(1)}, f32[40,8,128]{2,1,0:T(8,128)S(1)}, u32[]{:S(2)}, u32[]{:S(2)}) collective-permute-start(f32[40,8,128]{2,1,0:T(8,128)S(1)} %pass_pack.1.after_ref), channel_id=1, source_target_pairs={{0,5},{1,4},{2,18},{3,19},{4,1},{5,0},{6,22},{7,23},{8,13},{9,12},... | collective-permute-start | bytes 491528 | tf_op jit(solution)/shard_map/ppermute | solution.py:176
  9.3 1.1 %keep_own.1.own_ref = f32[8,8,1152]{2,1,0:T(8,128)S(1)} custom-call(f32[2,16,11,8,128]{4,3,2,1,0:T(8,128)S(1)} %get-tuple-element.27.buf, f32[56,144]{1,0:T(8,128)S(1)} %get-tuple-element.28.weights_ref, f32[40,8,128]{2,1,0:T(8,128)S(1)} %pass_pack.1.after_ref), custom_call_target="tpu_custom_call" | custom-call | flops 1000000000 | tf_op jit(solution)/shard_map/keep_own/pallas_call | solution.py:684
  10.3 0.0 collective-permute-done.1.got_ref
  10.4 0.2 keep_pack.1
  10.6 0.6 %collective-permute-start.4 = (f32[40,8,128]{2,1,0:T(8,128)S(1)}, f32[40,8,128]{2,1,0:T(8,128)S(1)}, u32[]{:S(2)}, u32[]{:S(2)}) collective-permute-start(f32[40,8,128]{2,1,0:T(8,128)S(1)} %get-tuple-element.38), channel_id=1, source_target_pairs={{0,4},{1,5},{2,26},{3,27},{4,0},{5,1},{6,30},{7,31},{8,12},{9,13},... | collective-permute-start | bytes 491528 | tf_op jit(solution)/shard_map/ppermute | solution.py:176
  11.2 0.1 collective-permute-start.5
  11.2 2.0 %collective-permute-start.2 = (f32[8,640]{1,0:T(8,128)S(1)}, f32[8,640]{1,0:T(8,128)S(1)}, u32[]{:S(2)}, u32[]{:S(2)}) collective-permute-start(f32[8,640]{1,0:T(8,128)S(1)} %get-tuple-element.33), channel_id=1, source_target_pairs={{0,1},{1,0},{2,3},{3,2},{4,5},{5,4},{6,7},{7,6},{8,9},{9,8},{10,11... | collective-permute-start | bytes 61448 | tf_op jit(solution)/shard_map/ppermute | solution.py:176
  13.2 0.0 copy-done
  13.2 0.0 copy-done.1
  13.2 0.0 copy-done.2
  13.2 0.7 %gram.1 = (f32[48,256]{1,0:T(8,128)S(1)}, f32[80,240]{1,0:T(8,128)S(1)}, f32[80,240]{1,0:T(8,128)S(1)}) custom-call(f32[1,512]{1,0:T(1,128)S(1)} %copy-done.2, f32[1,512]{1,0:T(1,128)S(1)} %copy-done.1, s32[1,512]{1,0:T(1,128)S(1)} %bitcast.4, f32[40,8,128]{2,1,0:T(8,128)S(1)} %get-tuple-element.34.after_ref.mine), custom_call_target="tpu_custom_call" | custom-call | tf_op jit(solution)/shard_map/gram/pallas_call | solution.py:711
  13.9 0.0 collective-permute-done.3.got_1
  13.9 2.0 %collective-permute-done.4.got_2 = f32[40,8,128]{2,1,0:T(8,128)S(1)} collective-permute-done((f32[40,8,128]{2,1,0:T(8,128)S(1)}, f32[40,8,128]{2,1,0:T(8,128)S(1)}, u32[]{:S(2)}, u32[]{:S(2)}) %collective-permute-start.4) | collective-permute-done | bytes 163872 | tf_op jit(solution)/shard_map/ppermute | solution.py:176
  15.9 0.5 %collective-permute-done.5.got_3 = f32[40,8,128]{2,1,0:T(8,128)S(1)} collective-permute-done((f32[40,8,128]{2,1,0:T(8,128)S(1)}, f32[40,8,128]{2,1,0:T(8,128)S(1)}, u32[]{:S(2)}, u32[]{:S(2)}) %collective-permute-start.5) | collective-permute-done | bytes 163872 | tf_op jit(solution)/shard_map/ppermute | solution.py:176
  16.5 0.1 middle_pack.1
  16.5 1.6 %collective-permute-start.6 = (f32[2,8,640]{2,1,0:T(8,128)S(1)}, f32[2,8,640]{2,1,0:T(8,128)S(1)}, u32[]{:S(2)}, u32[]{:S(2)}) collective-permute-start(f32[2,8,640]{2,1,0:T(8,128)S(1)} %get-tuple-element.41), channel_id=1, source_target_pairs={{0,8},{1,9},{2,7},{3,6},{4,12},{5,13},{6,3},{7,2},{8,0},{9,1},{10,... | collective-permute-start | bytes 122888 | tf_op jit(solution)/shard_map/ppermute | solution.py:176
  18.2 2.5 %collective-permute-start.7 = (f32[2,8,640]{2,1,0:T(8,128)S(1)}, f32[2,8,640]{2,1,0:T(8,128)S(1)}, u32[]{:S(2)}, u32[]{:S(2)}) collective-permute-start(f32[2,8,640]{2,1,0:T(8,128)S(1)} %get-tuple-element.42), channel_id=1, source_target_pairs={{0,24},{1,25},{2,6},{3,7},{4,28},{5,29},{6,2},{7,3},{8,16},{9,17},... | collective-permute-start | bytes 122888 | tf_op jit(solution)/shard_map/ppermute | solution.py:176
  20.7 0.1 collective-permute-start.8
  20.8 0.0 collective-permute-done.2.vol_got
  20.8 0.7 %first_normal.1.first_ref = f32[2,8,640]{2,1,0:T(8,128)S(1)} custom-call(f32[8,640]{1,0:T(8,128)S(1)} %get-tuple-element.32.vol_mine, f32[8,640]{1,0:T(8,128)S(1)} %collective-permute-done.2.vol_got, f32[48,256]{1,0:T(8,128)S(1)} %get-tuple-element.35.conv_ref, f32[80,240]{1,0:T(8,128)S(1)} %get-tuple-element.36.low_ref, ...), custom_call_target="tpu_custom_call" | custom-call | flops 1000000000 | tf_op jit(solution)/shard_map/first_normal/pallas_call | solution.py:731
  21.5 0.0 collective-permute-done.6.got_1
  21.5 2.5 %collective-permute-done.7.got_2 = f32[2,8,640]{2,1,0:T(8,128)S(1)} collective-permute-done((f32[2,8,640]{2,1,0:T(8,128)S(1)}, f32[2,8,640]{2,1,0:T(8,128)S(1)}, u32[]{:S(2)}, u32[]{:S(2)}) %collective-permute-start.7) | collective-permute-done | bytes 40992 | tf_op jit(solution)/shard_map/ppermute | solution.py:176
  24.0 2.0 %collective-permute-done.8.got_3 = f32[2,8,640]{2,1,0:T(8,128)S(1)} collective-permute-done((f32[2,8,640]{2,1,0:T(8,128)S(1)}, f32[2,8,640]{2,1,0:T(8,128)S(1)}, u32[]{:S(2)}, u32[]{:S(2)}) %collective-permute-start.8) | collective-permute-done | bytes 40992 | tf_op jit(solution)/shard_map/ppermute | solution.py:176
  26.0 0.1 collective-permute-start.9
  26.1 1.8 %collective-permute-start.10 = (f32[3,8,640]{2,1,0:T(8,128)S(1)}, f32[3,8,640]{2,1,0:T(8,128)S(1)}, u32[]{:S(2)}, u32[]{:S(2)}) collective-permute-start(f32[3,8,640]{2,1,0:T(8,128)S(1)} %get-tuple-element.46), channel_id=1, source_target_pairs={{0,4},{1,5},{2,6},{3,7},{4,0},{5,1},{6,2},{7,3},{8,12},{9,13},{10,... | collective-permute-start | bytes 184328 | tf_op jit(solution)/shard_map/ppermute | solution.py:176
  27.9 0.0 collective-permute-done.9.got_diag
  27.9 2.6 %collective-permute-done.10.got_x = f32[3,8,640]{2,1,0:T(8,128)S(1)} collective-permute-done((f32[3,8,640]{2,1,0:T(8,128)S(1)}, f32[3,8,640]{2,1,0:T(8,128)S(1)}, u32[]{:S(2)}, u32[]{:S(2)}) %collective-permute-start.10) | collective-permute-done | bytes 61472 | tf_op jit(solution)/shard_map/ppermute | solution.py:176
  30.5 1.5 %finish.1 = (f32[8,512]{1,0:T(8,128)S(1)}, f32[8,512]{1,0:T(8,128)S(1)}) custom-call(f32[4,8,640]{2,1,0:T(8,128)S(1)} %get-tuple-element.44.mine, f32[3,8,640]{2,1,0:T(8,128)S(1)} %collective-permute-done.9.got_diag, f32[3,8,640]{2,1,0:T(8,128)S(1)} %collective-permute-done.10.got_x, f32[48,256]{1,0:T(8,128)S(1)} %get-tuple-element.35.conv_ref, ...), custom_call_target="tpu_custom_call" | custom-call | tf_op jit(solution)/shard_map/finish/pallas_call | solution.py:753
  32.0 0.1 collective-permute-start.11
  32.1 1.2 %collective-permute-done.11.got_ref = f32[8,512]{1,0:T(8,128)S(1)} collective-permute-done((f32[8,512]{1,0:T(8,128)S(1)}, f32[8,512]{1,0:T(8,128)S(1)}, u32[]{:S(2)}, u32[]{:S(2)}) %collective-permute-start.11) | collective-permute-done | bytes 16416 | tf_op jit(solution)/shard_map/ppermute | solution.py:176
  33.2 0.3 collective-permute-start.12
  33.5 3.5 %collective-permute-done.12.got_y = f32[2,4,512]{2,1,0:T(4,128)S(1)} collective-permute-done((f32[2,4,512]{2,1,0:T(4,128)S(1)}, f32[2,4,512]{2,1,0:T(4,128)S(1)}, u32[]{:S(2)}, u32[]{:S(2)}) %collective-permute-start.12) | collective-permute-done | bytes 16416 | tf_op jit(solution)/shard_map/ppermute | solution.py:176
  37.0 0.6 %result.1 = f32[1,4,2048]{2,1,0:T(4,128)} custom-call(f32[8,512]{1,0:T(8,128)S(1)} %get-tuple-element.47.own_ref, f32[8,512]{1,0:T(8,128)S(1)} %collective-permute-done.11.got_ref, f32[2,4,512]{2,1,0:T(4,128)S(1)} %collective-permute-done.12.got_y), custom_call_target="tpu_custom_call" | custom-call | tf_op jit(solution)/shard_map/result/pallas_call | solution.py:763
  (2 shorter events, 0.0 us)
Async XLA Ops:
  2.4 2.8 %collective-permute-start = (f32[8,8,1152]{2,1,0:T(8,128)S(1)}, f32[8,8,1152]{2,1,0:T(8,128)S(1)}, u32[]{:S(2)}, u32[]{:S(2)}) collective-permute-start(f32[8,8,1152]{2,1,0:T(8,128)S(1)} %get-tuple-element.31), channel_id=1, source_target_pairs={{0,2},{1,3},{2,0},{3,1},{4,6},{5,7},{6,4},{7,5},{8,10},{9,11},{10,... | collective-permute-start | bytes 884744 | tf_op jit(solution)/shard_map/ppermute | solution.py:176
  4.0 6.3 %collective-permute-start.1 = (f32[9,8,1152]{2,1,0:T(8,128)S(1)}, f32[9,8,1152]{2,1,0:T(8,128)S(1)}, u32[]{:S(2)}, u32[]{:S(2)}) collective-permute-start(f32[9,8,1152]{2,1,0:T(8,128)S(1)} %keep_sibling.1.after_ref), channel_id=1, source_target_pairs={{0,2},{1,3},{2,0},{3,1},{4,6},{5,7},{6,4},{7,5},{8,10},{9,11},{10,... | collective-permute-start | bytes 995336 | tf_op jit(solution)/shard_map/ppermute | solution.py:176
  5.3 7.9 %copy-start = (s32[512]{0:T(512)S(1)}, s32[512]{0:T(512)}, u32[]{:S(2)}) copy-start(s32[512]{0:T(512)} %drift_hbm.1) | copy-start | bytes 6148
  5.3 7.9 %copy-start.1 = (f32[1,512]{1,0:T(1,128)S(1)}, f32[1,512]{1,0:T(1,128)}, u32[]{:S(2)}) copy-start(f32[1,512]{1,0:T(1,128)} %constant.8.clone.sec_ref) | copy-start | bytes 6148
  5.3 7.9 %copy-start.2 = (f32[1,512]{1,0:T(1,128)S(1)}, f32[1,512]{1,0:T(1,128)}, u32[]{:S(2)}) copy-start(f32[1,512]{1,0:T(1,128)} %constant.7.clone.tan_ref) | copy-start | bytes 6148
  5.3 8.6 %collective-permute-start.3 = (f32[40,8,128]{2,1,0:T(8,128)S(1)}, f32[40,8,128]{2,1,0:T(8,128)S(1)}, u32[]{:S(2)}, u32[]{:S(2)}) collective-permute-start(f32[40,8,128]{2,1,0:T(8,128)S(1)} %pass_pack.1.after_ref), channel_id=1, source_target_pairs={{0,5},{1,4},{2,18},{3,19},{4,1},{5,0},{6,22},{7,23},{8,13},{9,12},... | collective-permute-start | bytes 491528 | tf_op jit(solution)/shard_map/ppermute | solution.py:176
  10.6 5.4 %collective-permute-start.4 = (f32[40,8,128]{2,1,0:T(8,128)S(1)}, f32[40,8,128]{2,1,0:T(8,128)S(1)}, u32[]{:S(2)}, u32[]{:S(2)}) collective-permute-start(f32[40,8,128]{2,1,0:T(8,128)S(1)} %get-tuple-element.38), channel_id=1, source_target_pairs={{0,4},{1,5},{2,26},{3,27},{4,0},{5,1},{6,30},{7,31},{8,12},{9,13},... | collective-permute-start | bytes 491528 | tf_op jit(solution)/shard_map/ppermute | solution.py:176
  11.2 5.3 %collective-permute-start.5 = (f32[40,8,128]{2,1,0:T(8,128)S(1)}, f32[40,8,128]{2,1,0:T(8,128)S(1)}, u32[]{:S(2)}, u32[]{:S(2)}) collective-permute-start(f32[40,8,128]{2,1,0:T(8,128)S(1)} %get-tuple-element.39), channel_id=1, source_target_pairs={{0,1},{1,0},{2,10},{3,11},{4,5},{5,4},{6,14},{7,15},{8,9},{9,8},{1... | collective-permute-start | bytes 491528 | tf_op jit(solution)/shard_map/ppermute | solution.py:176
  11.2 9.5 %collective-permute-start.2 = (f32[8,640]{1,0:T(8,128)S(1)}, f32[8,640]{1,0:T(8,128)S(1)}, u32[]{:S(2)}, u32[]{:S(2)}) collective-permute-start(f32[8,640]{1,0:T(8,128)S(1)} %get-tuple-element.33), channel_id=1, source_target_pairs={{0,1},{1,0},{2,3},{3,2},{4,5},{5,4},{6,7},{7,6},{8,9},{9,8},{10,11... | collective-permute-start | bytes 61448 | tf_op jit(solution)/shard_map/ppermute | solution.py:176
  16.5 5.0 %collective-permute-start.6 = (f32[2,8,640]{2,1,0:T(8,128)S(1)}, f32[2,8,640]{2,1,0:T(8,128)S(1)}, u32[]{:S(2)}, u32[]{:S(2)}) collective-permute-start(f32[2,8,640]{2,1,0:T(8,128)S(1)} %get-tuple-element.41), channel_id=1, source_target_pairs={{0,8},{1,9},{2,7},{3,6},{4,12},{5,13},{6,3},{7,2},{8,0},{9,1},{10,... | collective-permute-start | bytes 122888 | tf_op jit(solution)/shard_map/ppermute | solution.py:176
  18.2 5.8 %collective-permute-start.7 = (f32[2,8,640]{2,1,0:T(8,128)S(1)}, f32[2,8,640]{2,1,0:T(8,128)S(1)}, u32[]{:S(2)}, u32[]{:S(2)}) collective-permute-start(f32[2,8,640]{2,1,0:T(8,128)S(1)} %get-tuple-element.42), channel_id=1, source_target_pairs={{0,24},{1,25},{2,6},{3,7},{4,28},{5,29},{6,2},{7,3},{8,16},{9,17},... | collective-permute-start | bytes 122888 | tf_op jit(solution)/shard_map/ppermute | solution.py:176
  20.7 5.3 %collective-permute-start.8 = (f32[2,8,640]{2,1,0:T(8,128)S(1)}, f32[2,8,640]{2,1,0:T(8,128)S(1)}, u32[]{:S(2)}, u32[]{:S(2)}) collective-permute-start(f32[2,8,640]{2,1,0:T(8,128)S(1)} %get-tuple-element.43), channel_id=1, source_target_pairs={{0,16},{1,17},{2,3},{3,2},{4,20},{5,21},{6,7},{7,6},{8,24},{9,25},... | collective-permute-start | bytes 122888 | tf_op jit(solution)/shard_map/ppermute | solution.py:176
  26.0 1.9 %collective-permute-start.9 = (f32[3,8,640]{2,1,0:T(8,128)S(1)}, f32[3,8,640]{2,1,0:T(8,128)S(1)}, u32[]{:S(2)}, u32[]{:S(2)}) collective-permute-start(f32[3,8,640]{2,1,0:T(8,128)S(1)} %get-tuple-element.45), channel_id=1, source_target_pairs={{0,2},{1,3},{2,0},{3,1},{4,8},{5,9},{6,10},{7,11},{8,4},{9,5},{10,... | collective-permute-start | bytes 184328 | tf_op jit(solution)/shard_map/ppermute | solution.py:176
  26.1 4.4 %collective-permute-start.10 = (f32[3,8,640]{2,1,0:T(8,128)S(1)}, f32[3,8,640]{2,1,0:T(8,128)S(1)}, u32[]{:S(2)}, u32[]{:S(2)}) collective-permute-start(f32[3,8,640]{2,1,0:T(8,128)S(1)} %get-tuple-element.46), channel_id=1, source_target_pairs={{0,4},{1,5},{2,6},{3,7},{4,0},{5,1},{6,2},{7,3},{8,12},{9,13},{10,... | collective-permute-start | bytes 184328 | tf_op jit(solution)/shard_map/ppermute | solution.py:176
  32.0 1.2 %collective-permute-start.11 = (f32[8,512]{1,0:T(8,128)S(1)}, f32[8,512]{1,0:T(8,128)S(1)}, u32[]{:S(2)}, u32[]{:S(2)}) collective-permute-start(f32[8,512]{1,0:T(8,128)S(1)} %get-tuple-element.48), channel_id=1, source_target_pairs={{0,2},{1,3},{2,0},{3,1},{4,6},{5,7},{6,4},{7,5},{8,10},{9,11},{10,... | collective-permute-start | bytes 49160 | tf_op jit(solution)/shard_map/ppermute | solution.py:176
  33.2 3.7 %collective-permute-start.12 = (f32[2,4,512]{2,1,0:T(4,128)S(1)}, f32[2,4,512]{2,1,0:T(4,128)S(1)}, u32[]{:S(2)}, u32[]{:S(2)}) collective-permute-start(f32[2,4,512]{2,1,0:T(4,128)S(1)} %result_pack.1), channel_id=1, source_target_pairs={{0,1},{1,0},{2,3},{3,2},{4,5},{5,4},{6,7},{7,6},{8,9},{9,8},{10,11... | collective-permute-start | bytes 49160 | tf_op jit(solution)/shard_map/ppermute | solution.py:176

commit v9 on v8

--- a/solution.py
+++ b/solution.py
@@ -423,7 +423,7 @@
             for t in range(tiles):
                 out[i, :, t * LANES : (t + 1) * LANES] = acc[first + i * pitch + t]
 
-    for out, bits, px, py in ((own_pair, 0, x, y), (send_1, 1, 1 - x, 1 - y), (send_2, 3, 1 - x, y), (send_3, 2, x, 1 - y)):
+    for out, bits, px, py in ((own_pair, 0, x, y), (send_1, 3, 1 - x, 1 - y), (send_2, 2, 1 - x, y), (send_3, 1, x, 1 - y)):
         depth_first = 2 * tiles * depth_partner(z, bits)
         plane_first = 2 * half_tiles * px + (tiles - 1) * py
         put(out, jnp.where(c == 0, depth_first, plane_first), jnp.where(c == 0, tiles, half_tiles))
@@ -724,9 +724,9 @@
         [pltpu.VMEM(message.shape, jnp.float32)],
         "middle_pack",
     )(mine, got_1, got_2, got_3)
-    got_1 = move(send_1, lambda z, x, c, y: (z, 1 - x, c, 1 - y) if c else (z ^ 1, x, c, y))
-    got_2 = move(send_2, lambda z, x, c, y: (z, 1 - x, c, y) if c else (z ^ 3, x, c, y))
-    got_3 = move(send_3, lambda z, x, c, y: (z, x, c, 1 - y) if c else (z ^ 2, x, c, y))
+    got_1 = move(send_1, lambda z, x, c, y: (z, 1 - x, c, 1 - y) if c else (z ^ 3, x, c, y))
+    got_2 = move(send_2, lambda z, x, c, y: (z, 1 - x, c, y) if c else (z ^ 2, x, c, y))
+    got_3 = move(send_3, lambda z, x, c, y: (z, x, c, 1 - y) if c else (z ^ 1, x, c, y))
 
     first = kernel_call(
         functools.partial(first_normal_kernel, band, cols),

time: 37.8 us -> 36.9 us (0.976)
  waiting for transfers between devices: 14.3 us -> 13.6 us
    ppermute x13, waiting for transfers between devices: 14.3 us -> 13.6 us  [move(): return lax.ppermute(value, ('wide', 'grp'), pairs)]
where the time goes in v9:
time: 36.9 us; the launch traced here: 36.7 us
  waiting for transfers between devices  13.6 us (37%)
  starting transfers between devices  13.5 us (37%)
  Pallas kernels  9.44 us (26%)
    ppermute x13, waiting for transfers between devices, move(): return lax.ppermute(value, ('wide', 'grp'), pairs)  13.6 us
    ppermute x13, starting transfers between devices, move(): return lax.ppermute(value, ('wide', 'grp'), pairs)  13.5 us
    pallas_call x1, Pallas kernels, summed_plan(): kernel_call(functools.partial(fetch_kernel, views, rows, band, scale), [h...  2.4 us
    pallas_call x2, Pallas kernels, own(): kernel_call(functools.partial(own_kernel, kept, views, rows, band), half_...  2.13 us
    pallas_call x1, Pallas kernels, summed_plan(): kernel_call(functools.partial(finish_kernel, band, slices, cols), [quarte...  1.46 us
    pallas_call x1, Pallas kernels, summed_plan(): kernel_call(functools.partial(sibling_kernel, views, rows, band), half_an...  1.08 us
  transfers between devices with their start and end apart: 13, of which 7 were waited for; matrix products, arithmetic and copies ran while one was open for 0% of the time, Pallas kernels for 13%

profile of v9, /device:TPU:0, one launch (start us, length us, event | category | flops | bytes accessed | tf_op | source)
XLA Modules:
  0.0 36.7 jit_solution(4924519200248959448)
XLA Ops:
  0.0 2.4 %pass_sibling.1 = (f32[8,8,1152]{2,1,0:T(8,128)S(1)}, f32[2,16,11,8,128]{4,3,2,1,0:T(8,128)S(1)}, f32[2,16,11,8,128]{4,3,2,1,0:T(8,128)S(1)}, f32[56,144]{1,0:T(8,128)S(1)}, f32[1,4,2048]{2,1,0:T(4,128)S(1)}) custom-call(f32[512]{0:T(512)} %constant.6.clone.tan_hbm, s32[512]{0:T(512)} %drift_hbm.1, f32[16,2,16,8,128]{4,3,2,1,0:T(8,128)} %bitcast.5, ...), custom_call_target="tpu_custom_call" | custom-call | flops 1000000000 | tf_op jit(solution)/shard_map/pass_sibling/pallas_call | solution.py:658
  2.4 0.5 %collective-permute-start = (f32[8,8,1152]{2,1,0:T(8,128)S(1)}, f32[8,8,1152]{2,1,0:T(8,128)S(1)}, u32[]{:S(2)}, u32[]{:S(2)}) collective-permute-start(f32[8,8,1152]{2,1,0:T(8,128)S(1)} %get-tuple-element.31), channel_id=1, source_target_pairs={{0,2},{1,3},{2,0},{3,1},{4,6},{5,7},{6,4},{7,5},{8,10},{9,11},{10,... | collective-permute-start | bytes 884744 | tf_op jit(solution)/shard_map/ppermute | solution.py:176
  2.9 1.1 %keep_sibling.1.after_ref = f32[9,8,1152]{2,1,0:T(8,128)S(1)} custom-call(f32[2,16,11,8,128]{4,3,2,1,0:T(8,128)S(1)} %get-tuple-element.29.buf, f32[56,144]{1,0:T(8,128)S(1)} %get-tuple-element.28.weights_ref, f32[1,4,2048]{2,1,0:T(4,128)S(1)} %get-tuple-element.30.vol_ref), custom_call_target="tpu_custom_call" | custom-call | flops 1000000000 | tf_op jit(solution)/shard_map/keep_sibling/pallas_call | solution.py:673
  4.0 0.1 collective-permute-start.1
  4.1 1.1 %pass_own.1.own_ref.pass_ref = f32[8,8,1152]{2,1,0:T(8,128)S(1)} custom-call(f32[2,16,11,8,128]{4,3,2,1,0:T(8,128)S(1)} %get-tuple-element.27.buf, f32[56,144]{1,0:T(8,128)S(1)} %get-tuple-element.28.weights_ref, f32[9,8,1152]{2,1,0:T(8,128)S(1)} %keep_sibling.1.after_ref), custom_call_target="tpu_custom_call" | custom-call | flops 1000000000 | tf_op jit(solution)/shard_map/pass_own/pallas_call | solution.py:684
  5.2 0.0 collective-permute-done.got_ref.pass_got
  5.2 0.1 pass_pack.1.after_ref
  5.3 0.0 copy-start
  5.3 0.0 copy-start.1
  5.3 0.0 copy-start.2
  5.3 4.0 %collective-permute-start.3 = (f32[40,8,128]{2,1,0:T(8,128)S(1)}, f32[40,8,128]{2,1,0:T(8,128)S(1)}, u32[]{:S(2)}, u32[]{:S(2)}) collective-permute-start(f32[40,8,128]{2,1,0:T(8,128)S(1)} %pass_pack.1.after_ref), channel_id=1, source_target_pairs={{0,5},{1,4},{2,18},{3,19},{4,1},{5,0},{6,22},{7,23},{8,13},{9,12},... | collective-permute-start | bytes 491528 | tf_op jit(solution)/shard_map/ppermute | solution.py:176
  9.3 1.1 %keep_own.1.own_ref = f32[8,8,1152]{2,1,0:T(8,128)S(1)} custom-call(f32[2,16,11,8,128]{4,3,2,1,0:T(8,128)S(1)} %get-tuple-element.27.buf, f32[56,144]{1,0:T(8,128)S(1)} %get-tuple-element.28.weights_ref, f32[40,8,128]{2,1,0:T(8,128)S(1)} %pass_pack.1.after_ref), custom_call_target="tpu_custom_call" | custom-call | flops 1000000000 | tf_op jit(solution)/shard_map/keep_own/pallas_call | solution.py:684
  10.3 0.0 collective-permute-done.1.got_ref
  10.4 0.2 keep_pack.1
  10.6 0.6 %collective-permute-start.4 = (f32[40,8,128]{2,1,0:T(8,128)S(1)}, f32[40,8,128]{2,1,0:T(8,128)S(1)}, u32[]{:S(2)}, u32[]{:S(2)}) collective-permute-start(f32[40,8,128]{2,1,0:T(8,128)S(1)} %get-tuple-element.38), channel_id=1, source_target_pairs={{0,4},{1,5},{2,26},{3,27},{4,0},{5,1},{6,30},{7,31},{8,12},{9,13},... | collective-permute-start | bytes 491528 | tf_op jit(solution)/shard_map/ppermute | solution.py:176
  11.2 0.1 collective-permute-start.5
  11.2 2.0 %collective-permute-start.2 = (f32[8,640]{1,0:T(8,128)S(1)}, f32[8,640]{1,0:T(8,128)S(1)}, u32[]{:S(2)}, u32[]{:S(2)}) collective-permute-start(f32[8,640]{1,0:T(8,128)S(1)} %get-tuple-element.33), channel_id=1, source_target_pairs={{0,1},{1,0},{2,3},{3,2},{4,5},{5,4},{6,7},{7,6},{8,9},{9,8},{10,11... | collective-permute-start | bytes 61448 | tf_op jit(solution)/shard_map/ppermute | solution.py:176
  13.2 0.0 copy-done
  13.2 0.0 copy-done.1
  13.2 0.0 copy-done.2
  13.2 0.7 %gram.1 = (f32[48,256]{1,0:T(8,128)S(1)}, f32[80,240]{1,0:T(8,128)S(1)}, f32[80,240]{1,0:T(8,128)S(1)}) custom-call(f32[1,512]{1,0:T(1,128)S(1)} %copy-done.2, f32[1,512]{1,0:T(1,128)S(1)} %copy-done.1, s32[1,512]{1,0:T(1,128)S(1)} %bitcast.4, f32[40,8,128]{2,1,0:T(8,128)S(1)} %get-tuple-element.34.after_ref.mine), custom_call_target="tpu_custom_call" | custom-call | tf_op jit(solution)/shard_map/gram/pallas_call | solution.py:711
  13.9 0.0 collective-permute-done.3.got_1
  13.9 2.0 %collective-permute-done.4.got_2 = f32[40,8,128]{2,1,0:T(8,128)S(1)} collective-permute-done((f32[40,8,128]{2,1,0:T(8,128)S(1)}, f32[40,8,128]{2,1,0:T(8,128)S(1)}, u32[]{:S(2)}, u32[]{:S(2)}) %collective-permute-start.4) | collective-permute-done | bytes 163872 | tf_op jit(solution)/shard_map/ppermute | solution.py:176
  15.9 0.5 %collective-permute-done.5.got_3 = f32[40,8,128]{2,1,0:T(8,128)S(1)} collective-permute-done((f32[40,8,128]{2,1,0:T(8,128)S(1)}, f32[40,8,128]{2,1,0:T(8,128)S(1)}, u32[]{:S(2)}, u32[]{:S(2)}) %collective-permute-start.5) | collective-permute-done | bytes 163872 | tf_op jit(solution)/shard_map/ppermute | solution.py:176
  16.5 0.1 middle_pack.1
  16.5 3.7 %collective-permute-start.6 = (f32[2,8,640]{2,1,0:T(8,128)S(1)}, f32[2,8,640]{2,1,0:T(8,128)S(1)}, u32[]{:S(2)}, u32[]{:S(2)}) collective-permute-start(f32[2,8,640]{2,1,0:T(8,128)S(1)} %get-tuple-element.41), channel_id=1, source_target_pairs={{0,24},{1,25},{2,7},{3,6},{4,28},{5,29},{6,3},{7,2},{8,16},{9,17},... | collective-permute-start | bytes 122888 | tf_op jit(solution)/shard_map/ppermute | solution.py:176
  20.2 0.0 collective-permute-start.7
  20.2 0.8 %collective-permute-start.8 = (f32[2,8,640]{2,1,0:T(8,128)S(1)}, f32[2,8,640]{2,1,0:T(8,128)S(1)}, u32[]{:S(2)}, u32[]{:S(2)}) collective-permute-start(f32[2,8,640]{2,1,0:T(8,128)S(1)} %get-tuple-element.43), channel_id=1, source_target_pairs={{0,8},{1,9},{2,3},{3,2},{4,12},{5,13},{6,7},{7,6},{8,0},{9,1},{10,... | collective-permute-start | bytes 122888 | tf_op jit(solution)/shard_map/ppermute | solution.py:176
  21.0 0.0 collective-permute-done.2.vol_got
  21.0 0.7 %first_normal.1.first_ref = f32[2,8,640]{2,1,0:T(8,128)S(1)} custom-call(f32[8,640]{1,0:T(8,128)S(1)} %get-tuple-element.32.vol_mine, f32[8,640]{1,0:T(8,128)S(1)} %collective-permute-done.2.vol_got, f32[48,256]{1,0:T(8,128)S(1)} %get-tuple-element.35.conv_ref, f32[80,240]{1,0:T(8,128)S(1)} %get-tuple-element.36.low_ref, ...), custom_call_target="tpu_custom_call" | custom-call | flops 1000000000 | tf_op jit(solution)/shard_map/first_normal/pallas_call | solution.py:731
  21.7 0.7 %collective-permute-done.6.got_1 = f32[2,8,640]{2,1,0:T(8,128)S(1)} collective-permute-done((f32[2,8,640]{2,1,0:T(8,128)S(1)}, f32[2,8,640]{2,1,0:T(8,128)S(1)}, u32[]{:S(2)}, u32[]{:S(2)}) %collective-permute-start.6) | collective-permute-done | bytes 40992 | tf_op jit(solution)/shard_map/ppermute | solution.py:176
  22.4 2.7 %collective-permute-done.7.got_2 = f32[2,8,640]{2,1,0:T(8,128)S(1)} collective-permute-done((f32[2,8,640]{2,1,0:T(8,128)S(1)}, f32[2,8,640]{2,1,0:T(8,128)S(1)}, u32[]{:S(2)}, u32[]{:S(2)}) %collective-permute-start.7) | collective-permute-done | bytes 40992 | tf_op jit(solution)/shard_map/ppermute | solution.py:176
  25.1 0.0 collective-permute-done.8.got_3
  25.1 0.1 collective-permute-start.9
  25.2 1.6 %collective-permute-start.10 = (f32[3,8,640]{2,1,0:T(8,128)S(1)}, f32[3,8,640]{2,1,0:T(8,128)S(1)}, u32[]{:S(2)}, u32[]{:S(2)}) collective-permute-start(f32[3,8,640]{2,1,0:T(8,128)S(1)} %get-tuple-element.46), channel_id=1, source_target_pairs={{0,4},{1,5},{2,6},{3,7},{4,0},{5,1},{6,2},{7,3},{8,12},{9,13},{10,... | collective-permute-start | bytes 184328 | tf_op jit(solution)/shard_map/ppermute | solution.py:176
  26.8 0.0 collective-permute-done.9.got_diag
  26.8 2.9 %collective-permute-done.10.got_x = f32[3,8,640]{2,1,0:T(8,128)S(1)} collective-permute-done((f32[3,8,640]{2,1,0:T(8,128)S(1)}, f32[3,8,640]{2,1,0:T(8,128)S(1)}, u32[]{:S(2)}, u32[]{:S(2)}) %collective-permute-start.10) | collective-permute-done | bytes 61472 | tf_op jit(solution)/shard_map/ppermute | solution.py:176
  29.6 1.5 %finish.1 = (f32[8,512]{1,0:T(8,128)S(1)}, f32[8,512]{1,0:T(8,128)S(1)}) custom-call(f32[4,8,640]{2,1,0:T(8,128)S(1)} %get-tuple-element.44.mine, f32[3,8,640]{2,1,0:T(8,128)S(1)} %collective-permute-done.9.got_diag, f32[3,8,640]{2,1,0:T(8,128)S(1)} %collective-permute-done.10.got_x, f32[48,256]{1,0:T(8,128)S(1)} %get-tuple-element.35.conv_ref, ...), custom_call_target="tpu_custom_call" | custom-call | tf_op jit(solution)/shard_map/finish/pallas_call | solution.py:753
  31.1 0.1 collective-permute-start.11
  31.2 1.2 %collective-permute-done.11.got_ref = f32[8,512]{1,0:T(8,128)S(1)} collective-permute-done((f32[8,512]{1,0:T(8,128)S(1)}, f32[8,512]{1,0:T(8,128)S(1)}, u32[]{:S(2)}, u32[]{:S(2)}) %collective-permute-start.11) | collective-permute-done | bytes 16416 | tf_op jit(solution)/shard_map/ppermute | solution.py:176
  32.4 0.1 collective-permute-start.12
  32.5 3.6 %collective-permute-done.12.got_y = f32[2,4,512]{2,1,0:T(4,128)S(1)} collective-permute-done((f32[2,4,512]{2,1,0:T(4,128)S(1)}, f32[2,4,512]{2,1,0:T(4,128)S(1)}, u32[]{:S(2)}, u32[]{:S(2)}) %collective-permute-start.12) | collective-permute-done | bytes 16416 | tf_op jit(solution)/shard_map/ppermute | solution.py:176
  36.1 0.6 %result.1 = f32[1,4,2048]{2,1,0:T(4,128)} custom-call(f32[8,512]{1,0:T(8,128)S(1)} %get-tuple-element.47.own_ref, f32[8,512]{1,0:T(8,128)S(1)} %collective-permute-done.11.got_ref, f32[2,4,512]{2,1,0:T(4,128)S(1)} %collective-permute-done.12.got_y), custom_call_target="tpu_custom_call" | custom-call | tf_op jit(solution)/shard_map/result/pallas_call | solution.py:763
  (2 shorter events, 0.0 us)
Async XLA Ops:
  2.4 2.8 %collective-permute-start = (f32[8,8,1152]{2,1,0:T(8,128)S(1)}, f32[8,8,1152]{2,1,0:T(8,128)S(1)}, u32[]{:S(2)}, u32[]{:S(2)}) collective-permute-start(f32[8,8,1152]{2,1,0:T(8,128)S(1)} %get-tuple-element.31), channel_id=1, source_target_pairs={{0,2},{1,3},{2,0},{3,1},{4,6},{5,7},{6,4},{7,5},{8,10},{9,11},{10,... | collective-permute-start | bytes 884744 | tf_op jit(solution)/shard_map/ppermute | solution.py:176
  4.0 6.3 %collective-permute-start.1 = (f32[9,8,1152]{2,1,0:T(8,128)S(1)}, f32[9,8,1152]{2,1,0:T(8,128)S(1)}, u32[]{:S(2)}, u32[]{:S(2)}) collective-permute-start(f32[9,8,1152]{2,1,0:T(8,128)S(1)} %keep_sibling.1.after_ref), channel_id=1, source_target_pairs={{0,2},{1,3},{2,0},{3,1},{4,6},{5,7},{6,4},{7,5},{8,10},{9,11},{10,... | collective-permute-start | bytes 995336 | tf_op jit(solution)/shard_map/ppermute | solution.py:176
  5.3 7.9 %copy-start = (s32[512]{0:T(512)S(1)}, s32[512]{0:T(512)}, u32[]{:S(2)}) copy-start(s32[512]{0:T(512)} %drift_hbm.1) | copy-start | bytes 6148
  5.3 7.9 %copy-start.1 = (f32[1,512]{1,0:T(1,128)S(1)}, f32[1,512]{1,0:T(1,128)}, u32[]{:S(2)}) copy-start(f32[1,512]{1,0:T(1,128)} %constant.8.clone.sec_ref) | copy-start | bytes 6148
  5.3 7.9 %copy-start.2 = (f32[1,512]{1,0:T(1,128)S(1)}, f32[1,512]{1,0:T(1,128)}, u32[]{:S(2)}) copy-start(f32[1,512]{1,0:T(1,128)} %constant.7.clone.tan_ref) | copy-start | bytes 6148
  5.3 8.6 %collective-permute-start.3 = (f32[40,8,128]{2,1,0:T(8,128)S(1)}, f32[40,8,128]{2,1,0:T(8,128)S(1)}, u32[]{:S(2)}, u32[]{:S(2)}) collective-permute-start(f32[40,8,128]{2,1,0:T(8,128)S(1)} %pass_pack.1.after_ref), channel_id=1, source_target_pairs={{0,5},{1,4},{2,18},{3,19},{4,1},{5,0},{6,22},{7,23},{8,13},{9,12},... | collective-permute-start | bytes 491528 | tf_op jit(solution)/shard_map/ppermute | solution.py:176
  10.6 5.4 %collective-permute-start.4 = (f32[40,8,128]{2,1,0:T(8,128)S(1)}, f32[40,8,128]{2,1,0:T(8,128)S(1)}, u32[]{:S(2)}, u32[]{:S(2)}) collective-permute-start(f32[40,8,128]{2,1,0:T(8,128)S(1)} %get-tuple-element.38), channel_id=1, source_target_pairs={{0,4},{1,5},{2,26},{3,27},{4,0},{5,1},{6,30},{7,31},{8,12},{9,13},... | collective-permute-start | bytes 491528 | tf_op jit(solution)/shard_map/ppermute | solution.py:176
  11.2 5.3 %collective-permute-start.5 = (f32[40,8,128]{2,1,0:T(8,128)S(1)}, f32[40,8,128]{2,1,0:T(8,128)S(1)}, u32[]{:S(2)}, u32[]{:S(2)}) collective-permute-start(f32[40,8,128]{2,1,0:T(8,128)S(1)} %get-tuple-element.39), channel_id=1, source_target_pairs={{0,1},{1,0},{2,10},{3,11},{4,5},{5,4},{6,14},{7,15},{8,9},{9,8},{1... | collective-permute-start | bytes 491528 | tf_op jit(solution)/shard_map/ppermute | solution.py:176
  11.2 9.8 %collective-permute-start.2 = (f32[8,640]{1,0:T(8,128)S(1)}, f32[8,640]{1,0:T(8,128)S(1)}, u32[]{:S(2)}, u32[]{:S(2)}) collective-permute-start(f32[8,640]{1,0:T(8,128)S(1)} %get-tuple-element.33), channel_id=1, source_target_pairs={{0,1},{1,0},{2,3},{3,2},{4,5},{5,4},{6,7},{7,6},{8,9},{9,8},{10,11... | collective-permute-start | bytes 61448 | tf_op jit(solution)/shard_map/ppermute | solution.py:176
  16.5 5.9 %collective-permute-start.6 = (f32[2,8,640]{2,1,0:T(8,128)S(1)}, f32[2,8,640]{2,1,0:T(8,128)S(1)}, u32[]{:S(2)}, u32[]{:S(2)}) collective-permute-start(f32[2,8,640]{2,1,0:T(8,128)S(1)} %get-tuple-element.41), channel_id=1, source_target_pairs={{0,24},{1,25},{2,7},{3,6},{4,28},{5,29},{6,3},{7,2},{8,16},{9,17},... | collective-permute-start | bytes 122888 | tf_op jit(solution)/shard_map/ppermute | solution.py:176
  20.2 4.9 %collective-permute-start.7 = (f32[2,8,640]{2,1,0:T(8,128)S(1)}, f32[2,8,640]{2,1,0:T(8,128)S(1)}, u32[]{:S(2)}, u32[]{:S(2)}) collective-permute-start(f32[2,8,640]{2,1,0:T(8,128)S(1)} %get-tuple-element.42), channel_id=1, source_target_pairs={{0,16},{1,17},{2,6},{3,7},{4,20},{5,21},{6,2},{7,3},{8,24},{9,25},... | collective-permute-start | bytes 122888 | tf_op jit(solution)/shard_map/ppermute | solution.py:176
  20.2 4.9 %collective-permute-start.8 = (f32[2,8,640]{2,1,0:T(8,128)S(1)}, f32[2,8,640]{2,1,0:T(8,128)S(1)}, u32[]{:S(2)}, u32[]{:S(2)}) collective-permute-start(f32[2,8,640]{2,1,0:T(8,128)S(1)} %get-tuple-element.43), channel_id=1, source_target_pairs={{0,8},{1,9},{2,3},{3,2},{4,12},{5,13},{6,7},{7,6},{8,0},{9,1},{10,... | collective-permute-start | bytes 122888 | tf_op jit(solution)/shard_map/ppermute | solution.py:176
  25.1 1.6 %collective-permute-start.9 = (f32[3,8,640]{2,1,0:T(8,128)S(1)}, f32[3,8,640]{2,1,0:T(8,128)S(1)}, u32[]{:S(2)}, u32[]{:S(2)}) collective-permute-start(f32[3,8,640]{2,1,0:T(8,128)S(1)} %get-tuple-element.45), channel_id=1, source_target_pairs={{0,2},{1,3},{2,0},{3,1},{4,8},{5,9},{6,10},{7,11},{8,4},{9,5},{10,... | collective-permute-start | bytes 184328 | tf_op jit(solution)/shard_map/ppermute | solution.py:176
  25.2 4.4 %collective-permute-start.10 = (f32[3,8,640]{2,1,0:T(8,128)S(1)}, f32[3,8,640]{2,1,0:T(8,128)S(1)}, u32[]{:S(2)}, u32[]{:S(2)}) collective-permute-start(f32[3,8,640]{2,1,0:T(8,128)S(1)} %get-tuple-element.46), channel_id=1, source_target_pairs={{0,4},{1,5},{2,6},{3,7},{4,0},{5,1},{6,2},{7,3},{8,12},{9,13},{10,... | collective-permute-start | bytes 184328 | tf_op jit(solution)/shard_map/ppermute | solution.py:176
  31.1 1.2 %collective-permute-start.11 = (f32[8,512]{1,0:T(8,128)S(1)}, f32[8,512]{1,0:T(8,128)S(1)}, u32[]{:S(2)}, u32[]{:S(2)}) collective-permute-start(f32[8,512]{1,0:T(8,128)S(1)} %get-tuple-element.48), channel_id=1, source_target_pairs={{0,2},{1,3},{2,0},{3,1},{4,6},{5,7},{6,4},{7,5},{8,10},{9,11},{10,... | collective-permute-start | bytes 49160 | tf_op jit(solution)/shard_map/ppermute | solution.py:176
  32.4 3.7 %collective-permute-start.12 = (f32[2,4,512]{2,1,0:T(4,128)S(1)}, f32[2,4,512]{2,1,0:T(4,128)S(1)}, u32[]{:S(2)}, u32[]{:S(2)}) collective-permute-start(f32[2,4,512]{2,1,0:T(4,128)S(1)} %result_pack.1), channel_id=1, source_target_pairs={{0,1},{1,0},{2,3},{3,2},{4,5},{5,4},{6,7},{7,6},{8,9},{9,8},{10,11... | collective-permute-start | bytes 49160 | tf_op jit(solution)/shard_map/ppermute | solution.py:176

commit v10 on v9

--- a/solution.py
+++ b/solution.py
@@ -293,7 +293,7 @@
 
 def fetch_kernel(views, rows, band, scale, tan_hbm, drift_hbm, meas_hbm, vol_hbm, out_ref, sibling_buf, own_buf,
                  weights_ref, vol_ref, tan_ref, drift_ref, terms, table_sem, sem):
-    _, _, c, _ = coords()
+    z, _, c, _ = coords()
     tiles = out_ref.shape[2] // LANES
     groups = sibling_buf.shape[0]
 
@@ -307,7 +307,8 @@
         pltpu.make_async_copy(drift_hbm, drift_ref, table_sem.at[1]),
     ]
     vol_copy = pltpu.make_async_copy(vol_hbm, vol_ref, table_sem.at[2])
-    first = [fetch(1 - c, sibling_buf, g, sem.at[0, g]) for g in range(groups)]
+    soon = jnp.where(c == 0, 1 - z // 2, 0)
+    first = [fetch(1 - c, sibling_buf, g, sem.at[0, g]) for g in (soon, 1 - soon)]
     later = [fetch(c, own_buf, g, sem.at[1, g]) for g in range(groups)]
     for copy in tables + first + [vol_copy] + later:
         copy.start()
@@ -322,9 +323,12 @@
     weights_ref[...] = weights.astype(jnp.float32)
     load = strip_loader(flat_rows(sibling_buf), 1 - c, False, views, tiles)
 
-    for copy in first:
-        copy.wait()
-    back_project(views, rows, band, weights, load, out_ref, terms)
+    def load_strip(n):
+        if n % 4 == 0:
+            first[n // 4].wait()
+        return load(n)
+
+    back_project(views, rows, band, weights, load_strip, out_ref, terms)
     vol_copy.wait()
     for copy in later:
         copy.wait()
@@ -457,53 +461,47 @@
     conv_ref[...] = jnp.concatenate([stacked, stacked], axis=1)
 
 
-def normal(volumes, conv, low_ref, high_ref, out, band, is_low, is_high):
+def normal(volumes, conv, low_ref, high_ref, band, is_low, is_high):
     rows, width = volumes[0].shape
-    count = len(volumes)
     step = conv.shape[1] // 2 // rows
     parts = conv.shape[0] // 2 // rows
-    for s in range(count):
-        moved = jnp.concatenate(
-            [pltpu.roll(volumes[s], (2 * band - j) % width, 1) for j in range(step)], axis=0
-        )
+    beyond = beyond_ends(volumes, low_ref, high_ref, band, is_low, is_high)
+    zero = jnp.zeros((rows, width - 2 * LANES), jnp.float32)
+    result = []
+    for volume, piece in zip(volumes, beyond):
+        moved = jnp.concatenate([pltpu.roll(volume, (2 * band - j) % width, 1) for j in range(step)], axis=0)
         spread = jnp.dot(conv, split_terms(moved), preferred_element_type=jnp.float32)
         spread = spread[: parts * rows] + spread[parts * rows :]
         total = spread[0:rows]
         for i in range(1, parts):
             total = total + pltpu.roll(spread[i * rows : (i + 1) * rows], width - step * i, 1)
-        out[s] = total
-
+        ends = [jnp.where(is_low, piece, 0.0), zero, jnp.where(is_high, piece, 0.0)]
+        result.append(total - jnp.concatenate(ends, axis=1))
+    return result
+
+
+def beyond_ends(volumes, low_ref, high_ref, band, is_low, is_high):
+    rows, width = volumes[0].shape
+    pitch = LANES // len(volumes)
     lane = lane_iota((rows, LANES))
-
-    @pl.when(is_low)
-    def _():
-        tiles = [v[:, :LANES] for v in volumes]
-        moved = jnp.concatenate(
-            [jnp.concatenate([pltpu.roll(t, LANES - k, 1) for k in range(1, band + 1)], axis=0) for t in tiles], axis=1
-        )
-        spread = jnp.dot(low_ref[...].astype(jnp.bfloat16), right_terms(moved), preferred_element_type=jnp.float32)
-        for s in range(count):
-            total = jnp.zeros((rows, LANES), jnp.float32)
-            for k in range(1, band + 1):
-                piece = spread[(k - 1) * rows : k * rows, s * LANES : (s + 1) * LANES]
-                piece = jnp.where((lane >= HALO - band) & (lane < HALO), piece, 0.0)
-                total = total + pltpu.roll(piece, k, 1)
-            out[s, :, 0:LANES] = out[s, :, 0:LANES] - total
-
-    @pl.when(is_high)
-    def _():
-        tiles = [v[:, width - LANES :] for v in volumes]
-        moved = jnp.concatenate(
-            [jnp.concatenate([pltpu.roll(t, k, 1) for k in range(band, 0, -1)], axis=0) for t in tiles], axis=1
-        )
-        spread = jnp.dot(high_ref[...].astype(jnp.bfloat16), right_terms(moved), preferred_element_type=jnp.float32)
-        for s in range(count):
-            total = jnp.zeros((rows, LANES), jnp.float32)
-            for k in range(band, 0, -1):
-                piece = spread[(band - k) * rows : (band - k + 1) * rows, s * LANES : (s + 1) * LANES]
-                piece = jnp.where((lane >= LANES - HALO) & (lane < LANES - HALO + band), piece, 0.0)
-                total = total + pltpu.roll(piece, LANES - k, 1)
-            out[s, :, width - LANES :] = out[s, :, width - LANES :] - total
+    packed = jnp.zeros((rows, LANES), jnp.float32)
+    for s, volume in enumerate(volumes):
+        tile = jnp.where(is_low, volume[:, :LANES], volume[:, width - LANES :])
+        inside = (lane >= s * pitch) & (lane < s * pitch + 2 * band)
+        packed = jnp.where(inside, pltpu.roll(tile, (s * pitch - (HALO - band)) % LANES, 1), packed)
+    offsets = [jnp.where(is_low, i + 1, LANES + i - band) for i in range(band)]
+    moved = jnp.concatenate([pltpu.roll(packed, LANES - k, 1) for k in offsets], axis=0)
+    matrix = jnp.where(is_low, low_ref[...], high_ref[...]).astype(jnp.bfloat16)
+    spread = jnp.dot(matrix, right_terms(moved), preferred_element_type=jnp.float32)
+    place = lane % pitch - jnp.where(is_low, 0, band)
+    total = jnp.zeros((rows, LANES), jnp.float32)
+    for i, k in enumerate(offsets):
+        piece = jnp.where((place >= 0) & (place < band), spread[i * rows : (i + 1) * rows], 0.0)
+        total = total + pltpu.roll(piece, k, 1)
+    near = (lane >= HALO - band) & (lane < HALO + band)
+    return [
+        jnp.where(near, pltpu.roll(total, (HALO - band - s * pitch) % LANES, 1), 0.0) for s in range(len(volumes))
+    ]
 
 
 def block_place(width, total_cols):
@@ -513,7 +511,7 @@
     return index * block - HALO, index == 0, index == total_cols // block - 1
 
 
-def first_normal_kernel(band, total_cols, vol_mine, vol_got, conv_ref, low_ref, high_ref, out, work):
+def first_normal_kernel(band, total_cols, vol_mine, vol_got, conv_ref, low_ref, high_ref, out):
     _, is_low, is_high = block_place(vol_mine.shape[1], total_cols)
     _, _, _, y = coords()
     part = vol_mine.shape[0] // 2
@@ -523,9 +521,9 @@
     volumes = [
         jnp.concatenate([upper[i * part : (i + 1) * part], lower[i * part : (i + 1) * part]], axis=0) for i in range(2)
     ]
-    normal(volumes, conv_ref[...].astype(jnp.bfloat16), low_ref, high_ref, work, band, is_low, is_high)
+    back = normal(volumes, conv_ref[...].astype(jnp.bfloat16), low_ref, high_ref, band, is_low, is_high)
     for i in range(2):
-        out[i] = volumes[i] - work[i]
+        out[i] = volumes[i] - back[i]
 
 
 def half_pair_kernel(first_ref, own_pair, got_1, got_2, got_3, mine, to_x, to_diag, corr):
@@ -552,7 +550,7 @@
         dz = jnp.where(keep, half[w + 1] - v, 0.0)
         dr = jnp.where(row < rows - 1, pltpu.roll(v, rows - 1, 0) - v, 0.0)
         dc = jnp.where(inside, pltpu.roll(v, width - 1, 1) - v, 0.0)
-        inverse = 1.0 / jnp.sqrt(dz * dz + dr * dr + dc * dc + SMOOTH_EPS * SMOOTH_EPS)
+        inverse = lax.rsqrt(dz * dz + dr * dr + dc * dc + SMOOTH_EPS * SMOOTH_EPS)
         units.append((dz * inverse, dr * inverse, dc * inverse))
     result = []
     for w in range(1, len(half) - 1):
@@ -563,7 +561,7 @@
 
 
 def finish_kernel(
-    band, depth, total_cols, mine, got_diag, got_x, conv_ref, low_ref, high_ref, keep_ref, send_ref, work, done
+    band, depth, total_cols, mine, got_diag, got_x, conv_ref, low_ref, high_ref, keep_ref, send_ref, done
 ):
     width = mine.shape[2]
     first_col, is_low, is_high = block_place(width, total_cols)
@@ -574,8 +572,8 @@
     corr = [before[2], mine[2], mine[3], after[2]]
     slice_0 = 4 * z + 2 * x
     volumes = variation_step(half, lambda w: slice_0 - 2 + w, first_col, depth, total_cols)
-    normal(volumes, conv_ref[...].astype(jnp.bfloat16), low_ref, high_ref, work, band, is_low, is_high)
-    half = [volumes[s] + corr[s] - work[s] for s in range(4)]
+    back = normal(volumes, conv_ref[...].astype(jnp.bfloat16), low_ref, high_ref, band, is_low, is_high)
+    half = [volumes[s] + corr[s] - back[s] for s in range(4)]
     volumes = variation_step(half, lambda w: slice_0 - 1 + w, first_col, depth, total_cols)
     for s in range(2):
         done[s] = pltpu.roll(volumes[s], width - HALO, 1)[:, : width - LANES]
@@ -732,7 +730,7 @@
         functools.partial(first_normal_kernel, band, cols),
         pair,
         [VMEM_SPEC] * 5,
-        [pltpu.VMEM((2, rows, width), jnp.float32)],
+        [],
         "first_normal",
         flops=10**9,
     )(vol_mine, vol_got, conv, low, high)
@@ -754,7 +752,7 @@
         functools.partial(finish_kernel, band, slices, cols),
         [quarter, quarter],
         [VMEM_SPEC] * 6,
-        [pltpu.VMEM((4, rows, width), jnp.float32), pltpu.VMEM((2, rows, block), jnp.float32)],
+        [pltpu.VMEM((2, rows, block), jnp.float32)],
         "finish",
     )(mine, got_diag, got_x, conv, low, high)
     swapped = move(send, lambda z, x, c, y: (z, x, 1 - c, y))

time: 36.9 us -> 36.3 us (0.984)
  Pallas kernels: 9.44 us -> 8.66 us
  starting transfers between devices: 13.5 us -> 13.9 us
    pallas_call x1, Pallas kernels: 1.46 us -> 1.04 us  [summed_plan(): kernel_call(functools.partial(finish_kernel, band, slices, cols), [quarte...]
where the time goes in v10:
time: 36.3 us; the launch traced here: 36.2 us
  starting transfers between devices  13.9 us (38%)
  waiting for transfers between devices  13.5 us (37%)
  Pallas kernels  8.66 us (24%)
    ppermute x13, starting transfers between devices, move(): return lax.ppermute(value, ('wide', 'grp'), pairs)  13.9 us
    ppermute x13, waiting for transfers between devices, move(): return lax.ppermute(value, ('wide', 'grp'), pairs)  13.5 us
    pallas_call x1, Pallas kernels, summed_plan(): kernel_call(functools.partial(fetch_kernel, views, rows, band, scale), [h...  2.28 us
    pallas_call x2, Pallas kernels, own(): kernel_call(functools.partial(own_kernel, kept, views, rows, band), half_...  2.13 us
    pallas_call x1, Pallas kernels, summed_plan(): kernel_call(functools.partial(sibling_kernel, views, rows, band), half_an...  1.08 us
    pallas_call x1, Pallas kernels, summed_plan(): kernel_call(functools.partial(finish_kernel, band, slices, cols), [quarte...  1.04 us
  transfers between devices with their start and end apart: 13, of which 7 were waited for; matrix products, arithmetic and copies ran while one was open for 0% of the time, Pallas kernels for 13%

profile of v10, /device:TPU:0, one launch (start us, length us, event | category | flops | bytes accessed | tf_op | source)
XLA Modules:
  0.0 36.2 jit_solution(903466488491532789)
XLA Ops:
  0.0 2.3 %pass_sibling.1 = (f32[8,8,1152]{2,1,0:T(8,128)S(1)}, f32[2,16,11,8,128]{4,3,2,1,0:T(8,128)S(1)}, f32[2,16,11,8,128]{4,3,2,1,0:T(8,128)S(1)}, f32[56,144]{1,0:T(8,128)S(1)}, f32[1,4,2048]{2,1,0:T(4,128)S(1)}) custom-call(f32[512]{0:T(512)} %constant.6.clone.tan_hbm, s32[512]{0:T(512)} %drift_hbm.1, f32[16,2,16,8,128]{4,3,2,1,0:T(8,128)} %bitcast.5, ...), custom_call_target="tpu_custom_call" | custom-call | flops 1000000000 | tf_op jit(solution)/shard_map/pass_sibling/pallas_call | solution.py:656
  2.3 0.5 %collective-permute-start = (f32[8,8,1152]{2,1,0:T(8,128)S(1)}, f32[8,8,1152]{2,1,0:T(8,128)S(1)}, u32[]{:S(2)}, u32[]{:S(2)}) collective-permute-start(f32[8,8,1152]{2,1,0:T(8,128)S(1)} %get-tuple-element.31), channel_id=1, source_target_pairs={{0,2},{1,3},{2,0},{3,1},{4,6},{5,7},{6,4},{7,5},{8,10},{9,11},{10,... | collective-permute-start | bytes 884744 | tf_op jit(solution)/shard_map/ppermute | solution.py:176
  2.8 1.1 %keep_sibling.1.after_ref = f32[9,8,1152]{2,1,0:T(8,128)S(1)} custom-call(f32[2,16,11,8,128]{4,3,2,1,0:T(8,128)S(1)} %get-tuple-element.29.buf, f32[56,144]{1,0:T(8,128)S(1)} %get-tuple-element.28.weights_ref, f32[1,4,2048]{2,1,0:T(4,128)S(1)} %get-tuple-element.30.vol_ref), custom_call_target="tpu_custom_call" | custom-call | flops 1000000000 | tf_op jit(solution)/shard_map/keep_sibling/pallas_call | solution.py:671
  3.9 0.1 collective-permute-start.1
  4.0 1.1 %pass_own.1.own_ref.pass_ref = f32[8,8,1152]{2,1,0:T(8,128)S(1)} custom-call(f32[2,16,11,8,128]{4,3,2,1,0:T(8,128)S(1)} %get-tuple-element.27.buf, f32[56,144]{1,0:T(8,128)S(1)} %get-tuple-element.28.weights_ref, f32[9,8,1152]{2,1,0:T(8,128)S(1)} %keep_sibling.1.after_ref), custom_call_target="tpu_custom_call" | custom-call | flops 1000000000 | tf_op jit(solution)/shard_map/pass_own/pallas_call | solution.py:682
  5.1 0.0 collective-permute-done.got_ref.pass_got
  5.1 0.1 pass_pack.1.after_ref
  5.2 0.0 copy-start
  5.2 0.0 copy-start.1
  5.2 0.0 copy-start.2
  5.2 4.0 %collective-permute-start.3 = (f32[40,8,128]{2,1,0:T(8,128)S(1)}, f32[40,8,128]{2,1,0:T(8,128)S(1)}, u32[]{:S(2)}, u32[]{:S(2)}) collective-permute-start(f32[40,8,128]{2,1,0:T(8,128)S(1)} %pass_pack.1.after_ref), channel_id=1, source_target_pairs={{0,5},{1,4},{2,18},{3,19},{4,1},{5,0},{6,22},{7,23},{8,13},{9,12},... | collective-permute-start | bytes 491528 | tf_op jit(solution)/shard_map/ppermute | solution.py:176
  9.2 1.1 %keep_own.1.own_ref = f32[8,8,1152]{2,1,0:T(8,128)S(1)} custom-call(f32[2,16,11,8,128]{4,3,2,1,0:T(8,128)S(1)} %get-tuple-element.27.buf, f32[56,144]{1,0:T(8,128)S(1)} %get-tuple-element.28.weights_ref, f32[40,8,128]{2,1,0:T(8,128)S(1)} %pass_pack.1.after_ref), custom_call_target="tpu_custom_call" | custom-call | flops 1000000000 | tf_op jit(solution)/shard_map/keep_own/pallas_call | solution.py:682
  10.2 0.0 collective-permute-done.1.got_ref
  10.2 0.2 keep_pack.1
  10.4 0.6 %collective-permute-start.4 = (f32[40,8,128]{2,1,0:T(8,128)S(1)}, f32[40,8,128]{2,1,0:T(8,128)S(1)}, u32[]{:S(2)}, u32[]{:S(2)}) collective-permute-start(f32[40,8,128]{2,1,0:T(8,128)S(1)} %get-tuple-element.38), channel_id=1, source_target_pairs={{0,4},{1,5},{2,26},{3,27},{4,0},{5,1},{6,30},{7,31},{8,12},{9,13},... | collective-permute-start | bytes 491528 | tf_op jit(solution)/shard_map/ppermute | solution.py:176
  11.0 0.1 collective-permute-start.5
  11.1 2.0 %collective-permute-start.2 = (f32[8,640]{1,0:T(8,128)S(1)}, f32[8,640]{1,0:T(8,128)S(1)}, u32[]{:S(2)}, u32[]{:S(2)}) collective-permute-start(f32[8,640]{1,0:T(8,128)S(1)} %get-tuple-element.33), channel_id=1, source_target_pairs={{0,1},{1,0},{2,3},{3,2},{4,5},{5,4},{6,7},{7,6},{8,9},{9,8},{10,11... | collective-permute-start | bytes 61448 | tf_op jit(solution)/shard_map/ppermute | solution.py:176
  13.1 0.0 copy-done
  13.1 0.0 copy-done.1
  13.1 0.0 copy-done.2
  13.1 0.7 %gram.1 = (f32[48,256]{1,0:T(8,128)S(1)}, f32[80,240]{1,0:T(8,128)S(1)}, f32[80,240]{1,0:T(8,128)S(1)}) custom-call(f32[1,512]{1,0:T(1,128)S(1)} %copy-done.2, f32[1,512]{1,0:T(1,128)S(1)} %copy-done.1, s32[1,512]{1,0:T(1,128)S(1)} %bitcast.4, f32[40,8,128]{2,1,0:T(8,128)S(1)} %get-tuple-element.34.after_ref.mine), custom_call_target="tpu_custom_call" | custom-call | tf_op jit(solution)/shard_map/gram/pallas_call | solution.py:709
  13.8 0.0 collective-permute-done.3.got_1
  13.8 2.0 %collective-permute-done.4.got_2 = f32[40,8,128]{2,1,0:T(8,128)S(1)} collective-permute-done((f32[40,8,128]{2,1,0:T(8,128)S(1)}, f32[40,8,128]{2,1,0:T(8,128)S(1)}, u32[]{:S(2)}, u32[]{:S(2)}) %collective-permute-start.4) | collective-permute-done | bytes 163872 | tf_op jit(solution)/shard_map/ppermute | solution.py:176
  15.8 0.5 %collective-permute-done.5.got_3 = f32[40,8,128]{2,1,0:T(8,128)S(1)} collective-permute-done((f32[40,8,128]{2,1,0:T(8,128)S(1)}, f32[40,8,128]{2,1,0:T(8,128)S(1)}, u32[]{:S(2)}, u32[]{:S(2)}) %collective-permute-start.5) | collective-permute-done | bytes 163872 | tf_op jit(solution)/shard_map/ppermute | solution.py:176
  16.4 0.1 middle_pack.1
  16.4 3.7 %collective-permute-start.6 = (f32[2,8,640]{2,1,0:T(8,128)S(1)}, f32[2,8,640]{2,1,0:T(8,128)S(1)}, u32[]{:S(2)}, u32[]{:S(2)}) collective-permute-start(f32[2,8,640]{2,1,0:T(8,128)S(1)} %get-tuple-element.41), channel_id=1, source_target_pairs={{0,24},{1,25},{2,7},{3,6},{4,28},{5,29},{6,3},{7,2},{8,16},{9,17},... | collective-permute-start | bytes 122888 | tf_op jit(solution)/shard_map/ppermute | solution.py:176
  20.1 0.0 collective-permute-start.7
  20.1 0.8 %collective-permute-start.8 = (f32[2,8,640]{2,1,0:T(8,128)S(1)}, f32[2,8,640]{2,1,0:T(8,128)S(1)}, u32[]{:S(2)}, u32[]{:S(2)}) collective-permute-start(f32[2,8,640]{2,1,0:T(8,128)S(1)} %get-tuple-element.43), channel_id=1, source_target_pairs={{0,8},{1,9},{2,3},{3,2},{4,12},{5,13},{6,7},{7,6},{8,0},{9,1},{10,... | collective-permute-start | bytes 122888 | tf_op jit(solution)/shard_map/ppermute | solution.py:176
  20.9 0.0 collective-permute-done.2.vol_got
  20.9 0.5 %first_normal.1.first_ref = f32[2,8,640]{2,1,0:T(8,128)S(1)} custom-call(f32[8,640]{1,0:T(8,128)S(1)} %get-tuple-element.32.vol_mine, f32[8,640]{1,0:T(8,128)S(1)} %collective-permute-done.2.vol_got, f32[48,256]{1,0:T(8,128)S(1)} %get-tuple-element.35.conv_ref, f32[80,240]{1,0:T(8,128)S(1)} %get-tuple-element.36.low_ref, ...), custom_call_target="tpu_custom_call" | custom-call | flops 1000000000 | tf_op jit(solution)/shard_map/first_normal/pallas_call | solution.py:729
  21.4 0.9 %collective-permute-done.6.got_1 = f32[2,8,640]{2,1,0:T(8,128)S(1)} collective-permute-done((f32[2,8,640]{2,1,0:T(8,128)S(1)}, f32[2,8,640]{2,1,0:T(8,128)S(1)}, u32[]{:S(2)}, u32[]{:S(2)}) %collective-permute-start.6) | collective-permute-done | bytes 40992 | tf_op jit(solution)/shard_map/ppermute | solution.py:176
  22.3 2.7 %collective-permute-done.7.got_2 = f32[2,8,640]{2,1,0:T(8,128)S(1)} collective-permute-done((f32[2,8,640]{2,1,0:T(8,128)S(1)}, f32[2,8,640]{2,1,0:T(8,128)S(1)}, u32[]{:S(2)}, u32[]{:S(2)}) %collective-permute-start.7) | collective-permute-done | bytes 40992 | tf_op jit(solution)/shard_map/ppermute | solution.py:176
  25.0 0.0 collective-permute-done.8.got_3
  25.0 0.1 collective-permute-start.9
  25.1 1.6 %collective-permute-start.10 = (f32[3,8,640]{2,1,0:T(8,128)S(1)}, f32[3,8,640]{2,1,0:T(8,128)S(1)}, u32[]{:S(2)}, u32[]{:S(2)}) collective-permute-start(f32[3,8,640]{2,1,0:T(8,128)S(1)} %get-tuple-element.46), channel_id=1, source_target_pairs={{0,4},{1,5},{2,6},{3,7},{4,0},{5,1},{6,2},{7,3},{8,12},{9,13},{10,... | collective-permute-start | bytes 184328 | tf_op jit(solution)/shard_map/ppermute | solution.py:176
  26.7 0.0 collective-permute-done.9.got_diag
  26.7 2.9 %collective-permute-done.10.got_x = f32[3,8,640]{2,1,0:T(8,128)S(1)} collective-permute-done((f32[3,8,640]{2,1,0:T(8,128)S(1)}, f32[3,8,640]{2,1,0:T(8,128)S(1)}, u32[]{:S(2)}, u32[]{:S(2)}) %collective-permute-start.10) | collective-permute-done | bytes 61472 | tf_op jit(solution)/shard_map/ppermute | solution.py:176
  29.5 1.0 %finish.1 = (f32[8,512]{1,0:T(8,128)S(1)}, f32[8,512]{1,0:T(8,128)S(1)}) custom-call(f32[4,8,640]{2,1,0:T(8,128)S(1)} %get-tuple-element.44.mine, f32[3,8,640]{2,1,0:T(8,128)S(1)} %collective-permute-done.9.got_diag, f32[3,8,640]{2,1,0:T(8,128)S(1)} %collective-permute-done.10.got_x, f32[48,256]{1,0:T(8,128)S(1)} %get-tuple-element.35.conv_ref, ...), custom_call_target="tpu_custom_call" | custom-call | tf_op jit(solution)/shard_map/finish/pallas_call | solution.py:751
  30.6 0.1 collective-permute-start.11
  30.6 1.2 %collective-permute-done.11.got_ref = f32[8,512]{1,0:T(8,128)S(1)} collective-permute-done((f32[8,512]{1,0:T(8,128)S(1)}, f32[8,512]{1,0:T(8,128)S(1)}, u32[]{:S(2)}, u32[]{:S(2)}) %collective-permute-start.11) | collective-permute-done | bytes 16416 | tf_op jit(solution)/shard_map/ppermute | solution.py:176
  31.8 0.5 %collective-permute-start.12 = (f32[2,4,512]{2,1,0:T(4,128)S(1)}, f32[2,4,512]{2,1,0:T(4,128)S(1)}, u32[]{:S(2)}, u32[]{:S(2)}) collective-permute-start(f32[2,4,512]{2,1,0:T(4,128)S(1)} %result_pack.1), channel_id=1, source_target_pairs={{0,1},{1,0},{2,3},{3,2},{4,5},{5,4},{6,7},{7,6},{8,9},{9,8},{10,11... | collective-permute-start | bytes 49160 | tf_op jit(solution)/shard_map/ppermute | solution.py:176
  32.3 3.2 %collective-permute-done.12.got_y = f32[2,4,512]{2,1,0:T(4,128)S(1)} collective-permute-done((f32[2,4,512]{2,1,0:T(4,128)S(1)}, f32[2,4,512]{2,1,0:T(4,128)S(1)}, u32[]{:S(2)}, u32[]{:S(2)}) %collective-permute-start.12) | collective-permute-done | bytes 16416 | tf_op jit(solution)/shard_map/ppermute | solution.py:176
  35.6 0.6 %result.1 = f32[1,4,2048]{2,1,0:T(4,128)} custom-call(f32[8,512]{1,0:T(8,128)S(1)} %get-tuple-element.47.own_ref, f32[8,512]{1,0:T(8,128)S(1)} %collective-permute-done.11.got_ref, f32[2,4,512]{2,1,0:T(4,128)S(1)} %collective-permute-done.12.got_y), custom_call_target="tpu_custom_call" | custom-call | tf_op jit(solution)/shard_map/result/pallas_call | solution.py:761
  (2 shorter events, 0.0 us)
Async XLA Ops:
  2.3 2.8 %collective-permute-start = (f32[8,8,1152]{2,1,0:T(8,128)S(1)}, f32[8,8,1152]{2,1,0:T(8,128)S(1)}, u32[]{:S(2)}, u32[]{:S(2)}) collective-permute-start(f32[8,8,1152]{2,1,0:T(8,128)S(1)} %get-tuple-element.31), channel_id=1, source_target_pairs={{0,2},{1,3},{2,0},{3,1},{4,6},{5,7},{6,4},{7,5},{8,10},{9,11},{10,... | collective-permute-start | bytes 884744 | tf_op jit(solution)/shard_map/ppermute | solution.py:176
  3.9 6.3 %collective-permute-start.1 = (f32[9,8,1152]{2,1,0:T(8,128)S(1)}, f32[9,8,1152]{2,1,0:T(8,128)S(1)}, u32[]{:S(2)}, u32[]{:S(2)}) collective-permute-start(f32[9,8,1152]{2,1,0:T(8,128)S(1)} %keep_sibling.1.after_ref), channel_id=1, source_target_pairs={{0,2},{1,3},{2,0},{3,1},{4,6},{5,7},{6,4},{7,5},{8,10},{9,11},{10,... | collective-permute-start | bytes 995336 | tf_op jit(solution)/shard_map/ppermute | solution.py:176
  5.2 7.9 %copy-start = (s32[512]{0:T(512)S(1)}, s32[512]{0:T(512)}, u32[]{:S(2)}) copy-start(s32[512]{0:T(512)} %drift_hbm.1) | copy-start | bytes 6148
  5.2 7.9 %copy-start.1 = (f32[1,512]{1,0:T(1,128)S(1)}, f32[1,512]{1,0:T(1,128)}, u32[]{:S(2)}) copy-start(f32[1,512]{1,0:T(1,128)} %constant.8.clone.sec_ref) | copy-start | bytes 6148
  5.2 7.9 %copy-start.2 = (f32[1,512]{1,0:T(1,128)S(1)}, f32[1,512]{1,0:T(1,128)}, u32[]{:S(2)}) copy-start(f32[1,512]{1,0:T(1,128)} %constant.7.clone.tan_ref) | copy-start | bytes 6148
  5.2 8.6 %collective-permute-start.3 = (f32[40,8,128]{2,1,0:T(8,128)S(1)}, f32[40,8,128]{2,1,0:T(8,128)S(1)}, u32[]{:S(2)}, u32[]{:S(2)}) collective-permute-start(f32[40,8,128]{2,1,0:T(8,128)S(1)} %pass_pack.1.after_ref), channel_id=1, source_target_pairs={{0,5},{1,4},{2,18},{3,19},{4,1},{5,0},{6,22},{7,23},{8,13},{9,12},... | collective-permute-start | bytes 491528 | tf_op jit(solution)/shard_map/ppermute | solution.py:176
  10.4 5.4 %collective-permute-start.4 = (f32[40,8,128]{2,1,0:T(8,128)S(1)}, f32[40,8,128]{2,1,0:T(8,128)S(1)}, u32[]{:S(2)}, u32[]{:S(2)}) collective-permute-start(f32[40,8,128]{2,1,0:T(8,128)S(1)} %get-tuple-element.38), channel_id=1, source_target_pairs={{0,4},{1,5},{2,26},{3,27},{4,0},{5,1},{6,30},{7,31},{8,12},{9,13},... | collective-permute-start | bytes 491528 | tf_op jit(solution)/shard_map/ppermute | solution.py:176
  11.0 5.3 %collective-permute-start.5 = (f32[40,8,128]{2,1,0:T(8,128)S(1)}, f32[40,8,128]{2,1,0:T(8,128)S(1)}, u32[]{:S(2)}, u32[]{:S(2)}) collective-permute-start(f32[40,8,128]{2,1,0:T(8,128)S(1)} %get-tuple-element.39), channel_id=1, source_target_pairs={{0,1},{1,0},{2,10},{3,11},{4,5},{5,4},{6,14},{7,15},{8,9},{9,8},{1... | collective-permute-start | bytes 491528 | tf_op jit(solution)/shard_map/ppermute | solution.py:176
  11.1 9.8 %collective-permute-start.2 = (f32[8,640]{1,0:T(8,128)S(1)}, f32[8,640]{1,0:T(8,128)S(1)}, u32[]{:S(2)}, u32[]{:S(2)}) collective-permute-start(f32[8,640]{1,0:T(8,128)S(1)} %get-tuple-element.33), channel_id=1, source_target_pairs={{0,1},{1,0},{2,3},{3,2},{4,5},{5,4},{6,7},{7,6},{8,9},{9,8},{10,11... | collective-permute-start | bytes 61448 | tf_op jit(solution)/shard_map/ppermute | solution.py:176
  16.4 5.9 %collective-permute-start.6 = (f32[2,8,640]{2,1,0:T(8,128)S(1)}, f32[2,8,640]{2,1,0:T(8,128)S(1)}, u32[]{:S(2)}, u32[]{:S(2)}) collective-permute-start(f32[2,8,640]{2,1,0:T(8,128)S(1)} %get-tuple-element.41), channel_id=1, source_target_pairs={{0,24},{1,25},{2,7},{3,6},{4,28},{5,29},{6,3},{7,2},{8,16},{9,17},... | collective-permute-start | bytes 122888 | tf_op jit(solution)/shard_map/ppermute | solution.py:176
  20.1 4.9 %collective-permute-start.7 = (f32[2,8,640]{2,1,0:T(8,128)S(1)}, f32[2,8,640]{2,1,0:T(8,128)S(1)}, u32[]{:S(2)}, u32[]{:S(2)}) collective-permute-start(f32[2,8,640]{2,1,0:T(8,128)S(1)} %get-tuple-element.42), channel_id=1, source_target_pairs={{0,16},{1,17},{2,6},{3,7},{4,20},{5,21},{6,2},{7,3},{8,24},{9,25},... | collective-permute-start | bytes 122888 | tf_op jit(solution)/shard_map/ppermute | solution.py:176
  20.1 4.9 %collective-permute-start.8 = (f32[2,8,640]{2,1,0:T(8,128)S(1)}, f32[2,8,640]{2,1,0:T(8,128)S(1)}, u32[]{:S(2)}, u32[]{:S(2)}) collective-permute-start(f32[2,8,640]{2,1,0:T(8,128)S(1)} %get-tuple-element.43), channel_id=1, source_target_pairs={{0,8},{1,9},{2,3},{3,2},{4,12},{5,13},{6,7},{7,6},{8,0},{9,1},{10,... | collective-permute-start | bytes 122888 | tf_op jit(solution)/shard_map/ppermute | solution.py:176
  25.0 1.6 %collective-permute-start.9 = (f32[3,8,640]{2,1,0:T(8,128)S(1)}, f32[3,8,640]{2,1,0:T(8,128)S(1)}, u32[]{:S(2)}, u32[]{:S(2)}) collective-permute-start(f32[3,8,640]{2,1,0:T(8,128)S(1)} %get-tuple-element.45), channel_id=1, source_target_pairs={{0,2},{1,3},{2,0},{3,1},{4,8},{5,9},{6,10},{7,11},{8,4},{9,5},{10,... | collective-permute-start | bytes 184328 | tf_op jit(solution)/shard_map/ppermute | solution.py:176
  25.1 4.4 %collective-permute-start.10 = (f32[3,8,640]{2,1,0:T(8,128)S(1)}, f32[3,8,640]{2,1,0:T(8,128)S(1)}, u32[]{:S(2)}, u32[]{:S(2)}) collective-permute-start(f32[3,8,640]{2,1,0:T(8,128)S(1)} %get-tuple-element.46), channel_id=1, source_target_pairs={{0,4},{1,5},{2,6},{3,7},{4,0},{5,1},{6,2},{7,3},{8,12},{9,13},{10,... | collective-permute-start | bytes 184328 | tf_op jit(solution)/shard_map/ppermute | solution.py:176
  30.6 1.2 %collective-permute-start.11 = (f32[8,512]{1,0:T(8,128)S(1)}, f32[8,512]{1,0:T(8,128)S(1)}, u32[]{:S(2)}, u32[]{:S(2)}) collective-permute-start(f32[8,512]{1,0:T(8,128)S(1)} %get-tuple-element.48), channel_id=1, source_target_pairs={{0,2},{1,3},{2,0},{3,1},{4,6},{5,7},{6,4},{7,5},{8,10},{9,11},{10,... | collective-permute-start | bytes 49160 | tf_op jit(solution)/shard_map/ppermute | solution.py:176
  31.8 3.7 %collective-permute-start.12 = (f32[2,4,512]{2,1,0:T(4,128)S(1)}, f32[2,4,512]{2,1,0:T(4,128)S(1)}, u32[]{:S(2)}, u32[]{:S(2)}) collective-permute-start(f32[2,4,512]{2,1,0:T(4,128)S(1)} %result_pack.1), channel_id=1, source_target_pairs={{0,1},{1,0},{2,3},{3,2},{4,5},{5,4},{6,7},{7,6},{8,9},{9,8},{10,11... | collective-permute-start | bytes 49160 | tf_op jit(solution)/shard_map/ppermute | solution.py:176

commit v11 on v10

--- a/solution.py
+++ b/solution.py
@@ -233,8 +233,8 @@
     return left_terms(weights).astype(jnp.bfloat16)
 
 
-def back_project(views, rows, band, weights, load_strip, out_ref, terms):
-    count, _, width = terms.shape
+def back_project(views, rows, band, weights, load_strip, begin, out_ref, terms):
+    count, _, width = terms.shape[0] // 2, *terms.shape[1:]
     out_cols = out_ref.shape[2]
     parts = 2 * band // STEP + 1
     for n in range(count):
@@ -243,16 +243,16 @@
         low = (strip - high.astype(jnp.float32)).astype(jnp.bfloat16)
         for j in range(STEP):
             moved = pltpu.roll(high, j, 1) if j else high
-            terms[n, j * views : (j + 1) * views] = moved
-            terms[n, (STEP + j) * views : (STEP + j + 1) * views] = pltpu.roll(low, j, 1) if j else low
-            terms[n, (2 * STEP + j) * views : (2 * STEP + j + 1) * views] = moved
+            terms[begin + n, j * views : (j + 1) * views] = moved
+            terms[begin + n, (STEP + j) * views : (STEP + j + 1) * views] = pltpu.roll(low, j, 1) if j else low
+            terms[begin + n, (2 * STEP + j) * views : (2 * STEP + j + 1) * views] = moved
     for n in range(count):
-        spread = jnp.dot(weights, terms[n], preferred_element_type=jnp.float32)
+        spread = jnp.dot(weights, terms[begin + n], preferred_element_type=jnp.float32)
         total = None
         for i in range(parts):
             piece = pltpu.roll(spread[i * rows : (i + 1) * rows], width - HALO - band + STEP * i, 1)
             total = piece if total is None else total + piece
-        out_ref[n] = total[:, :out_cols]
+        out_ref[begin + n] = total[:, :out_cols]
 
 
 def depth_partner(z, bits):
@@ -291,8 +291,8 @@
     return pltpu.roll(window, width - HALO, 1)[:, : half_cols + LANES]
 
 
-def fetch_kernel(views, rows, band, scale, tan_hbm, drift_hbm, meas_hbm, vol_hbm, out_ref, sibling_buf, own_buf,
-                 weights_ref, vol_ref, tan_ref, drift_ref, terms, table_sem, sem):
+def fetch_kernel(views, rows, band, scale, tan_hbm, drift_hbm, meas_hbm, vol_hbm, out_ref, own_buf, weights_ref, vol_ref,
+                 tan_ref, drift_ref, sibling_buf, terms, vbuf, table_sem, sem):
     z, _, c, _ = coords()
     tiles = out_ref.shape[2] // LANES
     groups = sibling_buf.shape[0]
@@ -321,15 +321,21 @@
         copy.wait()
     weights = view_weights(views, rows, band, scale, tan_ref, drift_ref)
     weights_ref[...] = weights.astype(jnp.float32)
-    load = strip_loader(flat_rows(sibling_buf), 1 - c, False, views, tiles)
+    load, load_kept = (strip_loader(flat_rows(sibling_buf), 1 - c, kept, views, tiles) for kept in (False, True))
 
     def load_strip(n):
         if n % 4 == 0:
             first[n // 4].wait()
         return load(n)
 
-    back_project(views, rows, band, weights, load_strip, out_ref, terms)
+    count = terms.shape[0] // 2
+    back_project(views, rows, band, weights, load_strip, 0, out_ref, terms)
+    back_project(views, rows, band, weights, load_kept, count, out_ref, terms)
     vol_copy.wait()
+    half_cols = out_ref.shape[2] - LANES
+    part = vol_ref.shape[1]
+    out_ref[2 * count, 0:part] = volume_window(vol_ref, 1 - c, half_cols, vbuf)
+    out_ref[2 * count, part:] = jnp.zeros((rows - part, half_cols + LANES), jnp.float32)
     for copy in later:
         copy.wait()
 
@@ -339,23 +345,13 @@
     return buf.reshape(groups, views * tiles * sub, lanes)
 
 
-def sibling_kernel(views, rows, band, buf, weights_ref, vol_ref, out_ref, terms, vbuf):
+def own_kernel(views, rows, band, buf, weights_ref, out_ref, terms):
     _, _, c, _ = coords()
     tiles = out_ref.shape[2] // LANES
-    load = strip_loader(flat_rows(buf), 1 - c, True, views, tiles)
-    back_project(views, rows, band, weights_ref[...].astype(jnp.bfloat16), load, out_ref, terms)
-    count = terms.shape[0]
-    half_cols = out_ref.shape[2] - LANES
-    part = vol_ref.shape[1]
-    out_ref[count, 0:part] = volume_window(vol_ref, 1 - c, half_cols, vbuf)
-    out_ref[count, part:] = jnp.zeros((rows - part, half_cols + LANES), jnp.float32)
-
-
-def own_kernel(kept, views, rows, band, buf, weights_ref, after_ref, out_ref, terms):
-    _, _, c, _ = coords()
-    tiles = out_ref.shape[2] // LANES
-    load = strip_loader(flat_rows(buf), c, kept, views, tiles)
-    back_project(views, rows, band, weights_ref[...].astype(jnp.bfloat16), load, out_ref, terms)
+    weights = weights_ref[...].astype(jnp.bfloat16)
+    for kept in (False, True):
+        load = strip_loader(flat_rows(buf), c, kept, views, tiles)
+        back_project(views, rows, band, weights, load, terms.shape[0] // 2 if kept else 0, out_ref, terms)
 
 
 def put_quarter(out, acc, py, tiles):
@@ -373,42 +369,31 @@
         out[t] = jnp.zeros(out.shape[1:], jnp.float32)
 
 
-def pass_pack_kernel(own_ref, got_ref, send, acc):
-    _, _, c, y = coords()
-    acc[...] = own_ref[...] + got_ref[...]
-
-    @pl.when(c == 0)
-    def _():
-        put_quarter(send, acc, 1 - y, send.shape[0] // acc.shape[0])
-
-    @pl.when(c == 1)
-    def _():
-        put_four(send, acc, 0)
-
-
-def keep_pack_kernel(pass_ref, pass_got, own_ref, got_ref, vol_ref, mine, send_2, send_3, vol_mine, vol_to_y,
+def plane_pack_kernel(own_ref, got_ref, vol_ref, mine, send_1, send_2, send_3, vol_mine, vol_to_y,
                      passed, acc, both, vbuf):
-    count, rows, half_width = own_ref.shape
+    count, _, half_width = passed.shape
     tiles = mine.shape[0] // count
     part = vol_ref.shape[1]
     _, _, c, y = coords()
-    passed[...] = pass_ref[...] + pass_got[...]
-    acc[...] = own_ref[...] + got_ref[0:count]
+    passed[...] = own_ref[0:count] + got_ref[0:count]
+    acc[...] = own_ref[count:] + got_ref[count : 2 * count]
 
     @pl.when(c == 0)
     def _():
+        put_quarter(send_1, passed, 1 - y, tiles)
         put_quarter(send_2, passed, y, tiles)
         put_quarter(send_3, acc, 1 - y, tiles)
         put_quarter(mine, acc, y, tiles)
 
     @pl.when(c == 1)
     def _():
+        put_four(send_1, passed, 0)
         put_four(send_2, passed, 4)
         put_four(send_3, acc, 0)
         put_four(mine, acc, 4)
 
     here = volume_window(vol_ref, c, half_width - LANES, vbuf)
-    there = got_ref[count, 0:part]
+    there = got_ref[2 * count, 0:part]
     both[0:part] = jnp.where(c == 0, here, there)
     both[part:] = jnp.where(c == 0, there, here)
     width = tiles * LANES
@@ -647,60 +632,44 @@
     tiled = measured.reshape(views, groups, SUB, cols // LANES, LANES).transpose(0, 1, 3, 2, 4)
     table = ((2 * band // STEP + 1) * rows, 3 * STEP * views)
     count = slices // 2
-    terms = pltpu.VMEM((count, 3 * STEP * views, half_width + LANES), jnp.bfloat16)
+    terms = pltpu.VMEM((slices, 3 * STEP * views, half_width + LANES), jnp.bfloat16)
     vbuf = pltpu.VMEM((part, cols + 2 * LANES), jnp.float32)
     half_of = f32(count, rows, half_width)
-    half_and = f32(count + 1, rows, half_width)
-    across = lambda z, x, c, y: (z, x, 1 - c, y)
-
-    pass_sibling, sibling_buf, own_buf, weights, volume = kernel_call(
+    sibling, own_buf, weights, volume = kernel_call(
         functools.partial(fetch_kernel, views, rows, band, scale),
-        [half_of, f32(*window), f32(*window), f32(*table), f32(1, part, cols)],
+        [f32(slices + 1, rows, half_width), f32(*window), f32(*table), f32(1, part, cols)],
         [HBM_SPEC] * 4,
         [
             pltpu.SMEM((total_angles,), jnp.float32),
             pltpu.SMEM((total_angles,), jnp.int32),
+            pltpu.VMEM(window, jnp.float32),
             terms,
+            vbuf,
             pltpu.SemaphoreType.DMA((3,)),
             pltpu.SemaphoreType.DMA((2, groups)),
         ],
-        "pass_sibling",
+        "other_share",
         flops=10**9,
     )(in_hbm(jnp.asarray(tangent)), in_hbm(drift), in_hbm(tiled), in_hbm(start_volume))
-    pass_got = move(pass_sibling, across)
-    keep_sibling = kernel_call(
-        functools.partial(sibling_kernel, views, rows, band),
-        half_and,
+    got = move(sibling, lambda z, x, c, y: (z, x, 1 - c, y))
+    own = kernel_call(
+        functools.partial(own_kernel, views, rows, band),
+        f32(slices, rows, half_width),
+        [VMEM_SPEC] * 2,
+        [terms],
+        "own_share",
+        flops=10**9,
+    )(own_buf, weights)
+
+    message = f32(count * width // LANES, rows, LANES)
+    mine, send_1, send_2, send_3, vol_mine, vol_to_y = kernel_call(
+        plane_pack_kernel,
+        [message] * 4 + [f32(rows, width)] * 2,
         [VMEM_SPEC] * 3,
-        [terms, vbuf],
-        "keep_sibling",
-        flops=10**9,
-    )(sibling_buf, weights, volume)
-    keep_got = move(keep_sibling, across)
-
-    def own(kept, after):
-        return kernel_call(
-            functools.partial(own_kernel, kept, views, rows, band),
-            half_of,
-            [VMEM_SPEC] * 2 + [ANY_SPEC],
-            [terms],
-            "keep_own" if kept else "pass_own",
-            flops=10**9,
-        )(own_buf, weights, after)
-
-    message = f32(count * width // LANES, rows, LANES)
-    pass_own = own(False, keep_sibling)
-    send_1 = kernel_call(pass_pack_kernel, message, [VMEM_SPEC] * 2, [pltpu.VMEM(half_of.shape, jnp.float32)], "pass_pack")(
-        pass_own, pass_got
-    )
+        [pltpu.VMEM(half_of.shape, jnp.float32)] * 2 + [pltpu.VMEM((rows, half_width), jnp.float32), vbuf],
+        "plane_pack",
+    )(own, got, volume)
     got_1 = move(send_1, lambda z, x, c, y: (z ^ 2, x, c, y) if c else (z, 1 - x, c, 1 - y))
-    mine, send_2, send_3, vol_mine, vol_to_y = kernel_call(
-        keep_pack_kernel,
-        [message] * 3 + [f32(rows, width)] * 2,
-        [VMEM_SPEC] * 5,
-        [pltpu.VMEM(half_of.shape, jnp.float32)] * 2 + [pltpu.VMEM((rows, half_width), jnp.float32), vbuf],
-        "keep_pack",
-    )(pass_own, pass_got, own(True, send_1), keep_got, volume)
     got_2 = move(send_2, lambda z, x, c, y: (z ^ 3, x, c, y) if c else (z, 1 - x, c, y))
     got_3 = move(send_3, lambda z, x, c, y: (z ^ 1, x, c, y) if c else (z, x, c, 1 - y))
     vol_got = move(vol_to_y, lambda z, x, c, y: (z, x, c, 1 - y))

time: 36.3 us -> 35.6 us (0.981)
  waiting for transfers between devices: 13.5 us -> 12.6 us
    ppermute x13 -> x12, waiting for transfers between devices: 13.5 us -> 12.6 us  [move(): return lax.ppermute(value, ('wide', 'grp'), pairs)]
    ppermute x13 -> x12, starting transfers between devices: 13.9 us -> 14.2 us  [move(): return lax.ppermute(value, ('wide', 'grp'), pairs)]
    pallas_call x6 -> x3, Pallas kernels: 5.74 us -> 5.63 us  [the longest x1 3.35 us: summed_plan(): kernel_call(functools.partial(fetch_kernel, views, rows, band, scale), [f...]
  transfers between devices with their start and end apart: 13 -> 12, of which waited for: 7 -> 7; matrix products, arithmetic and copies ran while one was open for 0% -> 0% of each run, Pallas kernels for 13% -> 9%
where the time goes in v11:
time: 35.6 us; the launch traced here: 35.4 us
  starting transfers between devices  14.2 us (40%)
  waiting for transfers between devices  12.6 us (35%)
  Pallas kernels  8.56 us (24%)
    ppermute x12, starting transfers between devices, move(): return lax.ppermute(value, ('wide', 'grp'), pairs)  14.2 us
    ppermute x12, waiting for transfers between devices, move(): return lax.ppermute(value, ('wide', 'grp'), pairs)  12.6 us
    pallas_call x1, Pallas kernels, summed_plan(): kernel_call(functools.partial(fetch_kernel, views, rows, band, scale), [f...  3.35 us
    pallas_call x1, Pallas kernels, summed_plan(): kernel_call(functools.partial(own_kernel, views, rows, band), f32(slices,...  2.08 us
    pallas_call x1, Pallas kernels, summed_plan(): kernel_call(functools.partial(finish_kernel, band, slices, cols), [quarte...  1.04 us
  transfers between devices with their start and end apart: 12, of which 7 were waited for; matrix products, arithmetic and copies ran while one was open for 0% of the time, Pallas kernels for 9%

profile of v11, /device:TPU:0, one launch (start us, length us, event | category | flops | bytes accessed | tf_op | source)
XLA Modules:
  0.0 35.4 jit_solution(12529908643203778916)
XLA Ops:
  0.0 3.4 %other_share.1 = (f32[17,8,1152]{2,1,0:T(8,128)S(1)}, f32[2,16,11,8,128]{4,3,2,1,0:T(8,128)S(1)}, f32[56,144]{1,0:T(8,128)S(1)}, f32[1,4,2048]{2,1,0:T(4,128)S(1)}) custom-call(f32[512]{0:T(512)} %constant.6.clone.tan_hbm, s32[512]{0:T(512)} %drift_hbm.1, f32[16,2,16,8,128]{4,3,2,1,0:T(8,128)} %bitcast.5, f32[1,4,2048]{2,1,0:T(4,128)} %vol_hbm.1), custom_call_target="tpu_custom_call" | custom-call | flops 1000000000 | tf_op jit(solution)/shard_map/other_share/pallas_call | solution.py:638
  3.4 0.5 %collective-permute-start = (f32[17,8,1152]{2,1,0:T(8,128)S(1)}, f32[17,8,1152]{2,1,0:T(8,128)S(1)}, u32[]{:S(2)}, u32[]{:S(2)}) collective-permute-start(f32[17,8,1152]{2,1,0:T(8,128)S(1)} %get-tuple-element.29), channel_id=1, source_target_pairs={{0,2},{1,3},{2,0},{3,1},{4,6},{5,7},{6,4},{7,5},{8,10},{9,11},{10,... | collective-permute-start | bytes 1880072 | tf_op jit(solution)/shard_map/ppermute | solution.py:176
  3.9 0.0 copy-start
  3.9 0.0 copy-start.1
  3.9 0.0 copy-start.2
  3.9 2.1 %own_share.1.own_ref = f32[16,8,1152]{2,1,0:T(8,128)S(1)} custom-call(f32[2,16,11,8,128]{4,3,2,1,0:T(8,128)S(1)} %get-tuple-element.27.buf, f32[56,144]{1,0:T(8,128)S(1)} %get-tuple-element.28.weights_ref), custom_call_target="tpu_custom_call" | custom-call | flops 1000000000 | tf_op jit(solution)/shard_map/own_share/pallas_call | solution.py:655
  6.0 0.0 collective-permute-done.got_ref
  6.0 0.2 plane_pack.1
  6.2 3.6 %collective-permute-start.2 = (f32[40,8,128]{2,1,0:T(8,128)S(1)}, f32[40,8,128]{2,1,0:T(8,128)S(1)}, u32[]{:S(2)}, u32[]{:S(2)}) collective-permute-start(f32[40,8,128]{2,1,0:T(8,128)S(1)} %get-tuple-element.37), channel_id=1, source_target_pairs={{0,5},{1,4},{2,18},{3,19},{4,1},{5,0},{6,22},{7,23},{8,13},{9,12},... | collective-permute-start | bytes 491528 | tf_op jit(solution)/shard_map/ppermute | solution.py:176
  9.7 0.5 %collective-permute-start.3 = (f32[40,8,128]{2,1,0:T(8,128)S(1)}, f32[40,8,128]{2,1,0:T(8,128)S(1)}, u32[]{:S(2)}, u32[]{:S(2)}) collective-permute-start(f32[40,8,128]{2,1,0:T(8,128)S(1)} %get-tuple-element.38), channel_id=1, source_target_pairs={{0,4},{1,5},{2,26},{3,27},{4,0},{5,1},{6,30},{7,31},{8,12},{9,13},... | collective-permute-start | bytes 491528 | tf_op jit(solution)/shard_map/ppermute | solution.py:176
  10.3 0.1 collective-permute-start.4
  10.4 1.9 %collective-permute-start.1 = (f32[8,640]{1,0:T(8,128)S(1)}, f32[8,640]{1,0:T(8,128)S(1)}, u32[]{:S(2)}, u32[]{:S(2)}) collective-permute-start(f32[8,640]{1,0:T(8,128)S(1)} %get-tuple-element.32), channel_id=1, source_target_pairs={{0,1},{1,0},{2,3},{3,2},{4,5},{5,4},{6,7},{7,6},{8,9},{9,8},{10,11... | collective-permute-start | bytes 61448 | tf_op jit(solution)/shard_map/ppermute | solution.py:176
  12.3 0.0 copy-done
  12.3 0.0 copy-done.1
  12.3 0.0 copy-done.2
  12.3 0.7 %gram.1 = (f32[48,256]{1,0:T(8,128)S(1)}, f32[80,240]{1,0:T(8,128)S(1)}, f32[80,240]{1,0:T(8,128)S(1)}) custom-call(f32[1,512]{1,0:T(1,128)S(1)} %copy-done.2, f32[1,512]{1,0:T(1,128)S(1)} %copy-done.1, s32[1,512]{1,0:T(1,128)S(1)} %bitcast.4, f32[40,8,128]{2,1,0:T(8,128)S(1)} %get-tuple-element.33.after_ref.mine), custom_call_target="tpu_custom_call" | custom-call | tf_op jit(solution)/shard_map/gram/pallas_call | solution.py:678
  13.0 0.0 collective-permute-done.2.got_1
  13.0 2.3 %collective-permute-done.3.got_2 = f32[40,8,128]{2,1,0:T(8,128)S(1)} collective-permute-done((f32[40,8,128]{2,1,0:T(8,128)S(1)}, f32[40,8,128]{2,1,0:T(8,128)S(1)}, u32[]{:S(2)}, u32[]{:S(2)}) %collective-permute-start.3) | collective-permute-done | bytes 163872 | tf_op jit(solution)/shard_map/ppermute | solution.py:176
  15.3 0.5 %collective-permute-done.4.got_3 = f32[40,8,128]{2,1,0:T(8,128)S(1)} collective-permute-done((f32[40,8,128]{2,1,0:T(8,128)S(1)}, f32[40,8,128]{2,1,0:T(8,128)S(1)}, u32[]{:S(2)}, u32[]{:S(2)}) %collective-permute-start.4) | collective-permute-done | bytes 163872 | tf_op jit(solution)/shard_map/ppermute | solution.py:176
  15.8 0.1 middle_pack.1
  15.9 3.4 %collective-permute-start.5 = (f32[2,8,640]{2,1,0:T(8,128)S(1)}, f32[2,8,640]{2,1,0:T(8,128)S(1)}, u32[]{:S(2)}, u32[]{:S(2)}) collective-permute-start(f32[2,8,640]{2,1,0:T(8,128)S(1)} %get-tuple-element.41), channel_id=1, source_target_pairs={{0,24},{1,25},{2,7},{3,6},{4,28},{5,29},{6,3},{7,2},{8,16},{9,17},... | collective-permute-start | bytes 122888 | tf_op jit(solution)/shard_map/ppermute | solution.py:176
  19.3 0.0 collective-permute-start.6
  19.3 1.0 %collective-permute-start.7 = (f32[2,8,640]{2,1,0:T(8,128)S(1)}, f32[2,8,640]{2,1,0:T(8,128)S(1)}, u32[]{:S(2)}, u32[]{:S(2)}) collective-permute-start(f32[2,8,640]{2,1,0:T(8,128)S(1)} %get-tuple-element.43), channel_id=1, source_target_pairs={{0,8},{1,9},{2,3},{3,2},{4,12},{5,13},{6,7},{7,6},{8,0},{9,1},{10,... | collective-permute-start | bytes 122888 | tf_op jit(solution)/shard_map/ppermute | solution.py:176
  20.3 0.0 collective-permute-done.1.vol_got
  20.3 0.5 %first_normal.1.first_ref = f32[2,8,640]{2,1,0:T(8,128)S(1)} custom-call(f32[8,640]{1,0:T(8,128)S(1)} %get-tuple-element.31.vol_mine, f32[8,640]{1,0:T(8,128)S(1)} %collective-permute-done.1.vol_got, f32[48,256]{1,0:T(8,128)S(1)} %get-tuple-element.34.conv_ref, f32[80,240]{1,0:T(8,128)S(1)} %get-tuple-element.35.low_ref, ...), custom_call_target="tpu_custom_call" | custom-call | flops 1000000000 | tf_op jit(solution)/shard_map/first_normal/pallas_call | solution.py:698
  20.8 0.9 %collective-permute-done.5.got_1 = f32[2,8,640]{2,1,0:T(8,128)S(1)} collective-permute-done((f32[2,8,640]{2,1,0:T(8,128)S(1)}, f32[2,8,640]{2,1,0:T(8,128)S(1)}, u32[]{:S(2)}, u32[]{:S(2)}) %collective-permute-start.5) | collective-permute-done | bytes 40992 | tf_op jit(solution)/shard_map/ppermute | solution.py:176
  21.7 2.5 %collective-permute-done.6.got_2 = f32[2,8,640]{2,1,0:T(8,128)S(1)} collective-permute-done((f32[2,8,640]{2,1,0:T(8,128)S(1)}, f32[2,8,640]{2,1,0:T(8,128)S(1)}, u32[]{:S(2)}, u32[]{:S(2)}) %collective-permute-start.6) | collective-permute-done | bytes 40992 | tf_op jit(solution)/shard_map/ppermute | solution.py:176
  24.2 0.0 collective-permute-done.7.got_3
  24.3 0.1 collective-permute-start.8
  24.3 1.6 %collective-permute-start.9 = (f32[3,8,640]{2,1,0:T(8,128)S(1)}, f32[3,8,640]{2,1,0:T(8,128)S(1)}, u32[]{:S(2)}, u32[]{:S(2)}) collective-permute-start(f32[3,8,640]{2,1,0:T(8,128)S(1)} %get-tuple-element.46), channel_id=1, source_target_pairs={{0,4},{1,5},{2,6},{3,7},{4,0},{5,1},{6,2},{7,3},{8,12},{9,13},{10,... | collective-permute-start | bytes 184328 | tf_op jit(solution)/shard_map/ppermute | solution.py:176
  25.9 0.0 collective-permute-done.8.got_diag
  25.9 2.9 %collective-permute-done.9.got_x = f32[3,8,640]{2,1,0:T(8,128)S(1)} collective-permute-done((f32[3,8,640]{2,1,0:T(8,128)S(1)}, f32[3,8,640]{2,1,0:T(8,128)S(1)}, u32[]{:S(2)}, u32[]{:S(2)}) %collective-permute-start.9) | collective-permute-done | bytes 61472 | tf_op jit(solution)/shard_map/ppermute | solution.py:176
  28.8 1.0 %finish.1 = (f32[8,512]{1,0:T(8,128)S(1)}, f32[8,512]{1,0:T(8,128)S(1)}) custom-call(f32[4,8,640]{2,1,0:T(8,128)S(1)} %get-tuple-element.44.mine, f32[3,8,640]{2,1,0:T(8,128)S(1)} %collective-permute-done.8.got_diag, f32[3,8,640]{2,1,0:T(8,128)S(1)} %collective-permute-done.9.got_x, f32[48,256]{1,0:T(8,128)S(1)} %get-tuple-element.34.conv_ref, ...), custom_call_target="tpu_custom_call" | custom-call | tf_op jit(solution)/shard_map/finish/pallas_call | solution.py:720
  29.8 0.1 collective-permute-start.10
  29.9 1.2 %collective-permute-done.10.got_ref = f32[8,512]{1,0:T(8,128)S(1)} collective-permute-done((f32[8,512]{1,0:T(8,128)S(1)}, f32[8,512]{1,0:T(8,128)S(1)}, u32[]{:S(2)}, u32[]{:S(2)}) %collective-permute-start.10) | collective-permute-done | bytes 16416 | tf_op jit(solution)/shard_map/ppermute | solution.py:176
  31.1 1.4 %collective-permute-start.11 = (f32[2,4,512]{2,1,0:T(4,128)S(1)}, f32[2,4,512]{2,1,0:T(4,128)S(1)}, u32[]{:S(2)}, u32[]{:S(2)}) collective-permute-start(f32[2,4,512]{2,1,0:T(4,128)S(1)} %result_pack.1), channel_id=1, source_target_pairs={{0,1},{1,0},{2,3},{3,2},{4,5},{5,4},{6,7},{7,6},{8,9},{9,8},{10,11... | collective-permute-start | bytes 49160 | tf_op jit(solution)/shard_map/ppermute | solution.py:176
  32.5 2.3 %collective-permute-done.11.got_y = f32[2,4,512]{2,1,0:T(4,128)S(1)} collective-permute-done((f32[2,4,512]{2,1,0:T(4,128)S(1)}, f32[2,4,512]{2,1,0:T(4,128)S(1)}, u32[]{:S(2)}, u32[]{:S(2)}) %collective-permute-start.11) | collective-permute-done | bytes 16416 | tf_op jit(solution)/shard_map/ppermute | solution.py:176
  34.8 0.6 %result.1 = f32[1,4,2048]{2,1,0:T(4,128)} custom-call(f32[8,512]{1,0:T(8,128)S(1)} %get-tuple-element.47.own_ref, f32[8,512]{1,0:T(8,128)S(1)} %collective-permute-done.10.got_ref, f32[2,4,512]{2,1,0:T(4,128)S(1)} %collective-permute-done.11.got_y), custom_call_target="tpu_custom_call" | custom-call | tf_op jit(solution)/shard_map/result/pallas_call | solution.py:730
  (2 shorter events, 0.0 us)
Async XLA Ops:
  3.4 2.6 %collective-permute-start = (f32[17,8,1152]{2,1,0:T(8,128)S(1)}, f32[17,8,1152]{2,1,0:T(8,128)S(1)}, u32[]{:S(2)}, u32[]{:S(2)}) collective-permute-start(f32[17,8,1152]{2,1,0:T(8,128)S(1)} %get-tuple-element.29), channel_id=1, source_target_pairs={{0,2},{1,3},{2,0},{3,1},{4,6},{5,7},{6,4},{7,5},{8,10},{9,11},{10,... | collective-permute-start | bytes 1880072 | tf_op jit(solution)/shard_map/ppermute | solution.py:176
  3.9 8.4 %copy-start = (s32[512]{0:T(512)S(1)}, s32[512]{0:T(512)}, u32[]{:S(2)}) copy-start(s32[512]{0:T(512)} %drift_hbm.1) | copy-start | bytes 6148
  3.9 8.4 %copy-start.1 = (f32[1,512]{1,0:T(1,128)S(1)}, f32[1,512]{1,0:T(1,128)}, u32[]{:S(2)}) copy-start(f32[1,512]{1,0:T(1,128)} %constant.8.clone.sec_ref) | copy-start | bytes 6148
  3.9 8.4 %copy-start.2 = (f32[1,512]{1,0:T(1,128)S(1)}, f32[1,512]{1,0:T(1,128)}, u32[]{:S(2)}) copy-start(f32[1,512]{1,0:T(1,128)} %constant.7.clone.tan_ref) | copy-start | bytes 6148
  6.2 6.9 %collective-permute-start.2 = (f32[40,8,128]{2,1,0:T(8,128)S(1)}, f32[40,8,128]{2,1,0:T(8,128)S(1)}, u32[]{:S(2)}, u32[]{:S(2)}) collective-permute-start(f32[40,8,128]{2,1,0:T(8,128)S(1)} %get-tuple-element.37), channel_id=1, source_target_pairs={{0,5},{1,4},{2,18},{3,19},{4,1},{5,0},{6,22},{7,23},{8,13},{9,12},... | collective-permute-start | bytes 491528 | tf_op jit(solution)/shard_map/ppermute | solution.py:176
  9.7 5.6 %collective-permute-start.3 = (f32[40,8,128]{2,1,0:T(8,128)S(1)}, f32[40,8,128]{2,1,0:T(8,128)S(1)}, u32[]{:S(2)}, u32[]{:S(2)}) collective-permute-start(f32[40,8,128]{2,1,0:T(8,128)S(1)} %get-tuple-element.38), channel_id=1, source_target_pairs={{0,4},{1,5},{2,26},{3,27},{4,0},{5,1},{6,30},{7,31},{8,12},{9,13},... | collective-permute-start | bytes 491528 | tf_op jit(solution)/shard_map/ppermute | solution.py:176
  10.3 5.5 %collective-permute-start.4 = (f32[40,8,128]{2,1,0:T(8,128)S(1)}, f32[40,8,128]{2,1,0:T(8,128)S(1)}, u32[]{:S(2)}, u32[]{:S(2)}) collective-permute-start(f32[40,8,128]{2,1,0:T(8,128)S(1)} %get-tuple-element.39), channel_id=1, source_target_pairs={{0,1},{1,0},{2,10},{3,11},{4,5},{5,4},{6,14},{7,15},{8,9},{9,8},{1... | collective-permute-start | bytes 491528 | tf_op jit(solution)/shard_map/ppermute | solution.py:176
  10.4 9.9 %collective-permute-start.1 = (f32[8,640]{1,0:T(8,128)S(1)}, f32[8,640]{1,0:T(8,128)S(1)}, u32[]{:S(2)}, u32[]{:S(2)}) collective-permute-start(f32[8,640]{1,0:T(8,128)S(1)} %get-tuple-element.32), channel_id=1, source_target_pairs={{0,1},{1,0},{2,3},{3,2},{4,5},{5,4},{6,7},{7,6},{8,9},{9,8},{10,11... | collective-permute-start | bytes 61448 | tf_op jit(solution)/shard_map/ppermute | solution.py:176
  15.9 5.9 %collective-permute-start.5 = (f32[2,8,640]{2,1,0:T(8,128)S(1)}, f32[2,8,640]{2,1,0:T(8,128)S(1)}, u32[]{:S(2)}, u32[]{:S(2)}) collective-permute-start(f32[2,8,640]{2,1,0:T(8,128)S(1)} %get-tuple-element.41), channel_id=1, source_target_pairs={{0,24},{1,25},{2,7},{3,6},{4,28},{5,29},{6,3},{7,2},{8,16},{9,17},... | collective-permute-start | bytes 122888 | tf_op jit(solution)/shard_map/ppermute | solution.py:176
  19.3 4.9 %collective-permute-start.6 = (f32[2,8,640]{2,1,0:T(8,128)S(1)}, f32[2,8,640]{2,1,0:T(8,128)S(1)}, u32[]{:S(2)}, u32[]{:S(2)}) collective-permute-start(f32[2,8,640]{2,1,0:T(8,128)S(1)} %get-tuple-element.42), channel_id=1, source_target_pairs={{0,16},{1,17},{2,6},{3,7},{4,20},{5,21},{6,2},{7,3},{8,24},{9,25},... | collective-permute-start | bytes 122888 | tf_op jit(solution)/shard_map/ppermute | solution.py:176
  19.3 4.9 %collective-permute-start.7 = (f32[2,8,640]{2,1,0:T(8,128)S(1)}, f32[2,8,640]{2,1,0:T(8,128)S(1)}, u32[]{:S(2)}, u32[]{:S(2)}) collective-permute-start(f32[2,8,640]{2,1,0:T(8,128)S(1)} %get-tuple-element.43), channel_id=1, source_target_pairs={{0,8},{1,9},{2,3},{3,2},{4,12},{5,13},{6,7},{7,6},{8,0},{9,1},{10,... | collective-permute-start | bytes 122888 | tf_op jit(solution)/shard_map/ppermute | solution.py:176
  24.3 1.6 %collective-permute-start.8 = (f32[3,8,640]{2,1,0:T(8,128)S(1)}, f32[3,8,640]{2,1,0:T(8,128)S(1)}, u32[]{:S(2)}, u32[]{:S(2)}) collective-permute-start(f32[3,8,640]{2,1,0:T(8,128)S(1)} %get-tuple-element.45), channel_id=1, source_target_pairs={{0,2},{1,3},{2,0},{3,1},{4,8},{5,9},{6,10},{7,11},{8,4},{9,5},{10,... | collective-permute-start | bytes 184328 | tf_op jit(solution)/shard_map/ppermute | solution.py:176
  24.3 4.4 %collective-permute-start.9 = (f32[3,8,640]{2,1,0:T(8,128)S(1)}, f32[3,8,640]{2,1,0:T(8,128)S(1)}, u32[]{:S(2)}, u32[]{:S(2)}) collective-permute-start(f32[3,8,640]{2,1,0:T(8,128)S(1)} %get-tuple-element.46), channel_id=1, source_target_pairs={{0,4},{1,5},{2,6},{3,7},{4,0},{5,1},{6,2},{7,3},{8,12},{9,13},{10,... | collective-permute-start | bytes 184328 | tf_op jit(solution)/shard_map/ppermute | solution.py:176
  29.8 1.2 %collective-permute-start.10 = (f32[8,512]{1,0:T(8,128)S(1)}, f32[8,512]{1,0:T(8,128)S(1)}, u32[]{:S(2)}, u32[]{:S(2)}) collective-permute-start(f32[8,512]{1,0:T(8,128)S(1)} %get-tuple-element.48), channel_id=1, source_target_pairs={{0,2},{1,3},{2,0},{3,1},{4,6},{5,7},{6,4},{7,5},{8,10},{9,11},{10,... | collective-permute-start | bytes 49160 | tf_op jit(solution)/shard_map/ppermute | solution.py:176
  31.1 3.7 %collective-permute-start.11 = (f32[2,4,512]{2,1,0:T(4,128)S(1)}, f32[2,4,512]{2,1,0:T(4,128)S(1)}, u32[]{:S(2)}, u32[]{:S(2)}) collective-permute-start(f32[2,4,512]{2,1,0:T(4,128)S(1)} %result_pack.1), channel_id=1, source_target_pairs={{0,1},{1,0},{2,3},{3,2},{4,5},{5,4},{6,7},{7,6},{8,9},{9,8},{10,11... | collective-permute-start | bytes 49160 | tf_op jit(solution)/shard_map/ppermute | solution.py:176

commit v12 on v11

--- a/solution.py
+++ b/solution.py
@@ -299,7 +299,7 @@
 
     def fetch(half, target, g, semaphore):
         return pltpu.make_async_copy(
-            meas_hbm.at[:, g, pl.ds(half * (tiles - 2), tiles)], target.at[g, :, 1 : tiles + 1], semaphore
+            meas_hbm.at[:, g, pl.ds(half * (tiles - 2), tiles)], target.at[g, 0:views, 1 : tiles + 1], semaphore
         )
 
     tables = [
@@ -310,13 +310,13 @@
     soon = jnp.where(c == 0, 1 - z // 2, 0)
     first = [fetch(1 - c, sibling_buf, g, sem.at[0, g]) for g in (soon, 1 - soon)]
     later = [fetch(c, own_buf, g, sem.at[1, g]) for g in range(groups)]
-    for copy in tables + first + [vol_copy] + later:
+    for copy in first[:1] + tables + first[1:] + [vol_copy] + later:
         copy.start()
     zero = jnp.zeros((views, SUB, LANES), jnp.float32)
     for g in range(groups):
         for target in (sibling_buf, own_buf):
-            target[g, :, 0] = zero
-            target[g, :, tiles + 1] = zero
+            target[g, 0:views, 0] = zero
+            target[g, 0:views, tiles + 1] = zero
     for copy in tables:
         copy.wait()
     weights = view_weights(views, rows, band, scale, tan_ref, drift_ref)
@@ -369,11 +369,9 @@
         out[t] = jnp.zeros(out.shape[1:], jnp.float32)
 
 
-def plane_pack_kernel(own_ref, got_ref, vol_ref, mine, send_1, send_2, send_3, vol_mine, vol_to_y,
-                     passed, acc, both, vbuf):
+def plane_pack_kernel(own_ref, got_ref, mine, send_1, send_2, send_3, passed, acc):
     count, _, half_width = passed.shape
     tiles = mine.shape[0] // count
-    part = vol_ref.shape[1]
     _, _, c, y = coords()
     passed[...] = own_ref[0:count] + got_ref[0:count]
     acc[...] = own_ref[count:] + got_ref[count : 2 * count]
@@ -381,8 +379,8 @@
     @pl.when(c == 0)
     def _():
         put_quarter(send_1, passed, 1 - y, tiles)
-        put_quarter(send_2, passed, y, tiles)
-        put_quarter(send_3, acc, 1 - y, tiles)
+        put_quarter(send_2, acc, 1 - y, tiles)
+        put_quarter(send_3, passed, y, tiles)
         put_quarter(mine, acc, y, tiles)
 
     @pl.when(c == 1)
@@ -392,11 +390,16 @@
         put_four(send_3, acc, 0)
         put_four(mine, acc, 4)
 
+
+def volume_pack_kernel(own_ref, got_ref, vol_ref, vol_mine, vol_to_y, both, vbuf):
+    count, rows, half_width = own_ref.shape
+    part = vol_ref.shape[1]
+    _, _, c, y = coords()
     here = volume_window(vol_ref, c, half_width - LANES, vbuf)
-    there = got_ref[2 * count, 0:part]
+    there = got_ref[count, 0:part]
     both[0:part] = jnp.where(c == 0, here, there)
     both[part:] = jnp.where(c == 0, there, here)
-    width = tiles * LANES
+    width = vol_mine.shape[1]
     for vol, py in ((vol_mine, y), (vol_to_y, 1 - y)):
         vol[...] = both[:, pl.ds(pl.multiple_of(py * (width - LANES), LANES), width)]
 
@@ -628,7 +631,7 @@
 
     tiles = half_width // LANES
     groups = slices // SUB
-    window = (groups, views, tiles + 2, SUB, LANES)
+    window = (groups, views + 1, tiles + 2, SUB, LANES)
     tiled = measured.reshape(views, groups, SUB, cols // LANES, LANES).transpose(0, 1, 3, 2, 4)
     table = ((2 * band // STEP + 1) * rows, 3 * STEP * views)
     count = slices // 2
@@ -662,16 +665,23 @@
     )(own_buf, weights)
 
     message = f32(count * width // LANES, rows, LANES)
-    mine, send_1, send_2, send_3, vol_mine, vol_to_y = kernel_call(
+    mine, send_1, send_2, send_3 = kernel_call(
         plane_pack_kernel,
-        [message] * 4 + [f32(rows, width)] * 2,
-        [VMEM_SPEC] * 3,
-        [pltpu.VMEM(half_of.shape, jnp.float32)] * 2 + [pltpu.VMEM((rows, half_width), jnp.float32), vbuf],
+        [message] * 4,
+        [VMEM_SPEC] * 2,
+        [pltpu.VMEM(half_of.shape, jnp.float32)] * 2,
         "plane_pack",
+    )(own, got)
+    vol_mine, vol_to_y = kernel_call(
+        volume_pack_kernel,
+        [f32(rows, width)] * 2,
+        [ANY_SPEC, VMEM_SPEC, VMEM_SPEC],
+        [pltpu.VMEM((rows, half_width), jnp.float32), vbuf],
+        "volume_pack",
     )(own, got, volume)
     got_1 = move(send_1, lambda z, x, c, y: (z ^ 2, x, c, y) if c else (z, 1 - x, c, 1 - y))
-    got_2 = move(send_2, lambda z, x, c, y: (z ^ 3, x, c, y) if c else (z, 1 - x, c, y))
-    got_3 = move(send_3, lambda z, x, c, y: (z ^ 1, x, c, y) if c else (z, x, c, 1 - y))
+    got_2 = move(send_2, lambda z, x, c, y: (z ^ 3, x, c, y) if c else (z, x, c, 1 - y))
+    got_3 = move(send_3, lambda z, x, c, y: (z ^ 1, x, c, y) if c else (z, 1 - x, c, y))
     vol_got = move(vol_to_y, lambda z, x, c, y: (z, x, c, 1 - y))
 
     edge = band * rows

time: 35.6 us -> 35.5 us (level)
  transfers between devices with their start and end apart: 12 -> 12, of which waited for: 7 -> 7; matrix products, arithmetic and copies ran while one was open for 0% -> 0% of each run, Pallas kernels for 9% -> 10%
where the time goes in v12:
time: 35.5 us; the launch traced here: 35.3 us
  starting transfers between devices  14.3 us (40%)
  waiting for transfers between devices  12.3 us (35%)
  Pallas kernels  8.55 us (24%)
    ppermute x12, starting transfers between devices, move(): return lax.ppermute(value, ('wide', 'grp'), pairs)  14.3 us
    ppermute x12, waiting for transfers between devices, move(): return lax.ppermute(value, ('wide', 'grp'), pairs)  12.3 us
    pallas_call x1, Pallas kernels, summed_plan(): kernel_call(functools.partial(fetch_kernel, views, rows, band, scale), [f...  3.35 us
    pallas_call x1, Pallas kernels, summed_plan(): kernel_call(functools.partial(own_kernel, views, rows, band), f32(slices,...  2.05 us
    pallas_call x1, Pallas kernels, summed_plan(): kernel_call(functools.partial(finish_kernel, band, slices, cols), [quarte...  1.04 us
  transfers between devices with their start and end apart: 12, of which 7 were waited for; matrix products, arithmetic and copies ran while one was open for 0% of the time, Pallas kernels for 10%

profile of v12, /device:TPU:0, one launch (start us, length us, event | category | flops | bytes accessed | tf_op | source)
XLA Modules:
  0.0 35.3 jit_solution(14892635234693789978)
XLA Ops:
  0.0 3.4 %other_share.1 = (f32[17,8,1152]{2,1,0:T(8,128)S(1)}, f32[2,17,11,8,128]{4,3,2,1,0:T(8,128)S(1)}, f32[56,144]{1,0:T(8,128)S(1)}, f32[1,4,2048]{2,1,0:T(4,128)S(1)}) custom-call(f32[512]{0:T(512)} %constant.6.clone.tan_hbm, s32[512]{0:T(512)} %drift_hbm.1, f32[16,2,16,8,128]{4,3,2,1,0:T(8,128)} %bitcast.5, f32[1,4,2048]{2,1,0:T(4,128)} %vol_hbm.1), custom_call_target="tpu_custom_call" | custom-call | flops 1000000000 | tf_op jit(solution)/shard_map/other_share/pallas_call | solution.py:641
  3.4 0.5 %collective-permute-start = (f32[17,8,1152]{2,1,0:T(8,128)S(1)}, f32[17,8,1152]{2,1,0:T(8,128)S(1)}, u32[]{:S(2)}, u32[]{:S(2)}) collective-permute-start(f32[17,8,1152]{2,1,0:T(8,128)S(1)} %get-tuple-element.29), channel_id=1, source_target_pairs={{0,2},{1,3},{2,0},{3,1},{4,6},{5,7},{6,4},{7,5},{8,10},{9,11},{10,... | collective-permute-start | bytes 1880072 | tf_op jit(solution)/shard_map/ppermute | solution.py:176
  3.9 2.1 %own_share.1.own_ref = f32[16,8,1152]{2,1,0:T(8,128)S(1)} custom-call(f32[2,17,11,8,128]{4,3,2,1,0:T(8,128)S(1)} %get-tuple-element.27.buf, f32[56,144]{1,0:T(8,128)S(1)} %get-tuple-element.28.weights_ref), custom_call_target="tpu_custom_call" | custom-call | flops 1000000000 | tf_op jit(solution)/shard_map/own_share/pallas_call | solution.py:658
  5.9 0.0 copy-start
  5.9 0.0 copy-start.1
  6.0 0.0 copy-start.2
  6.0 0.0 collective-permute-done.got_ref
  6.0 0.1 plane_pack.1
  6.1 3.6 %collective-permute-start.2 = (f32[40,8,128]{2,1,0:T(8,128)S(1)}, f32[40,8,128]{2,1,0:T(8,128)S(1)}, u32[]{:S(2)}, u32[]{:S(2)}) collective-permute-start(f32[40,8,128]{2,1,0:T(8,128)S(1)} %get-tuple-element.37), channel_id=1, source_target_pairs={{0,5},{1,4},{2,18},{3,19},{4,1},{5,0},{6,22},{7,23},{8,13},{9,12},... | collective-permute-start | bytes 491528 | tf_op jit(solution)/shard_map/ppermute | solution.py:176
  9.7 0.5 %collective-permute-start.3 = (f32[40,8,128]{2,1,0:T(8,128)S(1)}, f32[40,8,128]{2,1,0:T(8,128)S(1)}, u32[]{:S(2)}, u32[]{:S(2)}) collective-permute-start(f32[40,8,128]{2,1,0:T(8,128)S(1)} %get-tuple-element.38), channel_id=1, source_target_pairs={{0,1},{1,0},{2,26},{3,27},{4,5},{5,4},{6,30},{7,31},{8,9},{9,8},{1... | collective-permute-start | bytes 491528 | tf_op jit(solution)/shard_map/ppermute | solution.py:176
  10.2 0.1 collective-permute-start.4
  10.3 0.1 volume_pack.1
  10.4 2.0 %collective-permute-start.1 = (f32[8,640]{1,0:T(8,128)S(1)}, f32[8,640]{1,0:T(8,128)S(1)}, u32[]{:S(2)}, u32[]{:S(2)}) collective-permute-start(f32[8,640]{1,0:T(8,128)S(1)} %get-tuple-element.32), channel_id=1, source_target_pairs={{0,1},{1,0},{2,3},{3,2},{4,5},{5,4},{6,7},{7,6},{8,9},{9,8},{10,11... | collective-permute-start | bytes 61448 | tf_op jit(solution)/shard_map/ppermute | solution.py:176
  12.4 0.0 copy-done
  12.4 0.0 copy-done.1
  12.4 0.0 copy-done.2
  12.4 0.7 %gram.1 = (f32[48,256]{1,0:T(8,128)S(1)}, f32[80,240]{1,0:T(8,128)S(1)}, f32[80,240]{1,0:T(8,128)S(1)}) custom-call(f32[1,512]{1,0:T(1,128)S(1)} %copy-done.2, f32[1,512]{1,0:T(1,128)S(1)} %copy-done.1, s32[1,512]{1,0:T(1,128)S(1)} %bitcast.4, f32[40,8,128]{2,1,0:T(8,128)S(1)} %get-tuple-element.33.after_ref.mine), custom_call_target="tpu_custom_call" | custom-call | tf_op jit(solution)/shard_map/gram/pallas_call | solution.py:688
  13.1 0.0 collective-permute-done.2.got_1
  13.1 2.1 %collective-permute-done.3.got_2 = f32[40,8,128]{2,1,0:T(8,128)S(1)} collective-permute-done((f32[40,8,128]{2,1,0:T(8,128)S(1)}, f32[40,8,128]{2,1,0:T(8,128)S(1)}, u32[]{:S(2)}, u32[]{:S(2)}) %collective-permute-start.3) | collective-permute-done | bytes 163872 | tf_op jit(solution)/shard_map/ppermute | solution.py:176
  15.2 0.3 collective-permute-done.4.got_3
  15.5 0.1 middle_pack.1
  15.6 3.7 %collective-permute-start.5 = (f32[2,8,640]{2,1,0:T(8,128)S(1)}, f32[2,8,640]{2,1,0:T(8,128)S(1)}, u32[]{:S(2)}, u32[]{:S(2)}) collective-permute-start(f32[2,8,640]{2,1,0:T(8,128)S(1)} %get-tuple-element.41), channel_id=1, source_target_pairs={{0,24},{1,25},{2,7},{3,6},{4,28},{5,29},{6,3},{7,2},{8,16},{9,17},... | collective-permute-start | bytes 122888 | tf_op jit(solution)/shard_map/ppermute | solution.py:176
  19.2 0.0 collective-permute-start.6
  19.2 0.8 %collective-permute-start.7 = (f32[2,8,640]{2,1,0:T(8,128)S(1)}, f32[2,8,640]{2,1,0:T(8,128)S(1)}, u32[]{:S(2)}, u32[]{:S(2)}) collective-permute-start(f32[2,8,640]{2,1,0:T(8,128)S(1)} %get-tuple-element.43), channel_id=1, source_target_pairs={{0,8},{1,9},{2,3},{3,2},{4,12},{5,13},{6,7},{7,6},{8,0},{9,1},{10,... | collective-permute-start | bytes 122888 | tf_op jit(solution)/shard_map/ppermute | solution.py:176
  20.0 0.0 collective-permute-done.1.vol_got
  20.0 0.5 %first_normal.1.first_ref = f32[2,8,640]{2,1,0:T(8,128)S(1)} custom-call(f32[8,640]{1,0:T(8,128)S(1)} %get-tuple-element.31.vol_mine, f32[8,640]{1,0:T(8,128)S(1)} %collective-permute-done.1.vol_got, f32[48,256]{1,0:T(8,128)S(1)} %get-tuple-element.34.conv_ref, f32[80,240]{1,0:T(8,128)S(1)} %get-tuple-element.35.low_ref, ...), custom_call_target="tpu_custom_call" | custom-call | flops 1000000000 | tf_op jit(solution)/shard_map/first_normal/pallas_call | solution.py:708
  20.5 0.9 %collective-permute-done.5.got_1 = f32[2,8,640]{2,1,0:T(8,128)S(1)} collective-permute-done((f32[2,8,640]{2,1,0:T(8,128)S(1)}, f32[2,8,640]{2,1,0:T(8,128)S(1)}, u32[]{:S(2)}, u32[]{:S(2)}) %collective-permute-start.5) | collective-permute-done | bytes 40992 | tf_op jit(solution)/shard_map/ppermute | solution.py:176
  21.4 2.7 %collective-permute-done.6.got_2 = f32[2,8,640]{2,1,0:T(8,128)S(1)} collective-permute-done((f32[2,8,640]{2,1,0:T(8,128)S(1)}, f32[2,8,640]{2,1,0:T(8,128)S(1)}, u32[]{:S(2)}, u32[]{:S(2)}) %collective-permute-start.6) | collective-permute-done | bytes 40992 | tf_op jit(solution)/shard_map/ppermute | solution.py:176
  24.1 0.0 collective-permute-done.7.got_3
  24.2 0.1 collective-permute-start.8
  24.2 1.5 %collective-permute-start.9 = (f32[3,8,640]{2,1,0:T(8,128)S(1)}, f32[3,8,640]{2,1,0:T(8,128)S(1)}, u32[]{:S(2)}, u32[]{:S(2)}) collective-permute-start(f32[3,8,640]{2,1,0:T(8,128)S(1)} %get-tuple-element.46), channel_id=1, source_target_pairs={{0,4},{1,5},{2,6},{3,7},{4,0},{5,1},{6,2},{7,3},{8,12},{9,13},{10,... | collective-permute-start | bytes 184328 | tf_op jit(solution)/shard_map/ppermute | solution.py:176
  25.7 0.0 collective-permute-done.8.got_diag
  25.7 2.9 %collective-permute-done.9.got_x = f32[3,8,640]{2,1,0:T(8,128)S(1)} collective-permute-done((f32[3,8,640]{2,1,0:T(8,128)S(1)}, f32[3,8,640]{2,1,0:T(8,128)S(1)}, u32[]{:S(2)}, u32[]{:S(2)}) %collective-permute-start.9) | collective-permute-done | bytes 61472 | tf_op jit(solution)/shard_map/ppermute | solution.py:176
  28.7 1.0 %finish.1 = (f32[8,512]{1,0:T(8,128)S(1)}, f32[8,512]{1,0:T(8,128)S(1)}) custom-call(f32[4,8,640]{2,1,0:T(8,128)S(1)} %get-tuple-element.44.mine, f32[3,8,640]{2,1,0:T(8,128)S(1)} %collective-permute-done.8.got_diag, f32[3,8,640]{2,1,0:T(8,128)S(1)} %collective-permute-done.9.got_x, f32[48,256]{1,0:T(8,128)S(1)} %get-tuple-element.34.conv_ref, ...), custom_call_target="tpu_custom_call" | custom-call | tf_op jit(solution)/shard_map/finish/pallas_call | solution.py:730
  29.7 0.1 collective-permute-start.10
  29.8 1.2 %collective-permute-done.10.got_ref = f32[8,512]{1,0:T(8,128)S(1)} collective-permute-done((f32[8,512]{1,0:T(8,128)S(1)}, f32[8,512]{1,0:T(8,128)S(1)}, u32[]{:S(2)}, u32[]{:S(2)}) %collective-permute-start.10) | collective-permute-done | bytes 16416 | tf_op jit(solution)/shard_map/ppermute | solution.py:176
  31.0 1.5 %collective-permute-start.11 = (f32[2,4,512]{2,1,0:T(4,128)S(1)}, f32[2,4,512]{2,1,0:T(4,128)S(1)}, u32[]{:S(2)}, u32[]{:S(2)}) collective-permute-start(f32[2,4,512]{2,1,0:T(4,128)S(1)} %result_pack.1), channel_id=1, source_target_pairs={{0,1},{1,0},{2,3},{3,2},{4,5},{5,4},{6,7},{7,6},{8,9},{9,8},{10,11... | collective-permute-start | bytes 49160 | tf_op jit(solution)/shard_map/ppermute | solution.py:176
  32.5 2.2 %collective-permute-done.11.got_y = f32[2,4,512]{2,1,0:T(4,128)S(1)} collective-permute-done((f32[2,4,512]{2,1,0:T(4,128)S(1)}, f32[2,4,512]{2,1,0:T(4,128)S(1)}, u32[]{:S(2)}, u32[]{:S(2)}) %collective-permute-start.11) | collective-permute-done | bytes 16416 | tf_op jit(solution)/shard_map/ppermute | solution.py:176
  34.7 0.6 %result.1 = f32[1,4,2048]{2,1,0:T(4,128)} custom-call(f32[8,512]{1,0:T(8,128)S(1)} %get-tuple-element.47.own_ref, f32[8,512]{1,0:T(8,128)S(1)} %collective-permute-done.10.got_ref, f32[2,4,512]{2,1,0:T(4,128)S(1)} %collective-permute-done.11.got_y), custom_call_target="tpu_custom_call" | custom-call | tf_op jit(solution)/shard_map/result/pallas_call | solution.py:740
  (2 shorter events, 0.0 us)
Async XLA Ops:
  3.4 2.6 %collective-permute-start = (f32[17,8,1152]{2,1,0:T(8,128)S(1)}, f32[17,8,1152]{2,1,0:T(8,128)S(1)}, u32[]{:S(2)}, u32[]{:S(2)}) collective-permute-start(f32[17,8,1152]{2,1,0:T(8,128)S(1)} %get-tuple-element.29), channel_id=1, source_target_pairs={{0,2},{1,3},{2,0},{3,1},{4,6},{5,7},{6,4},{7,5},{8,10},{9,11},{10,... | collective-permute-start | bytes 1880072 | tf_op jit(solution)/shard_map/ppermute | solution.py:176
  5.9 6.5 %copy-start = (s32[512]{0:T(512)S(1)}, s32[512]{0:T(512)}, u32[]{:S(2)}) copy-start(s32[512]{0:T(512)} %drift_hbm.1) | copy-start | bytes 6148
  5.9 6.5 %copy-start.1 = (f32[1,512]{1,0:T(1,128)S(1)}, f32[1,512]{1,0:T(1,128)}, u32[]{:S(2)}) copy-start(f32[1,512]{1,0:T(1,128)} %constant.8.clone.sec_ref) | copy-start | bytes 6148
  6.0 6.4 %copy-start.2 = (f32[1,512]{1,0:T(1,128)S(1)}, f32[1,512]{1,0:T(1,128)}, u32[]{:S(2)}) copy-start(f32[1,512]{1,0:T(1,128)} %constant.7.clone.tan_ref) | copy-start | bytes 6148
  6.1 7.0 %collective-permute-start.2 = (f32[40,8,128]{2,1,0:T(8,128)S(1)}, f32[40,8,128]{2,1,0:T(8,128)S(1)}, u32[]{:S(2)}, u32[]{:S(2)}) collective-permute-start(f32[40,8,128]{2,1,0:T(8,128)S(1)} %get-tuple-element.37), channel_id=1, source_target_pairs={{0,5},{1,4},{2,18},{3,19},{4,1},{5,0},{6,22},{7,23},{8,13},{9,12},... | collective-permute-start | bytes 491528 | tf_op jit(solution)/shard_map/ppermute | solution.py:176
  9.7 5.5 %collective-permute-start.3 = (f32[40,8,128]{2,1,0:T(8,128)S(1)}, f32[40,8,128]{2,1,0:T(8,128)S(1)}, u32[]{:S(2)}, u32[]{:S(2)}) collective-permute-start(f32[40,8,128]{2,1,0:T(8,128)S(1)} %get-tuple-element.38), channel_id=1, source_target_pairs={{0,1},{1,0},{2,26},{3,27},{4,5},{5,4},{6,30},{7,31},{8,9},{9,8},{1... | collective-permute-start | bytes 491528 | tf_op jit(solution)/shard_map/ppermute | solution.py:176
  10.2 5.3 %collective-permute-start.4 = (f32[40,8,128]{2,1,0:T(8,128)S(1)}, f32[40,8,128]{2,1,0:T(8,128)S(1)}, u32[]{:S(2)}, u32[]{:S(2)}) collective-permute-start(f32[40,8,128]{2,1,0:T(8,128)S(1)} %get-tuple-element.39), channel_id=1, source_target_pairs={{0,4},{1,5},{2,10},{3,11},{4,0},{5,1},{6,14},{7,15},{8,12},{9,13},... | collective-permute-start | bytes 491528 | tf_op jit(solution)/shard_map/ppermute | solution.py:176
  10.4 9.6 %collective-permute-start.1 = (f32[8,640]{1,0:T(8,128)S(1)}, f32[8,640]{1,0:T(8,128)S(1)}, u32[]{:S(2)}, u32[]{:S(2)}) collective-permute-start(f32[8,640]{1,0:T(8,128)S(1)} %get-tuple-element.32), channel_id=1, source_target_pairs={{0,1},{1,0},{2,3},{3,2},{4,5},{5,4},{6,7},{7,6},{8,9},{9,8},{10,11... | collective-permute-start | bytes 61448 | tf_op jit(solution)/shard_map/ppermute | solution.py:176
  15.6 5.9 %collective-permute-start.5 = (f32[2,8,640]{2,1,0:T(8,128)S(1)}, f32[2,8,640]{2,1,0:T(8,128)S(1)}, u32[]{:S(2)}, u32[]{:S(2)}) collective-permute-start(f32[2,8,640]{2,1,0:T(8,128)S(1)} %get-tuple-element.41), channel_id=1, source_target_pairs={{0,24},{1,25},{2,7},{3,6},{4,28},{5,29},{6,3},{7,2},{8,16},{9,17},... | collective-permute-start | bytes 122888 | tf_op jit(solution)/shard_map/ppermute | solution.py:176
  19.2 4.9 %collective-permute-start.6 = (f32[2,8,640]{2,1,0:T(8,128)S(1)}, f32[2,8,640]{2,1,0:T(8,128)S(1)}, u32[]{:S(2)}, u32[]{:S(2)}) collective-permute-start(f32[2,8,640]{2,1,0:T(8,128)S(1)} %get-tuple-element.42), channel_id=1, source_target_pairs={{0,16},{1,17},{2,6},{3,7},{4,20},{5,21},{6,2},{7,3},{8,24},{9,25},... | collective-permute-start | bytes 122888 | tf_op jit(solution)/shard_map/ppermute | solution.py:176
  19.2 4.9 %collective-permute-start.7 = (f32[2,8,640]{2,1,0:T(8,128)S(1)}, f32[2,8,640]{2,1,0:T(8,128)S(1)}, u32[]{:S(2)}, u32[]{:S(2)}) collective-permute-start(f32[2,8,640]{2,1,0:T(8,128)S(1)} %get-tuple-element.43), channel_id=1, source_target_pairs={{0,8},{1,9},{2,3},{3,2},{4,12},{5,13},{6,7},{7,6},{8,0},{9,1},{10,... | collective-permute-start | bytes 122888 | tf_op jit(solution)/shard_map/ppermute | solution.py:176
  24.2 1.6 %collective-permute-start.8 = (f32[3,8,640]{2,1,0:T(8,128)S(1)}, f32[3,8,640]{2,1,0:T(8,128)S(1)}, u32[]{:S(2)}, u32[]{:S(2)}) collective-permute-start(f32[3,8,640]{2,1,0:T(8,128)S(1)} %get-tuple-element.45), channel_id=1, source_target_pairs={{0,2},{1,3},{2,0},{3,1},{4,8},{5,9},{6,10},{7,11},{8,4},{9,5},{10,... | collective-permute-start | bytes 184328 | tf_op jit(solution)/shard_map/ppermute | solution.py:176
  24.2 4.4 %collective-permute-start.9 = (f32[3,8,640]{2,1,0:T(8,128)S(1)}, f32[3,8,640]{2,1,0:T(8,128)S(1)}, u32[]{:S(2)}, u32[]{:S(2)}) collective-permute-start(f32[3,8,640]{2,1,0:T(8,128)S(1)} %get-tuple-element.46), channel_id=1, source_target_pairs={{0,4},{1,5},{2,6},{3,7},{4,0},{5,1},{6,2},{7,3},{8,12},{9,13},{10,... | collective-permute-start | bytes 184328 | tf_op jit(solution)/shard_map/ppermute | solution.py:176
  29.7 1.2 %collective-permute-start.10 = (f32[8,512]{1,0:T(8,128)S(1)}, f32[8,512]{1,0:T(8,128)S(1)}, u32[]{:S(2)}, u32[]{:S(2)}) collective-permute-start(f32[8,512]{1,0:T(8,128)S(1)} %get-tuple-element.48), channel_id=1, source_target_pairs={{0,2},{1,3},{2,0},{3,1},{4,6},{5,7},{6,4},{7,5},{8,10},{9,11},{10,... | collective-permute-start | bytes 49160 | tf_op jit(solution)/shard_map/ppermute | solution.py:176
  31.0 3.7 %collective-permute-start.11 = (f32[2,4,512]{2,1,0:T(4,128)S(1)}, f32[2,4,512]{2,1,0:T(4,128)S(1)}, u32[]{:S(2)}, u32[]{:S(2)}) collective-permute-start(f32[2,4,512]{2,1,0:T(4,128)S(1)} %result_pack.1), channel_id=1, source_target_pairs={{0,1},{1,0},{2,3},{3,2},{4,5},{5,4},{6,7},{7,6},{8,9},{9,8},{10,11... | collective-permute-start | bytes 49160 | tf_op jit(solution)/shard_map/ppermute | solution.py:176

commit v13 on v12

--- a/solution.py
+++ b/solution.py
@@ -438,28 +438,26 @@
     edge = band * rows
     low_ref[...] = left_terms(gram[edge + rows :, edge + rows :])
     high_ref[...] = left_terms(gram[:edge, :edge])
-    width = conv_ref.shape[1] // 2 * 3
+    lanes = conv_ref.shape[1] // 3
+    parts = conv_ref.shape[0] // rows
+    width = lanes * parts
     padded = jnp.concatenate([gram, jnp.zeros((span * rows, width - span * rows), jnp.float32)], axis=1)
     total = jnp.zeros((rows, width), jnp.float32)
     for k in range(span):
         total = total + pltpu.roll(padded[k * rows : (k + 1) * rows], rows * (2 * band - k), 1)
-    lanes = width // 3
-    stacked = jnp.concatenate([total[:, i * lanes : (i + 1) * lanes] for i in range(3)], axis=0)
-    stacked = split_rows(stacked)
-    conv_ref[...] = jnp.concatenate([stacked, stacked], axis=1)
+    conv_ref[...] = left_terms(jnp.concatenate([total[:, i * lanes : (i + 1) * lanes] for i in range(parts)], axis=0))
 
 
 def normal(volumes, conv, low_ref, high_ref, band, is_low, is_high):
     rows, width = volumes[0].shape
-    step = conv.shape[1] // 2 // rows
-    parts = conv.shape[0] // 2 // rows
+    step = conv.shape[1] // 3 // rows
+    parts = conv.shape[0] // rows
     beyond = beyond_ends(volumes, low_ref, high_ref, band, is_low, is_high)
     zero = jnp.zeros((rows, width - 2 * LANES), jnp.float32)
     result = []
     for volume, piece in zip(volumes, beyond):
         moved = jnp.concatenate([pltpu.roll(volume, (2 * band - j) % width, 1) for j in range(step)], axis=0)
-        spread = jnp.dot(conv, split_terms(moved), preferred_element_type=jnp.float32)
-        spread = spread[: parts * rows] + spread[parts * rows :]
+        spread = jnp.dot(conv, right_terms(moved), preferred_element_type=jnp.float32)
         total = spread[0:rows]
         for i in range(1, parts):
             total = total + pltpu.roll(spread[i * rows : (i + 1) * rows], width - step * i, 1)
@@ -472,24 +470,27 @@
     rows, width = volumes[0].shape
     pitch = LANES // len(volumes)
     lane = lane_iota((rows, LANES))
-    packed = jnp.zeros((rows, LANES), jnp.float32)
-    for s, volume in enumerate(volumes):
-        tile = jnp.where(is_low, volume[:, :LANES], volume[:, width - LANES :])
-        inside = (lane >= s * pitch) & (lane < s * pitch + 2 * band)
-        packed = jnp.where(inside, pltpu.roll(tile, (s * pitch - (HALO - band)) % LANES, 1), packed)
-    offsets = [jnp.where(is_low, i + 1, LANES + i - band) for i in range(band)]
-    moved = jnp.concatenate([pltpu.roll(packed, LANES - k, 1) for k in offsets], axis=0)
+    tiles = [jnp.where(is_low, volume[:, :LANES], volume[:, width - LANES :]) for volume in volumes]
+    offsets = [jnp.where(is_low, i + 1, i - band) for i in range(band)]
+    moved = []
+    for k in offsets:
+        packed = jnp.zeros((rows, LANES), jnp.float32)
+        for s, tile in enumerate(tiles):
+            piece = pltpu.roll(tile, (s * pitch - (HALO - band) - k) % LANES, 1)
+            packed = jnp.where((lane >= s * pitch) & (lane < (s + 1) * pitch), piece, packed)
+        moved.append(packed)
     matrix = jnp.where(is_low, low_ref[...], high_ref[...]).astype(jnp.bfloat16)
-    spread = jnp.dot(matrix, right_terms(moved), preferred_element_type=jnp.float32)
+    spread = jnp.dot(matrix, right_terms(jnp.concatenate(moved, axis=0)), preferred_element_type=jnp.float32)
     place = lane % pitch - jnp.where(is_low, 0, band)
-    total = jnp.zeros((rows, LANES), jnp.float32)
-    for i, k in enumerate(offsets):
-        piece = jnp.where((place >= 0) & (place < band), spread[i * rows : (i + 1) * rows], 0.0)
-        total = total + pltpu.roll(piece, k, 1)
+    kept = [jnp.where((place >= 0) & (place < band), spread[i * rows : (i + 1) * rows], 0.0) for i in range(band)]
     near = (lane >= HALO - band) & (lane < HALO + band)
-    return [
-        jnp.where(near, pltpu.roll(total, (HALO - band - s * pitch) % LANES, 1), 0.0) for s in range(len(volumes))
-    ]
+    result = []
+    for s in range(len(volumes)):
+        back = [pltpu.roll(kept[i], (HALO - band - s * pitch + k) % LANES, 1) for i, k in enumerate(offsets)]
+        while len(back) > 1:
+            back = [sum(back[i + 1 : i + 2], back[i]) for i in range(0, len(back), 2)]
+        result.append(jnp.where(near, back[0], 0.0))
+    return result
 
 
 def block_place(width, total_cols):
@@ -687,7 +688,7 @@
     edge = band * rows
     conv, low, high = kernel_call(
         functools.partial(gram_kernel, rows, band, scale),
-        [f32(6 * rows, 2 * LANES), f32(edge, 3 * edge), f32(edge, 3 * edge)],
+        [f32(6 * rows, 24 * rows), f32(edge, 3 * edge), f32(edge, 3 * edge)],
         [VMEM_SPEC] * 3 + [ANY_SPEC],
         [],
         "gram",

time: 35.5 us -> 35.4 us (level)
  no operation moved by 1% of the time
where the time goes in v13:
time: 35.4 us; the launch traced here: 35.2 us
  starting transfers between devices  14.3 us (40%)
  waiting for transfers between devices  12.3 us (35%)
  Pallas kernels  8.47 us (24%)
    ppermute x12, starting transfers between devices, move(): return lax.ppermute(value, ('wide', 'grp'), pairs)  14.3 us
    ppermute x12, waiting for transfers between devices, move(): return lax.ppermute(value, ('wide', 'grp'), pairs)  12.3 us
    pallas_call x1, Pallas kernels, summed_plan(): kernel_call(functools.partial(fetch_kernel, views, rows, band, scale), [f...  3.35 us
    pallas_call x1, Pallas kernels, summed_plan(): kernel_call(functools.partial(own_kernel, views, rows, band), f32(slices,...  2.05 us
    pallas_call x1, Pallas kernels, summed_plan(): kernel_call(functools.partial(finish_kernel, band, slices, cols), [quarte...  0.92 us
    pallas_call x1, Pallas kernels, summed_plan(): kernel_call(functools.partial(gram_kernel, rows, band, scale), [f32(6 * r...  0.79 us
  transfers between devices with their start and end apart: 12, of which 7 were waited for; matrix products, arithmetic and copies ran while one was open for 0% of the time, Pallas kernels for 10%

profile of v13, /device:TPU:0, one launch (start us, length us, event | category | flops | bytes accessed | tf_op | source)
XLA Modules:
  0.0 35.2 jit_solution(11964825993142722636)
XLA Ops:
  0.0 3.4 %other_share.1 = (f32[17,8,1152]{2,1,0:T(8,128)S(1)}, f32[2,17,11,8,128]{4,3,2,1,0:T(8,128)S(1)}, f32[56,144]{1,0:T(8,128)S(1)}, f32[1,4,2048]{2,1,0:T(4,128)S(1)}) custom-call(f32[512]{0:T(512)} %constant.6.clone.tan_hbm, s32[512]{0:T(512)} %drift_hbm.1, f32[16,2,16,8,128]{4,3,2,1,0:T(8,128)} %bitcast.5, f32[1,4,2048]{2,1,0:T(4,128)} %vol_hbm.1), custom_call_target="tpu_custom_call" | custom-call | flops 1000000000 | tf_op jit(solution)/shard_map/other_share/pallas_call | solution.py:642
  3.4 0.5 %collective-permute-start = (f32[17,8,1152]{2,1,0:T(8,128)S(1)}, f32[17,8,1152]{2,1,0:T(8,128)S(1)}, u32[]{:S(2)}, u32[]{:S(2)}) collective-permute-start(f32[17,8,1152]{2,1,0:T(8,128)S(1)} %get-tuple-element.29), channel_id=1, source_target_pairs={{0,2},{1,3},{2,0},{3,1},{4,6},{5,7},{6,4},{7,5},{8,10},{9,11},{10,... | collective-permute-start | bytes 1880072 | tf_op jit(solution)/shard_map/ppermute | solution.py:176
  3.9 2.1 %own_share.1.own_ref = f32[16,8,1152]{2,1,0:T(8,128)S(1)} custom-call(f32[2,17,11,8,128]{4,3,2,1,0:T(8,128)S(1)} %get-tuple-element.27.buf, f32[56,144]{1,0:T(8,128)S(1)} %get-tuple-element.28.weights_ref), custom_call_target="tpu_custom_call" | custom-call | flops 1000000000 | tf_op jit(solution)/shard_map/own_share/pallas_call | solution.py:659
  5.9 0.0 copy-start
  5.9 0.0 copy-start.1
  6.0 0.0 copy-start.2
  6.0 0.0 collective-permute-done.got_ref
  6.0 0.1 plane_pack.1
  6.1 3.6 %collective-permute-start.2 = (f32[40,8,128]{2,1,0:T(8,128)S(1)}, f32[40,8,128]{2,1,0:T(8,128)S(1)}, u32[]{:S(2)}, u32[]{:S(2)}) collective-permute-start(f32[40,8,128]{2,1,0:T(8,128)S(1)} %get-tuple-element.37), channel_id=1, source_target_pairs={{0,5},{1,4},{2,18},{3,19},{4,1},{5,0},{6,22},{7,23},{8,13},{9,12},... | collective-permute-start | bytes 491528 | tf_op jit(solution)/shard_map/ppermute | solution.py:176
  9.7 0.5 %collective-permute-start.3 = (f32[40,8,128]{2,1,0:T(8,128)S(1)}, f32[40,8,128]{2,1,0:T(8,128)S(1)}, u32[]{:S(2)}, u32[]{:S(2)}) collective-permute-start(f32[40,8,128]{2,1,0:T(8,128)S(1)} %get-tuple-element.38), channel_id=1, source_target_pairs={{0,1},{1,0},{2,26},{3,27},{4,5},{5,4},{6,30},{7,31},{8,9},{9,8},{1... | collective-permute-start | bytes 491528 | tf_op jit(solution)/shard_map/ppermute | solution.py:176
  10.2 0.1 collective-permute-start.4
  10.3 0.1 volume_pack.1
  10.4 2.0 %collective-permute-start.1 = (f32[8,640]{1,0:T(8,128)S(1)}, f32[8,640]{1,0:T(8,128)S(1)}, u32[]{:S(2)}, u32[]{:S(2)}) collective-permute-start(f32[8,640]{1,0:T(8,128)S(1)} %get-tuple-element.32), channel_id=1, source_target_pairs={{0,1},{1,0},{2,3},{3,2},{4,5},{5,4},{6,7},{7,6},{8,9},{9,8},{10,11... | collective-permute-start | bytes 61448 | tf_op jit(solution)/shard_map/ppermute | solution.py:176
  12.4 0.0 copy-done
  12.4 0.0 copy-done.1
  12.4 0.0 copy-done.2
  12.4 0.8 %gram.1 = (f32[48,192]{1,0:T(8,128)S(1)}, f32[80,240]{1,0:T(8,128)S(1)}, f32[80,240]{1,0:T(8,128)S(1)}) custom-call(f32[1,512]{1,0:T(1,128)S(1)} %copy-done.2, f32[1,512]{1,0:T(1,128)S(1)} %copy-done.1, s32[1,512]{1,0:T(1,128)S(1)} %bitcast.4, f32[40,8,128]{2,1,0:T(8,128)S(1)} %get-tuple-element.33.after_ref.mine), custom_call_target="tpu_custom_call" | custom-call | tf_op jit(solution)/shard_map/gram/pallas_call | solution.py:689
  13.2 0.0 collective-permute-done.2.got_1
  13.2 2.0 %collective-permute-done.3.got_2 = f32[40,8,128]{2,1,0:T(8,128)S(1)} collective-permute-done((f32[40,8,128]{2,1,0:T(8,128)S(1)}, f32[40,8,128]{2,1,0:T(8,128)S(1)}, u32[]{:S(2)}, u32[]{:S(2)}) %collective-permute-start.3) | collective-permute-done | bytes 163872 | tf_op jit(solution)/shard_map/ppermute | solution.py:176
  15.2 0.3 collective-permute-done.4.got_3
  15.5 0.1 middle_pack.1
  15.6 3.7 %collective-permute-start.5 = (f32[2,8,640]{2,1,0:T(8,128)S(1)}, f32[2,8,640]{2,1,0:T(8,128)S(1)}, u32[]{:S(2)}, u32[]{:S(2)}) collective-permute-start(f32[2,8,640]{2,1,0:T(8,128)S(1)} %get-tuple-element.41), channel_id=1, source_target_pairs={{0,24},{1,25},{2,7},{3,6},{4,28},{5,29},{6,3},{7,2},{8,16},{9,17},... | collective-permute-start | bytes 122888 | tf_op jit(solution)/shard_map/ppermute | solution.py:176
  19.2 0.0 collective-permute-start.6
  19.2 0.8 %collective-permute-start.7 = (f32[2,8,640]{2,1,0:T(8,128)S(1)}, f32[2,8,640]{2,1,0:T(8,128)S(1)}, u32[]{:S(2)}, u32[]{:S(2)}) collective-permute-start(f32[2,8,640]{2,1,0:T(8,128)S(1)} %get-tuple-element.43), channel_id=1, source_target_pairs={{0,8},{1,9},{2,3},{3,2},{4,12},{5,13},{6,7},{7,6},{8,0},{9,1},{10,... | collective-permute-start | bytes 122888 | tf_op jit(solution)/shard_map/ppermute | solution.py:176
  20.0 0.0 collective-permute-done.1.vol_got
  20.0 0.4 %first_normal.1.first_ref = f32[2,8,640]{2,1,0:T(8,128)S(1)} custom-call(f32[8,640]{1,0:T(8,128)S(1)} %get-tuple-element.31.vol_mine, f32[8,640]{1,0:T(8,128)S(1)} %collective-permute-done.1.vol_got, f32[48,192]{1,0:T(8,128)S(1)} %get-tuple-element.34.conv_ref, f32[80,240]{1,0:T(8,128)S(1)} %get-tuple-element.35.low_ref, ...), custom_call_target="tpu_custom_call" | custom-call | flops 1000000000 | tf_op jit(solution)/shard_map/first_normal/pallas_call | solution.py:709
  20.5 1.0 %collective-permute-done.5.got_1 = f32[2,8,640]{2,1,0:T(8,128)S(1)} collective-permute-done((f32[2,8,640]{2,1,0:T(8,128)S(1)}, f32[2,8,640]{2,1,0:T(8,128)S(1)}, u32[]{:S(2)}, u32[]{:S(2)}) %collective-permute-start.5) | collective-permute-done | bytes 40992 | tf_op jit(solution)/shard_map/ppermute | solution.py:176
  21.4 2.7 %collective-permute-done.6.got_2 = f32[2,8,640]{2,1,0:T(8,128)S(1)} collective-permute-done((f32[2,8,640]{2,1,0:T(8,128)S(1)}, f32[2,8,640]{2,1,0:T(8,128)S(1)}, u32[]{:S(2)}, u32[]{:S(2)}) %collective-permute-start.6) | collective-permute-done | bytes 40992 | tf_op jit(solution)/shard_map/ppermute | solution.py:176
  24.1 0.0 collective-permute-done.7.got_3
  24.2 0.1 collective-permute-start.8
  24.2 1.5 %collective-permute-start.9 = (f32[3,8,640]{2,1,0:T(8,128)S(1)}, f32[3,8,640]{2,1,0:T(8,128)S(1)}, u32[]{:S(2)}, u32[]{:S(2)}) collective-permute-start(f32[3,8,640]{2,1,0:T(8,128)S(1)} %get-tuple-element.46), channel_id=1, source_target_pairs={{0,4},{1,5},{2,6},{3,7},{4,0},{5,1},{6,2},{7,3},{8,12},{9,13},{10,... | collective-permute-start | bytes 184328 | tf_op jit(solution)/shard_map/ppermute | solution.py:176
  25.7 0.0 collective-permute-done.8.got_diag
  25.7 2.9 %collective-permute-done.9.got_x = f32[3,8,640]{2,1,0:T(8,128)S(1)} collective-permute-done((f32[3,8,640]{2,1,0:T(8,128)S(1)}, f32[3,8,640]{2,1,0:T(8,128)S(1)}, u32[]{:S(2)}, u32[]{:S(2)}) %collective-permute-start.9) | collective-permute-done | bytes 61472 | tf_op jit(solution)/shard_map/ppermute | solution.py:176
  28.7 0.9 %finish.1 = (f32[8,512]{1,0:T(8,128)S(1)}, f32[8,512]{1,0:T(8,128)S(1)}) custom-call(f32[4,8,640]{2,1,0:T(8,128)S(1)} %get-tuple-element.44.mine, f32[3,8,640]{2,1,0:T(8,128)S(1)} %collective-permute-done.8.got_diag, f32[3,8,640]{2,1,0:T(8,128)S(1)} %collective-permute-done.9.got_x, f32[48,192]{1,0:T(8,128)S(1)} %get-tuple-element.34.conv_ref, ...), custom_call_target="tpu_custom_call" | custom-call | tf_op jit(solution)/shard_map/finish/pallas_call | solution.py:731
  29.6 0.1 collective-permute-start.10
  29.7 1.2 %collective-permute-done.10.got_ref = f32[8,512]{1,0:T(8,128)S(1)} collective-permute-done((f32[8,512]{1,0:T(8,128)S(1)}, f32[8,512]{1,0:T(8,128)S(1)}, u32[]{:S(2)}, u32[]{:S(2)}) %collective-permute-start.10) | collective-permute-done | bytes 16416 | tf_op jit(solution)/shard_map/ppermute | solution.py:176
  30.8 1.5 %collective-permute-start.11 = (f32[2,4,512]{2,1,0:T(4,128)S(1)}, f32[2,4,512]{2,1,0:T(4,128)S(1)}, u32[]{:S(2)}, u32[]{:S(2)}) collective-permute-start(f32[2,4,512]{2,1,0:T(4,128)S(1)} %result_pack.1), channel_id=1, source_target_pairs={{0,1},{1,0},{2,3},{3,2},{4,5},{5,4},{6,7},{7,6},{8,9},{9,8},{10,11... | collective-permute-start | bytes 49160 | tf_op jit(solution)/shard_map/ppermute | solution.py:176
  32.4 2.2 %collective-permute-done.11.got_y = f32[2,4,512]{2,1,0:T(4,128)S(1)} collective-permute-done((f32[2,4,512]{2,1,0:T(4,128)S(1)}, f32[2,4,512]{2,1,0:T(4,128)S(1)}, u32[]{:S(2)}, u32[]{:S(2)}) %collective-permute-start.11) | collective-permute-done | bytes 16416 | tf_op jit(solution)/shard_map/ppermute | solution.py:176
  34.6 0.6 %result.1 = f32[1,4,2048]{2,1,0:T(4,128)} custom-call(f32[8,512]{1,0:T(8,128)S(1)} %get-tuple-element.47.own_ref, f32[8,512]{1,0:T(8,128)S(1)} %collective-permute-done.10.got_ref, f32[2,4,512]{2,1,0:T(4,128)S(1)} %collective-permute-done.11.got_y), custom_call_target="tpu_custom_call" | custom-call | tf_op jit(solution)/shard_map/result/pallas_call | solution.py:741
  (2 shorter events, 0.0 us)
Async XLA Ops:
  3.4 2.6 %collective-permute-start = (f32[17,8,1152]{2,1,0:T(8,128)S(1)}, f32[17,8,1152]{2,1,0:T(8,128)S(1)}, u32[]{:S(2)}, u32[]{:S(2)}) collective-permute-start(f32[17,8,1152]{2,1,0:T(8,128)S(1)} %get-tuple-element.29), channel_id=1, source_target_pairs={{0,2},{1,3},{2,0},{3,1},{4,6},{5,7},{6,4},{7,5},{8,10},{9,11},{10,... | collective-permute-start | bytes 1880072 | tf_op jit(solution)/shard_map/ppermute | solution.py:176
  5.9 6.5 %copy-start = (s32[512]{0:T(512)S(1)}, s32[512]{0:T(512)}, u32[]{:S(2)}) copy-start(s32[512]{0:T(512)} %drift_hbm.1) | copy-start | bytes 6148
  5.9 6.5 %copy-start.1 = (f32[1,512]{1,0:T(1,128)S(1)}, f32[1,512]{1,0:T(1,128)}, u32[]{:S(2)}) copy-start(f32[1,512]{1,0:T(1,128)} %constant.8.clone.sec_ref) | copy-start | bytes 6148
  6.0 6.4 %copy-start.2 = (f32[1,512]{1,0:T(1,128)S(1)}, f32[1,512]{1,0:T(1,128)}, u32[]{:S(2)}) copy-start(f32[1,512]{1,0:T(1,128)} %constant.7.clone.tan_ref) | copy-start | bytes 6148
  6.1 7.1 %collective-permute-start.2 = (f32[40,8,128]{2,1,0:T(8,128)S(1)}, f32[40,8,128]{2,1,0:T(8,128)S(1)}, u32[]{:S(2)}, u32[]{:S(2)}) collective-permute-start(f32[40,8,128]{2,1,0:T(8,128)S(1)} %get-tuple-element.37), channel_id=1, source_target_pairs={{0,5},{1,4},{2,18},{3,19},{4,1},{5,0},{6,22},{7,23},{8,13},{9,12},... | collective-permute-start | bytes 491528 | tf_op jit(solution)/shard_map/ppermute | solution.py:176
  9.7 5.5 %collective-permute-start.3 = (f32[40,8,128]{2,1,0:T(8,128)S(1)}, f32[40,8,128]{2,1,0:T(8,128)S(1)}, u32[]{:S(2)}, u32[]{:S(2)}) collective-permute-start(f32[40,8,128]{2,1,0:T(8,128)S(1)} %get-tuple-element.38), channel_id=1, source_target_pairs={{0,1},{1,0},{2,26},{3,27},{4,5},{5,4},{6,30},{7,31},{8,9},{9,8},{1... | collective-permute-start | bytes 491528 | tf_op jit(solution)/shard_map/ppermute | solution.py:176
  10.2 5.3 %collective-permute-start.4 = (f32[40,8,128]{2,1,0:T(8,128)S(1)}, f32[40,8,128]{2,1,0:T(8,128)S(1)}, u32[]{:S(2)}, u32[]{:S(2)}) collective-permute-start(f32[40,8,128]{2,1,0:T(8,128)S(1)} %get-tuple-element.39), channel_id=1, source_target_pairs={{0,4},{1,5},{2,10},{3,11},{4,0},{5,1},{6,14},{7,15},{8,12},{9,13},... | collective-permute-start | bytes 491528 | tf_op jit(solution)/shard_map/ppermute | solution.py:176
  10.4 9.6 %collective-permute-start.1 = (f32[8,640]{1,0:T(8,128)S(1)}, f32[8,640]{1,0:T(8,128)S(1)}, u32[]{:S(2)}, u32[]{:S(2)}) collective-permute-start(f32[8,640]{1,0:T(8,128)S(1)} %get-tuple-element.32), channel_id=1, source_target_pairs={{0,1},{1,0},{2,3},{3,2},{4,5},{5,4},{6,7},{7,6},{8,9},{9,8},{10,11... | collective-permute-start | bytes 61448 | tf_op jit(solution)/shard_map/ppermute | solution.py:176
  15.6 5.9 %collective-permute-start.5 = (f32[2,8,640]{2,1,0:T(8,128)S(1)}, f32[2,8,640]{2,1,0:T(8,128)S(1)}, u32[]{:S(2)}, u32[]{:S(2)}) collective-permute-start(f32[2,8,640]{2,1,0:T(8,128)S(1)} %get-tuple-element.41), channel_id=1, source_target_pairs={{0,24},{1,25},{2,7},{3,6},{4,28},{5,29},{6,3},{7,2},{8,16},{9,17},... | collective-permute-start | bytes 122888 | tf_op jit(solution)/shard_map/ppermute | solution.py:176
  19.2 4.9 %collective-permute-start.6 = (f32[2,8,640]{2,1,0:T(8,128)S(1)}, f32[2,8,640]{2,1,0:T(8,128)S(1)}, u32[]{:S(2)}, u32[]{:S(2)}) collective-permute-start(f32[2,8,640]{2,1,0:T(8,128)S(1)} %get-tuple-element.42), channel_id=1, source_target_pairs={{0,16},{1,17},{2,6},{3,7},{4,20},{5,21},{6,2},{7,3},{8,24},{9,25},... | collective-permute-start | bytes 122888 | tf_op jit(solution)/shard_map/ppermute | solution.py:176
  19.2 4.9 %collective-permute-start.7 = (f32[2,8,640]{2,1,0:T(8,128)S(1)}, f32[2,8,640]{2,1,0:T(8,128)S(1)}, u32[]{:S(2)}, u32[]{:S(2)}) collective-permute-start(f32[2,8,640]{2,1,0:T(8,128)S(1)} %get-tuple-element.43), channel_id=1, source_target_pairs={{0,8},{1,9},{2,3},{3,2},{4,12},{5,13},{6,7},{7,6},{8,0},{9,1},{10,... | collective-permute-start | bytes 122888 | tf_op jit(solution)/shard_map/ppermute | solution.py:176
  24.2 1.6 %collective-permute-start.8 = (f32[3,8,640]{2,1,0:T(8,128)S(1)}, f32[3,8,640]{2,1,0:T(8,128)S(1)}, u32[]{:S(2)}, u32[]{:S(2)}) collective-permute-start(f32[3,8,640]{2,1,0:T(8,128)S(1)} %get-tuple-element.45), channel_id=1, source_target_pairs={{0,2},{1,3},{2,0},{3,1},{4,8},{5,9},{6,10},{7,11},{8,4},{9,5},{10,... | collective-permute-start | bytes 184328 | tf_op jit(solution)/shard_map/ppermute | solution.py:176
  24.2 4.4 %collective-permute-start.9 = (f32[3,8,640]{2,1,0:T(8,128)S(1)}, f32[3,8,640]{2,1,0:T(8,128)S(1)}, u32[]{:S(2)}, u32[]{:S(2)}) collective-permute-start(f32[3,8,640]{2,1,0:T(8,128)S(1)} %get-tuple-element.46), channel_id=1, source_target_pairs={{0,4},{1,5},{2,6},{3,7},{4,0},{5,1},{6,2},{7,3},{8,12},{9,13},{10,... | collective-permute-start | bytes 184328 | tf_op jit(solution)/shard_map/ppermute | solution.py:176
  29.6 1.2 %collective-permute-start.10 = (f32[8,512]{1,0:T(8,128)S(1)}, f32[8,512]{1,0:T(8,128)S(1)}, u32[]{:S(2)}, u32[]{:S(2)}) collective-permute-start(f32[8,512]{1,0:T(8,128)S(1)} %get-tuple-element.48), channel_id=1, source_target_pairs={{0,2},{1,3},{2,0},{3,1},{4,6},{5,7},{6,4},{7,5},{8,10},{9,11},{10,... | collective-permute-start | bytes 49160 | tf_op jit(solution)/shard_map/ppermute | solution.py:176
  30.8 3.7 %collective-permute-start.11 = (f32[2,4,512]{2,1,0:T(4,128)S(1)}, f32[2,4,512]{2,1,0:T(4,128)S(1)}, u32[]{:S(2)}, u32[]{:S(2)}) collective-permute-start(f32[2,4,512]{2,1,0:T(4,128)S(1)} %result_pack.1), channel_id=1, source_target_pairs={{0,1},{1,0},{2,3},{3,2},{4,5},{5,4},{6,7},{7,6},{8,9},{9,8},{10,11... | collective-permute-start | bytes 49160 | tf_op jit(solution)/shard_map/ppermute | solution.py:176

commit v14 on v13

--- a/solution.py
+++ b/solution.py
@@ -550,7 +550,7 @@
 
 
 def finish_kernel(
-    band, depth, total_cols, mine, got_diag, got_x, conv_ref, low_ref, high_ref, keep_ref, send_ref, done
+    band, depth, total_cols, mine, got_diag, got_x, conv_ref, low_ref, high_ref, keep_ref, send_ref
 ):
     width = mine.shape[2]
     first_col, is_low, is_high = block_place(width, total_cols)
@@ -564,10 +564,10 @@
     back = normal(volumes, conv_ref[...].astype(jnp.bfloat16), low_ref, high_ref, band, is_low, is_high)
     half = [volumes[s] + corr[s] - back[s] for s in range(4)]
     volumes = variation_step(half, lambda w: slice_0 - 1 + w, first_col, depth, total_cols)
-    for s in range(2):
-        done[s] = pltpu.roll(volumes[s], width - HALO, 1)[:, : width - LANES]
-    keep_ref[...] = done[c]
-    send_ref[...] = done[1 - c]
+    kept = jnp.where(c == 0, volumes[0], volumes[1])
+    sent = jnp.where(c == 0, volumes[1], volumes[0])
+    keep_ref[...] = pltpu.roll(kept, width - HALO, 1)[:, : width - LANES]
+    send_ref[...] = pltpu.roll(sent, width - HALO, 1)[:, : width - LANES]
 
 
 def result_pack_kernel(own_ref, got_ref, to_y):
@@ -732,7 +732,7 @@
         functools.partial(finish_kernel, band, slices, cols),
         [quarter, quarter],
         [VMEM_SPEC] * 6,
-        [pltpu.VMEM((2, rows, block), jnp.float32)],
+        [],
         "finish",
     )(mine, got_diag, got_x, conv, low, high)
     swapped = move(send, lambda z, x, c, y: (z, x, 1 - c, y))

time: 35.4 us -> 35.3 us (level)
  no operation moved by 1% of the time
where the time goes in v14:
time: 35.3 us; the launch traced here: 35.1 us
  starting transfers between devices  14.2 us (40%)
  waiting for transfers between devices  12.3 us (35%)
  Pallas kernels  8.47 us (24%)
    ppermute x12, starting transfers between devices, move(): return lax.ppermute(value, ('wide', 'grp'), pairs)  14.2 us
    ppermute x12, waiting for transfers between devices, move(): return lax.ppermute(value, ('wide', 'grp'), pairs)  12.3 us
    pallas_call x1, Pallas kernels, summed_plan(): kernel_call(functools.partial(fetch_kernel, views, rows, band, scale), [f...  3.35 us
    pallas_call x1, Pallas kernels, summed_plan(): kernel_call(functools.partial(own_kernel, views, rows, band), f32(slices,...  2.05 us
    pallas_call x1, Pallas kernels, summed_plan(): kernel_call(functools.partial(finish_kernel, band, slices, cols), [quarte...  0.92 us
    pallas_call x1, Pallas kernels, summed_plan(): kernel_call(functools.partial(gram_kernel, rows, band, scale), [f32(6 * r...  0.79 us
  transfers between devices with their start and end apart: 12, of which 7 were waited for; matrix products, arithmetic and copies ran while one was open for 0% of the time, Pallas kernels for 10%

profile of v14, /device:TPU:0, one launch (start us, length us, event | category | flops | bytes accessed | tf_op | source)
XLA Modules:
  0.0 35.1 jit_solution(10589579463813776848)
XLA Ops:
  0.0 3.4 %other_share.1 = (f32[17,8,1152]{2,1,0:T(8,128)S(1)}, f32[2,17,11,8,128]{4,3,2,1,0:T(8,128)S(1)}, f32[56,144]{1,0:T(8,128)S(1)}, f32[1,4,2048]{2,1,0:T(4,128)S(1)}) custom-call(f32[512]{0:T(512)} %constant.6.clone.tan_hbm, s32[512]{0:T(512)} %drift_hbm.1, f32[16,2,16,8,128]{4,3,2,1,0:T(8,128)} %bitcast.5, f32[1,4,2048]{2,1,0:T(4,128)} %vol_hbm.1), custom_call_target="tpu_custom_call" | custom-call | flops 1000000000 | tf_op jit(solution)/shard_map/other_share/pallas_call | solution.py:642
  3.4 0.5 %collective-permute-start = (f32[17,8,1152]{2,1,0:T(8,128)S(1)}, f32[17,8,1152]{2,1,0:T(8,128)S(1)}, u32[]{:S(2)}, u32[]{:S(2)}) collective-permute-start(f32[17,8,1152]{2,1,0:T(8,128)S(1)} %get-tuple-element.29), channel_id=1, source_target_pairs={{0,2},{1,3},{2,0},{3,1},{4,6},{5,7},{6,4},{7,5},{8,10},{9,11},{10,... | collective-permute-start | bytes 1880072 | tf_op jit(solution)/shard_map/ppermute | solution.py:176
  3.9 2.1 %own_share.1.own_ref = f32[16,8,1152]{2,1,0:T(8,128)S(1)} custom-call(f32[2,17,11,8,128]{4,3,2,1,0:T(8,128)S(1)} %get-tuple-element.27.buf, f32[56,144]{1,0:T(8,128)S(1)} %get-tuple-element.28.weights_ref), custom_call_target="tpu_custom_call" | custom-call | flops 1000000000 | tf_op jit(solution)/shard_map/own_share/pallas_call | solution.py:659
  5.9 0.0 copy-start
  5.9 0.0 copy-start.1
  6.0 0.0 copy-start.2
  6.0 0.0 collective-permute-done.got_ref
  6.0 0.1 plane_pack.1
  6.1 3.6 %collective-permute-start.2 = (f32[40,8,128]{2,1,0:T(8,128)S(1)}, f32[40,8,128]{2,1,0:T(8,128)S(1)}, u32[]{:S(2)}, u32[]{:S(2)}) collective-permute-start(f32[40,8,128]{2,1,0:T(8,128)S(1)} %get-tuple-element.37), channel_id=1, source_target_pairs={{0,5},{1,4},{2,18},{3,19},{4,1},{5,0},{6,22},{7,23},{8,13},{9,12},... | collective-permute-start | bytes 491528 | tf_op jit(solution)/shard_map/ppermute | solution.py:176
  9.7 0.5 %collective-permute-start.3 = (f32[40,8,128]{2,1,0:T(8,128)S(1)}, f32[40,8,128]{2,1,0:T(8,128)S(1)}, u32[]{:S(2)}, u32[]{:S(2)}) collective-permute-start(f32[40,8,128]{2,1,0:T(8,128)S(1)} %get-tuple-element.38), channel_id=1, source_target_pairs={{0,1},{1,0},{2,26},{3,27},{4,5},{5,4},{6,30},{7,31},{8,9},{9,8},{1... | collective-permute-start | bytes 491528 | tf_op jit(solution)/shard_map/ppermute | solution.py:176
  10.2 0.1 collective-permute-start.4
  10.3 0.1 volume_pack.1
  10.4 2.0 %collective-permute-start.1 = (f32[8,640]{1,0:T(8,128)S(1)}, f32[8,640]{1,0:T(8,128)S(1)}, u32[]{:S(2)}, u32[]{:S(2)}) collective-permute-start(f32[8,640]{1,0:T(8,128)S(1)} %get-tuple-element.32), channel_id=1, source_target_pairs={{0,1},{1,0},{2,3},{3,2},{4,5},{5,4},{6,7},{7,6},{8,9},{9,8},{10,11... | collective-permute-start | bytes 61448 | tf_op jit(solution)/shard_map/ppermute | solution.py:176
  12.4 0.0 copy-done
  12.4 0.0 copy-done.1
  12.4 0.0 copy-done.2
  12.4 0.8 %gram.1 = (f32[48,192]{1,0:T(8,128)S(1)}, f32[80,240]{1,0:T(8,128)S(1)}, f32[80,240]{1,0:T(8,128)S(1)}) custom-call(f32[1,512]{1,0:T(1,128)S(1)} %copy-done.2, f32[1,512]{1,0:T(1,128)S(1)} %copy-done.1, s32[1,512]{1,0:T(1,128)S(1)} %bitcast.4, f32[40,8,128]{2,1,0:T(8,128)S(1)} %get-tuple-element.33.after_ref.mine), custom_call_target="tpu_custom_call" | custom-call | tf_op jit(solution)/shard_map/gram/pallas_call | solution.py:689
  13.2 0.0 collective-permute-done.2.got_1
  13.2 2.0 %collective-permute-done.3.got_2 = f32[40,8,128]{2,1,0:T(8,128)S(1)} collective-permute-done((f32[40,8,128]{2,1,0:T(8,128)S(1)}, f32[40,8,128]{2,1,0:T(8,128)S(1)}, u32[]{:S(2)}, u32[]{:S(2)}) %collective-permute-start.3) | collective-permute-done | bytes 163872 | tf_op jit(solution)/shard_map/ppermute | solution.py:176
  15.2 0.3 collective-permute-done.4.got_3
  15.5 0.1 middle_pack.1
  15.6 3.7 %collective-permute-start.5 = (f32[2,8,640]{2,1,0:T(8,128)S(1)}, f32[2,8,640]{2,1,0:T(8,128)S(1)}, u32[]{:S(2)}, u32[]{:S(2)}) collective-permute-start(f32[2,8,640]{2,1,0:T(8,128)S(1)} %get-tuple-element.41), channel_id=1, source_target_pairs={{0,24},{1,25},{2,7},{3,6},{4,28},{5,29},{6,3},{7,2},{8,16},{9,17},... | collective-permute-start | bytes 122888 | tf_op jit(solution)/shard_map/ppermute | solution.py:176
  19.2 0.0 collective-permute-start.6
  19.2 0.8 %collective-permute-start.7 = (f32[2,8,640]{2,1,0:T(8,128)S(1)}, f32[2,8,640]{2,1,0:T(8,128)S(1)}, u32[]{:S(2)}, u32[]{:S(2)}) collective-permute-start(f32[2,8,640]{2,1,0:T(8,128)S(1)} %get-tuple-element.43), channel_id=1, source_target_pairs={{0,8},{1,9},{2,3},{3,2},{4,12},{5,13},{6,7},{7,6},{8,0},{9,1},{10,... | collective-permute-start | bytes 122888 | tf_op jit(solution)/shard_map/ppermute | solution.py:176
  20.0 0.0 collective-permute-done.1.vol_got
  20.0 0.4 %first_normal.1.first_ref = f32[2,8,640]{2,1,0:T(8,128)S(1)} custom-call(f32[8,640]{1,0:T(8,128)S(1)} %get-tuple-element.31.vol_mine, f32[8,640]{1,0:T(8,128)S(1)} %collective-permute-done.1.vol_got, f32[48,192]{1,0:T(8,128)S(1)} %get-tuple-element.34.conv_ref, f32[80,240]{1,0:T(8,128)S(1)} %get-tuple-element.35.low_ref, ...), custom_call_target="tpu_custom_call" | custom-call | flops 1000000000 | tf_op jit(solution)/shard_map/first_normal/pallas_call | solution.py:709
  20.5 1.0 %collective-permute-done.5.got_1 = f32[2,8,640]{2,1,0:T(8,128)S(1)} collective-permute-done((f32[2,8,640]{2,1,0:T(8,128)S(1)}, f32[2,8,640]{2,1,0:T(8,128)S(1)}, u32[]{:S(2)}, u32[]{:S(2)}) %collective-permute-start.5) | collective-permute-done | bytes 40992 | tf_op jit(solution)/shard_map/ppermute | solution.py:176
  21.4 2.7 %collective-permute-done.6.got_2 = f32[2,8,640]{2,1,0:T(8,128)S(1)} collective-permute-done((f32[2,8,640]{2,1,0:T(8,128)S(1)}, f32[2,8,640]{2,1,0:T(8,128)S(1)}, u32[]{:S(2)}, u32[]{:S(2)}) %collective-permute-start.6) | collective-permute-done | bytes 40992 | tf_op jit(solution)/shard_map/ppermute | solution.py:176
  24.1 0.0 collective-permute-done.7.got_3
  24.2 0.1 collective-permute-start.8
  24.2 1.5 %collective-permute-start.9 = (f32[3,8,640]{2,1,0:T(8,128)S(1)}, f32[3,8,640]{2,1,0:T(8,128)S(1)}, u32[]{:S(2)}, u32[]{:S(2)}) collective-permute-start(f32[3,8,640]{2,1,0:T(8,128)S(1)} %get-tuple-element.46), channel_id=1, source_target_pairs={{0,4},{1,5},{2,6},{3,7},{4,0},{5,1},{6,2},{7,3},{8,12},{9,13},{10,... | collective-permute-start | bytes 184328 | tf_op jit(solution)/shard_map/ppermute | solution.py:176
  25.7 0.0 collective-permute-done.8.got_diag
  25.7 2.9 %collective-permute-done.9.got_x = f32[3,8,640]{2,1,0:T(8,128)S(1)} collective-permute-done((f32[3,8,640]{2,1,0:T(8,128)S(1)}, f32[3,8,640]{2,1,0:T(8,128)S(1)}, u32[]{:S(2)}, u32[]{:S(2)}) %collective-permute-start.9) | collective-permute-done | bytes 61472 | tf_op jit(solution)/shard_map/ppermute | solution.py:176
  28.7 0.9 %finish.1 = (f32[8,512]{1,0:T(8,128)S(1)}, f32[8,512]{1,0:T(8,128)S(1)}) custom-call(f32[4,8,640]{2,1,0:T(8,128)S(1)} %get-tuple-element.44.mine, f32[3,8,640]{2,1,0:T(8,128)S(1)} %collective-permute-done.8.got_diag, f32[3,8,640]{2,1,0:T(8,128)S(1)} %collective-permute-done.9.got_x, f32[48,192]{1,0:T(8,128)S(1)} %get-tuple-element.34.conv_ref, ...), custom_call_target="tpu_custom_call" | custom-call | tf_op jit(solution)/shard_map/finish/pallas_call | solution.py:731
  29.6 0.0 collective-permute-start.10
  29.6 1.2 %collective-permute-done.10.got_ref = f32[8,512]{1,0:T(8,128)S(1)} collective-permute-done((f32[8,512]{1,0:T(8,128)S(1)}, f32[8,512]{1,0:T(8,128)S(1)}, u32[]{:S(2)}, u32[]{:S(2)}) %collective-permute-start.10) | collective-permute-done | bytes 16416 | tf_op jit(solution)/shard_map/ppermute | solution.py:176
  30.8 1.5 %collective-permute-start.11 = (f32[2,4,512]{2,1,0:T(4,128)S(1)}, f32[2,4,512]{2,1,0:T(4,128)S(1)}, u32[]{:S(2)}, u32[]{:S(2)}) collective-permute-start(f32[2,4,512]{2,1,0:T(4,128)S(1)} %result_pack.1), channel_id=1, source_target_pairs={{0,1},{1,0},{2,3},{3,2},{4,5},{5,4},{6,7},{7,6},{8,9},{9,8},{10,11... | collective-permute-start | bytes 49160 | tf_op jit(solution)/shard_map/ppermute | solution.py:176
  32.3 2.2 %collective-permute-done.11.got_y = f32[2,4,512]{2,1,0:T(4,128)S(1)} collective-permute-done((f32[2,4,512]{2,1,0:T(4,128)S(1)}, f32[2,4,512]{2,1,0:T(4,128)S(1)}, u32[]{:S(2)}, u32[]{:S(2)}) %collective-permute-start.11) | collective-permute-done | bytes 16416 | tf_op jit(solution)/shard_map/ppermute | solution.py:176
  34.5 0.6 %result.1 = f32[1,4,2048]{2,1,0:T(4,128)} custom-call(f32[8,512]{1,0:T(8,128)S(1)} %get-tuple-element.47.own_ref, f32[8,512]{1,0:T(8,128)S(1)} %collective-permute-done.10.got_ref, f32[2,4,512]{2,1,0:T(4,128)S(1)} %collective-permute-done.11.got_y), custom_call_target="tpu_custom_call" | custom-call | tf_op jit(solution)/shard_map/result/pallas_call | solution.py:741
  (2 shorter events, 0.0 us)
Async XLA Ops:
  3.4 2.6 %collective-permute-start = (f32[17,8,1152]{2,1,0:T(8,128)S(1)}, f32[17,8,1152]{2,1,0:T(8,128)S(1)}, u32[]{:S(2)}, u32[]{:S(2)}) collective-permute-start(f32[17,8,1152]{2,1,0:T(8,128)S(1)} %get-tuple-element.29), channel_id=1, source_target_pairs={{0,2},{1,3},{2,0},{3,1},{4,6},{5,7},{6,4},{7,5},{8,10},{9,11},{10,... | collective-permute-start | bytes 1880072 | tf_op jit(solution)/shard_map/ppermute | solution.py:176
  5.9 6.5 %copy-start = (s32[512]{0:T(512)S(1)}, s32[512]{0:T(512)}, u32[]{:S(2)}) copy-start(s32[512]{0:T(512)} %drift_hbm.1) | copy-start | bytes 6148
  5.9 6.5 %copy-start.1 = (f32[1,512]{1,0:T(1,128)S(1)}, f32[1,512]{1,0:T(1,128)}, u32[]{:S(2)}) copy-start(f32[1,512]{1,0:T(1,128)} %constant.8.clone.sec_ref) | copy-start | bytes 6148
  6.0 6.4 %copy-start.2 = (f32[1,512]{1,0:T(1,128)S(1)}, f32[1,512]{1,0:T(1,128)}, u32[]{:S(2)}) copy-start(f32[1,512]{1,0:T(1,128)} %constant.7.clone.tan_ref) | copy-start | bytes 6148
  6.1 7.1 %collective-permute-start.2 = (f32[40,8,128]{2,1,0:T(8,128)S(1)}, f32[40,8,128]{2,1,0:T(8,128)S(1)}, u32[]{:S(2)}, u32[]{:S(2)}) collective-permute-start(f32[40,8,128]{2,1,0:T(8,128)S(1)} %get-tuple-element.37), channel_id=1, source_target_pairs={{0,5},{1,4},{2,18},{3,19},{4,1},{5,0},{6,22},{7,23},{8,13},{9,12},... | collective-permute-start | bytes 491528 | tf_op jit(solution)/shard_map/ppermute | solution.py:176
  9.7 5.5 %collective-permute-start.3 = (f32[40,8,128]{2,1,0:T(8,128)S(1)}, f32[40,8,128]{2,1,0:T(8,128)S(1)}, u32[]{:S(2)}, u32[]{:S(2)}) collective-permute-start(f32[40,8,128]{2,1,0:T(8,128)S(1)} %get-tuple-element.38), channel_id=1, source_target_pairs={{0,1},{1,0},{2,26},{3,27},{4,5},{5,4},{6,30},{7,31},{8,9},{9,8},{1... | collective-permute-start | bytes 491528 | tf_op jit(solution)/shard_map/ppermute | solution.py:176
  10.2 5.3 %collective-permute-start.4 = (f32[40,8,128]{2,1,0:T(8,128)S(1)}, f32[40,8,128]{2,1,0:T(8,128)S(1)}, u32[]{:S(2)}, u32[]{:S(2)}) collective-permute-start(f32[40,8,128]{2,1,0:T(8,128)S(1)} %get-tuple-element.39), channel_id=1, source_target_pairs={{0,4},{1,5},{2,10},{3,11},{4,0},{5,1},{6,14},{7,15},{8,12},{9,13},... | collective-permute-start | bytes 491528 | tf_op jit(solution)/shard_map/ppermute | solution.py:176
  10.4 9.6 %collective-permute-start.1 = (f32[8,640]{1,0:T(8,128)S(1)}, f32[8,640]{1,0:T(8,128)S(1)}, u32[]{:S(2)}, u32[]{:S(2)}) collective-permute-start(f32[8,640]{1,0:T(8,128)S(1)} %get-tuple-element.32), channel_id=1, source_target_pairs={{0,1},{1,0},{2,3},{3,2},{4,5},{5,4},{6,7},{7,6},{8,9},{9,8},{10,11... | collective-permute-start | bytes 61448 | tf_op jit(solution)/shard_map/ppermute | solution.py:176
  15.6 5.9 %collective-permute-start.5 = (f32[2,8,640]{2,1,0:T(8,128)S(1)}, f32[2,8,640]{2,1,0:T(8,128)S(1)}, u32[]{:S(2)}, u32[]{:S(2)}) collective-permute-start(f32[2,8,640]{2,1,0:T(8,128)S(1)} %get-tuple-element.41), channel_id=1, source_target_pairs={{0,24},{1,25},{2,7},{3,6},{4,28},{5,29},{6,3},{7,2},{8,16},{9,17},... | collective-permute-start | bytes 122888 | tf_op jit(solution)/shard_map/ppermute | solution.py:176
  19.2 4.9 %collective-permute-start.6 = (f32[2,8,640]{2,1,0:T(8,128)S(1)}, f32[2,8,640]{2,1,0:T(8,128)S(1)}, u32[]{:S(2)}, u32[]{:S(2)}) collective-permute-start(f32[2,8,640]{2,1,0:T(8,128)S(1)} %get-tuple-element.42), channel_id=1, source_target_pairs={{0,16},{1,17},{2,6},{3,7},{4,20},{5,21},{6,2},{7,3},{8,24},{9,25},... | collective-permute-start | bytes 122888 | tf_op jit(solution)/shard_map/ppermute | solution.py:176
  19.2 4.9 %collective-permute-start.7 = (f32[2,8,640]{2,1,0:T(8,128)S(1)}, f32[2,8,640]{2,1,0:T(8,128)S(1)}, u32[]{:S(2)}, u32[]{:S(2)}) collective-permute-start(f32[2,8,640]{2,1,0:T(8,128)S(1)} %get-tuple-element.43), channel_id=1, source_target_pairs={{0,8},{1,9},{2,3},{3,2},{4,12},{5,13},{6,7},{7,6},{8,0},{9,1},{10,... | collective-permute-start | bytes 122888 | tf_op jit(solution)/shard_map/ppermute | solution.py:176
  24.2 1.6 %collective-permute-start.8 = (f32[3,8,640]{2,1,0:T(8,128)S(1)}, f32[3,8,640]{2,1,0:T(8,128)S(1)}, u32[]{:S(2)}, u32[]{:S(2)}) collective-permute-start(f32[3,8,640]{2,1,0:T(8,128)S(1)} %get-tuple-element.45), channel_id=1, source_target_pairs={{0,2},{1,3},{2,0},{3,1},{4,8},{5,9},{6,10},{7,11},{8,4},{9,5},{10,... | collective-permute-start | bytes 184328 | tf_op jit(solution)/shard_map/ppermute | solution.py:176
  24.2 4.4 %collective-permute-start.9 = (f32[3,8,640]{2,1,0:T(8,128)S(1)}, f32[3,8,640]{2,1,0:T(8,128)S(1)}, u32[]{:S(2)}, u32[]{:S(2)}) collective-permute-start(f32[3,8,640]{2,1,0:T(8,128)S(1)} %get-tuple-element.46), channel_id=1, source_target_pairs={{0,4},{1,5},{2,6},{3,7},{4,0},{5,1},{6,2},{7,3},{8,12},{9,13},{10,... | collective-permute-start | bytes 184328 | tf_op jit(solution)/shard_map/ppermute | solution.py:176
  29.6 1.2 %collective-permute-start.10 = (f32[8,512]{1,0:T(8,128)S(1)}, f32[8,512]{1,0:T(8,128)S(1)}, u32[]{:S(2)}, u32[]{:S(2)}) collective-permute-start(f32[8,512]{1,0:T(8,128)S(1)} %get-tuple-element.48), channel_id=1, source_target_pairs={{0,2},{1,3},{2,0},{3,1},{4,6},{5,7},{6,4},{7,5},{8,10},{9,11},{10,... | collective-permute-start | bytes 49160 | tf_op jit(solution)/shard_map/ppermute | solution.py:176
  30.8 3.7 %collective-permute-start.11 = (f32[2,4,512]{2,1,0:T(4,128)S(1)}, f32[2,4,512]{2,1,0:T(4,128)S(1)}, u32[]{:S(2)}, u32[]{:S(2)}) collective-permute-start(f32[2,4,512]{2,1,0:T(4,128)S(1)} %result_pack.1), channel_id=1, source_target_pairs={{0,1},{1,0},{2,3},{3,2},{4,5},{5,4},{6,7},{7,6},{8,9},{9,8},{10,11... | collective-permute-start | bytes 49160 | tf_op jit(solution)/shard_map/ppermute | solution.py:176

commit v15 on v14

--- a/solution.py
+++ b/solution.py
@@ -458,9 +458,9 @@
     for volume, piece in zip(volumes, beyond):
         moved = jnp.concatenate([pltpu.roll(volume, (2 * band - j) % width, 1) for j in range(step)], axis=0)
         spread = jnp.dot(conv, right_terms(moved), preferred_element_type=jnp.float32)
-        total = spread[0:rows]
-        for i in range(1, parts):
-            total = total + pltpu.roll(spread[i * rows : (i + 1) * rows], width - step * i, 1)
+        pieces = [spread[0:rows]]
+        pieces += [pltpu.roll(spread[i * rows : (i + 1) * rows], width - step * i, 1) for i in range(1, parts)]
+        total = (pieces[0] + pieces[1]) + (pieces[2] + pieces[3]) + sum(pieces[5:], pieces[4])
         ends = [jnp.where(is_low, piece, 0.0), zero, jnp.where(is_high, piece, 0.0)]
         result.append(total - jnp.concatenate(ends, axis=1))
     return result

time: 35.3 us -> 35.3 us (level)
  no operation moved by 1% of the time
where the time goes in v15:
time: 35.3 us; the launch traced here: 35.1 us
  starting transfers between devices  14.2 us (40%)
  waiting for transfers between devices  12.3 us (35%)
  Pallas kernels  8.47 us (24%)
    ppermute x12, starting transfers between devices, move(): return lax.ppermute(value, ('wide', 'grp'), pairs)  14.2 us
    ppermute x12, waiting for transfers between devices, move(): return lax.ppermute(value, ('wide', 'grp'), pairs)  12.3 us
    pallas_call x1, Pallas kernels, summed_plan(): kernel_call(functools.partial(fetch_kernel, views, rows, band, scale), [f...  3.35 us
    pallas_call x1, Pallas kernels, summed_plan(): kernel_call(functools.partial(own_kernel, views, rows, band), f32(slices,...  2.05 us
    pallas_call x1, Pallas kernels, summed_plan(): kernel_call(functools.partial(finish_kernel, band, slices, cols), [quarte...  0.91 us
    pallas_call x1, Pallas kernels, summed_plan(): kernel_call(functools.partial(gram_kernel, rows, band, scale), [f32(6 * r...  0.79 us
  transfers between devices with their start and end apart: 12, of which 7 were waited for; matrix products, arithmetic and copies ran while one was open for 0% of the time, Pallas kernels for 10%

profile of v15, /device:TPU:0, one launch (start us, length us, event | category | flops | bytes accessed | tf_op | source)
XLA Modules:
  0.0 35.1 jit_solution(16971906185743687046)
XLA Ops:
  0.0 3.4 %other_share.1 = (f32[17,8,1152]{2,1,0:T(8,128)S(1)}, f32[2,17,11,8,128]{4,3,2,1,0:T(8,128)S(1)}, f32[56,144]{1,0:T(8,128)S(1)}, f32[1,4,2048]{2,1,0:T(4,128)S(1)}) custom-call(f32[512]{0:T(512)} %constant.6.clone.tan_hbm, s32[512]{0:T(512)} %drift_hbm.1, f32[16,2,16,8,128]{4,3,2,1,0:T(8,128)} %bitcast.5, f32[1,4,2048]{2,1,0:T(4,128)} %vol_hbm.1), custom_call_target="tpu_custom_call" | custom-call | flops 1000000000 | tf_op jit(solution)/shard_map/other_share/pallas_call | solution.py:642
  3.4 0.5 %collective-permute-start = (f32[17,8,1152]{2,1,0:T(8,128)S(1)}, f32[17,8,1152]{2,1,0:T(8,128)S(1)}, u32[]{:S(2)}, u32[]{:S(2)}) collective-permute-start(f32[17,8,1152]{2,1,0:T(8,128)S(1)} %get-tuple-element.29), channel_id=1, source_target_pairs={{0,2},{1,3},{2,0},{3,1},{4,6},{5,7},{6,4},{7,5},{8,10},{9,11},{10,... | collective-permute-start | bytes 1880072 | tf_op jit(solution)/shard_map/ppermute | solution.py:176
  3.9 2.1 %own_share.1.own_ref = f32[16,8,1152]{2,1,0:T(8,128)S(1)} custom-call(f32[2,17,11,8,128]{4,3,2,1,0:T(8,128)S(1)} %get-tuple-element.27.buf, f32[56,144]{1,0:T(8,128)S(1)} %get-tuple-element.28.weights_ref), custom_call_target="tpu_custom_call" | custom-call | flops 1000000000 | tf_op jit(solution)/shard_map/own_share/pallas_call | solution.py:659
  5.9 0.0 copy-start
  5.9 0.0 copy-start.1
  6.0 0.0 copy-start.2
  6.0 0.0 collective-permute-done.got_ref
  6.0 0.1 plane_pack.1
  6.1 3.6 %collective-permute-start.2 = (f32[40,8,128]{2,1,0:T(8,128)S(1)}, f32[40,8,128]{2,1,0:T(8,128)S(1)}, u32[]{:S(2)}, u32[]{:S(2)}) collective-permute-start(f32[40,8,128]{2,1,0:T(8,128)S(1)} %get-tuple-element.37), channel_id=1, source_target_pairs={{0,5},{1,4},{2,18},{3,19},{4,1},{5,0},{6,22},{7,23},{8,13},{9,12},... | collective-permute-start | bytes 491528 | tf_op jit(solution)/shard_map/ppermute | solution.py:176
  9.7 0.5 %collective-permute-start.3 = (f32[40,8,128]{2,1,0:T(8,128)S(1)}, f32[40,8,128]{2,1,0:T(8,128)S(1)}, u32[]{:S(2)}, u32[]{:S(2)}) collective-permute-start(f32[40,8,128]{2,1,0:T(8,128)S(1)} %get-tuple-element.38), channel_id=1, source_target_pairs={{0,1},{1,0},{2,26},{3,27},{4,5},{5,4},{6,30},{7,31},{8,9},{9,8},{1... | collective-permute-start | bytes 491528 | tf_op jit(solution)/shard_map/ppermute | solution.py:176
  10.2 0.1 collective-permute-start.4
  10.3 0.1 volume_pack.1
  10.4 2.0 %collective-permute-start.1 = (f32[8,640]{1,0:T(8,128)S(1)}, f32[8,640]{1,0:T(8,128)S(1)}, u32[]{:S(2)}, u32[]{:S(2)}) collective-permute-start(f32[8,640]{1,0:T(8,128)S(1)} %get-tuple-element.32), channel_id=1, source_target_pairs={{0,1},{1,0},{2,3},{3,2},{4,5},{5,4},{6,7},{7,6},{8,9},{9,8},{10,11... | collective-permute-start | bytes 61448 | tf_op jit(solution)/shard_map/ppermute | solution.py:176
  12.4 0.0 copy-done
  12.4 0.0 copy-done.1
  12.4 0.0 copy-done.2
  12.4 0.8 %gram.1 = (f32[48,192]{1,0:T(8,128)S(1)}, f32[80,240]{1,0:T(8,128)S(1)}, f32[80,240]{1,0:T(8,128)S(1)}) custom-call(f32[1,512]{1,0:T(1,128)S(1)} %copy-done.2, f32[1,512]{1,0:T(1,128)S(1)} %copy-done.1, s32[1,512]{1,0:T(1,128)S(1)} %bitcast.4, f32[40,8,128]{2,1,0:T(8,128)S(1)} %get-tuple-element.33.after_ref.mine), custom_call_target="tpu_custom_call" | custom-call | tf_op jit(solution)/shard_map/gram/pallas_call | solution.py:689
  13.2 0.0 collective-permute-done.2.got_1
  13.2 2.0 %collective-permute-done.3.got_2 = f32[40,8,128]{2,1,0:T(8,128)S(1)} collective-permute-done((f32[40,8,128]{2,1,0:T(8,128)S(1)}, f32[40,8,128]{2,1,0:T(8,128)S(1)}, u32[]{:S(2)}, u32[]{:S(2)}) %collective-permute-start.3) | collective-permute-done | bytes 163872 | tf_op jit(solution)/shard_map/ppermute | solution.py:176
  15.2 0.3 collective-permute-done.4.got_3
  15.5 0.1 middle_pack.1
  15.6 3.7 %collective-permute-start.5 = (f32[2,8,640]{2,1,0:T(8,128)S(1)}, f32[2,8,640]{2,1,0:T(8,128)S(1)}, u32[]{:S(2)}, u32[]{:S(2)}) collective-permute-start(f32[2,8,640]{2,1,0:T(8,128)S(1)} %get-tuple-element.41), channel_id=1, source_target_pairs={{0,24},{1,25},{2,7},{3,6},{4,28},{5,29},{6,3},{7,2},{8,16},{9,17},... | collective-permute-start | bytes 122888 | tf_op jit(solution)/shard_map/ppermute | solution.py:176
  19.2 0.0 collective-permute-start.6
  19.2 0.8 %collective-permute-start.7 = (f32[2,8,640]{2,1,0:T(8,128)S(1)}, f32[2,8,640]{2,1,0:T(8,128)S(1)}, u32[]{:S(2)}, u32[]{:S(2)}) collective-permute-start(f32[2,8,640]{2,1,0:T(8,128)S(1)} %get-tuple-element.43), channel_id=1, source_target_pairs={{0,8},{1,9},{2,3},{3,2},{4,12},{5,13},{6,7},{7,6},{8,0},{9,1},{10,... | collective-permute-start | bytes 122888 | tf_op jit(solution)/shard_map/ppermute | solution.py:176
  20.0 0.0 collective-permute-done.1.vol_got
  20.0 0.4 %first_normal.1.first_ref = f32[2,8,640]{2,1,0:T(8,128)S(1)} custom-call(f32[8,640]{1,0:T(8,128)S(1)} %get-tuple-element.31.vol_mine, f32[8,640]{1,0:T(8,128)S(1)} %collective-permute-done.1.vol_got, f32[48,192]{1,0:T(8,128)S(1)} %get-tuple-element.34.conv_ref, f32[80,240]{1,0:T(8,128)S(1)} %get-tuple-element.35.low_ref, ...), custom_call_target="tpu_custom_call" | custom-call | flops 1000000000 | tf_op jit(solution)/shard_map/first_normal/pallas_call | solution.py:709
  20.5 1.0 %collective-permute-done.5.got_1 = f32[2,8,640]{2,1,0:T(8,128)S(1)} collective-permute-done((f32[2,8,640]{2,1,0:T(8,128)S(1)}, f32[2,8,640]{2,1,0:T(8,128)S(1)}, u32[]{:S(2)}, u32[]{:S(2)}) %collective-permute-start.5) | collective-permute-done | bytes 40992 | tf_op jit(solution)/shard_map/ppermute | solution.py:176
  21.4 2.7 %collective-permute-done.6.got_2 = f32[2,8,640]{2,1,0:T(8,128)S(1)} collective-permute-done((f32[2,8,640]{2,1,0:T(8,128)S(1)}, f32[2,8,640]{2,1,0:T(8,128)S(1)}, u32[]{:S(2)}, u32[]{:S(2)}) %collective-permute-start.6) | collective-permute-done | bytes 40992 | tf_op jit(solution)/shard_map/ppermute | solution.py:176
  24.1 0.0 collective-permute-done.7.got_3
  24.2 0.1 collective-permute-start.8
  24.2 1.5 %collective-permute-start.9 = (f32[3,8,640]{2,1,0:T(8,128)S(1)}, f32[3,8,640]{2,1,0:T(8,128)S(1)}, u32[]{:S(2)}, u32[]{:S(2)}) collective-permute-start(f32[3,8,640]{2,1,0:T(8,128)S(1)} %get-tuple-element.46), channel_id=1, source_target_pairs={{0,4},{1,5},{2,6},{3,7},{4,0},{5,1},{6,2},{7,3},{8,12},{9,13},{10,... | collective-permute-start | bytes 184328 | tf_op jit(solution)/shard_map/ppermute | solution.py:176
  25.7 0.0 collective-permute-done.8.got_diag
  25.7 2.9 %collective-permute-done.9.got_x = f32[3,8,640]{2,1,0:T(8,128)S(1)} collective-permute-done((f32[3,8,640]{2,1,0:T(8,128)S(1)}, f32[3,8,640]{2,1,0:T(8,128)S(1)}, u32[]{:S(2)}, u32[]{:S(2)}) %collective-permute-start.9) | collective-permute-done | bytes 61472 | tf_op jit(solution)/shard_map/ppermute | solution.py:176
  28.7 0.9 %finish.1 = (f32[8,512]{1,0:T(8,128)S(1)}, f32[8,512]{1,0:T(8,128)S(1)}) custom-call(f32[4,8,640]{2,1,0:T(8,128)S(1)} %get-tuple-element.44.mine, f32[3,8,640]{2,1,0:T(8,128)S(1)} %collective-permute-done.8.got_diag, f32[3,8,640]{2,1,0:T(8,128)S(1)} %collective-permute-done.9.got_x, f32[48,192]{1,0:T(8,128)S(1)} %get-tuple-element.34.conv_ref, ...), custom_call_target="tpu_custom_call" | custom-call | tf_op jit(solution)/shard_map/finish/pallas_call | solution.py:731
  29.6 0.0 collective-permute-start.10
  29.6 1.2 %collective-permute-done.10.got_ref = f32[8,512]{1,0:T(8,128)S(1)} collective-permute-done((f32[8,512]{1,0:T(8,128)S(1)}, f32[8,512]{1,0:T(8,128)S(1)}, u32[]{:S(2)}, u32[]{:S(2)}) %collective-permute-start.10) | collective-permute-done | bytes 16416 | tf_op jit(solution)/shard_map/ppermute | solution.py:176
  30.8 1.5 %collective-permute-start.11 = (f32[2,4,512]{2,1,0:T(4,128)S(1)}, f32[2,4,512]{2,1,0:T(4,128)S(1)}, u32[]{:S(2)}, u32[]{:S(2)}) collective-permute-start(f32[2,4,512]{2,1,0:T(4,128)S(1)} %result_pack.1), channel_id=1, source_target_pairs={{0,1},{1,0},{2,3},{3,2},{4,5},{5,4},{6,7},{7,6},{8,9},{9,8},{10,11... | collective-permute-start | bytes 49160 | tf_op jit(solution)/shard_map/ppermute | solution.py:176
  32.3 2.2 %collective-permute-done.11.got_y = f32[2,4,512]{2,1,0:T(4,128)S(1)} collective-permute-done((f32[2,4,512]{2,1,0:T(4,128)S(1)}, f32[2,4,512]{2,1,0:T(4,128)S(1)}, u32[]{:S(2)}, u32[]{:S(2)}) %collective-permute-start.11) | collective-permute-done | bytes 16416 | tf_op jit(solution)/shard_map/ppermute | solution.py:176
  34.5 0.6 %result.1 = f32[1,4,2048]{2,1,0:T(4,128)} custom-call(f32[8,512]{1,0:T(8,128)S(1)} %get-tuple-element.47.own_ref, f32[8,512]{1,0:T(8,128)S(1)} %collective-permute-done.10.got_ref, f32[2,4,512]{2,1,0:T(4,128)S(1)} %collective-permute-done.11.got_y), custom_call_target="tpu_custom_call" | custom-call | tf_op jit(solution)/shard_map/result/pallas_call | solution.py:741
  (2 shorter events, 0.0 us)
Async XLA Ops:
  3.4 2.6 %collective-permute-start = (f32[17,8,1152]{2,1,0:T(8,128)S(1)}, f32[17,8,1152]{2,1,0:T(8,128)S(1)}, u32[]{:S(2)}, u32[]{:S(2)}) collective-permute-start(f32[17,8,1152]{2,1,0:T(8,128)S(1)} %get-tuple-element.29), channel_id=1, source_target_pairs={{0,2},{1,3},{2,0},{3,1},{4,6},{5,7},{6,4},{7,5},{8,10},{9,11},{10,... | collective-permute-start | bytes 1880072 | tf_op jit(solution)/shard_map/ppermute | solution.py:176
  5.9 6.5 %copy-start = (s32[512]{0:T(512)S(1)}, s32[512]{0:T(512)}, u32[]{:S(2)}) copy-start(s32[512]{0:T(512)} %drift_hbm.1) | copy-start | bytes 6148
  5.9 6.5 %copy-start.1 = (f32[1,512]{1,0:T(1,128)S(1)}, f32[1,512]{1,0:T(1,128)}, u32[]{:S(2)}) copy-start(f32[1,512]{1,0:T(1,128)} %constant.8.clone.sec_ref) | copy-start | bytes 6148
  6.0 6.4 %copy-start.2 = (f32[1,512]{1,0:T(1,128)S(1)}, f32[1,512]{1,0:T(1,128)}, u32[]{:S(2)}) copy-start(f32[1,512]{1,0:T(1,128)} %constant.7.clone.tan_ref) | copy-start | bytes 6148
  6.1 7.1 %collective-permute-start.2 = (f32[40,8,128]{2,1,0:T(8,128)S(1)}, f32[40,8,128]{2,1,0:T(8,128)S(1)}, u32[]{:S(2)}, u32[]{:S(2)}) collective-permute-start(f32[40,8,128]{2,1,0:T(8,128)S(1)} %get-tuple-element.37), channel_id=1, source_target_pairs={{0,5},{1,4},{2,18},{3,19},{4,1},{5,0},{6,22},{7,23},{8,13},{9,12},... | collective-permute-start | bytes 491528 | tf_op jit(solution)/shard_map/ppermute | solution.py:176
  9.7 5.5 %collective-permute-start.3 = (f32[40,8,128]{2,1,0:T(8,128)S(1)}, f32[40,8,128]{2,1,0:T(8,128)S(1)}, u32[]{:S(2)}, u32[]{:S(2)}) collective-permute-start(f32[40,8,128]{2,1,0:T(8,128)S(1)} %get-tuple-element.38), channel_id=1, source_target_pairs={{0,1},{1,0},{2,26},{3,27},{4,5},{5,4},{6,30},{7,31},{8,9},{9,8},{1... | collective-permute-start | bytes 491528 | tf_op jit(solution)/shard_map/ppermute | solution.py:176
  10.2 5.3 %collective-permute-start.4 = (f32[40,8,128]{2,1,0:T(8,128)S(1)}, f32[40,8,128]{2,1,0:T(8,128)S(1)}, u32[]{:S(2)}, u32[]{:S(2)}) collective-permute-start(f32[40,8,128]{2,1,0:T(8,128)S(1)} %get-tuple-element.39), channel_id=1, source_target_pairs={{0,4},{1,5},{2,10},{3,11},{4,0},{5,1},{6,14},{7,15},{8,12},{9,13},... | collective-permute-start | bytes 491528 | tf_op jit(solution)/shard_map/ppermute | solution.py:176
  10.4 9.6 %collective-permute-start.1 = (f32[8,640]{1,0:T(8,128)S(1)}, f32[8,640]{1,0:T(8,128)S(1)}, u32[]{:S(2)}, u32[]{:S(2)}) collective-permute-start(f32[8,640]{1,0:T(8,128)S(1)} %get-tuple-element.32), channel_id=1, source_target_pairs={{0,1},{1,0},{2,3},{3,2},{4,5},{5,4},{6,7},{7,6},{8,9},{9,8},{10,11... | collective-permute-start | bytes 61448 | tf_op jit(solution)/shard_map/ppermute | solution.py:176
  15.6 5.9 %collective-permute-start.5 = (f32[2,8,640]{2,1,0:T(8,128)S(1)}, f32[2,8,640]{2,1,0:T(8,128)S(1)}, u32[]{:S(2)}, u32[]{:S(2)}) collective-permute-start(f32[2,8,640]{2,1,0:T(8,128)S(1)} %get-tuple-element.41), channel_id=1, source_target_pairs={{0,24},{1,25},{2,7},{3,6},{4,28},{5,29},{6,3},{7,2},{8,16},{9,17},... | collective-permute-start | bytes 122888 | tf_op jit(solution)/shard_map/ppermute | solution.py:176
  19.2 4.9 %collective-permute-start.6 = (f32[2,8,640]{2,1,0:T(8,128)S(1)}, f32[2,8,640]{2,1,0:T(8,128)S(1)}, u32[]{:S(2)}, u32[]{:S(2)}) collective-permute-start(f32[2,8,640]{2,1,0:T(8,128)S(1)} %get-tuple-element.42), channel_id=1, source_target_pairs={{0,16},{1,17},{2,6},{3,7},{4,20},{5,21},{6,2},{7,3},{8,24},{9,25},... | collective-permute-start | bytes 122888 | tf_op jit(solution)/shard_map/ppermute | solution.py:176
  19.2 4.9 %collective-permute-start.7 = (f32[2,8,640]{2,1,0:T(8,128)S(1)}, f32[2,8,640]{2,1,0:T(8,128)S(1)}, u32[]{:S(2)}, u32[]{:S(2)}) collective-permute-start(f32[2,8,640]{2,1,0:T(8,128)S(1)} %get-tuple-element.43), channel_id=1, source_target_pairs={{0,8},{1,9},{2,3},{3,2},{4,12},{5,13},{6,7},{7,6},{8,0},{9,1},{10,... | collective-permute-start | bytes 122888 | tf_op jit(solution)/shard_map/ppermute | solution.py:176
  24.2 1.6 %collective-permute-start.8 = (f32[3,8,640]{2,1,0:T(8,128)S(1)}, f32[3,8,640]{2,1,0:T(8,128)S(1)}, u32[]{:S(2)}, u32[]{:S(2)}) collective-permute-start(f32[3,8,640]{2,1,0:T(8,128)S(1)} %get-tuple-element.45), channel_id=1, source_target_pairs={{0,2},{1,3},{2,0},{3,1},{4,8},{5,9},{6,10},{7,11},{8,4},{9,5},{10,... | collective-permute-start | bytes 184328 | tf_op jit(solution)/shard_map/ppermute | solution.py:176
  24.2 4.4 %collective-permute-start.9 = (f32[3,8,640]{2,1,0:T(8,128)S(1)}, f32[3,8,640]{2,1,0:T(8,128)S(1)}, u32[]{:S(2)}, u32[]{:S(2)}) collective-permute-start(f32[3,8,640]{2,1,0:T(8,128)S(1)} %get-tuple-element.46), channel_id=1, source_target_pairs={{0,4},{1,5},{2,6},{3,7},{4,0},{5,1},{6,2},{7,3},{8,12},{9,13},{10,... | collective-permute-start | bytes 184328 | tf_op jit(solution)/shard_map/ppermute | solution.py:176
  29.6 1.2 %collective-permute-start.10 = (f32[8,512]{1,0:T(8,128)S(1)}, f32[8,512]{1,0:T(8,128)S(1)}, u32[]{:S(2)}, u32[]{:S(2)}) collective-permute-start(f32[8,512]{1,0:T(8,128)S(1)} %get-tuple-element.48), channel_id=1, source_target_pairs={{0,2},{1,3},{2,0},{3,1},{4,6},{5,7},{6,4},{7,5},{8,10},{9,11},{10,... | collective-permute-start | bytes 49160 | tf_op jit(solution)/shard_map/ppermute | solution.py:176
  30.8 3.7 %collective-permute-start.11 = (f32[2,4,512]{2,1,0:T(4,128)S(1)}, f32[2,4,512]{2,1,0:T(4,128)S(1)}, u32[]{:S(2)}, u32[]{:S(2)}) collective-permute-start(f32[2,4,512]{2,1,0:T(4,128)S(1)} %result_pack.1), channel_id=1, source_target_pairs={{0,1},{1,0},{2,3},{3,2},{4,5},{5,4},{6,7},{7,6},{8,9},{9,8},{10,11... | collective-permute-start | bytes 49160 | tf_op jit(solution)/shard_map/ppermute | solution.py:176
